TPU v7x, 32 devices: a whole 2x2x4 slice. The times are simulated.
32 devices in a mesh: lat: 8 (over y, x, core), mem: 4 (over z).
Axes of the slice: x: 2, y: 2, z: 4, core: 2. Of those that a mesh axis runs over, the one named last changes fastest.
Arguments:
- latent: bfloat16 [1, 64, 23040], P(None, 'lat'), may hold values from -6 to 6
- member_seeds: int32 [8], replicated, may hold values from 0 to 1048575
- noise_scale: float32 [64], replicated, may hold values from 0.3 to 1.5
- kernel_one: bfloat16 [3, 3, 64, 32], replicated, may hold values from -0.5 to 0.5
- kernel_two: bfloat16 [3, 3, 32, 16], replicated, may hold values from -0.75 to 0.75
- targets: bfloat16 [1, 256, 23040], P(None, 'lat'), may hold values from -6 to 6
- land_words: int32 [256, 48], P('lat'), may hold values from 0 to 1073741823
- channel_weight: float32 [16], replicated, may hold values from 0.5 to 2
Outputs:
- latent_grad: float32 [1, 64, 23040], P(None, 'lat')
- grad_one: float32 [3, 3, 64, 32], replicated
- grad_two: float32 [3, 3, 32, 16], replicated
All inputs are finite; a program needn't handle non-finite values.
Results may differ from a plain program's by a relative error of at most 0.0031.
The roundings to bfloat16 on the way count: a program that leaves them out, or rounds other values in their place, can miss the bound.
Values may be sent and summed in bfloat16 or wider, within the bound.
No kernel may reach another device: no remote copies, remote signals or barrier semaphores. Data moves between devices by JAX's collectives and lax.ppermute only.
A program may use at most 256 MiB of HBM per device.

v0:
```python
import math

import jax
import jax.numpy as jnp
from jax import lax
from jax.sharding import PartitionSpec as P

SMOOTH = 0.01
HASH_CELL = 1103515245
HASH_SEED = 747796405
HASH_MIX = 277803737


def shifted(array, axis, by):
    peers = lax.axis_size(axis)
    pairs = [(i, i + by) for i in range(peers) if 0 <= i + by < peers]
    return lax.ppermute(array, axis, pairs)


def member_noise(seeds, sample_count, row_ids, span_cols, total_rows):
    sample_ids = jnp.arange(sample_count, dtype=jnp.int32)
    cell_ids = (
        sample_ids[:, None, None, None] * total_rows + row_ids[None, None, :, None]
    ) * span_cols
    cell_ids = cell_ids + jnp.arange(span_cols, dtype=jnp.int32)[None, None, None, :]
    hashed = cell_ids * HASH_CELL + seeds[None, :, None, None] * HASH_SEED
    hashed = jnp.bitwise_xor(hashed, jnp.right_shift(hashed, 15))
    hashed = hashed * HASH_MIX
    hashed = jnp.bitwise_xor(hashed, jnp.right_shift(hashed, 13))
    uniform_val = jnp.bitwise_and(hashed, 65535).astype(jnp.float32) / 65536.0 - 0.5
    return uniform_val * 3.4641016


def unpack_land(words):
    shifts = jnp.arange(30, dtype=jnp.int32)
    bits = jnp.bitwise_and(jnp.right_shift(words[:, :, None], shifts[None, None, :]), 1)
    return bits.reshape(words.shape[0], words.shape[1] * 30).astype(jnp.float32)


def loss_weight(land_words, channel_weight, row_ids, grid_total):
    latitude = math.pi / 2 - math.pi * (row_ids.astype(jnp.float32) + 0.5) / grid_total
    cosine = jnp.cos(latitude)
    land = unpack_land(land_words)
    weight_tensor = (cosine[:, None] * (1.0 + land))[:, :, None] * channel_weight[None, None, :]
    return weight_tensor.reshape(row_ids.shape[0], -1)


def smooth_sign(diff):
    return diff / jnp.sqrt(diff * diff + SMOOTH)


def member_gradients(own, all_members_total, observed_field, weight_tensor):
    count = all_members_total.shape[1]
    own_float = own.astype(jnp.float32)
    summed = jnp.zeros_like(own_float)
    for other_idx in range(count):
        summed = summed + smooth_sign(
            own_float - all_members_total[:, other_idx : other_idx + 1].astype(jnp.float32)
        )
    gradient_field = weight_tensor * (
        smooth_sign(own_float - observed_field.astype(jnp.float32)[:, None]) / count
        - summed / (count * (count - 1))
    )
    return gradient_field.astype(jnp.bfloat16)


def selectors():
    pair_ids = jnp.arange(2)
    row_sel = (
        jnp.arange(3)[None, None, :] == pair_ids[None, :, None] - 2 * pair_ids[:, None, None] + 1
    ).astype(jnp.float32)
    col_sel = (
        jnp.arange(3)[None, None, :]
        == jnp.arange(16)[None, :, None] - 2 * jnp.arange(9)[:, None, None] + 1
    ).astype(jnp.float32)
    return (row_sel, col_sel)


def band_parts(kernel):
    row_sel, col_sel = selectors()
    chan_in, chan_out = (kernel.shape[2], kernel.shape[3])
    banded = jnp.einsum(
        "rak,cbl,klio->rciabo",
        row_sel,
        col_sel,
        kernel.astype(jnp.float32),
        precision=lax.Precision.HIGHEST,
    )
    banded = banded.reshape(2, 9, chan_in, 2, 16 * chan_out).astype(jnp.bfloat16)
    mains = [
        [
            banded[which_row, :8, :, sub_row].reshape(8 * chan_in, 16 * chan_out)
            for sub_row in range(2)
        ]
        for which_row in range(2)
    ]
    tails = [[banded[which_row, 8, :, sub_row] for sub_row in range(2)] for which_row in range(2)]
    return (mains, tails)


def split_blocks(source_field, chan_in):
    leading = source_field.shape[:-1]
    blocks = source_field.reshape(leading + (source_field.shape[-1] // (8 * chan_in), 8 * chan_in))
    following = jnp.roll(blocks[..., :chan_in], -1, axis=-2)
    return (blocks, following)


def band_product(blocks, following, mains, tails, pair_count):
    halves = []
    for sub_row in range(2):
        total = None
        for which_row in range(2):
            block_rows = blocks[:, :, which_row : which_row + pair_count]
            tail_rows = following[:, :, which_row : which_row + pair_count]
            term = jnp.dot(
                block_rows, mains[which_row][sub_row], preferred_element_type=jnp.float32
            )
            term = term + jnp.dot(
                tail_rows, tails[which_row][sub_row], preferred_element_type=jnp.float32
            )
            total = term if total is None else total + term
        halves.append(total)
    stacked = jnp.stack(halves, axis=3)
    dims = stacked.shape
    return stacked.reshape(dims[:2] + (2 * pair_count, dims[4] * dims[5]))


def sub_rows(field, chan_out, sub_row):
    leading = field.shape[:-2]
    row_count, col_count = (field.shape[-2], field.shape[-1])
    split = field.reshape(
        leading + (row_count // 2, 2, col_count // (16 * chan_out), 16 * chan_out)
    )
    return split[..., sub_row, :, :]


def kernel_grad(blocks, following, grad_rows, chan_in, chan_out):
    halves = [sub_rows(grad_rows, chan_out, sub_row) for sub_row in range(2)]
    pair_count = halves[0].shape[2]
    flats = [half.reshape(-1, half.shape[-1]) for half in halves]
    pieces = []
    for which_row in range(2):
        block_rows = blocks[:, :, which_row : which_row + pair_count].reshape(-1, blocks.shape[-1])
        tail_rows = following[:, :, which_row : which_row + pair_count].reshape(
            -1, following.shape[-1]
        )
        pieces.append(
            jnp.concatenate(
                [
                    lax.dot_general(
                        block_rows,
                        flat,
                        (((0,), (0,)), ((), ())),
                        preferred_element_type=jnp.float32,
                    )
                    for flat in flats
                ],
                axis=1,
            )
        )
        pieces.append(
            jnp.concatenate(
                [
                    lax.dot_general(
                        tail_rows,
                        flat,
                        (((0,), (0,)), ((), ())),
                        preferred_element_type=jnp.float32,
                    )
                    for flat in flats
                ],
                axis=1,
            )
        )
    band_grad = jnp.concatenate(pieces, axis=0)
    row_sel, col_sel = selectors()
    return jnp.einsum(
        "rak,cbl,rciabo->klio",
        row_sel,
        col_sel,
        band_grad.reshape(2, 9, chan_in, 2, 16, chan_out),
        precision=lax.Precision.HIGHEST,
    )


def back_fold(grad_rows, mains, tails, chan_in, chan_out):
    halves = [sub_rows(grad_rows, chan_out, sub_row) for sub_row in range(2)]
    leading = halves[0].shape[:-2]
    block_count = halves[0].shape[-2]
    folded = []
    for which_row in range(2):
        main_part = None
        tail_part = None
        for sub_row in range(2):
            main_term = jnp.dot(
                halves[sub_row], mains[which_row][sub_row].T, preferred_element_type=jnp.float32
            )
            tail_term = jnp.dot(
                halves[sub_row], tails[which_row][sub_row].T, preferred_element_type=jnp.float32
            )
            main_part = main_term if main_part is None else main_part + main_term
            tail_part = tail_term if tail_part is None else tail_part + tail_term
        carried = jnp.roll(tail_part, 1, axis=-2)
        pad_spec = [(0, 0)] * (carried.ndim - 1) + [(0, 7 * chan_in)]
        merged = main_part + jnp.pad(carried, pad_spec)
        folded.append(merged.reshape(leading + (block_count * 8 * chan_in,)))
    return folded


def forward_pass(
    latent_ext,
    seeds,
    noise_scale,
    inside,
    row_ids,
    total_rows,
    parts_one,
    parts_two,
    chan_in,
    middle,
):
    sample_count = latent_ext.shape[0]
    span_cols = latent_ext.shape[2]
    noise = member_noise(seeds, sample_count, row_ids, span_cols, total_rows)
    scale_cols = jnp.tile(noise_scale, span_cols // chan_in)
    source_field = (latent_ext.astype(jnp.float32)[:, None] + noise * scale_cols) * inside[
        None, None, :, None
    ]
    source_field = source_field.astype(jnp.bfloat16)
    padded = jnp.concatenate([source_field, jnp.zeros_like(source_field[:, :, :1])], axis=2)
    blocks_first, follow_first = split_blocks(padded, chan_in)
    rows_one = 2 * latent_ext.shape[1] - 1
    preactivation_field = band_product(
        blocks_first, follow_first, parts_one[0], parts_one[1], padded.shape[2] - 1
    )[:, :, :rows_one]
    activated_field = jax.nn.gelu(preactivation_field).astype(jnp.bfloat16)
    blocks_second, follow_second = split_blocks(activated_field, middle)
    predicted_field = band_product(
        blocks_second, follow_second, parts_two[0], parts_two[1], rows_one - 1
    ).astype(jnp.bfloat16)
    return (
        blocks_first,
        follow_first,
        preactivation_field,
        blocks_second,
        follow_second,
        predicted_field,
    )


def backward(gradient_field, saved, parts_one, parts_two, chan_in, middle, chan_out, stride):
    blocks_first, follow_first, preactivation_field, blocks_second, follow_second = saved
    lead_two, tail_two = back_fold(gradient_field, parts_two[0], parts_two[1], middle, chan_out)
    rows_one = lead_two.shape[2]
    last_act = lead_two[:, :, rows_one - 1] + tail_two[:, :, rows_one - 2]
    _, last_pull = jax.vjp(jax.nn.gelu, preactivation_field[:, :, rows_one - 1])
    last_pre = last_pull(last_act)[0].astype(jnp.bfloat16)[:, :, None]
    rim_grad, rim_pre = shifted((gradient_field[:, :, -1:], last_pre), ("lat", "mem"), stride)
    rim_rows = jnp.concatenate([jnp.zeros_like(rim_grad), rim_grad], axis=2)
    _, rim_tail = back_fold(rim_rows, parts_two[0], parts_two[1], middle, chan_out)
    act_grad = lead_two + jnp.concatenate([rim_tail, tail_two[:, :, :-1]], axis=2)
    _, gelu_pull = jax.vjp(jax.nn.gelu, preactivation_field[:, :, :rows_one])
    pre_grad = gelu_pull(act_grad)[0].astype(jnp.bfloat16)
    second_grad = kernel_grad(blocks_second, follow_second, gradient_field, middle, chan_out)
    second_grad = lax.psum(second_grad, ("lat", "mem"))
    lead_one, tail_one = back_fold(pre_grad, parts_one[0], parts_one[1], chan_in, middle)
    rim_pre_rows = jnp.concatenate([jnp.zeros_like(rim_pre), rim_pre], axis=2)
    _, rim_tail_one = back_fold(rim_pre_rows, parts_one[0], parts_one[1], chan_in, middle)
    source_grad = lead_one + jnp.concatenate([rim_tail_one, tail_one[:, :, :-1]], axis=2)
    first_grad = kernel_grad(blocks_first, follow_first, pre_grad, chan_in, middle)
    first_grad = lax.psum(first_grad, ("lat", "mem"))
    return (source_grad, first_grad, second_grad)


def local(
    latent, member_seeds, noise_scale, kernel_one, kernel_two, targets, land_words, channel_weight
):
    sample_count, rows_zero, _ = latent.shape
    chan_in, middle, chan_out = (kernel_one.shape[2], kernel_one.shape[3], kernel_two.shape[3])
    lat_count = lax.axis_size("lat")
    mem_count = lax.axis_size("mem")
    lat_pos = lax.axis_index("lat")
    mem_pos = lax.axis_index("mem")
    member_list = member_seeds.shape[0]
    local_count = member_list // mem_count
    parts_one = band_parts(kernel_one)
    parts_two = band_parts(kernel_two)
    below = shifted(latent[:, :1], "lat", -1)
    latent_ext = jnp.concatenate([latent, below], axis=1)
    total_rows = rows_zero * lat_count
    rows_two = 4 * rows_zero
    grid_total = rows_two * lat_count
    row_ids = lat_pos * rows_zero + jnp.arange(rows_zero + 1, dtype=jnp.int32)
    inside = (row_ids < total_rows).astype(jnp.float32)
    grid_rows = lat_pos * rows_two + jnp.arange(rows_two, dtype=jnp.int32)
    weight_tensor = loss_weight(land_words, channel_weight, grid_rows, grid_total)
    own_seeds = lax.dynamic_slice_in_dim(member_seeds, mem_pos * local_count, local_count)
    results = forward_pass(
        latent_ext,
        own_seeds,
        noise_scale,
        inside,
        row_ids,
        total_rows,
        parts_one,
        parts_two,
        chan_in,
        middle,
    )
    saved, predicted_field = (results[:5], results[5])
    all_members_total = lax.all_gather(predicted_field, "mem", axis=1, tiled=True)
    gradient_field = member_gradients(predicted_field, all_members_total, targets, weight_tensor)
    source_grad, first_grad, second_grad = backward(
        gradient_field, saved, parts_one, parts_two, chan_in, middle, chan_out, mem_count
    )
    member_total = jnp.sum(source_grad, axis=1)
    latent_grad = lax.psum(member_total, "mem")
    norm_factor = 1.0 / math.sqrt(sample_count * rows_two * lat_count * targets.shape[2])
    return (latent_grad, first_grad * norm_factor, second_grad * norm_factor)


def solution(mesh):
    in_specs = (P(None, "lat", None), P(), P(), P(), P(), P(None, "lat", None), P("lat", None), P())
    out_specs = (P(None, "lat", None), P(), P())
    return jax.shard_map(local, mesh=mesh, in_specs=in_specs, out_specs=out_specs, check_vma=False)
```

profile of v0, /device:TPU:0, one launch (start us, length us, event | category | flops | bytes accessed | tf_op | source)
XLA Modules:
  0.0 735.1 jit_solution(8490729495558101488)
XLA Ops:
  21.4 5.5 copy.372
  69.9 4.9 fusion.92
  74.8 5.0 reshape.1102
  103.0 4.8 convert_element_type.210
  115.7 11.5 %mul.530.clone = f32[32,1440,16]{2,1,0:T(8,128)} broadcast(f32[32,1440]{1,0:T(8,128)} %add_multiply_fusion.1), dimensions={0,1} | broadcast | bytes 3133440 | tf_op jit(solution)/shard_map/mul | solution.py:44
  127.2 16.6 %mul.531 = f32[16,2,90,256]{3,2,1,0:T(8,128)} reshape(f32[32,1440,16]{2,1,0:T(8,128)} %mul.530.clone) | data formatting | bytes 5898240 | tf_op jit(solution)/shard_map/mul | solution.py:44
  150.0 13.7 %bitcast_multiply_fusion = f32[32,23040]{0,1:T(8,128)S(1)} fusion(f32[23040]{0:T(1024)} %mul.573, f32[32,1440]{0,1:T(8,128)} %copy.365), kind=kLoop, calls=%fused_computation.20 | loop fusion | flops 737280 | bytes 3225600 | tf_op jit(solution)/shard_map/mul | solution.py:44
  163.7 6.0 slice.361
  169.7 7.1 copy.586
  200.8 116.6 %all-gather.2.cloned.1.call-done = bf16[1,8,32,23040]{3,2,0,1:T(8,128)(2,1)} async-done(((bf16[1,2,32,23040]{3,2,0,1:T(8,128)(2,1)}), bf16[1,8,32,23040]{3,2,0,1:T(8,128)(2,1)}) %all-gather.2.cloned.1.call-update) | async-done | bytes 11796496 | tf_op jit(solution)/shard_map/all_gather | solution.py:311
  317.4 17.0 %fusion.175 = (f32[32,23040]{1,0:T(8,128)}, f32[32,23040]{1,0:T(8,128)}, f32[32,23040]{1,0:T(8,128)}, f32[32,23040]{1,0:T(8,128)}, f32[32,23040]{1,0:T(8,128)}, ...) fusion(bf16[1,8,32,23040]{3,2,0,1:T(8,128)(2,1)} %all-gather.2., ...), kind=kLoop, calls=%fused_computation.230 | loop fusion | flops 5898240 | bytes 58982400 | tf_op jit(solution)/shard_map/sub | solution.py:58
  359.3 18.4 %fusion.42 = bf16[1,2,16,2,90,256]{5,4,2,1,3,0:T(8,128)(2,1)S(1)} fusion(bf16[1,2,16,1,90,256]{5,4,2,1,3,0:T(8,128)(2,1)} %copy-done.10, bf16[1,2,16,1,90,256]{5,4,2,1,3,0:T(8,128)(2,1)} %copy-done.11, f32[16,2,90,256]{3,2,1,0:T(8,128)} %mul.531, f32[256]{0:T(256)S(1)} %mul.533, f32[16,2,90,256]{3,2,1,0:T(8,128)} %sub.445, f32[16,2,90,256]{3,2,1,0:T(8,128)} %sub.448, ...), kind=kLoop, calls=%fused_computation.61 | loop fusion | flops 77414400 | bytes 35390464 | tf_op jit(solution)/shard_map/convert_element_type | solution.py:64
  426.1 4.6 bitcast_add_fusion
  434.0 20.9 %fusion.70 = (f32[1,2,32,23040]{3,2,1,0:T(8,128)S(1)}, f32[1,2,32,23040]{3,2,1,0:T(8,128)S(1)}, f32[1,2,32,23040]{3,2,1,0:T(8,128)}, f32[1,2,32,23040]{3,2,1,0:T...) fusion(bf16[1,2,32,23040]{3,2,1,0:T(8,128)(2,1)} %convert_element_type.210, ...), kind=kLoop, calls=%fused_computation.90 | loop fusion | flops 58982400 | bytes 64880640 | tf_op jit(solution)/shard_map/add | solution.py:57
  472.2 4.6 reshape.1130
  482.8 5.3 fusion.99
  526.5 4.7 pad_maximum_fusion.1
  531.3 6.3 concatenate.131
  537.7 11.2 %reshape.1125 = f32[2,9,64,2,16,32]{2,1,0,5,4,3:T(8,128)} reshape(f32[1152,1024]{0,1:T(8,128)} %concatenate.131) | data formatting | bytes 9437184 | tf_op jit(solution)/shard_map/reshape | solution.py:181
  548.9 9.7 %fusion.148 = f32[2,64,2,32,3]{1,4,3,2,0:T(4,128)S(1)} fusion(f32[2,9,64,2,16,32]{2,1,0,5,4,3:T(8,128)} %reshape.1125, s32[9,16]{0,1:T(8,128)S(1)} %copy-done.57), kind=kOutput, calls=%fused_computation.196 | convolution fusion | flops 42467760 | bytes 4817472 | tf_op jit(solution)/shard_map/rak,cbl,rciabo->klio/dot_general | solution.py:177
  564.0 5.5 fusion.154
  569.9 38.4 %psum.23 = f32[3,3,32,16]{2,0,1,3:T(4,128)S(1)} all-reduce(f32[3,3,32,16]{2,0,1,3:T(4,128)S(1)} %convolution_bitcast_fusion.2), channel_id=1, replica_groups=mesh['lat'=8,'mem'=4] {'lat','mem'}, use_global_device_ids=true, to_apply=%region_3.4 | all-reduce | flops 4608 | bytes 36864 | tf_op jit(solution)/shard_map/psum | solution.py:265
  609.0 70.8 %all-reduce.14.cloned.1.call-done = f32[3,3,64,32]{2,0,1,3:T(4,128)} async-done(((f32[3,3,64,32]{2,0,1,3:T(4,128)}), f32[3,3,64,32]{2,0,1,3:T(4,128)}) %all-reduce.14.cloned.1.call-update) | async-done | bytes 73744 | tf_op jit(solution)/shard_map/psum | solution.py:271
  681.5 44.8 %all-reduce.12.cloned.1.call-done = f32[1,8,23040]{2,1,0:T(8,128)} async-done(((f32[1,8,23040]{2,1,0:T(8,128)}), f32[1,8,23040]{2,1,0:T(8,128)}) %all-reduce.12.cloned.1.call-update) | async-done | bytes 737296 | tf_op jit(solution)/shard_map/psum | solution.py:317
  (331 shorter events, 265.9 us)
Async XLA Ops:
  7.2 310.2 %all-gather.2.cloned.1.call-start = ((), (), s32[]{:S(2)}) async-start(), calls=%async_computation | async-start | bytes 14745600 | tf_op jit(solution)/shard_map/all_gather | solution.py:311
  8.9 38.4 %collective-permute-start = (bf16[1,1,23040]{2,1,0:T(2,128)(2,1)}, bf16[1,1,23040]{2,1,0:T(2,128)(2,1)}, u32[]{:S(2)}, u32[]{:S(2)}) collective-permute-start(bf16[1,1,23040]{2,1,0:T(2,128)(2,1)} %slice.243), channel_id=1, source_target_pairs={{4,0},{8,4},{12,8},{16,12},{20,16},{24,20},{28,24},{5,1},{9,5},{13... | collective-permute-start | bytes 138248 | tf_op jit(solution)/shard_map/ppermute | solution.py:17
  16.8 14.8 %copy-start.14 = (bf16[2,9,32,2,16,16]{2,5,4,3,1,0:T(8,128)(2,1)}, bf16[2,9,32,2,16,16]{2,5,4,3,1,0:T(8,128)(2,1)S(1)}, u32[]{:S(2)}) copy-start(bf16[2,9,32,2,16,16]{2,5,4,3,1,0:T(8,128)(2,1)S(1)} %copy.389) | copy-start | bytes 1769476
  34.7 22.5 %copy-start.20 = (bf16[1,8,64,1,512]{4,2,1,3,0:T(8,128)(2,1)}, bf16[1,8,64,1,512]{4,2,1,3,0:T(8,128)(2,1)S(1)}, u32[]{:S(2)}) copy-start(bf16[1,8,64,1,512]{4,2,1,3,0:T(8,128)(2,1)S(1)} %copy.382) | copy-start | bytes 1572868
  37.9 8.5 %copy-start.35 = (bf16[1,8,32,1,256]{2,4,3,1,0:T(8,128)(2,1)S(1)}, bf16[1,8,32,1,256]{2,4,3,1,0:T(8,128)(2,1)}, u32[]{:S(2)}) copy-start(bf16[1,8,32,1,256]{2,4,3,1,0:T(8,128)(2,1)} %get-tuple-element.53) | copy-start | bytes 393220
  37.9 9.4 %copy-start.51 = (bf16[1,8,23040]{2,1,0:T(8,128)(2,1)S(1)}, bf16[1,8,23040]{2,1,0:T(8,128)(2,1)}, u32[]{:S(2)}) copy-start(bf16[1,8,23040]{2,1,0:T(8,128)(2,1)} %param.8) | copy-start | bytes 1105924
  38.2 19.6 %copy-start.15 = (bf16[1,8,64,1,512]{4,2,1,3,0:T(8,128)(2,1)}, bf16[1,8,64,1,512]{4,2,1,3,0:T(8,128)(2,1)S(1)}, u32[]{:S(2)}) copy-start(bf16[1,8,64,1,512]{4,2,1,3,0:T(8,128)(2,1)S(1)} %copy.378) | copy-start | bytes 1572868
  38.2 10.0 %copy-start.19 = (s32[9,23040]{1,0:T(8,128)S(1)}, s32[9,23040]{1,0:T(8,128)}, u32[]{:S(2)}) copy-start(s32[9,23040]{1,0:T(8,128)} %add_multiply_fusion) | copy-start | bytes 2488324
  69.9 110.1 %copy-start = (f32[1,2,18,23040]{3,1,2,0:T(2,128)}, f32[1,2,18,23040]{3,1,2,0:T(2,128)S(1)}, u32[]{:S(2)}) copy-start(f32[1,2,18,23040]{3,1,2,0:T(2,128)S(1)} %reshape.1101) | copy-start | bytes 9953284
  107.8 572.0 %all-reduce.14.cloned.1.call-start = ((), (), s32[]{:S(2)}) async-start(), calls=%async_computation.2 | async-start | bytes 393216 | tf_op jit(solution)/shard_map/psum | solution.py:271
  127.2 16.6 %copy-start.62 = (f32[16]{0:T(128)S(1)}, f32[16]{0:T(128)}, u32[]{:S(2)}) copy-start(f32[16]{0:T(128)} %param.15) | copy-start | bytes 196
  184.1 7.5 %copy-start.30 = (bf16[1,2,10,44,64]{4,3,1,2,0:T(8,128)(2,1)S(1)}, bf16[1,2,10,44,64]{4,3,1,2,0:T(8,128)(2,1)}, u32[]{:S(2)}) copy-start(bf16[1,2,10,44,64]{4,3,1,2,0:T(8,128)(2,1)} %copy-done.29) | copy-start | bytes 337924
  359.3 20.7 %copy-start.47 = (bf16[1,8,32,1,256]{4,2,1,3,0:T(8,128)(2,1)S(1)}, bf16[1,8,32,1,256]{4,2,1,3,0:T(8,128)(2,1)}, u32[]{:S(2)}) copy-start(bf16[1,8,32,1,256]{4,2,1,3,0:T(8,128)(2,1)} %copy.390) | copy-start | bytes 393220
  434.0 21.0 %copy-start.55 = (f32[1,23040]{1,0:T(1,128)S(1)}, f32[1,23040]{1,0:T(1,128)}, u32[]{:S(2)}) copy-start(f32[1,23040]{1,0:T(1,128)} %copy.586) | copy-start | bytes 276484
  434.0 31.1 %copy-start.1 = (f32[1,2,18,23040]{3,1,2,0:T(2,128)S(1)}, f32[1,2,18,23040]{3,1,2,0:T(2,128)}, u32[]{:S(2)}) copy-start(f32[1,2,18,23040]{3,1,2,0:T(2,128)} %copy-done) | copy-start | bytes 9953284
  459.4 17.5 %collective-permute-start.1 = (bf16[1,2,1,23040]{3,2,1,0:T(2,128)(2,1)}, bf16[1,2,1,23040]{3,2,1,0:T(2,128)(2,1)}, u32[]{:S(2)}, u32[]{:S(2)}) collective-permute-start(bf16[1,2,1,23040]{3,2,1,0:T(2,128)(2,1)} %multiply_convert_fusion), channel_id=1, source_target_pairs={{0,4},{1,5},{2,6},{3,7},{4,8},{5,9},{6,10},{7,11},{8,12},{9,13},{1... | collective-permute-start | bytes 276488 | tf_op jit(solution)/shard_map/ppermute | solution.py:17
  466.2 55.6 %collective-permute-start.2 = (bf16[1,2,1,23040]{3,1,2,0:T(2,128)(2,1)}, bf16[1,2,1,23040]{3,1,2,0:T(2,128)(2,1)}, u32[]{:S(2)}, u32[]{:S(2)}) collective-permute-start(bf16[1,2,1,23040]{3,1,2,0:T(2,128)(2,1)} %fusion.216), channel_id=1, source_target_pairs={{0,4},{1,5},{2,6},{3,7},{4,8},{5,9},{6,10},{7,11},{8,12},{9,13},{1... | collective-permute-start | bytes 276488 | tf_op jit(solution)/shard_map/ppermute | solution.py:17
  472.2 10.0 %copy-start.43 = (bf16[1,8,32,1,256]{4,2,1,3,0:T(8,128)(2,1)S(1)}, bf16[1,8,32,1,256]{4,2,1,3,0:T(8,128)(2,1)}, u32[]{:S(2)}) copy-start(bf16[1,8,32,1,256]{4,2,1,3,0:T(8,128)(2,1)} %copy.395) | copy-start | bytes 393220
  488.1 6.2 copy-start.16
  537.7 11.2 %copy-start.57 = (s32[9,16]{0,1:T(8,128)S(1)}, s32[9,16]{0,1:T(8,128)}, u32[]{:S(2)}) copy-start(s32[9,16]{0,1:T(8,128)} %copy-done.56) | copy-start | bytes 1732
  548.9 9.8 %copy-start.61 = (s32[2,2]{0,1:T(2,128)S(1)}, s32[2,2]{0,1:T(2,128)}, u32[]{:S(2)}) copy-start(s32[2,2]{0,1:T(2,128)} %copy-done.60) | copy-start | bytes 52
  548.9 11.1 %copy-start.17 = (bf16[1,8,64,1,512]{4,2,1,3,0:T(8,128)(2,1)S(1)}, bf16[1,8,64,1,512]{4,2,1,3,0:T(8,128)(2,1)}, u32[]{:S(2)}) copy-start(bf16[1,8,64,1,512]{4,2,1,3,0:T(8,128)(2,1)} %copy-done.15) | copy-start | bytes 1572868
  548.9 11.4 %copy-start.33 = (bf16[1,8,64,1,512]{4,2,1,3,0:T(8,128)(2,1)S(1)}, bf16[1,8,64,1,512]{4,2,1,3,0:T(8,128)(2,1)}, u32[]{:S(2)}) copy-start(bf16[1,8,64,1,512]{4,2,1,3,0:T(8,128)(2,1)} %copy.380) | copy-start | bytes 1572868
  559.9 166.4 %all-reduce.12.cloned.1.call-start = ((), (), s32[]{:S(2)}) async-start(), calls=%async_computation.1 | async-start | bytes 1474560 | tf_op jit(solution)/shard_map/psum | solution.py:317
  (48 other events, 144.4 us)
Sparse Core Ops, SparseCore 0:
  107.9 209.4 all-gather.1
  560.0 119.7 all-reduce.13
  682.8 43.4 all-reduce.11
where the time goes:
time: 743 us; the launch traced here: 735 us
  waiting for transfers between devices  232 us (31%)
  local copies, waits for them, and re-layouts  223 us (30%)
  other arithmetic  111 us (15%)
  matrix products  108 us (15%)
  blocking collectives  38.4 us (5%)
  between operations  15.1 us (2%)
    all_gather x1, waiting for transfers between devices, local(): lax.all_gather(predicted_field, 'mem', axis=1, tiled=True)  117 us
    psum x1, waiting for transfers between devices, backward(): first_grad = lax.psum(first_grad, ('lat', 'mem'))  70.8 us
    psum x1, waiting for transfers between devices, local(): latent_grad = lax.psum(member_total, 'mem')  44.8 us
    psum x1, blocking collectives, backward(): second_grad = lax.psum(second_grad, ('lat', 'mem'))  38.4 us
    mul x6, local copies, waits for them, and re-layouts, loss_weight(): (cosine[:, None] * (1.0 + land))[:, :, None] * channel_weight[None, None, :]  31.1 us
    sub x8, local copies, waits for them, and re-layouts, member_gradients(): own_float - all_members_total[:, other_idx:other_idx + 1].astype(jnp.floa...  24.8 us
    dot_general x12, matrix products, back_fold(): jnp.dot(halves[sub_row], mains[which_row][sub_row].T, preferred_element_t...  24 us
    convert_element_type x2, other arithmetic, member_gradients(): return gradient_field.astype(jnp.bfloat16)  22.8 us
  transfers between devices with their start and end apart: 6, of which 3 were waited for; matrix products, arithmetic and copies ran while one was open for 26% of the time, Pallas kernels for 0%

commit v1 on v0

v1 whole, which is shorter than its diff:
```python
import functools
import math

import jax
import jax.numpy as jnp
from jax import lax
from jax.experimental import pallas as pl
from jax.experimental.pallas import tpu as pltpu
from jax.sharding import PartitionSpec as P

SMOOTH = 0.01
HASH_CELL = 1103515245
HASH_SEED = 747796405
HASH_MIX = 277803737
LANES = 128
MEM = 8
GELU_A = math.sqrt(2.0 / math.pi)
GELU_B = 0.044715


def shifted(array, axis, by):
    peers = lax.axis_size(axis)
    pairs = [(i, i + by) for i in range(peers) if 0 <= i + by < peers]
    return lax.ppermute(array, axis, pairs)


def iota(shape, axis):
    return lax.broadcasted_iota(jnp.int32, shape, axis)


def lane_table(ref, count):
    lane = iota((8, LANES), 1) % count
    total = jnp.zeros((8, LANES), jnp.float32)
    for k in range(count):
        total = jnp.where(lane == k, ref[k], total)
    return total


def build_band(kernel_ref, band_ref, back_ref):
    chan_in, chan_out = kernel_ref.shape[2], kernel_ref.shape[3]
    cells = LANES // chan_in
    repeat = (iota((chan_out, LANES), 1) % chan_out == iota((chan_out, LANES), 0)).astype(jnp.bfloat16)
    wide = {}
    for a in range(3):
        for b in range(3):
            wide[a, b] = jnp.dot(kernel_ref[a, b], repeat, preferred_element_type=jnp.float32)
    column = iota((chan_in, LANES), 1) // chan_out
    zero = jnp.zeros((chan_in, LANES), jnp.float32)
    for block in range(2):
        for row in range(2):
            for cell in range(cells):
                at = block * 256 + row * LANES + cell * chan_in
                for sub in range(2):
                    a = sub - 2 * row + 1
                    part = zero
                    for q in range(2 * cells):
                        b = q - 2 * (cell + block * cells) + 1
                        if 0 <= a <= 2 and 0 <= b <= 2:
                            part = jnp.where(column == q, wide[a, b], part)
                    band_ref[at : at + chan_in, sub * LANES : (sub + 1) * LANES] = part.astype(jnp.bfloat16)
    for block in range(2):
        square = band_ref[block * 256 : (block + 1) * 256, :].astype(jnp.float32)
        back_ref[block * 256 : (block + 1) * 256, :] = square.T.astype(jnp.bfloat16)


def tap_sums(total, chan_in, chan_out):
    cells = LANES // chan_in
    column = iota((chan_in, LANES), 1) // chan_out
    sums = {}
    for a in range(3):
        row, sub = ((1, 1), (0, 0), (0, 1))[a]
        for b in range(3):
            part = jnp.zeros((chan_in, LANES), jnp.float32)
            for reach in range(cells + 1):
                q = 2 * reach + b - 1
                if 0 <= q < 2 * cells:
                    block, cell = reach // cells, reach % cells
                    at = block * 256 + row * LANES + cell * chan_in
                    piece = total[at : at + chan_in, sub * LANES : (sub + 1) * LANES]
                    part = jnp.where(column == q, piece, part)
            sums[a, b] = part
    return sums


def fold_to(part, chan_out, at):
    fold = (iota((LANES, LANES), 0) % chan_out == iota((LANES, LANES), 1) - at).astype(jnp.float32)
    return jnp.dot(part, fold, precision=lax.Precision.HIGHEST, preferred_element_type=jnp.float32)


def band_kernel(
    half,
    norm,
    seeds,
    scale,
    channel_weight,
    land,
    land_above,
    latent,
    above,
    below,
    targets,
    targets_above,
    kernel_one,
    kernel_two,
    out_lat,
    out_taps,
    lat_rows,
    tgt_rows,
    weight_rows,
    band_one,
    back_one,
    band_two,
    back_two,
    source,
    pre,
    act,
    slope,
    cast,
    fgrad,
    carry,
    pgrad,
    sums,
    acc_one,
    acc_two,
):
    rows = latent.shape[1]
    span = latent.shape[2]
    blocks = span // LANES
    lat_count = lax.axis_size("lat")
    own = blocks // lax.axis_size("mem")
    total_rows = rows * lat_count
    grid_rows = 4 * rows
    grid_total = grid_rows * lat_count
    lat_pos = lax.axis_index("lat")
    mem_pos = lax.axis_index("mem")
    wide = half + 2
    front = half + 1
    chan0, chan1, chan2 = kernel_one.shape[2], kernel_one.shape[3], kernel_two.shape[3]
    f32, bf16 = jnp.float32, jnp.bfloat16

    def block_of(part, t):
        at = mem_pos * own + part * half + t + (blocks - 1)
        at = jnp.where(at >= blocks, at - blocks, at)
        return jnp.where(at >= blocks, at - blocks, at)

    def load_blocks(t, _):
        for part in range(2):
            off = pl.multiple_of(block_of(part, t) * LANES, LANES)
            slot = t * 2 + part
            lat_rows[slot, 0:rows] = latent[0, :, pl.ds(off, LANES)].astype(f32)
            lat_rows[slot, rows : rows + 1] = below[0, :, pl.ds(off, LANES)].astype(f32)
            lat_rows[slot, rows + 1 : rows + 2] = above[0, :, pl.ds(off, LANES)].astype(f32)

            @pl.when(t < front)
            def _():
                tgt_rows[slot, 0:grid_rows] = targets[0, :, pl.ds(off, LANES)].astype(f32)
                tgt_rows[slot, grid_rows : grid_rows + 4] = targets_above[0, :, pl.ds(off, LANES)].astype(f32)

        return 0

    lax.fori_loop(0, wide, load_blocks, 0)

    pad_rows = weight_rows.shape[0]
    grid_row = iota((pad_rows, LANES), 0) + (lat_pos * grid_rows - 4)
    latitude = math.pi / 2 - math.pi * (grid_row.astype(f32) + 0.5) / grid_total
    channels = lane_table(channel_weight, chan2)
    cosine = jnp.where(grid_row >= 0, jnp.cos(latitude), 0.0)
    weight_rows[...] = cosine * (jnp.tile(channels, (pad_rows // 8, 1)) * (1.0 / (MEM * (MEM - 1))))

    build_band(kernel_one, band_one, back_one)
    build_band(kernel_two, band_two, back_two)

    source[rows + 2] = jnp.zeros(source.shape[1:], bf16)
    source[:, wide] = jnp.zeros((source.shape[0],) + source.shape[2:], bf16)
    fgrad[:, 0] = jnp.zeros((2,) + fgrad.shape[2:], bf16)
    carry[...] = jnp.zeros(carry.shape, f32)
    acc_one[...] = jnp.zeros(acc_one.shape, f32)
    acc_two[...] = jnp.zeros(acc_two.shape, f32)

    sublane = iota((8, LANES), 0)
    seed_table = jnp.zeros((8, LANES), jnp.int32)
    for m in range(MEM):
        seed_table = jnp.where(sublane == m, seeds[m], seed_table)
    hash_table = iota((8, LANES), 1) * HASH_CELL + seed_table * HASH_SEED
    scale_table = lane_table(scale, chan0)

    def make_source(i, _):
        row = lat_pos * rows - 1 + i
        inside = jnp.where(row < total_rows, 1.0, 0.0).astype(f32)
        at = jnp.where(i == 0, rows + 1, i - 1)
        for t in range(wide):
            parts = []
            for part in range(2):
                first = (row * span + block_of(part, t) * LANES) * HASH_CELL
                h = hash_table + first
                h = jnp.bitwise_xor(h, jnp.right_shift(h, 15))
                h = h * HASH_MIX
                h = jnp.bitwise_xor(h, jnp.right_shift(h, 13))
                noise = jnp.bitwise_and(h, 65535).astype(f32) * (1.0 / 65536.0) - 0.5
                noise = noise * 3.4641016
                cell = lat_rows[t * 2 + part, pl.ds(at, 1), :]
                parts.append((cell + noise * scale_table) * inside)
            source[i, t] = jnp.concatenate(parts, axis=0).astype(bf16)
        return 0

    lax.fori_loop(0, rows + 2, make_source, 0)

    def operand(ref, i, start, count):
        def piece(r, at):
            return ref[r, pl.ds(at, count)].reshape(count * 16, LANES)

        return jnp.concatenate(
            [piece(i, start), piece(i + 1, start), piece(i, start + 1), piece(i + 1, start + 1)], axis=1
        )

    def first_segment(i, _):
        pre[...] = jnp.dot(operand(source, i, 0, wide), band_one[...], preferred_element_type=f32)
        for t in range(wide):
            for sub in range(2):
                x = pre[t * 16 : (t + 1) * 16, sub * LANES : (sub + 1) * LANES]
                square = x * x
                th = jnp.tanh(x * (GELU_A + (GELU_A * GELU_B) * square))
                plus = 0.5 + 0.5 * th
                act[2 * i + sub, t] = (x * plus).astype(bf16)
                if t < front:
                    d = plus + (x * plus) * (1.0 - th) * (GELU_A + (3.0 * GELU_A * GELU_B) * square)
                    if t == half:
                        d = jnp.where(iota((16, LANES), 0) < 8, d, 0.0)
                    slope[2 * i + sub, t] = d
        return 0

    lax.fori_loop(0, rows + 2, first_segment, 0)

    bit_table = jnp.left_shift(1, iota((8, LANES), 1) // chan2)
    members = front * 16
    owner = iota((48, members), 0)
    group = iota((48, members), 1) // 8
    place = (group % 2) * half + group // 2
    real = (group // 2 > 0) & (place - 1 < own)
    pick_own = (real & (place - 1 == owner)).astype(bf16)
    pick_prev = ((group // 2 < half) & (place == owner)).astype(bf16)
    pick = jnp.concatenate([pick_own, pick_prev], axis=0)

    def land_bits(p, part, t):
        cell = block_of(part, t) * (LANES // chan2)
        word = lax.shift_right_logical(cell * 2185, 16)
        bit = cell - 30 * word
        after = jnp.minimum(word + 1, land.shape[1] - 1)
        inner = p >= 4
        line = jnp.where(inner, p - 4, 0)
        edge = jnp.where(inner, 0, p)
        low = jnp.where(inner, land[line, word], land_above[edge, word])
        high = jnp.where(inner, land[line, after], land_above[edge, after])
        return jnp.bitwise_or(lax.shift_right_logical(low, bit), lax.shift_left(high, 30 - bit))

    def second_segment(j, _):
        taken = operand(act, j, 0, front)
        cast[...] = jnp.dot(taken, band_two[...], preferred_element_type=f32)
        for sub in range(2):
            p = 2 * j + sub
            line = jnp.where(p >= 4, p - 4, p + grid_rows)
            base = jnp.broadcast_to(weight_rows[pl.ds(p, 1), :], (8, LANES))
            twice = base + base
            for t in range(front):
                parts = []
                for part in range(2):
                    if t == half and part == 1:
                        parts.append(jnp.zeros((8, LANES), f32))
                        continue
                    at = t * 16 + part * 8
                    f = cast[at : at + 8, sub * LANES : (sub + 1) * LANES].astype(bf16).astype(f32)
                    y = tgt_rows[t * 2 + part, pl.ds(line, 1), :]
                    d = f - y
                    goal = d * lax.rsqrt(d * d + SMOOTH)
                    gs = []
                    for k in range(1, 5):
                        d = f - pltpu.roll(f, k, 0)
                        gs.append(d * lax.rsqrt(d * d + SMOOTH))
                    back = gs[2]
                    for k in (1, 0):
                        back = gs[k] + pltpu.roll(back, MEM - 1, 0)
                    back = pltpu.roll(back, MEM - 1, 0)
                    spread = (gs[0] + gs[1]) + (gs[2] + gs[3]) - back
                    land_hit = jnp.bitwise_and(land_bits(p, part, t), bit_table) != 0
                    weight = jnp.where(land_hit, twice, base)
                    parts.append(weight * ((MEM - 1.0) * goal - spread))
                fgrad[sub, t + 1] = jnp.concatenate(parts, axis=0).astype(bf16)

        def flat(sub, at, count):
            return fgrad[sub, at : at + count].reshape(count * 16, LANES)

        @pl.when(j >= 2)
        def _():
            g = jnp.concatenate([flat(0, 2, half), flat(1, 2, half)], axis=1)
            x = operand(act, j, 1, half)
            acc_two[...] += lax.dot_general(g, x, (((0,), (0,)), ((), ())), preferred_element_type=f32)

        g = jnp.concatenate([flat(0, 1, front), flat(1, 1, front), flat(0, 0, front), flat(1, 0, front)], axis=1)
        pulled = jnp.dot(g, back_two[...], preferred_element_type=f32)
        grad = pulled[:, :LANES] + carry[...]
        carry[...] = pulled[:, LANES:]
        grad = (grad * slope[j].reshape(members, LANES)).astype(bf16)
        pgrad[j] = grad.reshape(front, 16, LANES)
        sums[j] = jnp.dot(pick, grad, preferred_element_type=f32)
        return 0

    lax.fori_loop(0, 2 * rows + 2, second_segment, 0)

    def first_taps(i, _):
        g = jnp.concatenate(
            [pgrad[2 * i + sub, pl.ds(1, half)].reshape(half * 16, LANES) for sub in range(2)], axis=1
        )
        x = operand(source, i, 1, half)
        acc_one[...] += lax.dot_general(g, x, (((0,), (0,)), ((), ())), preferred_element_type=f32)
        return 0

    lax.fori_loop(1, rows + 1, first_taps, 0)

    z = sums[...].reshape(rows + 1, 2, 96, LANES)
    z = [z[:, sub, at : at + 48].reshape((rows + 1) * 48, LANES) for at in (0, 48) for sub in range(2)]
    z = jnp.concatenate(z, axis=1)
    high = z.astype(bf16)
    low = (z - high.astype(f32)).astype(bf16)
    pulled = jnp.dot(high, back_one[...], preferred_element_type=f32)
    pulled = pulled + jnp.dot(low, back_one[...], preferred_element_type=f32)
    pulled = pulled.reshape(rows + 1, 48, 2 * LANES)
    result = pulled[1:, :, :LANES] + pulled[:-1, :, LANES:]
    out_lat[...] = result[:, :own, :].astype(out_lat.dtype)

    one = tap_sums(acc_one[...].T, chan0, chan1)
    two = tap_sums(acc_two[...].T, chan1, chan2)
    for a in range(3):
        block = fold_to(one[a, 0], chan1, 0) + fold_to(one[a, 1], chan1, chan1) + fold_to(one[a, 2], chan1, 2 * chan1)
        top = fold_to(two[a, 0], chan2, 3 * chan1) + fold_to(two[a, 1], chan2, 3 * chan1 + chan2)
        bottom = fold_to(two[a, 2], chan2, 3 * chan1)
        block = (block + jnp.concatenate([top, bottom], axis=0)) * norm
        out_taps[a * chan0 : (a + 1) * chan0, :] = block


def local(
    latent, member_seeds, noise_scale, kernel_one, kernel_two, targets, land_words, channel_weight
):
    sample_count, rows, span = latent.shape
    chan0, chan1, chan2 = kernel_one.shape[2], kernel_one.shape[3], kernel_two.shape[3]
    lat_count = lax.axis_size("lat")
    own = span // LANES // lax.axis_size("mem")
    half = (own + 1) // 2
    assert sample_count == 1 and member_seeds.shape[0] == MEM and own % 2 == 1
    assert 4 * chan2 == 2 * chan1 == chan0 and chan0 == 64
    below = shifted(latent[:, :1], "lat", -1)
    above = shifted(latent[:, rows - 1 :], "lat", 1)
    targets_above = shifted(targets[:, 4 * rows - 4 :], "lat", 1)
    land_above = shifted(land_words[4 * rows - 4 :], "lat", 1)
    norm = 1.0 / math.sqrt(sample_count * 4 * rows * lat_count * targets.shape[2])
    vmem = pl.BlockSpec(memory_space=pltpu.VMEM)
    smem = pl.BlockSpec(memory_space=pltpu.SMEM)
    f32, bf16 = jnp.float32, jnp.bfloat16
    wide, front = half + 2, half + 1
    lat_grad, taps = pl.pallas_call(
        functools.partial(band_kernel, half, norm),
        in_specs=[smem] * 5 + [vmem] * 7,
        out_specs=[vmem, vmem],
        out_shape=[
            jax.ShapeDtypeStruct((rows, own, LANES), bf16),
            jax.ShapeDtypeStruct((3 * chan0, LANES), f32),
        ],
        scratch_shapes=[
            pltpu.VMEM((2 * wide, rows + 8, LANES), f32),
            pltpu.VMEM((2 * front, 4 * rows + 8, LANES), f32),
            pltpu.VMEM((4 * rows + 8, LANES), f32),
            pltpu.VMEM((512, 256), bf16),
            pltpu.VMEM((512, 256), bf16),
            pltpu.VMEM((512, 256), bf16),
            pltpu.VMEM((512, 256), bf16),
            pltpu.VMEM((rows + 3, wide + 1, 16, LANES), bf16),
            pltpu.VMEM((wide * 16, 2 * LANES), f32),
            pltpu.VMEM((2 * rows + 4, wide, 16, LANES), bf16),
            pltpu.VMEM((2 * rows + 4, front, 16, LANES), f32),
            pltpu.VMEM((front * 16, 2 * LANES), f32),
            pltpu.VMEM((2, front + 1, 16, LANES), bf16),
            pltpu.VMEM((front * 16, LANES), f32),
            pltpu.VMEM((2 * rows + 2, front, 16, LANES), bf16),
            pltpu.VMEM((2 * rows + 2, 96, LANES), f32),
            pltpu.VMEM((256, 512), f32),
            pltpu.VMEM((256, 512), f32),
        ],
        compiler_params=pltpu.CompilerParams(vmem_limit_bytes=56 * 1024 * 1024),
        name="band",
    )(
        member_seeds,
        noise_scale,
        channel_weight,
        land_words,
        land_above,
        latent,
        above,
        below,
        targets,
        targets_above,
        kernel_one,
        kernel_two,
    )
    taps = lax.psum(taps, ("lat", "mem"))
    whole = lax.all_gather(lat_grad, "mem", axis=1, tiled=True)
    latent_grad = whole.astype(f32).reshape(1, rows, span)
    one = taps[:, : 3 * chan1].reshape(3, chan0, 3, chan1).transpose(0, 2, 1, 3)
    two = taps[:, 3 * chan1 :].reshape(3, 2, chan1, 2, chan2)
    two = jnp.stack([two[:, 0, :, 0], two[:, 0, :, 1], two[:, 1, :, 0]], axis=1)
    return (latent_grad, one, two)


def solution(mesh):
    in_specs = (P(None, "lat", None), P(), P(), P(), P(), P(None, "lat", None), P("lat", None), P())
    out_specs = (P(None, "lat", None), P(), P())
    return jax.shard_map(local, mesh=mesh, in_specs=in_specs, out_specs=out_specs, check_vma=False)
```

time: 743 us -> 217 us (0.29)
  local copies, waits for them, and re-layouts: 223 us -> 11.4 us
  waiting for transfers between devices: 232 us -> 121 us
  other arithmetic: 111 us -> 1.55 us
  matrix products: 108 us -> 0 us
  Pallas kernels: 0 us -> 41 us
  blocking collectives: 38.4 us -> 15.2 us
    all_gather x1 -> x0, waiting for transfers between devices: 117 us -> none  [local(): lax.all_gather(predicted_field, 'mem', axis=1, tiled=True)]
    dot_general x64 -> x0, matrix products: 108 us -> none  [the longest x12 24 us: back_fold(): jnp.dot(halves[sub_row], mains[which_row][sub_row].T, preferred_element_t...]
    reshape x19 -> x2, local copies, waits for them, and re-layouts: 49.4 us -> 0.24 us  [the longest x1 0.13 us: local(): two = taps[:, 3 * chan1:].reshape(3, 2, chan1, 2, chan2)]
    pallas_call x0 -> x1, Pallas kernels: none -> 41 us  [local(): pl.pallas_call(functools.partial(band_kernel, half, norm), in_specs=[smem...]
    convert_element_type x9 -> x0, other arithmetic: 40 us -> none  [the longest x2 22.8 us: member_gradients(): return gradient_field.astype(jnp.bfloat16)]
    psum x1 -> x0, blocking collectives: 38.4 us -> none  [backward(): second_grad = lax.psum(second_grad, ('lat', 'mem'))]
    slice x33 -> x7, local copies, waits for them, and re-layouts: 39.7 us -> 3.86 us  [the longest x1 1.09 us: local(): targets_above = shifted(targets[:, 4 * rows - 4:], 'lat', 1)]
    mul x8 -> x0, local copies, waits for them, and re-layouts: 34 us -> none  [the longest x6 31.1 us: loss_weight(): (cosine[:, None] * (1.0 + land))[:, :, None] * channel_weight[None, None, :]]
  transfers between devices with their start and end apart: 6 -> 5, of which waited for: 3 -> 1; matrix products, arithmetic and copies ran while one was open for 26% -> 3% of each run, Pallas kernels for 0% -> 0%
where the time goes in v1:
time: 217 us; the launch traced here: 216 us
  waiting for transfers between devices  121 us (56%)
  Pallas kernels  41 us (19%)
  blocking collectives  15.2 us (7%)
  between operations  14.2 us (7%)
  local copies, waits for them, and re-layouts  11.4 us (5%)
  starting transfers between devices  11.2 us (5%)
    psum x1, waiting for transfers between devices, local(): taps = lax.psum(taps, ('lat', 'mem'))  121 us
    pallas_call x1, Pallas kernels, local(): pl.pallas_call(functools.partial(band_kernel, half, norm), in_specs=[smem...  41 us
    all_gather x1, blocking collectives, local(): whole = lax.all_gather(lat_grad, 'mem', axis=1, tiled=True)  15.2 us
    ppermute x4, starting transfers between devices, shifted(): return lax.ppermute(array, axis, pairs)  11.2 us
    unnamed x11, local copies, waits for them, and re-layouts  5.15 us
  transfers between devices with their start and end apart: 5, of which 1 were waited for; matrix products, arithmetic and copies ran while one was open for 3% of the time, Pallas kernels for 0%

profile of v1, /device:TPU:0, one launch (start us, length us, event | category | flops | bytes accessed | tf_op | source)
XLA Modules:
  0.0 215.8 jit_solution(11529308327455174266)
XLA Ops:
  7.2 1.1 slice.30
  8.3 2.4 %collective-permute-start.3 = (bf16[1,4,23040]{2,1,0:T(4,128)(2,1)S(1)}, bf16[1,4,23040]{2,1,0:T(4,128)(2,1)S(1)}, u32[]{:S(2)}, u32[]{:S(2)}) collective-permute-start(bf16[1,4,23040]{2,1,0:T(4,128)(2,1)S(1)} %slice.30), channel_id=1, source_target_pairs={{0,4},{4,8},{8,12},{12,16},{16,20},{20,24},{24,28},{1,5},{5,9},{9,... | collective-permute-start | bytes 552968 | tf_op jit(solution)/shard_map/ppermute | solution.py:24
  10.7 1.2 fusion
  11.9 4.5 %collective-permute-start.1 = (bf16[1,1,23040]{2,1,0:T(2,128)(2,1)S(1)}, bf16[1,1,23040]{2,1,0:T(2,128)(2,1)S(1)}, u32[]{:S(2)}, u32[]{:S(2)}) collective-permute-start(bf16[1,1,23040]{2,1,0:T(2,128)(2,1)S(1)} %get-tuple-element.23), channel_id=1, source_target_pairs={{0,4},{4,8},{8,12},{12,16},{16,20},{20,24},{24,28},{1,5},{5,9},{9,... | collective-permute-start | bytes 138248 | tf_op jit(solution)/shard_map/ppermute | solution.py:24
  16.4 1.3 collective-permute-start.2
  17.7 0.7 slice.27
  18.4 3.0 %collective-permute-start = (s32[4,48]{1,0:T(4,128)S(1)}, s32[4,48]{1,0:T(4,128)S(1)}, u32[]{:S(2)}, u32[]{:S(2)}) collective-permute-start(s32[4,48]{1,0:T(4,128)S(1)} %slice.27), channel_id=1, source_target_pairs={{0,4},{4,8},{8,12},{12,16},{16,20},{20,24},{24,28},{1,5},{5,9},{9,... | collective-permute-start | bytes 2312 | tf_op jit(solution)/shard_map/ppermute | solution.py:24
  21.5 1.7 copy.52.kernel_one
  23.1 1.5 copy.53.kernel_two
  24.7 0.5 copy-done.3
  25.2 0.1 copy-done.1
  25.3 0.7 copy-done
  26.0 41.0 %band.1 = (bf16[8,45,128]{2,1,0:T(8,128)(2,1)}, f32[192,128]{1,0:T(8,128)}) custom-call(s32[8]{0:T(128)} %seeds.1, f32[64]{0:T(128)} %scale.1, f32[16]{0:T(128)} %channel_weight.1, s32[32,48]{1,0:T(8,128)} %land.1, s32[4,48]{1,0:T(4,128)} %copy-done.3, bf16[1,8,23040]{2,1,0:T(8,128)(2,1)} %latent.1, bf16[1,1,23040]{2,1,0:T(2,128)(2,1)} %copy-done.1, ...), custom_call_target="tpu_custom_call" | custom-call | tf_op jit(solution)/shard_map/band/pallas_call | solution.py:359
  67.0 0.9 copy.54
  67.9 15.2 %all_gather.3 = bf16[8,180,128]{2,0,1:T(8,128)(2,1)S(1)} all-gather(bf16[8,45,128]{2,0,1:T(8,128)(2,1)S(1)} %copy.54), channel_id=1, replica_groups=mesh['lat'=8,'mem'=4] {'mem'}, dimensions={1}, use_global_device_ids=true | all-gather | bytes 460800 | tf_op jit(solution)/shard_map/all_gather | solution.py:404
  83.1 0.9 bitcast_convert_fusion
  84.0 121.3 %all-reduce.2.cloned.1.call-done = f32[192,128]{1,0:T(8,128)} async-done(((f32[192,128]{1,0:T(8,128)}), f32[192,128]{1,0:T(8,128)}) %all-reduce.2.cloned.1.call-update) | async-done | bytes 98320 | tf_op jit(solution)/shard_map/psum | solution.py:403
  205.3 1.0 copy.55
  206.3 0.1 reshape.20
  206.4 0.7 copy.60
  207.1 1.0 slice.37
  208.1 0.1 copy.56
  208.1 0.1 reshape.21
  208.4 0.6 pad_maximum_fusion
  (14 shorter events, 0.2 us)
Async XLA Ops:
  7.2 198.1 %all-reduce.2.cloned.1.call-start = ((), (), s32[]{:S(2)}) async-start(), calls=%async_computation | async-start | bytes 196608 | tf_op jit(solution)/shard_map/psum | solution.py:403
  8.3 16.4 %collective-permute-start.3 = (bf16[1,4,23040]{2,1,0:T(4,128)(2,1)S(1)}, bf16[1,4,23040]{2,1,0:T(4,128)(2,1)S(1)}, u32[]{:S(2)}, u32[]{:S(2)}) collective-permute-start(bf16[1,4,23040]{2,1,0:T(4,128)(2,1)S(1)} %slice.30), channel_id=1, source_target_pairs={{0,4},{4,8},{8,12},{12,16},{16,20},{20,24},{24,28},{1,5},{5,9},{9,... | collective-permute-start | bytes 552968 | tf_op jit(solution)/shard_map/ppermute | solution.py:24
  11.9 12.7 %collective-permute-start.1 = (bf16[1,1,23040]{2,1,0:T(2,128)(2,1)S(1)}, bf16[1,1,23040]{2,1,0:T(2,128)(2,1)S(1)}, u32[]{:S(2)}, u32[]{:S(2)}) collective-permute-start(bf16[1,1,23040]{2,1,0:T(2,128)(2,1)S(1)} %get-tuple-element.23), channel_id=1, source_target_pairs={{0,4},{4,8},{8,12},{12,16},{16,20},{20,24},{24,28},{1,5},{5,9},{9,... | collective-permute-start | bytes 138248 | tf_op jit(solution)/shard_map/ppermute | solution.py:24
  16.4 8.2 %collective-permute-start.2 = (bf16[1,1,23040]{2,1,0:T(2,128)(2,1)S(1)}, bf16[1,1,23040]{2,1,0:T(2,128)(2,1)S(1)}, u32[]{:S(2)}, u32[]{:S(2)}) collective-permute-start(bf16[1,1,23040]{2,1,0:T(2,128)(2,1)S(1)} %get-tuple-element.22), channel_id=1, source_target_pairs={{4,0},{8,4},{12,8},{16,12},{20,16},{24,20},{28,24},{5,1},{9,5},{13... | collective-permute-start | bytes 138248 | tf_op jit(solution)/shard_map/ppermute | solution.py:24
  18.4 6.2 %collective-permute-start = (s32[4,48]{1,0:T(4,128)S(1)}, s32[4,48]{1,0:T(4,128)S(1)}, u32[]{:S(2)}, u32[]{:S(2)}) collective-permute-start(s32[4,48]{1,0:T(4,128)S(1)} %slice.27), channel_id=1, source_target_pairs={{0,4},{4,8},{8,12},{12,16},{16,20},{20,24},{24,28},{1,5},{5,9},{9,... | collective-permute-start | bytes 2312 | tf_op jit(solution)/shard_map/ppermute | solution.py:24
  24.6 0.6 copy-start.3
  24.6 0.6 copy-start.1
  24.6 0.7 copy-start.2
  25.3 0.7 copy-start
Sparse Core Ops, SparseCore 0:
  83.2 122.0 all-reduce.1

commit v2 on v1

--- a/solution.py
+++ b/solution.py
@@ -37,13 +37,15 @@
 
 
 def build_band(kernel_ref, band_ref, back_ref):
-    chan_in, chan_out = kernel_ref.shape[2], kernel_ref.shape[3]
+    chan_out, chan_in = kernel_ref.shape[2], kernel_ref.shape[3]
     cells = LANES // chan_in
     repeat = (iota((chan_out, LANES), 1) % chan_out == iota((chan_out, LANES), 0)).astype(jnp.bfloat16)
     wide = {}
     for a in range(3):
         for b in range(3):
-            wide[a, b] = jnp.dot(kernel_ref[a, b], repeat, preferred_element_type=jnp.float32)
+            wide[a, b] = lax.dot_general(
+                kernel_ref[a, b], repeat, (((0,), (0,)), ((), ())), preferred_element_type=jnp.float32
+            )
     column = iota((chan_in, LANES), 1) // chan_out
     zero = jnp.zeros((chan_in, LANES), jnp.float32)
     for block in range(2):
@@ -63,28 +65,83 @@
         back_ref[block * 256 : (block + 1) * 256, :] = square.T.astype(jnp.bfloat16)
 
 
-def tap_sums(total, chan_in, chan_out):
+def pack_taps(acc_ref, out_ref, first, chan_in, chan_out, norm):
     cells = LANES // chan_in
-    column = iota((chan_in, LANES), 1) // chan_out
-    sums = {}
-    for a in range(3):
+    group = iota((chan_out, LANES), 1) // chan_in
+    packed = None
+    for k in range(9):
+        a, b = divmod(k, 3)
         row, sub = ((1, 1), (0, 0), (0, 1))[a]
-        for b in range(3):
-            part = jnp.zeros((chan_in, LANES), jnp.float32)
-            for reach in range(cells + 1):
-                q = 2 * reach + b - 1
-                if 0 <= q < 2 * cells:
-                    block, cell = reach // cells, reach % cells
-                    at = block * 256 + row * LANES + cell * chan_in
-                    piece = total[at : at + chan_in, sub * LANES : (sub + 1) * LANES]
-                    part = jnp.where(column == q, piece, part)
-            sums[a, b] = part
-    return sums
-
-
-def fold_to(part, chan_out, at):
-    fold = (iota((LANES, LANES), 0) % chan_out == iota((LANES, LANES), 1) - at).astype(jnp.float32)
-    return jnp.dot(part, fold, precision=lax.Precision.HIGHEST, preferred_element_type=jnp.float32)
+        slot = k % cells
+        part = None
+        for reach in range(cells + 1):
+            q = 2 * reach + b - 1
+            if 0 <= q < 2 * cells:
+                block, cell = reach // cells, reach % cells
+                lines = sub * LANES + q * chan_out
+                lanes = block * 256 + row * LANES
+                piece = acc_ref[lines : lines + chan_out, lanes : lanes + LANES]
+                turn = (slot - cell) % cells * chan_in
+                piece = pltpu.roll(piece, turn, 1) if turn else piece
+                part = piece if part is None else part + piece
+        packed = part if slot == 0 else jnp.where(group == slot, part, packed)
+        if slot == cells - 1 or k == 8:
+            at = first + k // cells * chan_out
+            out_ref[at : at + chan_out, :] = packed * norm
+
+
+def window_block(mem_pos, own, half, blocks, part, t):
+    at = mem_pos * own + part * half + t + (blocks - 1)
+    at = jnp.where(at >= blocks, at - blocks, at)
+    return jnp.where(at >= blocks, at - blocks, at)
+
+
+def land_of(words, block, chan):
+    cell = block * (LANES // chan) + iota(words.shape, 1) // chan
+    word = jnp.right_shift(cell * 2185, 16)
+    picked = jnp.take_along_axis(words, word, axis=1, mode="promise_in_bounds")
+    return jnp.bitwise_and(jnp.right_shift(picked, cell - 30 * word), 1).astype(jnp.float32)
+
+
+def edge_kernel(half, chan, latent, targets, land, down, up, words):
+    rows = latent.shape[1]
+    blocks = latent.shape[2] // LANES
+    own = blocks // lax.axis_size("mem")
+    mem_pos = lax.axis_index("mem")
+    words[...] = jnp.zeros(words.shape, jnp.int32)
+    words[:, : land.shape[1]] = land[...]
+    line = iota((8, LANES), 0)
+    for t in range(half + 2):
+        for part in range(2):
+            block = window_block(mem_pos, own, half, blocks, part, t)
+            off = pl.multiple_of(block * LANES, LANES)
+            slot = t * 2 + part
+            cells = latent[0, :, pl.ds(off, LANES)].astype(jnp.float32)
+            aims = targets[0, :, pl.ds(off, LANES)].astype(jnp.float32)
+            mask = land_of(words[...], block, chan)
+            pack = pltpu.roll(cells, 1, 0)
+            pack = jnp.where((line >= 1) & (line <= 3), pltpu.roll(aims, 4, 0), pack)
+            pack = jnp.where((line >= 4) & (line <= 6), pltpu.roll(mask, 7, 0), pack)
+            down[slot] = pack.astype(jnp.bfloat16)
+            up[:, slot * LANES : (slot + 1) * LANES] = cells[0:1].astype(jnp.bfloat16)
+
+
+def place_kernel(own, part0, part1, part2, part3, taps, latent_grad, grad_one, grad_two):
+    mem_pos = lax.axis_index("mem")
+    for k, part in enumerate((part0, part1, part2, part3)):
+        off = pl.multiple_of(jnp.bitwise_xor(mem_pos, k) * own * LANES, LANES)
+        latent_grad[0, :, pl.ds(off, own * LANES)] = part[...].astype(jnp.float32)
+    first = 0
+    for out in (grad_one, grad_two):
+        chan_out, chan_in = out.shape[2], out.shape[3]
+        cells = LANES // chan_in
+        for k in range(9):
+            at = first + k // cells * chan_out
+            block = taps[at : at + chan_out, :]
+            turn = (-(k % cells)) % cells * chan_in
+            block = pltpu.roll(block, turn, 1) if turn else block
+            out[k // 3, k % 3] = block[:, :chan_in]
+        first += -(-9 // cells) * chan_out
 
 
 def band_kernel(
@@ -93,13 +150,11 @@
     seeds,
     scale,
     channel_weight,
-    land,
-    land_above,
     latent,
     above,
     below,
     targets,
-    targets_above,
+    land,
     kernel_one,
     kernel_two,
     out_lat,
@@ -107,6 +162,7 @@
     lat_rows,
     tgt_rows,
     weight_rows,
+    words,
     band_one,
     back_one,
     band_two,
@@ -135,37 +191,36 @@
     mem_pos = lax.axis_index("mem")
     wide = half + 2
     front = half + 1
-    chan0, chan1, chan2 = kernel_one.shape[2], kernel_one.shape[3], kernel_two.shape[3]
+    chan0, chan1, chan2 = kernel_one.shape[3], kernel_two.shape[3], kernel_two.shape[2]
     f32, bf16 = jnp.float32, jnp.bfloat16
 
     def block_of(part, t):
-        at = mem_pos * own + part * half + t + (blocks - 1)
-        at = jnp.where(at >= blocks, at - blocks, at)
-        return jnp.where(at >= blocks, at - blocks, at)
-
-    def load_blocks(t, _):
-        for part in range(2):
-            off = pl.multiple_of(block_of(part, t) * LANES, LANES)
-            slot = t * 2 + part
-            lat_rows[slot, 0:rows] = latent[0, :, pl.ds(off, LANES)].astype(f32)
-            lat_rows[slot, rows : rows + 1] = below[0, :, pl.ds(off, LANES)].astype(f32)
-            lat_rows[slot, rows + 1 : rows + 2] = above[0, :, pl.ds(off, LANES)].astype(f32)
-
-            @pl.when(t < front)
-            def _():
-                tgt_rows[slot, 0:grid_rows] = targets[0, :, pl.ds(off, LANES)].astype(f32)
-                tgt_rows[slot, grid_rows : grid_rows + 4] = targets_above[0, :, pl.ds(off, LANES)].astype(f32)
-
-        return 0
-
-    lax.fori_loop(0, wide, load_blocks, 0)
-
-    pad_rows = weight_rows.shape[0]
-    grid_row = iota((pad_rows, LANES), 0) + (lat_pos * grid_rows - 4)
+        return window_block(mem_pos, own, half, blocks, part, t)
+
+    pad_rows = grid_rows + 8
+    grid_row = iota((pad_rows, LANES), 0)
+    grid_row = jnp.where(grid_row < grid_rows, grid_row, grid_row - (grid_rows + 4)) + lat_pos * grid_rows
     latitude = math.pi / 2 - math.pi * (grid_row.astype(f32) + 0.5) / grid_total
     channels = lane_table(channel_weight, chan2)
     cosine = jnp.where(grid_row >= 0, jnp.cos(latitude), 0.0)
-    weight_rows[...] = cosine * (jnp.tile(channels, (pad_rows // 8, 1)) * (1.0 / (MEM * (MEM - 1))))
+    base_rows = cosine * (jnp.tile(channels, (pad_rows // 8, 1)) * (1.0 / (MEM * (MEM - 1))))
+
+    words[...] = jnp.zeros(words.shape, jnp.int32)
+    words[:, : land.shape[1]] = land[...]
+    for t in range(wide):
+        for part in range(2):
+            block = block_of(part, t)
+            off = pl.multiple_of(block * LANES, LANES)
+            slot = t * 2 + part
+            edge = above[slot].astype(f32)
+            lat_rows[slot, 0:rows] = latent[0, :, pl.ds(off, LANES)].astype(f32)
+            lat_rows[slot, rows : rows + 1] = below[:, slot * LANES : (slot + 1) * LANES].astype(f32)
+            lat_rows[slot, rows + 1 : rows + 2] = edge[0:1]
+            if t < front:
+                tgt_rows[slot, 0:grid_rows] = targets[0, :, pl.ds(off, LANES)].astype(f32)
+                tgt_rows[slot, grid_rows:] = edge
+                mask = jnp.concatenate([land_of(words[...], block, chan2), pltpu.roll(edge, 5, 0)], axis=0)
+                weight_rows[slot] = base_rows + base_rows * mask
 
     build_band(kernel_one, band_one, back_one)
     build_band(kernel_two, band_two, back_two)
@@ -231,7 +286,6 @@
 
     lax.fori_loop(0, rows + 2, first_segment, 0)
 
-    bit_table = jnp.left_shift(1, iota((8, LANES), 1) // chan2)
     members = front * 16
     owner = iota((48, members), 0)
     group = iota((48, members), 1) // 8
@@ -241,26 +295,12 @@
     pick_prev = ((group // 2 < half) & (place == owner)).astype(bf16)
     pick = jnp.concatenate([pick_own, pick_prev], axis=0)
 
-    def land_bits(p, part, t):
-        cell = block_of(part, t) * (LANES // chan2)
-        word = lax.shift_right_logical(cell * 2185, 16)
-        bit = cell - 30 * word
-        after = jnp.minimum(word + 1, land.shape[1] - 1)
-        inner = p >= 4
-        line = jnp.where(inner, p - 4, 0)
-        edge = jnp.where(inner, 0, p)
-        low = jnp.where(inner, land[line, word], land_above[edge, word])
-        high = jnp.where(inner, land[line, after], land_above[edge, after])
-        return jnp.bitwise_or(lax.shift_right_logical(low, bit), lax.shift_left(high, 30 - bit))
-
     def second_segment(j, _):
         taken = operand(act, j, 0, front)
         cast[...] = jnp.dot(taken, band_two[...], preferred_element_type=f32)
         for sub in range(2):
             p = 2 * j + sub
             line = jnp.where(p >= 4, p - 4, p + grid_rows)
-            base = jnp.broadcast_to(weight_rows[pl.ds(p, 1), :], (8, LANES))
-            twice = base + base
             for t in range(front):
                 parts = []
                 for part in range(2):
@@ -281,8 +321,7 @@
                         back = gs[k] + pltpu.roll(back, MEM - 1, 0)
                     back = pltpu.roll(back, MEM - 1, 0)
                     spread = (gs[0] + gs[1]) + (gs[2] + gs[3]) - back
-                    land_hit = jnp.bitwise_and(land_bits(p, part, t), bit_table) != 0
-                    weight = jnp.where(land_hit, twice, base)
+                    weight = weight_rows[t * 2 + part, pl.ds(line, 1), :]
                     parts.append(weight * ((MEM - 1.0) * goal - spread))
                 fgrad[sub, t + 1] = jnp.concatenate(parts, axis=0).astype(bf16)
 
@@ -324,17 +363,19 @@
     pulled = jnp.dot(high, back_one[...], preferred_element_type=f32)
     pulled = pulled + jnp.dot(low, back_one[...], preferred_element_type=f32)
     pulled = pulled.reshape(rows + 1, 48, 2 * LANES)
-    result = pulled[1:, :, :LANES] + pulled[:-1, :, LANES:]
-    out_lat[...] = result[:, :own, :].astype(out_lat.dtype)
-
-    one = tap_sums(acc_one[...].T, chan0, chan1)
-    two = tap_sums(acc_two[...].T, chan1, chan2)
-    for a in range(3):
-        block = fold_to(one[a, 0], chan1, 0) + fold_to(one[a, 1], chan1, chan1) + fold_to(one[a, 2], chan1, 2 * chan1)
-        top = fold_to(two[a, 0], chan2, 3 * chan1) + fold_to(two[a, 1], chan2, 3 * chan1 + chan2)
-        bottom = fold_to(two[a, 2], chan2, 3 * chan1)
-        block = (block + jnp.concatenate([top, bottom], axis=0)) * norm
-        out_taps[a * chan0 : (a + 1) * chan0, :] = block
+    result = (pulled[1:, :, :LANES] + pulled[:-1, :, LANES:]).astype(bf16)
+    swap_to, swap_from = iota((own * rows, rows * 48), 0), iota((own * rows, rows * 48), 1)
+    swap = (swap_to // rows == swap_from % 48) & (swap_to % rows == swap_from // 48)
+    result = jnp.dot(swap.astype(bf16), result.reshape(rows * 48, LANES), preferred_element_type=f32)
+    for t in range(own):
+        out_lat[:, t * LANES : (t + 1) * LANES] = result[t * rows : (t + 1) * rows].astype(bf16)
+
+    pack_taps(acc_one, out_taps, 0, chan0, chan1, norm)
+    pack_taps(acc_two, out_taps, -(-9 // (LANES // chan0)) * chan1, chan1, chan2, norm)
+
+
+def swapped(array, axis, bit):
+    return lax.ppermute(array, axis, [(i, i ^ bit) for i in range(lax.axis_size(axis))])
 
 
 def local(
@@ -345,29 +386,50 @@
     lat_count = lax.axis_size("lat")
     own = span // LANES // lax.axis_size("mem")
     half = (own + 1) // 2
-    assert sample_count == 1 and member_seeds.shape[0] == MEM and own % 2 == 1
+    assert sample_count == 1 and member_seeds.shape[0] == MEM and own % 2 == 1 and lax.axis_size("mem") == 4
     assert 4 * chan2 == 2 * chan1 == chan0 and chan0 == 64
-    below = shifted(latent[:, :1], "lat", -1)
-    above = shifted(latent[:, rows - 1 :], "lat", 1)
-    targets_above = shifted(targets[:, 4 * rows - 4 :], "lat", 1)
-    land_above = shifted(land_words[4 * rows - 4 :], "lat", 1)
-    norm = 1.0 / math.sqrt(sample_count * 4 * rows * lat_count * targets.shape[2])
     vmem = pl.BlockSpec(memory_space=pltpu.VMEM)
     smem = pl.BlockSpec(memory_space=pltpu.SMEM)
     f32, bf16 = jnp.float32, jnp.bfloat16
     wide, front = half + 2, half + 1
+    params = pltpu.CompilerParams(vmem_limit_bytes=56 * 1024 * 1024)
+    kernel_one = kernel_one.transpose(0, 1, 3, 2)
+    kernel_two = kernel_two.transpose(0, 1, 3, 2)
+    down, up = pl.pallas_call(
+        functools.partial(edge_kernel, half, chan2),
+        grid=(1,),
+        in_specs=[
+            pl.BlockSpec((1, 8, span), lambda i: (0, 0, 0)),
+            pl.BlockSpec((1, 8, span), lambda i: (0, rows // 2 - 1, 0)),
+            pl.BlockSpec((8, land_words.shape[1]), lambda i: (rows // 2 - 1, 0)),
+        ],
+        out_specs=[
+            pl.BlockSpec((2 * wide, 8, LANES), lambda i: (0, 0, 0)),
+            pl.BlockSpec((1, 2 * wide * LANES), lambda i: (0, 0)),
+        ],
+        out_shape=[
+            jax.ShapeDtypeStruct((2 * wide, 8, LANES), bf16),
+            jax.ShapeDtypeStruct((1, 2 * wide * LANES), bf16),
+        ],
+        scratch_shapes=[pltpu.VMEM((8, LANES), jnp.int32)],
+        name="edges",
+    )(latent, targets, land_words)
+    above = shifted(down, "lat", 1)
+    below = shifted(up, "lat", -1)
+    norm = 1.0 / math.sqrt(sample_count * 4 * rows * lat_count * targets.shape[2])
     lat_grad, taps = pl.pallas_call(
         functools.partial(band_kernel, half, norm),
-        in_specs=[smem] * 5 + [vmem] * 7,
+        in_specs=[smem] * 3 + [vmem] * 7,
         out_specs=[vmem, vmem],
         out_shape=[
-            jax.ShapeDtypeStruct((rows, own, LANES), bf16),
-            jax.ShapeDtypeStruct((3 * chan0, LANES), f32),
+            jax.ShapeDtypeStruct((rows, own * LANES), bf16),
+            jax.ShapeDtypeStruct((5 * chan1 + 3 * chan2, LANES), f32),
         ],
         scratch_shapes=[
             pltpu.VMEM((2 * wide, rows + 8, LANES), f32),
             pltpu.VMEM((2 * front, 4 * rows + 8, LANES), f32),
-            pltpu.VMEM((4 * rows + 8, LANES), f32),
+            pltpu.VMEM((2 * front, 4 * rows + 8, LANES), f32),
+            pltpu.VMEM((4 * rows, LANES), jnp.int32),
             pltpu.VMEM((512, 256), bf16),
             pltpu.VMEM((512, 256), bf16),
             pltpu.VMEM((512, 256), bf16),
@@ -384,29 +446,38 @@
             pltpu.VMEM((256, 512), f32),
             pltpu.VMEM((256, 512), f32),
         ],
-        compiler_params=pltpu.CompilerParams(vmem_limit_bytes=56 * 1024 * 1024),
+        compiler_params=params,
         name="band",
     )(
         member_seeds,
         noise_scale,
         channel_weight,
-        land_words,
-        land_above,
         latent,
         above,
         below,
         targets,
-        targets_above,
+        land_words,
         kernel_one,
         kernel_two,
     )
-    taps = lax.psum(taps, ("lat", "mem"))
-    whole = lax.all_gather(lat_grad, "mem", axis=1, tiled=True)
-    latent_grad = whole.astype(f32).reshape(1, rows, span)
-    one = taps[:, : 3 * chan1].reshape(3, chan0, 3, chan1).transpose(0, 2, 1, 3)
-    two = taps[:, 3 * chan1 :].reshape(3, 2, chan1, 2, chan2)
-    two = jnp.stack([two[:, 0, :, 0], two[:, 0, :, 1], two[:, 1, :, 0]], axis=1)
-    return (latent_grad, one, two)
+    quarters = [lat_grad] + [swapped(lat_grad, "mem", k) for k in range(1, 4)]
+    for axis in ("lat", "mem"):
+        bit = 1
+        while bit < lax.axis_size(axis):
+            taps = taps + swapped(taps, axis, bit)
+            bit *= 2
+    latent_grad, one, two = pl.pallas_call(
+        functools.partial(place_kernel, own),
+        in_specs=[vmem] * 5,
+        out_specs=[vmem] * 3,
+        out_shape=[
+            jax.ShapeDtypeStruct((1, rows, span), f32),
+            jax.ShapeDtypeStruct(kernel_one.shape, f32),
+            jax.ShapeDtypeStruct(kernel_two.shape, f32),
+        ],
+        name="place",
+    )(*quarters, taps)
+    return (latent_grad, one.transpose(0, 1, 3, 2), two.transpose(0, 1, 3, 2))
 
 
 def solution(mesh):

time: 217 us -> 86.4 us (0.40)
  waiting for transfers between devices: 121 us -> 21.9 us
  blocking collectives: 15.2 us -> 0 us
  between operations: 14.2 us -> 0.67 us
  local copies, waits for them, and re-layouts: 11.4 us -> 1.92 us
  starting transfers between devices: 11.2 us -> 18.3 us
    psum x1 -> x0, waiting for transfers between devices: 121 us -> none  [local(): taps = lax.psum(taps, ('lat', 'mem'))]
    ppermute x0 -> x8, waiting for transfers between devices: none -> 17.7 us  [swapped(): lax.ppermute(array, axis, [(i, i ^ bit) for i in range(lax.axis_size(axis...]
    all_gather x1 -> x0, blocking collectives: 15.2 us -> none  [local(): whole = lax.all_gather(lat_grad, 'mem', axis=1, tiled=True)]
    ppermute x0 -> x8, starting transfers between devices: none -> 14.7 us  [swapped(): lax.ppermute(array, axis, [(i, i ^ bit) for i in range(lax.axis_size(axis...]
    ppermute x4 -> x2, starting transfers between devices: 11.2 us -> 3.64 us  [shifted(): return lax.ppermute(array, axis, pairs)]
    slice x8 -> x0, local copies, waits for them, and re-layouts: 5.1 us -> none  [the longest x1 1.25 us: local(): below = shifted(latent[:, :1], 'lat', -1)]
    ppermute x4 -> x2, waiting for transfers between devices: 0.01 us -> 4.11 us  [shifted(): return lax.ppermute(array, axis, pairs)]
    pallas_call x0 -> x2, Pallas kernels: none -> 4.04 us  [the longest x1 2.06 us: local(): pl.pallas_call(functools.partial(place_kernel, own), in_specs=[vmem] * 5,...]
  transfers between devices with their start and end apart: 5 -> 10, of which waited for: 1 -> 7; matrix products, arithmetic and copies ran while one was open for 3% -> 1% of each run, Pallas kernels for 0% -> 0%
where the time goes in v2:
time: 86.4 us; the launch traced here: 86.2 us
  Pallas kernels  41.8 us (48%)
  waiting for transfers between devices  21.9 us (25%)
  starting transfers between devices  18.3 us (21%)
  local copies, waits for them, and re-layouts  1.92 us (2%)
  other arithmetic  1.61 us (2%)
    pallas_call x1, Pallas kernels, local(): pl.pallas_call(functools.partial(band_kernel, half, norm), in_specs=[smem...  37.8 us
    ppermute x8, waiting for transfers between devices, swapped(): lax.ppermute(array, axis, [(i, i ^ bit) for i in range(lax.axis_size(axis...  17.7 us
    ppermute x8, starting transfers between devices, swapped(): lax.ppermute(array, axis, [(i, i ^ bit) for i in range(lax.axis_size(axis...  14.7 us
    ppermute x2, waiting for transfers between devices, shifted(): return lax.ppermute(array, axis, pairs)  4.11 us
    ppermute x2, starting transfers between devices, shifted(): return lax.ppermute(array, axis, pairs)  3.64 us
    pallas_call x1, Pallas kernels, local(): pl.pallas_call(functools.partial(place_kernel, own), in_specs=[vmem] * 5,...  2.06 us
    pallas_call x1, Pallas kernels, local(): pl.pallas_call(functools.partial(edge_kernel, half, chan2), grid=(1,), in...  1.98 us
    unnamed x10, local copies, waits for them, and re-layouts  1.92 us
  transfers between devices with their start and end apart: 10, of which 7 were waited for; matrix products, arithmetic and copies ran while one was open for 1% of the time, Pallas kernels for 0%

profile of v2, /device:TPU:0, one launch (start us, length us, event | category | flops | bytes accessed | tf_op | source)
XLA Modules:
  0.0 86.2 jit_solution(2173772017827853649)
XLA Ops:
  0.6 2.0 %edges.1 = (bf16[50,8,128]{2,1,0:T(8,128)(2,1)}, bf16[1,6400]{1,0:T(2,128)(2,1)}) custom-call(bf16[1,8,23040]{2,1,0:T(8,128)(2,1)} %latent.3, bf16[1,32,23040]{2,1,0:T(8,128)(2,1)} %targets.3, s32[32,48]{1,0:T(8,128)} %land.3), custom_call_target="tpu_custom_call" | custom-call | tf_op jit(solution)/shard_map/edges/pallas_call | solution.py:398
  2.6 2.4 %collective-permute-start = (bf16[50,8,128]{2,1,0:T(8,128)(2,1)}, bf16[50,8,128]{2,1,0:T(8,128)(2,1)S(1)}, u32[]{:S(2)}, u32[]{:S(2)}) collective-permute-start(bf16[50,8,128]{2,1,0:T(8,128)(2,1)} %get-tuple-element.10), channel_id=1, source_target_pairs={{0,4},{4,8},{8,12},{12,16},{16,20},{20,24},{24,28},{1,5},{5,9},{9,... | collective-permute-start | bytes 307208 | tf_op jit(solution)/shard_map/ppermute | solution.py:24
  5.0 1.3 %collective-permute-start.1 = (bf16[1,6400]{1,0:T(2,128)(2,1)}, bf16[1,6400]{1,0:T(2,128)(2,1)S(1)}, u32[]{:S(2)}, u32[]{:S(2)}) collective-permute-start(bf16[1,6400]{1,0:T(2,128)(2,1)} %get-tuple-element.11), channel_id=1, source_target_pairs={{4,0},{8,4},{12,8},{16,12},{20,16},{24,20},{28,24},{5,1},{9,5},{13... | collective-permute-start | bytes 38408 | tf_op jit(solution)/shard_map/ppermute | solution.py:24
  6.3 4.1 %collective-permute-done.1.below = bf16[1,6400]{1,0:T(2,128)(2,1)S(1)} collective-permute-done((bf16[1,6400]{1,0:T(2,128)(2,1)}, bf16[1,6400]{1,0:T(2,128)(2,1)S(1)}, u32[]{:S(2)}, u32[]{:S(2)}) %collective-permute-start.1) | collective-permute-done | bytes 12832 | tf_op jit(solution)/shard_map/ppermute | solution.py:24
  11.0 37.8 %band.1 = (bf16[8,5760]{1,0:T(8,128)(2,1)}, f32[208,128]{1,0:T(8,128)}) custom-call(s32[8]{0:T(128)} %seeds.1, f32[64]{0:T(128)} %scale.1, f32[16]{0:T(128)} %channel_weight.1, bf16[1,8,23040]{2,1,0:T(8,128)(2,1)} %latent.3, bf16[50,8,128]{2,1,0:T(8,128)(2,1)} %copy-done, bf16[1,6400]{1,0:T(2,128)(2,1)} %copy-done.4, bf16[1,32,23040]{2,1,0:T(8,128)(2,1)} %targets.3, ...), custom_call_target="tpu_custom_call" | custom-call | tf_op jit(solution)/shard_map/band/pallas_call | solution.py:420
  48.8 2.6 %collective-permute-start.5 = (f32[208,128]{1,0:T(8,128)}, f32[208,128]{1,0:T(8,128)S(1)}, u32[]{:S(2)}, u32[]{:S(2)}) collective-permute-start(f32[208,128]{1,0:T(8,128)} %get-tuple-element.13), channel_id=1, source_target_pairs={{0,4},{4,0},{8,12},{12,8},{16,20},{20,16},{24,28},{28,24},{1,5},{5... | collective-permute-start | bytes 319496 | tf_op jit(solution)/shard_map/ppermute | solution.py:378
  51.4 1.2 %collective-permute-done.5 = f32[208,128]{1,0:T(8,128)S(1)} collective-permute-done((f32[208,128]{1,0:T(8,128)}, f32[208,128]{1,0:T(8,128)S(1)}, u32[]{:S(2)}, u32[]{:S(2)}) %collective-permute-start.5) | collective-permute-done | bytes 106528 | tf_op jit(solution)/shard_map/ppermute | solution.py:378
  52.5 0.9 %add.15 = f32[208,128]{1,0:T(8,128)S(1)} add(f32[208,128]{1,0:T(8,128)} %get-tuple-element.13, f32[208,128]{1,0:T(8,128)S(1)} %collective-permute-done.5) | non-fusion elementwise | flops 26624 | bytes 319488 | tf_op jit(solution)/shard_map/add | solution.py:467
  53.4 2.5 %collective-permute-start.6 = (f32[208,128]{1,0:T(8,128)S(1)}, f32[208,128]{1,0:T(8,128)S(1)}, u32[]{:S(2)}, u32[]{:S(2)}) collective-permute-start(f32[208,128]{1,0:T(8,128)S(1)} %add.15), channel_id=1, source_target_pairs={{0,8},{4,12},{8,0},{12,4},{16,24},{20,28},{24,16},{28,20},{1,9},{5... | collective-permute-start | bytes 319496 | tf_op jit(solution)/shard_map/ppermute | solution.py:378
  55.9 3.5 %collective-permute-done.6 = f32[208,128]{1,0:T(8,128)S(1)} collective-permute-done((f32[208,128]{1,0:T(8,128)S(1)}, f32[208,128]{1,0:T(8,128)S(1)}, u32[]{:S(2)}, u32[]{:S(2)}) %collective-permute-start.6) | collective-permute-done | bytes 106528 | tf_op jit(solution)/shard_map/ppermute | solution.py:378
  59.4 0.9 %collective-permute-start.7 = (f32[208,128]{1,0:T(8,128)S(1)}, f32[208,128]{1,0:T(8,128)S(1)}, u32[]{:S(2)}, u32[]{:S(2)}) collective-permute-start(f32[208,128]{1,0:T(8,128)S(1)} %add.16), channel_id=1, source_target_pairs={{0,16},{4,20},{8,24},{12,28},{16,0},{20,4},{24,8},{28,12},{1,17},{... | collective-permute-start | bytes 319496 | tf_op jit(solution)/shard_map/ppermute | solution.py:378
  60.3 3.8 %collective-permute-done.7 = f32[208,128]{1,0:T(8,128)S(1)} collective-permute-done((f32[208,128]{1,0:T(8,128)S(1)}, f32[208,128]{1,0:T(8,128)S(1)}, u32[]{:S(2)}, u32[]{:S(2)}) %collective-permute-start.7) | collective-permute-done | bytes 106528 | tf_op jit(solution)/shard_map/ppermute | solution.py:378
  64.2 1.6 %collective-permute-start.8 = (f32[208,128]{1,0:T(8,128)S(1)}, f32[208,128]{1,0:T(8,128)S(1)}, u32[]{:S(2)}, u32[]{:S(2)}) collective-permute-start(f32[208,128]{1,0:T(8,128)S(1)} %add.17), channel_id=1, source_target_pairs={{0,1},{1,0},{2,3},{3,2},{4,5},{5,4},{6,7},{7,6},{8,9},{9,8},{10,11... | collective-permute-start | bytes 319496 | tf_op jit(solution)/shard_map/ppermute | solution.py:378
  65.8 3.1 %collective-permute-done.8 = f32[208,128]{1,0:T(8,128)S(1)} collective-permute-done((f32[208,128]{1,0:T(8,128)S(1)}, f32[208,128]{1,0:T(8,128)S(1)}, u32[]{:S(2)}, u32[]{:S(2)}) %collective-permute-start.8) | collective-permute-done | bytes 106528 | tf_op jit(solution)/shard_map/ppermute | solution.py:378
  69.0 2.7 %collective-permute-start.9 = (f32[208,128]{1,0:T(8,128)S(1)}, f32[208,128]{1,0:T(8,128)S(1)}, u32[]{:S(2)}, u32[]{:S(2)}) collective-permute-start(f32[208,128]{1,0:T(8,128)S(1)} %add.18), channel_id=1, source_target_pairs={{0,2},{1,3},{2,0},{3,1},{4,6},{5,7},{6,4},{7,5},{8,10},{9,11},{10,... | collective-permute-start | bytes 319496 | tf_op jit(solution)/shard_map/ppermute | solution.py:378
  71.6 1.3 %collective-permute-start.4 = (bf16[8,5760]{1,0:T(8,128)(2,1)}, bf16[8,5760]{1,0:T(8,128)(2,1)S(1)}, u32[]{:S(2)}, u32[]{:S(2)}) collective-permute-start(bf16[8,5760]{1,0:T(8,128)(2,1)} %get-tuple-element.12.part0), channel_id=1, source_target_pairs={{0,3},{1,2},{2,1},{3,0},{4,7},{5,6},{6,5},{7,4},{8,11},{9,10},{10,... | collective-permute-start | bytes 276488 | tf_op jit(solution)/shard_map/ppermute | solution.py:378
  73.0 1.7 %collective-permute-start.3 = (bf16[8,5760]{1,0:T(8,128)(2,1)}, bf16[8,5760]{1,0:T(8,128)(2,1)S(1)}, u32[]{:S(2)}, u32[]{:S(2)}) collective-permute-start(bf16[8,5760]{1,0:T(8,128)(2,1)} %get-tuple-element.12.part0), channel_id=1, source_target_pairs={{0,2},{1,3},{2,0},{3,1},{4,6},{5,7},{6,4},{7,5},{8,10},{9,11},{10,... | collective-permute-start | bytes 276488 | tf_op jit(solution)/shard_map/ppermute | solution.py:378
  74.7 1.3 %collective-permute-start.2 = (bf16[8,5760]{1,0:T(8,128)(2,1)}, bf16[8,5760]{1,0:T(8,128)(2,1)S(1)}, u32[]{:S(2)}, u32[]{:S(2)}) collective-permute-start(bf16[8,5760]{1,0:T(8,128)(2,1)} %get-tuple-element.12.part0), channel_id=1, source_target_pairs={{0,1},{1,0},{2,3},{3,2},{4,5},{5,4},{6,7},{7,6},{8,9},{9,8},{10,11... | collective-permute-start | bytes 276488 | tf_op jit(solution)/shard_map/ppermute | solution.py:378
  76.0 4.8 %collective-permute-done.9 = f32[208,128]{1,0:T(8,128)S(1)} collective-permute-done((f32[208,128]{1,0:T(8,128)S(1)}, f32[208,128]{1,0:T(8,128)S(1)}, u32[]{:S(2)}, u32[]{:S(2)}) %collective-permute-start.9) | collective-permute-done | bytes 106528 | tf_op jit(solution)/shard_map/ppermute | solution.py:378
  80.8 0.7 add.19.taps
  81.5 1.3 %collective-permute-done.3.part2 = bf16[8,5760]{1,0:T(8,128)(2,1)S(1)} collective-permute-done((bf16[8,5760]{1,0:T(8,128)(2,1)}, bf16[8,5760]{1,0:T(8,128)(2,1)S(1)}, u32[]{:S(2)}, u32[]{:S(2)}) %collective-permute-start.3) | collective-permute-done | bytes 92192 | tf_op jit(solution)/shard_map/ppermute | solution.py:378
  82.8 0.6 copy-done.2
  83.5 0.6 copy-done.3
  84.1 2.1 %place.1 = (f32[1,8,23040]{2,1,0:T(8,128)}, f32[3,3,32,64]{3,2,1,0:T(8,128)}, f32[3,3,16,32]{3,2,1,0:T(8,128)}) custom-call(bf16[8,5760]{1,0:T(8,128)(2,1)} %get-tuple-element.12.part0, bf16[8,5760]{1,0:T(8,128)(2,1)} %copy-done.3, bf16[8,5760]{1,0:T(8,128)(2,1)} %copy-done.2, bf16[8,5760]{1,0:T(8,128)(2,1)} %copy-done.1, f32[208,128]{1,0:T(8,128)} %add.19.taps), custom_call_target="tpu_custom_call" | custom-call | tf_op jit(solution)/shard_map/place/pallas_call | solution.py:469
  (14 shorter events, 0.7 us)
Async XLA Ops:
  2.6 7.8 %collective-permute-start = (bf16[50,8,128]{2,1,0:T(8,128)(2,1)}, bf16[50,8,128]{2,1,0:T(8,128)(2,1)S(1)}, u32[]{:S(2)}, u32[]{:S(2)}) collective-permute-start(bf16[50,8,128]{2,1,0:T(8,128)(2,1)} %get-tuple-element.10), channel_id=1, source_target_pairs={{0,4},{4,8},{8,12},{12,16},{16,20},{20,24},{24,28},{1,5},{5,9},{9,... | collective-permute-start | bytes 307208 | tf_op jit(solution)/shard_map/ppermute | solution.py:24
  5.0 5.4 %collective-permute-start.1 = (bf16[1,6400]{1,0:T(2,128)(2,1)}, bf16[1,6400]{1,0:T(2,128)(2,1)S(1)}, u32[]{:S(2)}, u32[]{:S(2)}) collective-permute-start(bf16[1,6400]{1,0:T(2,128)(2,1)} %get-tuple-element.11), channel_id=1, source_target_pairs={{4,0},{8,4},{12,8},{16,12},{20,16},{24,20},{28,24},{5,1},{9,5},{13... | collective-permute-start | bytes 38408 | tf_op jit(solution)/shard_map/ppermute | solution.py:24
  10.4 0.6 copy-start.4
  10.4 0.6 copy-start
  48.8 3.7 %collective-permute-start.5 = (f32[208,128]{1,0:T(8,128)}, f32[208,128]{1,0:T(8,128)S(1)}, u32[]{:S(2)}, u32[]{:S(2)}) collective-permute-start(f32[208,128]{1,0:T(8,128)} %get-tuple-element.13), channel_id=1, source_target_pairs={{0,4},{4,0},{8,12},{12,8},{16,20},{20,16},{24,28},{28,24},{1,5},{5... | collective-permute-start | bytes 319496 | tf_op jit(solution)/shard_map/ppermute | solution.py:378
  53.4 5.9 %collective-permute-start.6 = (f32[208,128]{1,0:T(8,128)S(1)}, f32[208,128]{1,0:T(8,128)S(1)}, u32[]{:S(2)}, u32[]{:S(2)}) collective-permute-start(f32[208,128]{1,0:T(8,128)S(1)} %add.15), channel_id=1, source_target_pairs={{0,8},{4,12},{8,0},{12,4},{16,24},{20,28},{24,16},{28,20},{1,9},{5... | collective-permute-start | bytes 319496 | tf_op jit(solution)/shard_map/ppermute | solution.py:378
  59.4 4.8 %collective-permute-start.7 = (f32[208,128]{1,0:T(8,128)S(1)}, f32[208,128]{1,0:T(8,128)S(1)}, u32[]{:S(2)}, u32[]{:S(2)}) collective-permute-start(f32[208,128]{1,0:T(8,128)S(1)} %add.16), channel_id=1, source_target_pairs={{0,16},{4,20},{8,24},{12,28},{16,0},{20,4},{24,8},{28,12},{1,17},{... | collective-permute-start | bytes 319496 | tf_op jit(solution)/shard_map/ppermute | solution.py:378
  64.2 4.8 %collective-permute-start.8 = (f32[208,128]{1,0:T(8,128)S(1)}, f32[208,128]{1,0:T(8,128)S(1)}, u32[]{:S(2)}, u32[]{:S(2)}) collective-permute-start(f32[208,128]{1,0:T(8,128)S(1)} %add.17), channel_id=1, source_target_pairs={{0,1},{1,0},{2,3},{3,2},{4,5},{5,4},{6,7},{7,6},{8,9},{9,8},{10,11... | collective-permute-start | bytes 319496 | tf_op jit(solution)/shard_map/ppermute | solution.py:378
  69.0 11.9 %collective-permute-start.9 = (f32[208,128]{1,0:T(8,128)S(1)}, f32[208,128]{1,0:T(8,128)S(1)}, u32[]{:S(2)}, u32[]{:S(2)}) collective-permute-start(f32[208,128]{1,0:T(8,128)S(1)} %add.18), channel_id=1, source_target_pairs={{0,2},{1,3},{2,0},{3,1},{4,6},{5,7},{6,4},{7,5},{8,10},{9,11},{10,... | collective-permute-start | bytes 319496 | tf_op jit(solution)/shard_map/ppermute | solution.py:378
  71.6 9.9 %collective-permute-start.4 = (bf16[8,5760]{1,0:T(8,128)(2,1)}, bf16[8,5760]{1,0:T(8,128)(2,1)S(1)}, u32[]{:S(2)}, u32[]{:S(2)}) collective-permute-start(bf16[8,5760]{1,0:T(8,128)(2,1)} %get-tuple-element.12.part0), channel_id=1, source_target_pairs={{0,3},{1,2},{2,1},{3,0},{4,7},{5,6},{6,5},{7,4},{8,11},{9,10},{10,... | collective-permute-start | bytes 276488 | tf_op jit(solution)/shard_map/ppermute | solution.py:378
  73.0 9.9 %collective-permute-start.3 = (bf16[8,5760]{1,0:T(8,128)(2,1)}, bf16[8,5760]{1,0:T(8,128)(2,1)S(1)}, u32[]{:S(2)}, u32[]{:S(2)}) collective-permute-start(bf16[8,5760]{1,0:T(8,128)(2,1)} %get-tuple-element.12.part0), channel_id=1, source_target_pairs={{0,2},{1,3},{2,0},{3,1},{4,6},{5,7},{6,4},{7,5},{8,10},{9,11},{10,... | collective-permute-start | bytes 276488 | tf_op jit(solution)/shard_map/ppermute | solution.py:378
  74.7 8.2 %collective-permute-start.2 = (bf16[8,5760]{1,0:T(8,128)(2,1)}, bf16[8,5760]{1,0:T(8,128)(2,1)S(1)}, u32[]{:S(2)}, u32[]{:S(2)}) collective-permute-start(bf16[8,5760]{1,0:T(8,128)(2,1)} %get-tuple-element.12.part0), channel_id=1, source_target_pairs={{0,1},{1,0},{2,3},{3,2},{4,5},{5,4},{6,7},{7,6},{8,9},{9,8},{10,11... | collective-permute-start | bytes 276488 | tf_op jit(solution)/shard_map/ppermute | solution.py:378
  81.5 1.3 %copy-start.1 = (bf16[8,5760]{1,0:T(8,128)(2,1)}, bf16[8,5760]{1,0:T(8,128)(2,1)S(1)}, u32[]{:S(2)}) copy-start(bf16[8,5760]{1,0:T(8,128)(2,1)S(1)} %collective-permute-done.4.part3) | copy-start | bytes 276484
  82.8 0.6 copy-start.2
  83.5 0.6 copy-start.3

commit v3 on v2

--- a/solution.py
+++ b/solution.py
@@ -36,7 +36,7 @@
     return total
 
 
-def build_band(kernel_ref, band_ref, back_ref):
+def build_band(kernel_ref, band_ref):
     chan_out, chan_in = kernel_ref.shape[2], kernel_ref.shape[3]
     cells = LANES // chan_in
     repeat = (iota((chan_out, LANES), 1) % chan_out == iota((chan_out, LANES), 0)).astype(jnp.bfloat16)
@@ -60,9 +60,29 @@
                         if 0 <= a <= 2 and 0 <= b <= 2:
                             part = jnp.where(column == q, wide[a, b], part)
                     band_ref[at : at + chan_in, sub * LANES : (sub + 1) * LANES] = part.astype(jnp.bfloat16)
+
+
+def build_back(kernel_ref, back_ref):
+    chan_out, chan_in = kernel_ref.shape[2], kernel_ref.shape[3]
+    cells = LANES // chan_in
+    repeat = (iota((chan_in, LANES), 1) % chan_in == iota((chan_in, LANES), 0)).astype(jnp.bfloat16)
+    flat = kernel_ref[...].reshape(9 * chan_out, chan_in)
+    wide = jnp.dot(flat, repeat, preferred_element_type=jnp.float32)
+    column = iota((chan_out, LANES), 1) // chan_in
+    zero = jnp.zeros((chan_out, LANES), jnp.float32)
     for block in range(2):
-        square = band_ref[block * 256 : (block + 1) * 256, :].astype(jnp.float32)
-        back_ref[block * 256 : (block + 1) * 256, :] = square.T.astype(jnp.bfloat16)
+        for sub in range(2):
+            for q in range(2 * cells):
+                at = block * 256 + sub * LANES + q * chan_out
+                for row in range(2):
+                    a = sub - 2 * row + 1
+                    part = zero
+                    for cell in range(cells):
+                        b = q - 2 * (cell + block * cells) + 1
+                        if 0 <= a <= 2 and 0 <= b <= 2:
+                            tap = (3 * a + b) * chan_out
+                            part = jnp.where(column == cell, wide[tap : tap + chan_out], part)
+                    back_ref[at : at + chan_out, row * LANES : (row + 1) * LANES] = part.astype(jnp.bfloat16)
 
 
 def pack_taps(acc_ref, out_ref, first, chan_in, chan_out, norm):
@@ -126,11 +146,18 @@
             up[:, slot * LANES : (slot + 1) * LANES] = cells[0:1].astype(jnp.bfloat16)
 
 
-def place_kernel(own, part0, part1, part2, part3, taps, latent_grad, grad_one, grad_two):
+def place_kernel(own, part0, part1, part2, part3, latent_grad):
     mem_pos = lax.axis_index("mem")
     for k, part in enumerate((part0, part1, part2, part3)):
         off = pl.multiple_of(jnp.bitwise_xor(mem_pos, k) * own * LANES, LANES)
         latent_grad[0, :, pl.ds(off, own * LANES)] = part[...].astype(jnp.float32)
+
+
+def taps_kernel(mine, other, grad_one, grad_two, taps):
+    count = mine.shape[0]
+    odd = jnp.bitwise_and(lax.axis_index("lat"), 1)
+    taps[pl.ds(pl.multiple_of(odd * count, 8), count), :] = mine[...]
+    taps[pl.ds(pl.multiple_of((1 - odd) * count, 8), count), :] = other[...]
     first = 0
     for out in (grad_one, grad_two):
         chan_out, chan_in = out.shape[2], out.shape[3]
@@ -142,6 +169,25 @@
             block = pltpu.roll(block, turn, 1) if turn else block
             out[k // 3, k % 3] = block[:, :chan_in]
         first += -(-9 // cells) * chan_out
+
+
+def latent_kernel(rows, own, sums, kernel_one, out_lat, back_one):
+    bf16, f32 = jnp.bfloat16, jnp.float32
+    build_back(kernel_one, back_one)
+    z = sums[...].reshape(rows + 1, 2, 96, LANES)
+    z = [z[:, sub, at : at + 48].reshape((rows + 1) * 48, LANES) for at in (0, 48) for sub in range(2)]
+    z = jnp.concatenate(z, axis=1)
+    high = z.astype(bf16)
+    low = (z - high.astype(f32)).astype(bf16)
+    pulled = jnp.dot(high, back_one[...], preferred_element_type=f32)
+    pulled = pulled + jnp.dot(low, back_one[...], preferred_element_type=f32)
+    pulled = pulled.reshape(rows + 1, 48, 2 * LANES)
+    result = (pulled[1:, :, :LANES] + pulled[:-1, :, LANES:]).astype(bf16)
+    swap_to, swap_from = iota((own * rows, rows * 48), 0), iota((own * rows, rows * 48), 1)
+    swap = (swap_to // rows == swap_from % 48) & (swap_to % rows == swap_from // 48)
+    result = jnp.dot(swap.astype(bf16), result.reshape(rows * 48, LANES), preferred_element_type=f32)
+    for t in range(own):
+        out_lat[:, t * LANES : (t + 1) * LANES] = result[t * rows : (t + 1) * rows].astype(bf16)
 
 
 def band_kernel(
@@ -157,14 +203,14 @@
     land,
     kernel_one,
     kernel_two,
-    out_lat,
-    out_taps,
+    sums,
+    taps_keep,
+    taps_send,
     lat_rows,
     tgt_rows,
     weight_rows,
     words,
     band_one,
-    back_one,
     band_two,
     back_two,
     source,
@@ -175,7 +221,7 @@
     fgrad,
     carry,
     pgrad,
-    sums,
+    taps,
     acc_one,
     acc_two,
 ):
@@ -222,8 +268,9 @@
                 mask = jnp.concatenate([land_of(words[...], block, chan2), pltpu.roll(edge, 5, 0)], axis=0)
                 weight_rows[slot] = base_rows + base_rows * mask
 
-    build_band(kernel_one, band_one, back_one)
-    build_band(kernel_two, band_two, back_two)
+    build_band(kernel_one, band_one)
+    build_band(kernel_two, band_two)
+    build_back(kernel_two, back_two)
 
     source[rows + 2] = jnp.zeros(source.shape[1:], bf16)
     source[:, wide] = jnp.zeros((source.shape[0],) + source.shape[2:], bf16)
@@ -355,27 +402,24 @@
 
     lax.fori_loop(1, rows + 1, first_taps, 0)
 
-    z = sums[...].reshape(rows + 1, 2, 96, LANES)
-    z = [z[:, sub, at : at + 48].reshape((rows + 1) * 48, LANES) for at in (0, 48) for sub in range(2)]
-    z = jnp.concatenate(z, axis=1)
-    high = z.astype(bf16)
-    low = (z - high.astype(f32)).astype(bf16)
-    pulled = jnp.dot(high, back_one[...], preferred_element_type=f32)
-    pulled = pulled + jnp.dot(low, back_one[...], preferred_element_type=f32)
-    pulled = pulled.reshape(rows + 1, 48, 2 * LANES)
-    result = (pulled[1:, :, :LANES] + pulled[:-1, :, LANES:]).astype(bf16)
-    swap_to, swap_from = iota((own * rows, rows * 48), 0), iota((own * rows, rows * 48), 1)
-    swap = (swap_to // rows == swap_from % 48) & (swap_to % rows == swap_from // 48)
-    result = jnp.dot(swap.astype(bf16), result.reshape(rows * 48, LANES), preferred_element_type=f32)
-    for t in range(own):
-        out_lat[:, t * LANES : (t + 1) * LANES] = result[t * rows : (t + 1) * rows].astype(bf16)
-
-    pack_taps(acc_one, out_taps, 0, chan0, chan1, norm)
-    pack_taps(acc_two, out_taps, -(-9 // (LANES // chan0)) * chan1, chan1, chan2, norm)
+    pack_taps(acc_one, taps, 0, chan0, chan1, norm)
+    pack_taps(acc_two, taps, -(-9 // (LANES // chan0)) * chan1, chan1, chan2, norm)
+    count = taps_keep.shape[0]
+    odd = jnp.bitwise_and(lat_pos, 1)
+    taps_keep[...] = taps[pl.ds(pl.multiple_of(odd * count, 8), count), :]
+    taps_send[...] = taps[pl.ds(pl.multiple_of((1 - odd) * count, 8), count), :]
 
 
 def swapped(array, axis, bit):
     return lax.ppermute(array, axis, [(i, i ^ bit) for i in range(lax.axis_size(axis))])
+
+
+def total(array, axis, bits):
+    if len(bits) == 1:
+        return array + swapped(array, axis, bits[0])
+    first, second = bits
+    one, two, three = (swapped(array, axis, k) for k in (first, second, first ^ second))
+    return (array + one) + (two + three)
 
 
 def local(
@@ -392,7 +436,7 @@
     smem = pl.BlockSpec(memory_space=pltpu.SMEM)
     f32, bf16 = jnp.float32, jnp.bfloat16
     wide, front = half + 2, half + 1
-    params = pltpu.CompilerParams(vmem_limit_bytes=56 * 1024 * 1024)
+    params = pltpu.CompilerParams(vmem_limit_bytes=32 * 1024 * 1024)
     kernel_one = kernel_one.transpose(0, 1, 3, 2)
     kernel_two = kernel_two.transpose(0, 1, 3, 2)
     down, up = pl.pallas_call(
@@ -417,20 +461,21 @@
     above = shifted(down, "lat", 1)
     below = shifted(up, "lat", -1)
     norm = 1.0 / math.sqrt(sample_count * 4 * rows * lat_count * targets.shape[2])
-    lat_grad, taps = pl.pallas_call(
+    tap_rows = 5 * chan1 + 3 * chan2
+    sums, taps, taps_send = pl.pallas_call(
         functools.partial(band_kernel, half, norm),
         in_specs=[smem] * 3 + [vmem] * 7,
-        out_specs=[vmem, vmem],
+        out_specs=[vmem] * 3,
         out_shape=[
-            jax.ShapeDtypeStruct((rows, own * LANES), bf16),
-            jax.ShapeDtypeStruct((5 * chan1 + 3 * chan2, LANES), f32),
+            jax.ShapeDtypeStruct((2 * rows + 2, 96, LANES), f32),
+            jax.ShapeDtypeStruct((tap_rows // 2, LANES), f32),
+            jax.ShapeDtypeStruct((tap_rows // 2, LANES), f32),
         ],
         scratch_shapes=[
             pltpu.VMEM((2 * wide, rows + 8, LANES), f32),
             pltpu.VMEM((2 * front, 4 * rows + 8, LANES), f32),
             pltpu.VMEM((2 * front, 4 * rows + 8, LANES), f32),
             pltpu.VMEM((4 * rows, LANES), jnp.int32),
-            pltpu.VMEM((512, 256), bf16),
             pltpu.VMEM((512, 256), bf16),
             pltpu.VMEM((512, 256), bf16),
             pltpu.VMEM((512, 256), bf16),
@@ -442,7 +487,7 @@
             pltpu.VMEM((2, front + 1, 16, LANES), bf16),
             pltpu.VMEM((front * 16, LANES), f32),
             pltpu.VMEM((2 * rows + 2, front, 16, LANES), bf16),
-            pltpu.VMEM((2 * rows + 2, 96, LANES), f32),
+            pltpu.VMEM((tap_rows, LANES), f32),
             pltpu.VMEM((256, 512), f32),
             pltpu.VMEM((256, 512), f32),
         ],
@@ -460,23 +505,40 @@
         kernel_one,
         kernel_two,
     )
-    quarters = [lat_grad] + [swapped(lat_grad, "mem", k) for k in range(1, 4)]
-    for axis in ("lat", "mem"):
-        bit = 1
-        while bit < lax.axis_size(axis):
-            taps = taps + swapped(taps, axis, bit)
-            bit *= 2
-    latent_grad, one, two = pl.pallas_call(
+    lat_grad = pl.pallas_call(
+        functools.partial(latent_kernel, rows, own),
+        in_specs=[vmem] * 2,
+        out_specs=vmem,
+        out_shape=jax.ShapeDtypeStruct((rows, own * LANES), bf16),
+        scratch_shapes=[pltpu.VMEM((512, 256), bf16)],
+        name="latent",
+    )(sums, kernel_one)
+    quarters = [swapped(lat_grad, "mem", k) for k in range(1, 4)]
+    taps = taps + swapped(taps_send, "lat", 1)
+    bits = [1 << k for k in range(1, lat_count.bit_length() - 1)]
+    for k in range(0, len(bits), 2):
+        taps = total(taps, "lat", bits[k : k + 2])
+    taps, quarters = lax.optimization_barrier((taps, quarters))
+    latent_grad = pl.pallas_call(
         functools.partial(place_kernel, own),
-        in_specs=[vmem] * 5,
-        out_specs=[vmem] * 3,
+        in_specs=[vmem] * 4,
+        out_specs=vmem,
+        out_shape=jax.ShapeDtypeStruct((1, rows, span), f32),
+        name="place",
+    )(lat_grad, *quarters)
+    taps = total(taps, "mem", [1, 2])
+    other = swapped(taps, "lat", 1)
+    one, two = pl.pallas_call(
+        taps_kernel,
+        in_specs=[vmem] * 2,
+        out_specs=[vmem] * 2,
         out_shape=[
-            jax.ShapeDtypeStruct((1, rows, span), f32),
             jax.ShapeDtypeStruct(kernel_one.shape, f32),
             jax.ShapeDtypeStruct(kernel_two.shape, f32),
         ],
-        name="place",
-    )(*quarters, taps)
+        scratch_shapes=[pltpu.VMEM((tap_rows, LANES), f32)],
+        name="taps",
+    )(taps, other)
     return (latent_grad, one.transpose(0, 1, 3, 2), two.transpose(0, 1, 3, 2))
 
 

time: 86.4 us -> 83.6 us (0.968)
  waiting for transfers between devices: 21.9 us -> 17.1 us
  Pallas kernels: 41.8 us -> 43.5 us
  other arithmetic: 1.61 us -> 0.04 us
  local copies, waits for them, and re-layouts: 1.92 us -> 3.22 us
    ppermute x8 -> x11, waiting for transfers between devices: 17.7 us -> 13 us  [swapped(): lax.ppermute(array, axis, [(i, i ^ bit) for i in range(lax.axis_size(axis...]
    pallas_call x1 -> x3, Pallas kernels: 2.06 us -> 6.28 us  [the longest x1 2.72 us: local(): pl.pallas_call(functools.partial(latent_kernel, rows, own), in_specs=[vme...]
    pallas_call x1, Pallas kernels: 37.8 us -> 35.1 us  [local(): pl.pallas_call(functools.partial(band_kernel, half, norm), in_specs=[smem...]
    add x5 -> x3, other arithmetic: 1.61 us -> 0.04 us  [the longest x2 0.03 us: total(): return array + one + (two + three)]
    unnamed x10 -> x28, local copies, waits for them, and re-layouts: 1.92 us -> 3.22 us
    ppermute x8 -> x11, starting transfers between devices: 14.7 us -> 14.8 us  [swapped(): lax.ppermute(array, axis, [(i, i ^ bit) for i in range(lax.axis_size(axis...]
  transfers between devices with their start and end apart: 10 -> 13, of which waited for: 7 -> 6; matrix products, arithmetic and copies ran while one was open for 1% -> 0% of each run, Pallas kernels for 0% -> 6%
where the time goes in v3:
time: 83.6 us; the launch traced here: 83.1 us
  Pallas kernels  43.5 us (52%)
  starting transfers between devices  18.4 us (22%)
  waiting for transfers between devices  17.1 us (20%)
  local copies, waits for them, and re-layouts  3.22 us (4%)
    pallas_call x1, Pallas kernels, local(): pl.pallas_call(functools.partial(band_kernel, half, norm), in_specs=[smem...  35.1 us
    ppermute x11, starting transfers between devices, swapped(): lax.ppermute(array, axis, [(i, i ^ bit) for i in range(lax.axis_size(axis...  14.8 us
    ppermute x11, waiting for transfers between devices, swapped(): lax.ppermute(array, axis, [(i, i ^ bit) for i in range(lax.axis_size(axis...  13 us
    ppermute x2, waiting for transfers between devices, shifted(): return lax.ppermute(array, axis, pairs)  4.11 us
    ppermute x2, starting transfers between devices, shifted(): return lax.ppermute(array, axis, pairs)  3.64 us
    unnamed x28, local copies, waits for them, and re-layouts  3.22 us
    pallas_call x1, Pallas kernels, local(): pl.pallas_call(functools.partial(latent_kernel, rows, own), in_specs=[vme...  2.72 us
    pallas_call x1, Pallas kernels, local(): pl.pallas_call(functools.partial(edge_kernel, half, chan2), grid=(1,), in...  2.1 us
  transfers between devices with their start and end apart: 13, of which 6 were waited for; matrix products, arithmetic and copies ran while one was open for 0% of the time, Pallas kernels for 6%

profile of v3, /device:TPU:0, one launch (start us, length us, event | category | flops | bytes accessed | tf_op | source)
XLA Modules:
  0.0 83.1 jit_solution(7134214246558416461)
XLA Ops:
  0.7 2.1 %edges.1 = (bf16[50,8,128]{2,1,0:T(8,128)(2,1)}, bf16[1,6400]{1,0:T(2,128)(2,1)}) custom-call(bf16[1,8,23040]{2,1,0:T(8,128)(2,1)} %latent.4, bf16[1,32,23040]{2,1,0:T(8,128)(2,1)} %targets.3, s32[32,48]{1,0:T(8,128)} %land.3), custom_call_target="tpu_custom_call" | custom-call | tf_op jit(solution)/shard_map/edges/pallas_call | solution.py:442
  2.8 2.4 %collective-permute-start = (bf16[50,8,128]{2,1,0:T(8,128)(2,1)}, bf16[50,8,128]{2,1,0:T(8,128)(2,1)S(1)}, u32[]{:S(2)}, u32[]{:S(2)}) collective-permute-start(bf16[50,8,128]{2,1,0:T(8,128)(2,1)} %get-tuple-element.14), channel_id=1, source_target_pairs={{0,4},{4,8},{8,12},{12,16},{16,20},{20,24},{24,28},{1,5},{5,9},{9,... | collective-permute-start | bytes 307208 | tf_op jit(solution)/shard_map/ppermute | solution.py:24
  5.2 1.3 %collective-permute-start.1 = (bf16[1,6400]{1,0:T(2,128)(2,1)}, bf16[1,6400]{1,0:T(2,128)(2,1)S(1)}, u32[]{:S(2)}, u32[]{:S(2)}) collective-permute-start(bf16[1,6400]{1,0:T(2,128)(2,1)} %get-tuple-element.15), channel_id=1, source_target_pairs={{4,0},{8,4},{12,8},{16,12},{20,16},{24,20},{28,24},{5,1},{9,5},{13... | collective-permute-start | bytes 38408 | tf_op jit(solution)/shard_map/ppermute | solution.py:24
  6.5 4.1 %collective-permute-done.1.below = bf16[1,6400]{1,0:T(2,128)(2,1)S(1)} collective-permute-done((bf16[1,6400]{1,0:T(2,128)(2,1)}, bf16[1,6400]{1,0:T(2,128)(2,1)S(1)}, u32[]{:S(2)}, u32[]{:S(2)}) %collective-permute-start.1) | collective-permute-done | bytes 12832 | tf_op jit(solution)/shard_map/ppermute | solution.py:24
  10.6 0.9 %copy-done.3 = bf16[3,3,64,32]{2,3,1,0:T(8,128)(2,1)S(1)} copy-done((bf16[3,3,64,32]{2,3,1,0:T(8,128)(2,1)S(1)}, bf16[3,3,64,32]{2,3,1,0:T(8,128)(2,1)}, u32[]{:S(2)}) %copy-start.3) | copy-done | bytes 36888
  11.5 0.8 copy-done.5
  12.3 35.1 %band.1 = (f32[18,96,128]{2,1,0:T(8,128)S(1)}, f32[104,128]{1,0:T(8,128)S(1)}, f32[104,128]{1,0:T(8,128)S(1)}) custom-call(s32[8]{0:T(128)S(1)} %copy-done.6, f32[64]{0:T(128)S(1)} %copy-done.7, f32[16]{0:T(128)S(1)} %copy-done.8, bf16[1,8,23040]{2,1,0:T(8,128)(2,1)S(1)} %copy-done.1, bf16[50,8,128]{2,1,0:T(8,128)(2,1)S(1)} %collective-permute-done.above, ...), custom_call_target="tpu_custom_call" | custom-call | tf_op jit(solution)/shard_map/band/pallas_call | solution.py:465
  47.4 0.9 %copy-done.2 = f32[18,96,128]{2,1,0:T(8,128)} copy-done((f32[18,96,128]{2,1,0:T(8,128)}, f32[18,96,128]{2,1,0:T(8,128)S(1)}, u32[]{:S(2)}) %copy-start.2) | copy-done | bytes 884760
  48.3 2.6 %collective-permute-start.2 = (f32[104,128]{1,0:T(8,128)S(1)}, f32[104,128]{1,0:T(8,128)S(1)}, u32[]{:S(2)}, u32[]{:S(2)}) collective-permute-start(f32[104,128]{1,0:T(8,128)S(1)} %get-tuple-element.18), channel_id=1, source_target_pairs={{0,4},{4,0},{8,12},{12,8},{16,20},{20,16},{24,28},{28,24},{1,5},{5... | collective-permute-start | bytes 159752 | tf_op jit(solution)/shard_map/ppermute | solution.py:414
  50.9 0.9 %collective-permute-done.2 = f32[104,128]{1,0:T(8,128)S(1)} collective-permute-done((f32[104,128]{1,0:T(8,128)S(1)}, f32[104,128]{1,0:T(8,128)S(1)}, u32[]{:S(2)}, u32[]{:S(2)}) %collective-permute-start.2) | collective-permute-done | bytes 53280 | tf_op jit(solution)/shard_map/ppermute | solution.py:414
  51.8 1.5 %collective-permute-start.4 = (f32[104,128]{1,0:T(8,128)S(1)}, f32[104,128]{1,0:T(8,128)S(1)}, u32[]{:S(2)}, u32[]{:S(2)}) collective-permute-start(f32[104,128]{1,0:T(8,128)S(1)} %add.21), channel_id=1, source_target_pairs={{0,16},{4,20},{8,24},{12,28},{16,0},{20,4},{24,8},{28,12},{1,17},{... | collective-permute-start | bytes 159752 | tf_op jit(solution)/shard_map/ppermute | solution.py:414
  53.3 2.3 %collective-permute-start.5 = (f32[104,128]{1,0:T(8,128)S(1)}, f32[104,128]{1,0:T(8,128)S(1)}, u32[]{:S(2)}, u32[]{:S(2)}) collective-permute-start(f32[104,128]{1,0:T(8,128)S(1)} %add.21), channel_id=1, source_target_pairs={{0,24},{4,28},{8,16},{12,20},{16,8},{20,12},{24,0},{28,4},{1,25},{... | collective-permute-start | bytes 159752 | tf_op jit(solution)/shard_map/ppermute | solution.py:414
  55.7 2.7 %latent.5.part0 = bf16[8,5760]{1,0:T(8,128)(2,1)} custom-call(f32[18,96,128]{2,1,0:T(8,128)} %copy-done.2, bf16[3,3,32,64]{3,2,1,0:T(8,128)(2,1)} %bitcast.4), custom_call_target="tpu_custom_call" | custom-call | tf_op jit(solution)/shard_map/latent/pallas_call | solution.py:508
  58.4 1.6 %collective-permute-start.6 = (bf16[8,5760]{1,0:T(8,128)(2,1)}, bf16[8,5760]{1,0:T(8,128)(2,1)S(1)}, u32[]{:S(2)}, u32[]{:S(2)}) collective-permute-start(bf16[8,5760]{1,0:T(8,128)(2,1)} %latent.5.part0), channel_id=1, source_target_pairs={{0,1},{1,0},{2,3},{3,2},{4,5},{5,4},{6,7},{7,6},{8,9},{9,8},{10,11... | collective-permute-start | bytes 276488 | tf_op jit(solution)/shard_map/ppermute | solution.py:414
  60.0 2.6 %collective-permute-start.7 = (bf16[8,5760]{1,0:T(8,128)(2,1)}, bf16[8,5760]{1,0:T(8,128)(2,1)S(1)}, u32[]{:S(2)}, u32[]{:S(2)}) collective-permute-start(bf16[8,5760]{1,0:T(8,128)(2,1)} %latent.5.part0), channel_id=1, source_target_pairs={{0,2},{1,3},{2,0},{3,1},{4,6},{5,7},{6,4},{7,5},{8,10},{9,11},{10,... | collective-permute-start | bytes 276488 | tf_op jit(solution)/shard_map/ppermute | solution.py:414
  62.8 0.3 collective-permute-done.6.part1
  63.1 7.0 %collective-permute-done.7.part2 = bf16[8,5760]{1,0:T(8,128)(2,1)S(1)} collective-permute-done((bf16[8,5760]{1,0:T(8,128)(2,1)}, bf16[8,5760]{1,0:T(8,128)(2,1)S(1)}, u32[]{:S(2)}, u32[]{:S(2)}) %collective-permute-start.7) | collective-permute-done | bytes 92192 | tf_op jit(solution)/shard_map/ppermute | solution.py:414
  70.2 2.5 %collective-permute-start.10 = (f32[104,128]{1,0:T(8,128)S(1)}, f32[104,128]{1,0:T(8,128)S(1)}, u32[]{:S(2)}, u32[]{:S(2)}) collective-permute-start(f32[104,128]{1,0:T(8,128)S(1)} %add_add_fusion.1), channel_id=1, source_target_pairs={{0,2},{1,3},{2,0},{3,1},{4,6},{5,7},{6,4},{7,5},{8,10},{9,11},{10,... | collective-permute-start | bytes 159752 | tf_op jit(solution)/shard_map/ppermute | solution.py:414
  72.7 1.4 %collective-permute-start.11 = (f32[104,128]{1,0:T(8,128)S(1)}, f32[104,128]{1,0:T(8,128)S(1)}, u32[]{:S(2)}, u32[]{:S(2)}) collective-permute-start(f32[104,128]{1,0:T(8,128)S(1)} %add_add_fusion.1), channel_id=1, source_target_pairs={{0,3},{1,2},{2,1},{3,0},{4,7},{5,6},{6,5},{7,4},{8,11},{9,10},{10,... | collective-permute-start | bytes 159752 | tf_op jit(solution)/shard_map/ppermute | solution.py:414
  74.1 1.2 %collective-permute-done.10 = f32[104,128]{1,0:T(8,128)S(1)} collective-permute-done((f32[104,128]{1,0:T(8,128)S(1)}, f32[104,128]{1,0:T(8,128)S(1)}, u32[]{:S(2)}, u32[]{:S(2)}) %collective-permute-start.10) | collective-permute-done | bytes 53280 | tf_op jit(solution)/shard_map/ppermute | solution.py:414
  75.3 3.4 %collective-permute-done.11 = f32[104,128]{1,0:T(8,128)S(1)} collective-permute-done((f32[104,128]{1,0:T(8,128)S(1)}, f32[104,128]{1,0:T(8,128)S(1)}, u32[]{:S(2)}, u32[]{:S(2)}) %collective-permute-start.11) | collective-permute-done | bytes 53280 | tf_op jit(solution)/shard_map/ppermute | solution.py:414
  78.9 1.9 %place.1 = f32[1,8,23040]{2,1,0:T(8,128)} custom-call(bf16[8,5760]{1,0:T(8,128)(2,1)} %latent.5.part0, bf16[8,5760]{1,0:T(8,128)(2,1)} %copy-done.10, bf16[8,5760]{1,0:T(8,128)(2,1)} %copy-done.11, bf16[8,5760]{1,0:T(8,128)(2,1)} %copy-done.12), custom_call_target="tpu_custom_call" | custom-call | tf_op jit(solution)/shard_map/place/pallas_call | solution.py:522
  80.9 0.6 copy-done.13
  81.5 1.6 %taps.1 = (f32[3,3,32,64]{3,2,1,0:T(8,128)}, f32[3,3,16,32]{3,2,1,0:T(8,128)}) custom-call(f32[104,128]{1,0:T(8,128)} %copy-done.9, f32[104,128]{1,0:T(8,128)} %copy-done.13), custom_call_target="tpu_custom_call" | custom-call | tf_op jit(solution)/shard_map/taps/pallas_call | solution.py:531
  (38 shorter events, 0.4 us)
Async XLA Ops:
  0.6 9.9 %copy-start.1 = (bf16[1,8,23040]{2,1,0:T(8,128)(2,1)S(1)}, bf16[1,8,23040]{2,1,0:T(8,128)(2,1)}, u32[]{:S(2)}) copy-start(bf16[1,8,23040]{2,1,0:T(8,128)(2,1)} %latent.4) | copy-start | bytes 1105924
  0.6 9.9 %copy-start = (bf16[1,32,23040]{2,1,0:T(8,128)(2,1)S(1)}, bf16[1,32,23040]{2,1,0:T(8,128)(2,1)}, u32[]{:S(2)}) copy-start(bf16[1,32,23040]{2,1,0:T(8,128)(2,1)} %targets.3) | copy-start | bytes 4423684
  0.7 9.9 %copy-start.4 = (s32[32,48]{1,0:T(8,128)S(1)}, s32[32,48]{1,0:T(8,128)}, u32[]{:S(2)}) copy-start(s32[32,48]{1,0:T(8,128)} %land.3) | copy-start | bytes 18436
  0.7 9.9 %copy-start.6 = (s32[8]{0:T(128)S(1)}, s32[8]{0:T(128)}, u32[]{:S(2)}) copy-start(s32[8]{0:T(128)} %seeds.1) | copy-start | bytes 100
  0.7 9.9 %copy-start.7 = (f32[64]{0:T(128)S(1)}, f32[64]{0:T(128)}, u32[]{:S(2)}) copy-start(f32[64]{0:T(128)} %scale.1) | copy-start | bytes 772
  0.7 9.9 %copy-start.8 = (f32[16]{0:T(128)S(1)}, f32[16]{0:T(128)}, u32[]{:S(2)}) copy-start(f32[16]{0:T(128)} %channel_weight.1) | copy-start | bytes 196
  2.8 7.8 %collective-permute-start = (bf16[50,8,128]{2,1,0:T(8,128)(2,1)}, bf16[50,8,128]{2,1,0:T(8,128)(2,1)S(1)}, u32[]{:S(2)}, u32[]{:S(2)}) collective-permute-start(bf16[50,8,128]{2,1,0:T(8,128)(2,1)} %get-tuple-element.14), channel_id=1, source_target_pairs={{0,4},{4,8},{8,12},{12,16},{16,20},{20,24},{24,28},{1,5},{5,9},{9,... | collective-permute-start | bytes 307208 | tf_op jit(solution)/shard_map/ppermute | solution.py:24
  5.2 5.4 %collective-permute-start.1 = (bf16[1,6400]{1,0:T(2,128)(2,1)}, bf16[1,6400]{1,0:T(2,128)(2,1)S(1)}, u32[]{:S(2)}, u32[]{:S(2)}) collective-permute-start(bf16[1,6400]{1,0:T(2,128)(2,1)} %get-tuple-element.15), channel_id=1, source_target_pairs={{4,0},{8,4},{12,8},{16,12},{20,16},{24,20},{28,24},{5,1},{9,5},{13... | collective-permute-start | bytes 38408 | tf_op jit(solution)/shard_map/ppermute | solution.py:24
  47.4 0.9 %copy-start.2 = (f32[18,96,128]{2,1,0:T(8,128)}, f32[18,96,128]{2,1,0:T(8,128)S(1)}, u32[]{:S(2)}) copy-start(f32[18,96,128]{2,1,0:T(8,128)S(1)} %get-tuple-element.16.sums) | copy-start | bytes 2654212
  48.3 3.4 %collective-permute-start.2 = (f32[104,128]{1,0:T(8,128)S(1)}, f32[104,128]{1,0:T(8,128)S(1)}, u32[]{:S(2)}, u32[]{:S(2)}) collective-permute-start(f32[104,128]{1,0:T(8,128)S(1)} %get-tuple-element.18), channel_id=1, source_target_pairs={{0,4},{4,0},{8,12},{12,8},{16,20},{20,16},{24,28},{28,24},{1,5},{5... | collective-permute-start | bytes 159752 | tf_op jit(solution)/shard_map/ppermute | solution.py:414
  51.8 10.8 %collective-permute-start.4 = (f32[104,128]{1,0:T(8,128)S(1)}, f32[104,128]{1,0:T(8,128)S(1)}, u32[]{:S(2)}, u32[]{:S(2)}) collective-permute-start(f32[104,128]{1,0:T(8,128)S(1)} %add.21), channel_id=1, source_target_pairs={{0,16},{4,20},{8,24},{12,28},{16,0},{20,4},{24,8},{28,12},{1,17},{... | collective-permute-start | bytes 159752 | tf_op jit(solution)/shard_map/ppermute | solution.py:414
  53.3 9.4 %collective-permute-start.5 = (f32[104,128]{1,0:T(8,128)S(1)}, f32[104,128]{1,0:T(8,128)S(1)}, u32[]{:S(2)}, u32[]{:S(2)}) collective-permute-start(f32[104,128]{1,0:T(8,128)S(1)} %add.21), channel_id=1, source_target_pairs={{0,24},{4,28},{8,16},{12,20},{16,8},{20,12},{24,0},{28,4},{1,25},{... | collective-permute-start | bytes 159752 | tf_op jit(solution)/shard_map/ppermute | solution.py:414
  55.7 7.1 %collective-permute-start.3 = (f32[104,128]{1,0:T(8,128)S(1)}, f32[104,128]{1,0:T(8,128)S(1)}, u32[]{:S(2)}, u32[]{:S(2)}) collective-permute-start(f32[104,128]{1,0:T(8,128)S(1)} %add.21), channel_id=1, source_target_pairs={{0,8},{4,12},{8,0},{12,4},{16,24},{20,28},{24,16},{28,20},{1,9},{5... | collective-permute-start | bytes 159752 | tf_op jit(solution)/shard_map/ppermute | solution.py:414
  58.4 4.8 %collective-permute-start.6 = (bf16[8,5760]{1,0:T(8,128)(2,1)}, bf16[8,5760]{1,0:T(8,128)(2,1)S(1)}, u32[]{:S(2)}, u32[]{:S(2)}) collective-permute-start(bf16[8,5760]{1,0:T(8,128)(2,1)} %latent.5.part0), channel_id=1, source_target_pairs={{0,1},{1,0},{2,3},{3,2},{4,5},{5,4},{6,7},{7,6},{8,9},{9,8},{10,11... | collective-permute-start | bytes 276488 | tf_op jit(solution)/shard_map/ppermute | solution.py:414
  60.0 10.2 %collective-permute-start.7 = (bf16[8,5760]{1,0:T(8,128)(2,1)}, bf16[8,5760]{1,0:T(8,128)(2,1)S(1)}, u32[]{:S(2)}, u32[]{:S(2)}) collective-permute-start(bf16[8,5760]{1,0:T(8,128)(2,1)} %latent.5.part0), channel_id=1, source_target_pairs={{0,2},{1,3},{2,0},{3,1},{4,6},{5,7},{6,4},{7,5},{8,10},{9,11},{10,... | collective-permute-start | bytes 276488 | tf_op jit(solution)/shard_map/ppermute | solution.py:414
  62.6 7.6 %collective-permute-start.8 = (bf16[8,5760]{1,0:T(8,128)(2,1)}, bf16[8,5760]{1,0:T(8,128)(2,1)S(1)}, u32[]{:S(2)}, u32[]{:S(2)}) collective-permute-start(bf16[8,5760]{1,0:T(8,128)(2,1)} %latent.5.part0), channel_id=1, source_target_pairs={{0,3},{1,2},{2,1},{3,0},{4,7},{5,6},{6,5},{7,4},{8,11},{9,10},{10,... | collective-permute-start | bytes 276488 | tf_op jit(solution)/shard_map/ppermute | solution.py:414
  63.1 15.8 %copy-start.10 = (bf16[8,5760]{1,0:T(8,128)(2,1)}, bf16[8,5760]{1,0:T(8,128)(2,1)S(1)}, u32[]{:S(2)}) copy-start(bf16[8,5760]{1,0:T(8,128)(2,1)S(1)} %collective-permute-done.6.part1) | copy-start | bytes 276484
  70.2 8.7 %copy-start.11 = (bf16[8,5760]{1,0:T(8,128)(2,1)}, bf16[8,5760]{1,0:T(8,128)(2,1)S(1)}, u32[]{:S(2)}) copy-start(bf16[8,5760]{1,0:T(8,128)(2,1)S(1)} %collective-permute-done.7.part2) | copy-start | bytes 276484
  70.2 8.7 %copy-start.12 = (bf16[8,5760]{1,0:T(8,128)(2,1)}, bf16[8,5760]{1,0:T(8,128)(2,1)S(1)}, u32[]{:S(2)}) copy-start(bf16[8,5760]{1,0:T(8,128)(2,1)S(1)} %collective-permute-done.8.part3) | copy-start | bytes 276484
  70.2 5.1 %collective-permute-start.10 = (f32[104,128]{1,0:T(8,128)S(1)}, f32[104,128]{1,0:T(8,128)S(1)}, u32[]{:S(2)}, u32[]{:S(2)}) collective-permute-start(f32[104,128]{1,0:T(8,128)S(1)} %add_add_fusion.1), channel_id=1, source_target_pairs={{0,2},{1,3},{2,0},{3,1},{4,6},{5,7},{6,4},{7,5},{8,10},{9,11},{10,... | collective-permute-start | bytes 159752 | tf_op jit(solution)/shard_map/ppermute | solution.py:414
  72.7 6.0 %collective-permute-start.11 = (f32[104,128]{1,0:T(8,128)S(1)}, f32[104,128]{1,0:T(8,128)S(1)}, u32[]{:S(2)}, u32[]{:S(2)}) collective-permute-start(f32[104,128]{1,0:T(8,128)S(1)} %add_add_fusion.1), channel_id=1, source_target_pairs={{0,3},{1,2},{2,1},{3,0},{4,7},{5,6},{6,5},{7,4},{8,11},{9,10},{10,... | collective-permute-start | bytes 159752 | tf_op jit(solution)/shard_map/ppermute | solution.py:414
  74.1 4.7 %collective-permute-start.9 = (f32[104,128]{1,0:T(8,128)S(1)}, f32[104,128]{1,0:T(8,128)S(1)}, u32[]{:S(2)}, u32[]{:S(2)}) collective-permute-start(f32[104,128]{1,0:T(8,128)S(1)} %add_add_fusion.1), channel_id=1, source_target_pairs={{0,1},{1,0},{2,3},{3,2},{4,5},{5,4},{6,7},{7,6},{8,9},{9,8},{10,11... | collective-permute-start | bytes 159752 | tf_op jit(solution)/shard_map/ppermute | solution.py:414
  78.8 2.1 %copy-start.9 = (f32[104,128]{1,0:T(8,128)}, f32[104,128]{1,0:T(8,128)S(1)}, u32[]{:S(2)}) copy-start(f32[104,128]{1,0:T(8,128)S(1)} %add_add_fusion.mine) | copy-start | bytes 159748
  78.8 2.1 %collective-permute-start.12 = (f32[104,128]{1,0:T(8,128)S(1)}, f32[104,128]{1,0:T(8,128)S(1)}, u32[]{:S(2)}, u32[]{:S(2)}) collective-permute-start(f32[104,128]{1,0:T(8,128)S(1)} %add_add_fusion.mine), channel_id=1, source_target_pairs={{0,4},{4,0},{8,12},{12,8},{16,20},{20,16},{24,28},{28,24},{1,5},{5... | collective-permute-start | bytes 159752 | tf_op jit(solution)/shard_map/ppermute | solution.py:414
  (3 other events, 2.3 us)

commit v4 on v3

--- a/solution.py
+++ b/solution.py
@@ -110,6 +110,10 @@
             out_ref[at : at + chan_out, :] = packed * norm
 
 
+def spread_line(ref, slot, at):
+    return ref[slot, pl.ds(at, 8, stride=0), :]
+
+
 def window_block(mem_pos, own, half, blocks, part, t):
     at = mem_pos * own + part * half + t + (blocks - 1)
     at = jnp.where(at >= blocks, at - blocks, at)
@@ -214,13 +218,15 @@
     band_two,
     back_two,
     source,
-    pre,
+    pre_even,
+    pre_odd,
     act,
     slope,
-    cast,
-    fgrad,
+    cast_even,
+    cast_odd,
+    fgrad_even,
+    fgrad_odd,
     carry,
-    pgrad,
     taps,
     acc_one,
     acc_two,
@@ -272,9 +278,10 @@
     build_band(kernel_two, band_two)
     build_back(kernel_two, back_two)
 
-    source[rows + 2] = jnp.zeros(source.shape[1:], bf16)
+    source[rows + 2 :] = jnp.zeros((2,) + source.shape[1:], bf16)
     source[:, wide] = jnp.zeros((source.shape[0],) + source.shape[2:], bf16)
-    fgrad[:, 0] = jnp.zeros((2,) + fgrad.shape[2:], bf16)
+    fgrad_even[:, 0] = jnp.zeros((4,) + fgrad_even.shape[2:], bf16)
+    fgrad_odd[...] = jnp.zeros(fgrad_odd.shape, bf16)
     carry[...] = jnp.zeros(carry.shape, f32)
     acc_one[...] = jnp.zeros(acc_one.shape, f32)
     acc_two[...] = jnp.zeros(acc_two.shape, f32)
@@ -300,7 +307,7 @@
                 h = jnp.bitwise_xor(h, jnp.right_shift(h, 13))
                 noise = jnp.bitwise_and(h, 65535).astype(f32) * (1.0 / 65536.0) - 0.5
                 noise = noise * 3.4641016
-                cell = lat_rows[t * 2 + part, pl.ds(at, 1), :]
+                cell = spread_line(lat_rows, t * 2 + part, at)
                 parts.append((cell + noise * scale_table) * inside)
             source[i, t] = jnp.concatenate(parts, axis=0).astype(bf16)
         return 0
@@ -315,8 +322,10 @@
             [piece(i, start), piece(i + 1, start), piece(i, start + 1), piece(i + 1, start + 1)], axis=1
         )
 
-    def first_segment(i, _):
+    def first_product(i, pre):
         pre[...] = jnp.dot(operand(source, i, 0, wide), band_one[...], preferred_element_type=f32)
+
+    def first_gelu(i, pre):
         for t in range(wide):
             for sub in range(2):
                 x = pre[t * 16 : (t + 1) * 16, sub * LANES : (sub + 1) * LANES]
@@ -329,9 +338,16 @@
                     if t == half:
                         d = jnp.where(iota((16, LANES), 0) < 8, d, 0.0)
                     slope[2 * i + sub, t] = d
+
+    def first_segment(m, _):
+        first_product(2 * m + 1, pre_odd)
+        first_gelu(2 * m, pre_even)
+        first_product(2 * m + 2, pre_even)
+        first_gelu(2 * m + 1, pre_odd)
         return 0
 
-    lax.fori_loop(0, rows + 2, first_segment, 0)
+    first_product(0, pre_even)
+    lax.fori_loop(0, rows // 2 + 1, first_segment, 0)
 
     members = front * 16
     owner = iota((48, members), 0)
@@ -342,22 +358,26 @@
     pick_prev = ((group // 2 < half) & (place == owner)).astype(bf16)
     pick = jnp.concatenate([pick_own, pick_prev], axis=0)
 
-    def second_segment(j, _):
-        taken = operand(act, j, 0, front)
-        cast[...] = jnp.dot(taken, band_two[...], preferred_element_type=f32)
-        for sub in range(2):
-            p = 2 * j + sub
-            line = jnp.where(p >= 4, p - 4, p + grid_rows)
+    def second_product(n, cast):
+        taken = jnp.concatenate([operand(act, 2 * n + k, 0, front) for k in range(2)], axis=0)
+        out = jnp.dot(taken, band_two[...], preferred_element_type=f32).astype(bf16)
+        for k in range(2):
+            for sub in range(2):
+                part = out[k * members : (k + 1) * members, sub * LANES : (sub + 1) * LANES]
+                cast[2 * k + sub] = part.reshape(front, 16, LANES)
+
+    def loss_gradient(n, cast, fgrad):
+        first = jnp.where(n >= 1, 4 * (n - 1), grid_rows)
+        for line in range(4):
             for t in range(front):
+                both = cast[line, t].astype(f32)
                 parts = []
                 for part in range(2):
                     if t == half and part == 1:
                         parts.append(jnp.zeros((8, LANES), f32))
                         continue
-                    at = t * 16 + part * 8
-                    f = cast[at : at + 8, sub * LANES : (sub + 1) * LANES].astype(bf16).astype(f32)
-                    y = tgt_rows[t * 2 + part, pl.ds(line, 1), :]
-                    d = f - y
+                    f = both[part * 8 : part * 8 + 8]
+                    d = f - spread_line(tgt_rows, t * 2 + part, first + line)
                     goal = d * lax.rsqrt(d * d + SMOOTH)
                     gs = []
                     for k in range(1, 5):
@@ -368,39 +388,57 @@
                         back = gs[k] + pltpu.roll(back, MEM - 1, 0)
                     back = pltpu.roll(back, MEM - 1, 0)
                     spread = (gs[0] + gs[1]) + (gs[2] + gs[3]) - back
-                    weight = weight_rows[t * 2 + part, pl.ds(line, 1), :]
+                    weight = spread_line(weight_rows, t * 2 + part, first + line)
                     parts.append(weight * ((MEM - 1.0) * goal - spread))
-                fgrad[sub, t + 1] = jnp.concatenate(parts, axis=0).astype(bf16)
-
-        def flat(sub, at, count):
-            return fgrad[sub, at : at + count].reshape(count * 16, LANES)
-
-        @pl.when(j >= 2)
-        def _():
-            g = jnp.concatenate([flat(0, 2, half), flat(1, 2, half)], axis=1)
-            x = operand(act, j, 1, half)
-            acc_two[...] += lax.dot_general(g, x, (((0,), (0,)), ((), ())), preferred_element_type=f32)
-
-        g = jnp.concatenate([flat(0, 1, front), flat(1, 1, front), flat(0, 0, front), flat(1, 0, front)], axis=1)
-        pulled = jnp.dot(g, back_two[...], preferred_element_type=f32)
-        grad = pulled[:, :LANES] + carry[...]
-        carry[...] = pulled[:, LANES:]
-        grad = (grad * slope[j].reshape(members, LANES)).astype(bf16)
-        pgrad[j] = grad.reshape(front, 16, LANES)
-        sums[j] = jnp.dot(pick, grad, preferred_element_type=f32)
+                fgrad[line, t + 1] = jnp.concatenate(parts, axis=0).astype(bf16)
+
+    def pull_back(n, fgrad):
+        at = jnp.maximum(n, 0)
+        keep = jnp.where(n >= 1, 1.0, 0.0).astype(bf16)
+
+        def flat(line, start, count):
+            return fgrad[line, start : start + count].reshape(count * 16, LANES)
+
+        def product(g, x):
+            return lax.dot_general(g, x, (((0,), (0,)), ((), ())), preferred_element_type=f32)
+
+        g = [
+            jnp.concatenate(
+                [flat(2 * k, 1, front), flat(2 * k + 1, 1, front), flat(2 * k, 0, front), flat(2 * k + 1, 0, front)],
+                axis=1,
+            )
+            for k in range(2)
+        ]
+        pulled = jnp.dot(jnp.concatenate(g, axis=0), back_two[...], preferred_element_type=f32)
+        g = [jnp.concatenate([flat(2 * k, 2, half), flat(2 * k + 1, 2, half)], axis=1) for k in range(2)]
+        x = [operand(act, 2 * at + k, 1, half) for k in range(2)]
+        acc_two[...] += product(jnp.concatenate(g, axis=0) * keep, jnp.concatenate(x, axis=0))
+        grads = [
+            pulled[:members, :LANES] + carry[...],
+            pulled[members:, :LANES] + pulled[:members, LANES:],
+        ]
+        carry[...] = pulled[members:, LANES:]
+        grads = [(grads[k] * slope[2 * at + k].reshape(members, LANES)).astype(bf16) for k in range(2)]
+        grads = jnp.concatenate(grads, axis=1)
+        total_grad = jnp.dot(pick, grads, preferred_element_type=f32)
+        for k in range(2):
+            sums[2 * at + k] = total_grad[:, k * LANES : (k + 1) * LANES]
+        acc_one[...] += product(grads[16:] * keep, operand(source, at, 1, half))
+
+    def second_segment(m, _):
+        second_product(2 * m + 1, cast_odd)
+        loss_gradient(2 * m, cast_even, fgrad_even)
+        pull_back(2 * m - 1, fgrad_odd)
+        second_product(2 * m + 2, cast_even)
+        loss_gradient(2 * m + 1, cast_odd, fgrad_odd)
+        pull_back(2 * m, fgrad_even)
         return 0
 
-    lax.fori_loop(0, 2 * rows + 2, second_segment, 0)
-
-    def first_taps(i, _):
-        g = jnp.concatenate(
-            [pgrad[2 * i + sub, pl.ds(1, half)].reshape(half * 16, LANES) for sub in range(2)], axis=1
-        )
-        x = operand(source, i, 1, half)
-        acc_one[...] += lax.dot_general(g, x, (((0,), (0,)), ((), ())), preferred_element_type=f32)
-        return 0
-
-    lax.fori_loop(1, rows + 1, first_taps, 0)
+    second_product(0, cast_even)
+    lax.fori_loop(0, rows // 2, second_segment, 0)
+    loss_gradient(rows, cast_even, fgrad_even)
+    pull_back(rows - 1, fgrad_odd)
+    pull_back(rows, fgrad_even)
 
     pack_taps(acc_one, taps, 0, chan0, chan1, norm)
     pack_taps(acc_two, taps, -(-9 // (LANES // chan0)) * chan1, chan1, chan2, norm)
@@ -430,7 +468,7 @@
     lat_count = lax.axis_size("lat")
     own = span // LANES // lax.axis_size("mem")
     half = (own + 1) // 2
-    assert sample_count == 1 and member_seeds.shape[0] == MEM and own % 2 == 1 and lax.axis_size("mem") == 4
+    assert sample_count == 1 and member_seeds.shape[0] == MEM and rows % 2 == 0 and own % 2 == 1 and lax.axis_size("mem") == 4
     assert 4 * chan2 == 2 * chan1 == chan0 and chan0 == 64
     vmem = pl.BlockSpec(memory_space=pltpu.VMEM)
     smem = pl.BlockSpec(memory_space=pltpu.SMEM)
@@ -479,14 +517,16 @@
             pltpu.VMEM((512, 256), bf16),
             pltpu.VMEM((512, 256), bf16),
             pltpu.VMEM((512, 256), bf16),
-            pltpu.VMEM((rows + 3, wide + 1, 16, LANES), bf16),
+            pltpu.VMEM((rows + 4, wide + 1, 16, LANES), bf16),
+            pltpu.VMEM((wide * 16, 2 * LANES), f32),
             pltpu.VMEM((wide * 16, 2 * LANES), f32),
             pltpu.VMEM((2 * rows + 4, wide, 16, LANES), bf16),
             pltpu.VMEM((2 * rows + 4, front, 16, LANES), f32),
-            pltpu.VMEM((front * 16, 2 * LANES), f32),
-            pltpu.VMEM((2, front + 1, 16, LANES), bf16),
+            pltpu.VMEM((4, front, 16, LANES), bf16),
+            pltpu.VMEM((4, front, 16, LANES), bf16),
+            pltpu.VMEM((4, front + 1, 16, LANES), bf16),
+            pltpu.VMEM((4, front + 1, 16, LANES), bf16),
             pltpu.VMEM((front * 16, LANES), f32),
-            pltpu.VMEM((2 * rows + 2, front, 16, LANES), bf16),
             pltpu.VMEM((tap_rows, LANES), f32),
             pltpu.VMEM((256, 512), f32),
             pltpu.VMEM((256, 512), f32),

time: 83.6 us -> 71.7 us (0.86)
  Pallas kernels: 43.5 us -> 31.6 us
    pallas_call x1, Pallas kernels: 35.1 us -> 23.3 us  [local(): pl.pallas_call(functools.partial(band_kernel, half, norm), in_specs=[smem...]
  transfers between devices with their start and end apart: 13 -> 13, of which waited for: 6 -> 6; matrix products, arithmetic and copies ran while one was open for 0% -> 0% of each run, Pallas kernels for 6% -> 7%
where the time goes in v4:
time: 71.7 us; the launch traced here: 71.3 us
  Pallas kernels  31.6 us (44%)
  starting transfers between devices  18.5 us (26%)
  waiting for transfers between devices  17.1 us (24%)
  local copies, waits for them, and re-layouts  3.22 us (4%)
  between operations  0.81 us (1%)
    pallas_call x1, Pallas kernels, local(): pl.pallas_call(functools.partial(band_kernel, half, norm), in_specs=[smem...  23.3 us
    ppermute x11, starting transfers between devices, swapped(): lax.ppermute(array, axis, [(i, i ^ bit) for i in range(lax.axis_size(axis...  14.8 us
    ppermute x11, waiting for transfers between devices, swapped(): lax.ppermute(array, axis, [(i, i ^ bit) for i in range(lax.axis_size(axis...  13 us
    ppermute x2, waiting for transfers between devices, shifted(): return lax.ppermute(array, axis, pairs)  4.11 us
    ppermute x2, starting transfers between devices, shifted(): return lax.ppermute(array, axis, pairs)  3.64 us
    unnamed x28, local copies, waits for them, and re-layouts  3.22 us
    pallas_call x1, Pallas kernels, local(): pl.pallas_call(functools.partial(latent_kernel, rows, own), in_specs=[vme...  2.72 us
    pallas_call x1, Pallas kernels, local(): pl.pallas_call(functools.partial(edge_kernel, half, chan2), grid=(1,), in...  2.1 us
  transfers between devices with their start and end apart: 13, of which 6 were waited for; matrix products, arithmetic and copies ran while one was open for 0% of the time, Pallas kernels for 7%

profile of v4, /device:TPU:0, one launch (start us, length us, event | category | flops | bytes accessed | tf_op | source)
XLA Modules:
  0.0 71.3 jit_solution(12563137791144559712)
XLA Ops:
  0.7 2.1 %edges.1 = (bf16[50,8,128]{2,1,0:T(8,128)(2,1)}, bf16[1,6400]{1,0:T(2,128)(2,1)}) custom-call(bf16[1,8,23040]{2,1,0:T(8,128)(2,1)} %latent.4, bf16[1,32,23040]{2,1,0:T(8,128)(2,1)} %targets.3, s32[32,48]{1,0:T(8,128)} %land.3), custom_call_target="tpu_custom_call" | custom-call | tf_op jit(solution)/shard_map/edges/pallas_call | solution.py:480
  2.8 2.4 %collective-permute-start = (bf16[50,8,128]{2,1,0:T(8,128)(2,1)}, bf16[50,8,128]{2,1,0:T(8,128)(2,1)S(1)}, u32[]{:S(2)}, u32[]{:S(2)}) collective-permute-start(bf16[50,8,128]{2,1,0:T(8,128)(2,1)} %get-tuple-element.14), channel_id=1, source_target_pairs={{0,4},{4,8},{8,12},{12,16},{16,20},{20,24},{24,28},{1,5},{5,9},{9,... | collective-permute-start | bytes 307208 | tf_op jit(solution)/shard_map/ppermute | solution.py:24
  5.2 1.3 %collective-permute-start.1 = (bf16[1,6400]{1,0:T(2,128)(2,1)}, bf16[1,6400]{1,0:T(2,128)(2,1)S(1)}, u32[]{:S(2)}, u32[]{:S(2)}) collective-permute-start(bf16[1,6400]{1,0:T(2,128)(2,1)} %get-tuple-element.15), channel_id=1, source_target_pairs={{4,0},{8,4},{12,8},{16,12},{20,16},{24,20},{28,24},{5,1},{9,5},{13... | collective-permute-start | bytes 38408 | tf_op jit(solution)/shard_map/ppermute | solution.py:24
  6.5 4.1 %collective-permute-done.1.below = bf16[1,6400]{1,0:T(2,128)(2,1)S(1)} collective-permute-done((bf16[1,6400]{1,0:T(2,128)(2,1)}, bf16[1,6400]{1,0:T(2,128)(2,1)S(1)}, u32[]{:S(2)}, u32[]{:S(2)}) %collective-permute-start.1) | collective-permute-done | bytes 12832 | tf_op jit(solution)/shard_map/ppermute | solution.py:24
  10.6 0.9 %copy-done.3 = bf16[3,3,64,32]{2,3,1,0:T(8,128)(2,1)S(1)} copy-done((bf16[3,3,64,32]{2,3,1,0:T(8,128)(2,1)S(1)}, bf16[3,3,64,32]{2,3,1,0:T(8,128)(2,1)}, u32[]{:S(2)}) %copy-start.3) | copy-done | bytes 36888
  11.5 0.8 %copy-done.5 = bf16[3,3,32,16]{2,3,1,0:T(8,128)(2,1)S(1)} copy-done((bf16[3,3,32,16]{2,3,1,0:T(8,128)(2,1)S(1)}, bf16[3,3,32,16]{2,3,1,0:T(8,128)(2,1)}, u32[]{:S(2)}) %copy-start.5) | copy-done | bytes 9240
  12.3 23.3 %band.1 = (f32[18,96,128]{2,1,0:T(8,128)S(1)}, f32[104,128]{1,0:T(8,128)S(1)}, f32[104,128]{1,0:T(8,128)S(1)}) custom-call(s32[8]{0:T(128)S(1)} %copy-done.6, f32[64]{0:T(128)S(1)} %copy-done.7, f32[16]{0:T(128)S(1)} %copy-done.8, bf16[1,8,23040]{2,1,0:T(8,128)(2,1)S(1)} %copy-done.1, bf16[50,8,128]{2,1,0:T(8,128)(2,1)S(1)} %collective-permute-done.above, ...), custom_call_target="tpu_custom_call" | custom-call | tf_op jit(solution)/shard_map/band/pallas_call | solution.py:503
  35.5 0.9 %copy-done.2 = f32[18,96,128]{2,1,0:T(8,128)} copy-done((f32[18,96,128]{2,1,0:T(8,128)}, f32[18,96,128]{2,1,0:T(8,128)S(1)}, u32[]{:S(2)}) %copy-start.2) | copy-done | bytes 884760
  36.5 2.6 %collective-permute-start.2 = (f32[104,128]{1,0:T(8,128)S(1)}, f32[104,128]{1,0:T(8,128)S(1)}, u32[]{:S(2)}, u32[]{:S(2)}) collective-permute-start(f32[104,128]{1,0:T(8,128)S(1)} %get-tuple-element.18), channel_id=1, source_target_pairs={{0,4},{4,0},{8,12},{12,8},{16,20},{20,16},{24,28},{28,24},{1,5},{5... | collective-permute-start | bytes 159752 | tf_op jit(solution)/shard_map/ppermute | solution.py:452
  39.0 0.9 %collective-permute-done.2 = f32[104,128]{1,0:T(8,128)S(1)} collective-permute-done((f32[104,128]{1,0:T(8,128)S(1)}, f32[104,128]{1,0:T(8,128)S(1)}, u32[]{:S(2)}, u32[]{:S(2)}) %collective-permute-start.2) | collective-permute-done | bytes 53280 | tf_op jit(solution)/shard_map/ppermute | solution.py:452
  39.9 1.5 %collective-permute-start.4 = (f32[104,128]{1,0:T(8,128)S(1)}, f32[104,128]{1,0:T(8,128)S(1)}, u32[]{:S(2)}, u32[]{:S(2)}) collective-permute-start(f32[104,128]{1,0:T(8,128)S(1)} %add.21), channel_id=1, source_target_pairs={{0,16},{4,20},{8,24},{12,28},{16,0},{20,4},{24,8},{28,12},{1,17},{... | collective-permute-start | bytes 159752 | tf_op jit(solution)/shard_map/ppermute | solution.py:452
  41.5 2.3 %collective-permute-start.5 = (f32[104,128]{1,0:T(8,128)S(1)}, f32[104,128]{1,0:T(8,128)S(1)}, u32[]{:S(2)}, u32[]{:S(2)}) collective-permute-start(f32[104,128]{1,0:T(8,128)S(1)} %add.21), channel_id=1, source_target_pairs={{0,24},{4,28},{8,16},{12,20},{16,8},{20,12},{24,0},{28,4},{1,25},{... | collective-permute-start | bytes 159752 | tf_op jit(solution)/shard_map/ppermute | solution.py:452
  43.8 2.7 %latent.5.part0 = bf16[8,5760]{1,0:T(8,128)(2,1)} custom-call(f32[18,96,128]{2,1,0:T(8,128)} %copy-done.2, bf16[3,3,32,64]{3,2,1,0:T(8,128)(2,1)} %bitcast.4), custom_call_target="tpu_custom_call" | custom-call | tf_op jit(solution)/shard_map/latent/pallas_call | solution.py:548
  46.5 1.6 %collective-permute-start.6 = (bf16[8,5760]{1,0:T(8,128)(2,1)}, bf16[8,5760]{1,0:T(8,128)(2,1)S(1)}, u32[]{:S(2)}, u32[]{:S(2)}) collective-permute-start(bf16[8,5760]{1,0:T(8,128)(2,1)} %latent.5.part0), channel_id=1, source_target_pairs={{0,1},{1,0},{2,3},{3,2},{4,5},{5,4},{6,7},{7,6},{8,9},{9,8},{10,11... | collective-permute-start | bytes 276488 | tf_op jit(solution)/shard_map/ppermute | solution.py:452
  48.1 2.6 %collective-permute-start.7 = (bf16[8,5760]{1,0:T(8,128)(2,1)}, bf16[8,5760]{1,0:T(8,128)(2,1)S(1)}, u32[]{:S(2)}, u32[]{:S(2)}) collective-permute-start(bf16[8,5760]{1,0:T(8,128)(2,1)} %latent.5.part0), channel_id=1, source_target_pairs={{0,2},{1,3},{2,0},{3,1},{4,6},{5,7},{6,4},{7,5},{8,10},{9,11},{10,... | collective-permute-start | bytes 276488 | tf_op jit(solution)/shard_map/ppermute | solution.py:452
  50.9 0.3 collective-permute-done.6.part1
  51.3 7.0 %collective-permute-done.7.part2 = bf16[8,5760]{1,0:T(8,128)(2,1)S(1)} collective-permute-done((bf16[8,5760]{1,0:T(8,128)(2,1)}, bf16[8,5760]{1,0:T(8,128)(2,1)S(1)}, u32[]{:S(2)}, u32[]{:S(2)}) %collective-permute-start.7) | collective-permute-done | bytes 92192 | tf_op jit(solution)/shard_map/ppermute | solution.py:452
  58.3 2.5 %collective-permute-start.10 = (f32[104,128]{1,0:T(8,128)S(1)}, f32[104,128]{1,0:T(8,128)S(1)}, u32[]{:S(2)}, u32[]{:S(2)}) collective-permute-start(f32[104,128]{1,0:T(8,128)S(1)} %add_add_fusion.1), channel_id=1, source_target_pairs={{0,2},{1,3},{2,0},{3,1},{4,6},{5,7},{6,4},{7,5},{8,10},{9,11},{10,... | collective-permute-start | bytes 159752 | tf_op jit(solution)/shard_map/ppermute | solution.py:452
  60.9 1.4 %collective-permute-start.11 = (f32[104,128]{1,0:T(8,128)S(1)}, f32[104,128]{1,0:T(8,128)S(1)}, u32[]{:S(2)}, u32[]{:S(2)}) collective-permute-start(f32[104,128]{1,0:T(8,128)S(1)} %add_add_fusion.1), channel_id=1, source_target_pairs={{0,3},{1,2},{2,1},{3,0},{4,7},{5,6},{6,5},{7,4},{8,11},{9,10},{10,... | collective-permute-start | bytes 159752 | tf_op jit(solution)/shard_map/ppermute | solution.py:452
  62.2 1.2 %collective-permute-done.10 = f32[104,128]{1,0:T(8,128)S(1)} collective-permute-done((f32[104,128]{1,0:T(8,128)S(1)}, f32[104,128]{1,0:T(8,128)S(1)}, u32[]{:S(2)}, u32[]{:S(2)}) %collective-permute-start.10) | collective-permute-done | bytes 53280 | tf_op jit(solution)/shard_map/ppermute | solution.py:452
  63.5 3.4 %collective-permute-done.11 = f32[104,128]{1,0:T(8,128)S(1)} collective-permute-done((f32[104,128]{1,0:T(8,128)S(1)}, f32[104,128]{1,0:T(8,128)S(1)}, u32[]{:S(2)}, u32[]{:S(2)}) %collective-permute-start.11) | collective-permute-done | bytes 53280 | tf_op jit(solution)/shard_map/ppermute | solution.py:452
  67.1 1.9 %place.1 = f32[1,8,23040]{2,1,0:T(8,128)} custom-call(bf16[8,5760]{1,0:T(8,128)(2,1)} %latent.5.part0, bf16[8,5760]{1,0:T(8,128)(2,1)} %copy-done.10, bf16[8,5760]{1,0:T(8,128)(2,1)} %copy-done.11, bf16[8,5760]{1,0:T(8,128)(2,1)} %copy-done.12), custom_call_target="tpu_custom_call" | custom-call | tf_op jit(solution)/shard_map/place/pallas_call | solution.py:562
  69.0 0.6 copy-done.13
  69.6 1.6 %taps.1 = (f32[3,3,32,64]{3,2,1,0:T(8,128)}, f32[3,3,16,32]{3,2,1,0:T(8,128)}) custom-call(f32[104,128]{1,0:T(8,128)} %copy-done.9, f32[104,128]{1,0:T(8,128)} %copy-done.13), custom_call_target="tpu_custom_call" | custom-call | tf_op jit(solution)/shard_map/taps/pallas_call | solution.py:571
  (38 shorter events, 0.4 us)
Async XLA Ops:
  0.6 9.9 %copy-start.1 = (bf16[1,8,23040]{2,1,0:T(8,128)(2,1)S(1)}, bf16[1,8,23040]{2,1,0:T(8,128)(2,1)}, u32[]{:S(2)}) copy-start(bf16[1,8,23040]{2,1,0:T(8,128)(2,1)} %latent.4) | copy-start | bytes 1105924
  0.6 9.9 %copy-start = (bf16[1,32,23040]{2,1,0:T(8,128)(2,1)S(1)}, bf16[1,32,23040]{2,1,0:T(8,128)(2,1)}, u32[]{:S(2)}) copy-start(bf16[1,32,23040]{2,1,0:T(8,128)(2,1)} %targets.3) | copy-start | bytes 4423684
  0.7 9.9 %copy-start.4 = (s32[32,48]{1,0:T(8,128)S(1)}, s32[32,48]{1,0:T(8,128)}, u32[]{:S(2)}) copy-start(s32[32,48]{1,0:T(8,128)} %land.3) | copy-start | bytes 18436
  0.7 9.9 %copy-start.6 = (s32[8]{0:T(128)S(1)}, s32[8]{0:T(128)}, u32[]{:S(2)}) copy-start(s32[8]{0:T(128)} %seeds.1) | copy-start | bytes 100
  0.7 9.9 %copy-start.7 = (f32[64]{0:T(128)S(1)}, f32[64]{0:T(128)}, u32[]{:S(2)}) copy-start(f32[64]{0:T(128)} %scale.1) | copy-start | bytes 772
  0.7 9.9 %copy-start.8 = (f32[16]{0:T(128)S(1)}, f32[16]{0:T(128)}, u32[]{:S(2)}) copy-start(f32[16]{0:T(128)} %channel_weight.1) | copy-start | bytes 196
  2.8 7.8 %collective-permute-start = (bf16[50,8,128]{2,1,0:T(8,128)(2,1)}, bf16[50,8,128]{2,1,0:T(8,128)(2,1)S(1)}, u32[]{:S(2)}, u32[]{:S(2)}) collective-permute-start(bf16[50,8,128]{2,1,0:T(8,128)(2,1)} %get-tuple-element.14), channel_id=1, source_target_pairs={{0,4},{4,8},{8,12},{12,16},{16,20},{20,24},{24,28},{1,5},{5,9},{9,... | collective-permute-start | bytes 307208 | tf_op jit(solution)/shard_map/ppermute | solution.py:24
  5.2 5.4 %collective-permute-start.1 = (bf16[1,6400]{1,0:T(2,128)(2,1)}, bf16[1,6400]{1,0:T(2,128)(2,1)S(1)}, u32[]{:S(2)}, u32[]{:S(2)}) collective-permute-start(bf16[1,6400]{1,0:T(2,128)(2,1)} %get-tuple-element.15), channel_id=1, source_target_pairs={{4,0},{8,4},{12,8},{16,12},{20,16},{24,20},{28,24},{5,1},{9,5},{13... | collective-permute-start | bytes 38408 | tf_op jit(solution)/shard_map/ppermute | solution.py:24
  35.5 0.9 %copy-start.2 = (f32[18,96,128]{2,1,0:T(8,128)}, f32[18,96,128]{2,1,0:T(8,128)S(1)}, u32[]{:S(2)}) copy-start(f32[18,96,128]{2,1,0:T(8,128)S(1)} %get-tuple-element.16.sums) | copy-start | bytes 2654212
  36.5 3.5 %collective-permute-start.2 = (f32[104,128]{1,0:T(8,128)S(1)}, f32[104,128]{1,0:T(8,128)S(1)}, u32[]{:S(2)}, u32[]{:S(2)}) collective-permute-start(f32[104,128]{1,0:T(8,128)S(1)} %get-tuple-element.18), channel_id=1, source_target_pairs={{0,4},{4,0},{8,12},{12,8},{16,20},{20,16},{24,28},{28,24},{1,5},{5... | collective-permute-start | bytes 159752 | tf_op jit(solution)/shard_map/ppermute | solution.py:452
  39.9 10.8 %collective-permute-start.4 = (f32[104,128]{1,0:T(8,128)S(1)}, f32[104,128]{1,0:T(8,128)S(1)}, u32[]{:S(2)}, u32[]{:S(2)}) collective-permute-start(f32[104,128]{1,0:T(8,128)S(1)} %add.21), channel_id=1, source_target_pairs={{0,16},{4,20},{8,24},{12,28},{16,0},{20,4},{24,8},{28,12},{1,17},{... | collective-permute-start | bytes 159752 | tf_op jit(solution)/shard_map/ppermute | solution.py:452
  41.5 9.5 %collective-permute-start.5 = (f32[104,128]{1,0:T(8,128)S(1)}, f32[104,128]{1,0:T(8,128)S(1)}, u32[]{:S(2)}, u32[]{:S(2)}) collective-permute-start(f32[104,128]{1,0:T(8,128)S(1)} %add.21), channel_id=1, source_target_pairs={{0,24},{4,28},{8,16},{12,20},{16,8},{20,12},{24,0},{28,4},{1,25},{... | collective-permute-start | bytes 159752 | tf_op jit(solution)/shard_map/ppermute | solution.py:452
  43.8 7.1 %collective-permute-start.3 = (f32[104,128]{1,0:T(8,128)S(1)}, f32[104,128]{1,0:T(8,128)S(1)}, u32[]{:S(2)}, u32[]{:S(2)}) collective-permute-start(f32[104,128]{1,0:T(8,128)S(1)} %add.21), channel_id=1, source_target_pairs={{0,8},{4,12},{8,0},{12,4},{16,24},{20,28},{24,16},{28,20},{1,9},{5... | collective-permute-start | bytes 159752 | tf_op jit(solution)/shard_map/ppermute | solution.py:452
  46.5 4.8 %collective-permute-start.6 = (bf16[8,5760]{1,0:T(8,128)(2,1)}, bf16[8,5760]{1,0:T(8,128)(2,1)S(1)}, u32[]{:S(2)}, u32[]{:S(2)}) collective-permute-start(bf16[8,5760]{1,0:T(8,128)(2,1)} %latent.5.part0), channel_id=1, source_target_pairs={{0,1},{1,0},{2,3},{3,2},{4,5},{5,4},{6,7},{7,6},{8,9},{9,8},{10,11... | collective-permute-start | bytes 276488 | tf_op jit(solution)/shard_map/ppermute | solution.py:452
  48.1 10.2 %collective-permute-start.7 = (bf16[8,5760]{1,0:T(8,128)(2,1)}, bf16[8,5760]{1,0:T(8,128)(2,1)S(1)}, u32[]{:S(2)}, u32[]{:S(2)}) collective-permute-start(bf16[8,5760]{1,0:T(8,128)(2,1)} %latent.5.part0), channel_id=1, source_target_pairs={{0,2},{1,3},{2,0},{3,1},{4,6},{5,7},{6,4},{7,5},{8,10},{9,11},{10,... | collective-permute-start | bytes 276488 | tf_op jit(solution)/shard_map/ppermute | solution.py:452
  50.7 7.6 %collective-permute-start.8 = (bf16[8,5760]{1,0:T(8,128)(2,1)}, bf16[8,5760]{1,0:T(8,128)(2,1)S(1)}, u32[]{:S(2)}, u32[]{:S(2)}) collective-permute-start(bf16[8,5760]{1,0:T(8,128)(2,1)} %latent.5.part0), channel_id=1, source_target_pairs={{0,3},{1,2},{2,1},{3,0},{4,7},{5,6},{6,5},{7,4},{8,11},{9,10},{10,... | collective-permute-start | bytes 276488 | tf_op jit(solution)/shard_map/ppermute | solution.py:452
  51.3 15.8 %copy-start.10 = (bf16[8,5760]{1,0:T(8,128)(2,1)}, bf16[8,5760]{1,0:T(8,128)(2,1)S(1)}, u32[]{:S(2)}) copy-start(bf16[8,5760]{1,0:T(8,128)(2,1)S(1)} %collective-permute-done.6.part1) | copy-start | bytes 276484
  58.3 8.7 %copy-start.11 = (bf16[8,5760]{1,0:T(8,128)(2,1)}, bf16[8,5760]{1,0:T(8,128)(2,1)S(1)}, u32[]{:S(2)}) copy-start(bf16[8,5760]{1,0:T(8,128)(2,1)S(1)} %collective-permute-done.7.part2) | copy-start | bytes 276484
  58.3 8.7 %copy-start.12 = (bf16[8,5760]{1,0:T(8,128)(2,1)}, bf16[8,5760]{1,0:T(8,128)(2,1)S(1)}, u32[]{:S(2)}) copy-start(bf16[8,5760]{1,0:T(8,128)(2,1)S(1)} %collective-permute-done.8.part3) | copy-start | bytes 276484
  58.3 5.1 %collective-permute-start.10 = (f32[104,128]{1,0:T(8,128)S(1)}, f32[104,128]{1,0:T(8,128)S(1)}, u32[]{:S(2)}, u32[]{:S(2)}) collective-permute-start(f32[104,128]{1,0:T(8,128)S(1)} %add_add_fusion.1), channel_id=1, source_target_pairs={{0,2},{1,3},{2,0},{3,1},{4,6},{5,7},{6,4},{7,5},{8,10},{9,11},{10,... | collective-permute-start | bytes 159752 | tf_op jit(solution)/shard_map/ppermute | solution.py:452
  60.9 6.0 %collective-permute-start.11 = (f32[104,128]{1,0:T(8,128)S(1)}, f32[104,128]{1,0:T(8,128)S(1)}, u32[]{:S(2)}, u32[]{:S(2)}) collective-permute-start(f32[104,128]{1,0:T(8,128)S(1)} %add_add_fusion.1), channel_id=1, source_target_pairs={{0,3},{1,2},{2,1},{3,0},{4,7},{5,6},{6,5},{7,4},{8,11},{9,10},{10,... | collective-permute-start | bytes 159752 | tf_op jit(solution)/shard_map/ppermute | solution.py:452
  62.2 4.7 %collective-permute-start.9 = (f32[104,128]{1,0:T(8,128)S(1)}, f32[104,128]{1,0:T(8,128)S(1)}, u32[]{:S(2)}, u32[]{:S(2)}) collective-permute-start(f32[104,128]{1,0:T(8,128)S(1)} %add_add_fusion.1), channel_id=1, source_target_pairs={{0,1},{1,0},{2,3},{3,2},{4,5},{5,4},{6,7},{7,6},{8,9},{9,8},{10,11... | collective-permute-start | bytes 159752 | tf_op jit(solution)/shard_map/ppermute | solution.py:452
  67.0 2.1 %copy-start.9 = (f32[104,128]{1,0:T(8,128)}, f32[104,128]{1,0:T(8,128)S(1)}, u32[]{:S(2)}) copy-start(f32[104,128]{1,0:T(8,128)S(1)} %add_add_fusion.mine) | copy-start | bytes 159748
  67.0 2.1 %collective-permute-start.12 = (f32[104,128]{1,0:T(8,128)S(1)}, f32[104,128]{1,0:T(8,128)S(1)}, u32[]{:S(2)}, u32[]{:S(2)}) collective-permute-start(f32[104,128]{1,0:T(8,128)S(1)} %add_add_fusion.mine), channel_id=1, source_target_pairs={{0,4},{4,0},{8,12},{12,8},{16,20},{20,16},{24,28},{28,24},{1,5},{5... | collective-permute-start | bytes 159752 | tf_op jit(solution)/shard_map/ppermute | solution.py:452
  (3 other events, 2.3 us)

commit v5 on v4

--- a/solution.py
+++ b/solution.py
@@ -175,48 +175,83 @@
         first += -(-9 // cells) * chan_out
 
 
-def latent_kernel(rows, own, sums, kernel_one, out_lat, back_one):
-    bf16, f32 = jnp.bfloat16, jnp.float32
+def make_source(i, row, total_rows, span, own, half, seeds, scale, chan, line, store):
+    blocks = span // LANES
+    mem_pos = lax.axis_index("mem")
+    sublane = iota((8, LANES), 0)
+    seed_table = jnp.zeros((8, LANES), jnp.int32)
+    for m in range(MEM):
+        seed_table = jnp.where(sublane == m, seeds[m], seed_table)
+    hash_table = iota((8, LANES), 1) * HASH_CELL + seed_table * HASH_SEED
+    scale_table = lane_table(scale, chan)
+    inside = jnp.where(row < total_rows, 1.0, 0.0).astype(jnp.float32)
+    for t in range(half + 2):
+        parts = []
+        for part in range(2):
+            first = (row * span + window_block(mem_pos, own, half, blocks, part, t) * LANES) * HASH_CELL
+            h = hash_table + first
+            h = jnp.bitwise_xor(h, jnp.right_shift(h, 15))
+            h = h * HASH_MIX
+            h = jnp.bitwise_xor(h, jnp.right_shift(h, 13))
+            noise = jnp.bitwise_and(h, 65535).astype(jnp.float32) * (1.0 / 65536.0) - 0.5
+            noise = noise * 3.4641016
+            parts.append((line(t * 2 + part, i) + noise * scale_table) * inside)
+        store(i, t, jnp.concatenate(parts, axis=0).astype(jnp.bfloat16))
+
+
+def prepare_kernel(half, seeds, scale, latent, kernel_one, kernel_two, source, band_one, band_two, back_one, back_two, lines):
+    rows, span = latent.shape[1], latent.shape[2]
+    blocks = span // LANES
+    own = blocks // lax.axis_size("mem")
+    total_rows = rows * lax.axis_size("lat")
+    lat_pos, mem_pos = lax.axis_index("lat"), lax.axis_index("mem")
+    for t in range(half + 2):
+        for part in range(2):
+            off = pl.multiple_of(window_block(mem_pos, own, half, blocks, part, t) * LANES, LANES)
+            lines[t * 2 + part] = latent[0, :, pl.ds(off, LANES)].astype(jnp.float32)
+
+    def line(slot, i):
+        return spread_line(lines, slot, i)
+
+    def store(i, t, value):
+        source[i, t] = value
+
+    def step(i, _):
+        make_source(
+            i, lat_pos * rows + i, total_rows, span, own, half, seeds, scale, kernel_one.shape[3], line, store
+        )
+        return 0
+
+    lax.fori_loop(0, rows, step, 0)
+    build_band(kernel_one, band_one)
+    build_band(kernel_two, band_two)
     build_back(kernel_one, back_one)
-    z = sums[...].reshape(rows + 1, 2, 96, LANES)
-    z = [z[:, sub, at : at + 48].reshape((rows + 1) * 48, LANES) for at in (0, 48) for sub in range(2)]
-    z = jnp.concatenate(z, axis=1)
-    high = z.astype(bf16)
-    low = (z - high.astype(f32)).astype(bf16)
-    pulled = jnp.dot(high, back_one[...], preferred_element_type=f32)
-    pulled = pulled + jnp.dot(low, back_one[...], preferred_element_type=f32)
-    pulled = pulled.reshape(rows + 1, 48, 2 * LANES)
-    result = (pulled[1:, :, :LANES] + pulled[:-1, :, LANES:]).astype(bf16)
-    swap_to, swap_from = iota((own * rows, rows * 48), 0), iota((own * rows, rows * 48), 1)
-    swap = (swap_to // rows == swap_from % 48) & (swap_to % rows == swap_from // 48)
-    result = jnp.dot(swap.astype(bf16), result.reshape(rows * 48, LANES), preferred_element_type=f32)
-    for t in range(own):
-        out_lat[:, t * LANES : (t + 1) * LANES] = result[t * rows : (t + 1) * rows].astype(bf16)
+    build_back(kernel_two, back_two)
 
 
 def band_kernel(
     half,
+    chans,
     norm,
     seeds,
     scale,
     channel_weight,
-    latent,
+    own_source,
     above,
     below,
     targets,
     land,
-    kernel_one,
-    kernel_two,
-    sums,
+    band_one,
+    band_two,
+    back_one,
+    back_two,
+    out_lat,
     taps_keep,
     taps_send,
     lat_rows,
     tgt_rows,
     weight_rows,
     words,
-    band_one,
-    band_two,
-    back_two,
     source,
     pre_even,
     pre_odd,
@@ -227,12 +262,14 @@
     fgrad_even,
     fgrad_odd,
     carry,
+    carry_lat,
+    lat_lines,
     taps,
     acc_one,
     acc_two,
 ):
-    rows = latent.shape[1]
-    span = latent.shape[2]
+    rows = own_source.shape[0]
+    span = targets.shape[2]
     blocks = span // LANES
     lat_count = lax.axis_size("lat")
     own = blocks // lax.axis_size("mem")
@@ -243,7 +280,7 @@
     mem_pos = lax.axis_index("mem")
     wide = half + 2
     front = half + 1
-    chan0, chan1, chan2 = kernel_one.shape[3], kernel_two.shape[3], kernel_two.shape[2]
+    chan0, chan1, chan2 = chans
     f32, bf16 = jnp.float32, jnp.bfloat16
 
     def block_of(part, t):
@@ -265,54 +302,36 @@
             off = pl.multiple_of(block * LANES, LANES)
             slot = t * 2 + part
             edge = above[slot].astype(f32)
-            lat_rows[slot, 0:rows] = latent[0, :, pl.ds(off, LANES)].astype(f32)
-            lat_rows[slot, rows : rows + 1] = below[:, slot * LANES : (slot + 1) * LANES].astype(f32)
-            lat_rows[slot, rows + 1 : rows + 2] = edge[0:1]
+            lat_rows[slot, 0:1] = edge[0:1]
+            lat_rows[slot, 1:2] = below[:, slot * LANES : (slot + 1) * LANES].astype(f32)
             if t < front:
                 tgt_rows[slot, 0:grid_rows] = targets[0, :, pl.ds(off, LANES)].astype(f32)
                 tgt_rows[slot, grid_rows:] = edge
                 mask = jnp.concatenate([land_of(words[...], block, chan2), pltpu.roll(edge, 5, 0)], axis=0)
                 weight_rows[slot] = base_rows + base_rows * mask
 
-    build_band(kernel_one, band_one)
-    build_band(kernel_two, band_two)
-    build_back(kernel_two, back_two)
-
     source[rows + 2 :] = jnp.zeros((2,) + source.shape[1:], bf16)
     source[:, wide] = jnp.zeros((source.shape[0],) + source.shape[2:], bf16)
     fgrad_even[:, 0] = jnp.zeros((4,) + fgrad_even.shape[2:], bf16)
     fgrad_odd[...] = jnp.zeros(fgrad_odd.shape, bf16)
     carry[...] = jnp.zeros(carry.shape, f32)
+    carry_lat[...] = jnp.zeros(carry_lat.shape, f32)
     acc_one[...] = jnp.zeros(acc_one.shape, f32)
     acc_two[...] = jnp.zeros(acc_two.shape, f32)
 
-    sublane = iota((8, LANES), 0)
-    seed_table = jnp.zeros((8, LANES), jnp.int32)
-    for m in range(MEM):
-        seed_table = jnp.where(sublane == m, seeds[m], seed_table)
-    hash_table = iota((8, LANES), 1) * HASH_CELL + seed_table * HASH_SEED
-    scale_table = lane_table(scale, chan0)
-
-    def make_source(i, _):
-        row = lat_pos * rows - 1 + i
-        inside = jnp.where(row < total_rows, 1.0, 0.0).astype(f32)
-        at = jnp.where(i == 0, rows + 1, i - 1)
-        for t in range(wide):
-            parts = []
-            for part in range(2):
-                first = (row * span + block_of(part, t) * LANES) * HASH_CELL
-                h = hash_table + first
-                h = jnp.bitwise_xor(h, jnp.right_shift(h, 15))
-                h = h * HASH_MIX
-                h = jnp.bitwise_xor(h, jnp.right_shift(h, 13))
-                noise = jnp.bitwise_and(h, 65535).astype(f32) * (1.0 / 65536.0) - 0.5
-                noise = noise * 3.4641016
-                cell = spread_line(lat_rows, t * 2 + part, at)
-                parts.append((cell + noise * scale_table) * inside)
-            source[i, t] = jnp.concatenate(parts, axis=0).astype(bf16)
+    def line(slot, i):
+        return spread_line(lat_rows, slot, i)
+
+    def store(i, t, value):
+        source[i * (rows + 1), t] = value
+
+    def edge_source(i, _):
+        row = lat_pos * rows - 1 + i * (rows + 1)
+        make_source(i, row, total_rows, span, own, half, seeds, scale, chan0, line, store)
         return 0
 
-    lax.fori_loop(0, rows + 2, make_source, 0)
+    lax.fori_loop(0, 2, edge_source, 0)
+    source[1 : rows + 1, 0:wide] = own_source[...]
 
     def operand(ref, i, start, count):
         def piece(r, at):
@@ -420,9 +439,14 @@
         carry[...] = pulled[members:, LANES:]
         grads = [(grads[k] * slope[2 * at + k].reshape(members, LANES)).astype(bf16) for k in range(2)]
         grads = jnp.concatenate(grads, axis=1)
-        total_grad = jnp.dot(pick, grads, preferred_element_type=f32)
-        for k in range(2):
-            sums[2 * at + k] = total_grad[:, k * LANES : (k + 1) * LANES]
+        z = jnp.dot(pick, grads, preferred_element_type=f32)
+        z = jnp.concatenate([z[:48], z[48:]], axis=1)
+        high = z.astype(bf16)
+        z = jnp.concatenate([high, (z - high.astype(f32)).astype(bf16)], axis=0)
+        z = jnp.dot(z, back_one[...], preferred_element_type=f32)
+        z = z[:48] + z[48:]
+        lat_lines[pl.ds(jnp.maximum(n - 1, 0), 48, stride=rows), :] = z[:, :LANES] + carry_lat[...]
+        carry_lat[...] = z[:, LANES:]
         acc_one[...] += product(grads[16:] * keep, operand(source, at, 1, half))
 
     def second_segment(m, _):
@@ -440,6 +464,8 @@
     pull_back(rows - 1, fgrad_odd)
     pull_back(rows, fgrad_even)
 
+    for t in range(own):
+        out_lat[:, t * LANES : (t + 1) * LANES] = lat_lines[t * rows : (t + 1) * rows].astype(bf16)
     pack_taps(acc_one, taps, 0, chan0, chan1, norm)
     pack_taps(acc_two, taps, -(-9 // (LANES // chan0)) * chan1, chan1, chan2, norm)
     count = taps_keep.shape[0]
@@ -452,10 +478,7 @@
     return lax.ppermute(array, axis, [(i, i ^ bit) for i in range(lax.axis_size(axis))])
 
 
-def total(array, axis, bits):
-    if len(bits) == 1:
-        return array + swapped(array, axis, bits[0])
-    first, second = bits
+def total(array, axis, first, second):
     one, two, three = (swapped(array, axis, k) for k in (first, second, first ^ second))
     return (array + one) + (two + three)
 
@@ -475,6 +498,7 @@
     f32, bf16 = jnp.float32, jnp.bfloat16
     wide, front = half + 2, half + 1
     params = pltpu.CompilerParams(vmem_limit_bytes=32 * 1024 * 1024)
+    small = pltpu.CompilerParams(vmem_limit_bytes=8 * 1024 * 1024)
     kernel_one = kernel_one.transpose(0, 1, 3, 2)
     kernel_two = kernel_two.transpose(0, 1, 3, 2)
     down, up = pl.pallas_call(
@@ -494,29 +518,38 @@
             jax.ShapeDtypeStruct((1, 2 * wide * LANES), bf16),
         ],
         scratch_shapes=[pltpu.VMEM((8, LANES), jnp.int32)],
+        compiler_params=small,
         name="edges",
     )(latent, targets, land_words)
     above = shifted(down, "lat", 1)
     below = shifted(up, "lat", -1)
+    band = jax.ShapeDtypeStruct((512, 256), bf16)
+    source, *bands = pl.pallas_call(
+        functools.partial(prepare_kernel, half),
+        in_specs=[smem] * 2 + [vmem] * 3,
+        out_specs=[vmem] * 5,
+        out_shape=[jax.ShapeDtypeStruct((rows, wide, 16, LANES), bf16)] + [band] * 4,
+        scratch_shapes=[pltpu.VMEM((2 * wide, rows, LANES), f32)],
+        compiler_params=small,
+        cost_estimate=pl.CostEstimate(flops=10**8, bytes_accessed=10**7, transcendentals=0),
+        name="prepare",
+    )(member_seeds, noise_scale, latent, kernel_one, kernel_two)
     norm = 1.0 / math.sqrt(sample_count * 4 * rows * lat_count * targets.shape[2])
     tap_rows = 5 * chan1 + 3 * chan2
-    sums, taps, taps_send = pl.pallas_call(
-        functools.partial(band_kernel, half, norm),
-        in_specs=[smem] * 3 + [vmem] * 7,
+    lat_grad, taps, taps_send = pl.pallas_call(
+        functools.partial(band_kernel, half, (chan0, chan1, chan2), norm),
+        in_specs=[smem] * 3 + [vmem] * 9,
         out_specs=[vmem] * 3,
         out_shape=[
-            jax.ShapeDtypeStruct((2 * rows + 2, 96, LANES), f32),
+            jax.ShapeDtypeStruct((rows, own * LANES), bf16),
             jax.ShapeDtypeStruct((tap_rows // 2, LANES), f32),
             jax.ShapeDtypeStruct((tap_rows // 2, LANES), f32),
         ],
         scratch_shapes=[
-            pltpu.VMEM((2 * wide, rows + 8, LANES), f32),
+            pltpu.VMEM((2 * wide, 8, LANES), f32),
             pltpu.VMEM((2 * front, 4 * rows + 8, LANES), f32),
             pltpu.VMEM((2 * front, 4 * rows + 8, LANES), f32),
             pltpu.VMEM((4 * rows, LANES), jnp.int32),
-            pltpu.VMEM((512, 256), bf16),
-            pltpu.VMEM((512, 256), bf16),
-            pltpu.VMEM((512, 256), bf16),
             pltpu.VMEM((rows + 4, wide + 1, 16, LANES), bf16),
             pltpu.VMEM((wide * 16, 2 * LANES), f32),
             pltpu.VMEM((wide * 16, 2 * LANES), f32),
@@ -527,6 +560,8 @@
             pltpu.VMEM((4, front + 1, 16, LANES), bf16),
             pltpu.VMEM((4, front + 1, 16, LANES), bf16),
             pltpu.VMEM((front * 16, LANES), f32),
+            pltpu.VMEM((48, LANES), f32),
+            pltpu.VMEM((48 * rows, LANES), f32),
             pltpu.VMEM((tap_rows, LANES), f32),
             pltpu.VMEM((256, 512), f32),
             pltpu.VMEM((256, 512), f32),
@@ -537,36 +572,31 @@
         member_seeds,
         noise_scale,
         channel_weight,
-        latent,
+        source,
         above,
         below,
         targets,
         land_words,
-        kernel_one,
-        kernel_two,
+        *bands,
     )
-    lat_grad = pl.pallas_call(
-        functools.partial(latent_kernel, rows, own),
-        in_specs=[vmem] * 2,
-        out_specs=vmem,
-        out_shape=jax.ShapeDtypeStruct((rows, own * LANES), bf16),
-        scratch_shapes=[pltpu.VMEM((512, 256), bf16)],
-        name="latent",
-    )(sums, kernel_one)
-    quarters = [swapped(lat_grad, "mem", k) for k in range(1, 4)]
+    one, two, three = (swapped(lat_grad, "mem", k) for k in range(1, 4))
     taps = taps + swapped(taps_send, "lat", 1)
     bits = [1 << k for k in range(1, lat_count.bit_length() - 1)]
-    for k in range(0, len(bits), 2):
-        taps = total(taps, "lat", bits[k : k + 2])
-    taps, quarters = lax.optimization_barrier((taps, quarters))
+    for bit in bits:
+        if bit == bits[-1]:
+            taps, three = lax.optimization_barrier((taps, three))
+        taps = taps + swapped(taps, "lat", bit)
+    taps, two = lax.optimization_barrier((taps, two))
     latent_grad = pl.pallas_call(
         functools.partial(place_kernel, own),
         in_specs=[vmem] * 4,
         out_specs=vmem,
         out_shape=jax.ShapeDtypeStruct((1, rows, span), f32),
+        compiler_params=small,
         name="place",
-    )(lat_grad, *quarters)
-    taps = total(taps, "mem", [1, 2])
+    )(lat_grad, one, two, three)
+    taps = total(taps, "mem", 1, 2)
+    taps, latent_grad = lax.optimization_barrier((taps, latent_grad))
     other = swapped(taps, "lat", 1)
     one, two = pl.pallas_call(
         taps_kernel,
@@ -577,6 +607,7 @@
             jax.ShapeDtypeStruct(kernel_two.shape, f32),
         ],
         scratch_shapes=[pltpu.VMEM((tap_rows, LANES), f32)],
+        compiler_params=small,
         name="taps",
     )(taps, other)
     return (latent_grad, one.transpose(0, 1, 3, 2), two.transpose(0, 1, 3, 2))

time: 71.7 us -> 62.6 us (0.87)
  waiting for transfers between devices: 17.1 us -> 6.22 us
  starting transfers between devices: 18.5 us -> 22.9 us
  Pallas kernels: 31.6 us -> 27.6 us
  local copies, waits for them, and re-layouts: 3.22 us -> 4.74 us
    ppermute x11 -> x10, waiting for transfers between devices: 13 us -> 6.15 us  [swapped(): lax.ppermute(array, axis, [(i, i ^ bit) for i in range(lax.axis_size(axis...]
    ppermute x11 -> x10, starting transfers between devices: 14.8 us -> 19.1 us  [swapped(): lax.ppermute(array, axis, [(i, i ^ bit) for i in range(lax.axis_size(axis...]
    ppermute x2, waiting for transfers between devices: 4.11 us -> 0.06 us  [shifted(): return lax.ppermute(array, axis, pairs)]
    pallas_call x1, Pallas kernels: 2.1 us -> 0.24 us  [local(): pl.pallas_call(functools.partial(edge_kernel, half, chan2), grid=(1,), in...]
    unnamed x28 -> x22, local copies, waits for them, and re-layouts: 3.22 us -> 4.74 us
    pallas_call x1, Pallas kernels: 1.94 us -> 0.92 us  [local(): pl.pallas_call(functools.partial(place_kernel, own), in_specs=[vmem] * 4,...]
    pallas_call x1, Pallas kernels: 1.61 us -> 0.78 us  [local(): pl.pallas_call(taps_kernel, in_specs=[vmem] * 2, out_specs=[vmem] * 2, ou...]
  transfers between devices with their start and end apart: 13 -> 12, of which waited for: 6 -> 6; matrix products, arithmetic and copies ran while one was open for 0% -> 0% of each run, Pallas kernels for 7% -> 5%
where the time goes in v5:
time: 62.6 us; the launch traced here: 62.3 us
  Pallas kernels  27.6 us (44%)
  starting transfers between devices  22.9 us (37%)
  waiting for transfers between devices  6.22 us (10%)
  local copies, waits for them, and re-layouts  4.74 us (8%)
  between operations  0.78 us (1%)
    pallas_call x1, Pallas kernels, local(): pl.pallas_call(functools.partial(band_kernel, half, (chan0, chan1, chan2)...  23.5 us
    ppermute x10, starting transfers between devices, swapped(): lax.ppermute(array, axis, [(i, i ^ bit) for i in range(lax.axis_size(axis...  19.1 us
    ppermute x10, waiting for transfers between devices, swapped(): lax.ppermute(array, axis, [(i, i ^ bit) for i in range(lax.axis_size(axis...  6.15 us
    unnamed x22, local copies, waits for them, and re-layouts  4.74 us
    ppermute x2, starting transfers between devices, shifted(): return lax.ppermute(array, axis, pairs)  3.79 us
    pallas_call x1, Pallas kernels, local(): pl.pallas_call(functools.partial(prepare_kernel, half), in_specs=[smem] *...  2.14 us
  transfers between devices with their start and end apart: 12, of which 6 were waited for; matrix products, arithmetic and copies ran while one was open for 0% of the time, Pallas kernels for 5%

profile of v5, /device:TPU:0, one launch (start us, length us, event | category | flops | bytes accessed | tf_op | source)
XLA Modules:
  0.0 62.3 jit_solution(13075244255046014752)
XLA Ops:
  0.6 1.4 %copy-done = bf16[1,32,23040]{2,1,0:T(8,128)(2,1)S(1)} copy-done((bf16[1,32,23040]{2,1,0:T(8,128)(2,1)S(1)}, bf16[1,32,23040]{2,1,0:T(8,128)(2,1)}, u32[]{:S(2)}) %copy-start) | copy-done | bytes 1474584
  2.0 1.0 %copy-done.2 = bf16[1,8,23040]{2,1,0:T(8,128)(2,1)S(1)} copy-done((bf16[1,8,23040]{2,1,0:T(8,128)(2,1)S(1)}, bf16[1,8,23040]{2,1,0:T(8,128)(2,1)}, u32[]{:S(2)}) %copy-start.2) | copy-done | bytes 368664
  3.0 0.7 %copy-done.5 = s32[32,48]{1,0:T(8,128)S(1)} copy-done((s32[32,48]{1,0:T(8,128)S(1)}, s32[32,48]{1,0:T(8,128)}, u32[]{:S(2)}) %copy-start.5) | copy-done | bytes 6168
  4.0 2.5 %collective-permute-start = (bf16[50,8,128]{2,1,0:T(8,128)(2,1)S(1)}, bf16[50,8,128]{2,1,0:T(8,128)(2,1)S(1)}, u32[]{:S(2)}, u32[]{:S(2)}) collective-permute-start(bf16[50,8,128]{2,1,0:T(8,128)(2,1)S(1)} %get-tuple-element.22), channel_id=1, source_target_pairs={{0,4},{4,8},{8,12},{12,16},{16,20},{20,24},{24,28},{1,5},{5,9},{9,... | collective-permute-start | bytes 307208 | tf_op jit(solution)/shard_map/ppermute | solution.py:24
  6.5 1.3 %collective-permute-start.1 = (bf16[1,6400]{1,0:T(2,128)(2,1)S(1)}, bf16[1,6400]{1,0:T(2,128)(2,1)S(1)}, u32[]{:S(2)}, u32[]{:S(2)}) collective-permute-start(bf16[1,6400]{1,0:T(2,128)(2,1)S(1)} %get-tuple-element.23), channel_id=1, source_target_pairs={{4,0},{8,4},{12,8},{16,12},{20,16},{24,20},{28,24},{5,1},{9,5},{13... | collective-permute-start | bytes 38408 | tf_op jit(solution)/shard_map/ppermute | solution.py:24
  7.8 0.9 %copy-done.4 = bf16[3,3,64,32]{2,3,1,0:T(8,128)(2,1)S(1)} copy-done((bf16[3,3,64,32]{2,3,1,0:T(8,128)(2,1)S(1)}, bf16[3,3,64,32]{2,3,1,0:T(8,128)(2,1)}, u32[]{:S(2)}) %copy-start.4) | copy-done | bytes 36888
  8.7 0.8 %copy-done.7 = bf16[3,3,32,16]{2,3,1,0:T(8,128)(2,1)S(1)} copy-done((bf16[3,3,32,16]{2,3,1,0:T(8,128)(2,1)S(1)}, bf16[3,3,32,16]{2,3,1,0:T(8,128)(2,1)}, u32[]{:S(2)}) %copy-start.7) | copy-done | bytes 9240
  9.5 2.1 %prepare.1 = (bf16[8,25,16,128]{3,2,1,0:T(8,128)(2,1)S(1)}, bf16[512,256]{1,0:T(8,128)(2,1)S(1)}, bf16[512,256]{1,0:T(8,128)(2,1)S(1)}, bf16[512,256]{1,0:T(8,128)(2,1)S(1)}, bf16[512,256]{1,0:T(8,128)(2,1)S(1)}) custom-call(s32[8]{0:T(128)S(1)} %copy-done.8, f32[64]{0:T(128)S(1)} %copy-done.9, bf16[1,8,23040]{2,1,0:T(8,128)(2,1)S(1)} %copy-done.3, ...), custom_call_target="tpu_custom_call" | custom-call | flops 100000000 | bytes 10000000 | tf_op jit(solution)/shard_map/prepare/pallas_call | solution.py:527
  11.7 23.5 %band.1 = (bf16[8,5760]{1,0:T(8,128)(2,1)S(1)}, f32[104,128]{1,0:T(8,128)S(1)}, f32[104,128]{1,0:T(8,128)S(1)}) custom-call(s32[8]{0:T(128)S(1)} %copy-done.8, f32[64]{0:T(128)S(1)} %copy-done.9, f32[16]{0:T(128)S(1)} %copy-done.10, bf16[8,25,16,128]{3,2,1,0:T(8,128)(2,1)S(1)} %get-tuple-element.21.own_source, ...), custom_call_target="tpu_custom_call" | custom-call | tf_op jit(solution)/shard_map/band/pallas_call | solution.py:539
  35.2 3.3 %collective-permute-start.2 = (f32[104,128]{1,0:T(8,128)S(1)}, f32[104,128]{1,0:T(8,128)S(1)}, u32[]{:S(2)}, u32[]{:S(2)}) collective-permute-start(f32[104,128]{1,0:T(8,128)S(1)} %get-tuple-element.29), channel_id=1, source_target_pairs={{0,4},{4,0},{8,12},{12,8},{16,20},{20,16},{24,28},{28,24},{1,5},{5... | collective-permute-start | bytes 159752 | tf_op jit(solution)/shard_map/ppermute | solution.py:478
  38.5 3.6 %collective-permute-start.4 = (bf16[8,5760]{1,0:T(8,128)(2,1)S(1)}, bf16[8,5760]{1,0:T(8,128)(2,1)S(1)}, u32[]{:S(2)}, u32[]{:S(2)}) collective-permute-start(bf16[8,5760]{1,0:T(8,128)(2,1)S(1)} %get-tuple-element.30.part0), channel_id=1, source_target_pairs={{0,3},{1,2},{2,1},{3,0},{4,7},{5,6},{6,5},{7,4},{8,11},{9,10},{10,... | collective-permute-start | bytes 276488 | tf_op jit(solution)/shard_map/ppermute | solution.py:478
  42.1 1.8 %collective-permute-start.3 = (f32[104,128]{1,0:T(8,128)S(1)}, f32[104,128]{1,0:T(8,128)S(1)}, u32[]{:S(2)}, u32[]{:S(2)}) collective-permute-start(f32[104,128]{1,0:T(8,128)S(1)} %add.18), channel_id=1, source_target_pairs={{0,8},{4,12},{8,0},{12,4},{16,24},{20,28},{24,16},{28,20},{1,9},{5... | collective-permute-start | bytes 159752 | tf_op jit(solution)/shard_map/ppermute | solution.py:478
  44.0 2.3 %collective-permute-done.3 = f32[104,128]{1,0:T(8,128)S(1)} collective-permute-done((f32[104,128]{1,0:T(8,128)S(1)}, f32[104,128]{1,0:T(8,128)S(1)}, u32[]{:S(2)}, u32[]{:S(2)}) %collective-permute-start.3) | collective-permute-done | bytes 53280 | tf_op jit(solution)/shard_map/ppermute | solution.py:478
  46.3 2.7 %collective-permute-start.5 = (f32[104,128]{1,0:T(8,128)S(1)}, f32[104,128]{1,0:T(8,128)S(1)}, u32[]{:S(2)}, u32[]{:S(2)}) collective-permute-start(f32[104,128]{1,0:T(8,128)S(1)} %add.19), channel_id=1, source_target_pairs={{0,16},{4,20},{8,24},{12,28},{16,0},{20,4},{24,8},{28,12},{1,17},{... | collective-permute-start | bytes 159752 | tf_op jit(solution)/shard_map/ppermute | solution.py:478
  49.0 3.1 %collective-permute-start.10 = (bf16[8,5760]{1,0:T(8,128)(2,1)S(1)}, bf16[8,5760]{1,0:T(8,128)(2,1)S(1)}, u32[]{:S(2)}, u32[]{:S(2)}) collective-permute-start(bf16[8,5760]{1,0:T(8,128)(2,1)S(1)} %get-tuple-element.30.part0), channel_id=1, source_target_pairs={{0,1},{1,0},{2,3},{3,2},{4,5},{5,4},{6,7},{7,6},{8,9},{9,8},{10,11... | collective-permute-start | bytes 276488 | tf_op jit(solution)/shard_map/ppermute | solution.py:478
  52.1 2.1 %collective-permute-start.9 = (f32[104,128]{1,0:T(8,128)S(1)}, f32[104,128]{1,0:T(8,128)S(1)}, u32[]{:S(2)}, u32[]{:S(2)}) collective-permute-start(f32[104,128]{1,0:T(8,128)S(1)} %add.20), channel_id=1, source_target_pairs={{0,3},{1,2},{2,1},{3,0},{4,7},{5,6},{6,5},{7,4},{8,11},{9,10},{10,... | collective-permute-start | bytes 159752 | tf_op jit(solution)/shard_map/ppermute | solution.py:478
  54.3 1.5 %collective-permute-start.8 = (f32[104,128]{1,0:T(8,128)S(1)}, f32[104,128]{1,0:T(8,128)S(1)}, u32[]{:S(2)}, u32[]{:S(2)}) collective-permute-start(f32[104,128]{1,0:T(8,128)S(1)} %add.20), channel_id=1, source_target_pairs={{0,2},{1,3},{2,0},{3,1},{4,6},{5,7},{6,4},{7,5},{8,10},{9,11},{10,... | collective-permute-start | bytes 159752 | tf_op jit(solution)/shard_map/ppermute | solution.py:478
  55.8 0.8 %collective-permute-start.7 = (f32[104,128]{1,0:T(8,128)S(1)}, f32[104,128]{1,0:T(8,128)S(1)}, u32[]{:S(2)}, u32[]{:S(2)}) collective-permute-start(f32[104,128]{1,0:T(8,128)S(1)} %add.20), channel_id=1, source_target_pairs={{0,1},{1,0},{2,3},{3,2},{4,5},{5,4},{6,7},{7,6},{8,9},{9,8},{10,11... | collective-permute-start | bytes 159752 | tf_op jit(solution)/shard_map/ppermute | solution.py:478
  56.6 0.9 %place.1 = f32[1,8,23040]{2,1,0:T(8,128)} custom-call(bf16[8,5760]{1,0:T(8,128)(2,1)S(1)} %get-tuple-element.30.part0, bf16[8,5760]{1,0:T(8,128)(2,1)S(1)} %collective-permute-done.10.part1, bf16[8,5760]{1,0:T(8,128)(2,1)S(1)} %collective-permute-done.6.part2, bf16[8,5760]{1,0:T(8,128)(2,1)S(1)} %collective-permute-done.4.part3), custom_call_target="tpu_custom_call" | custom-call | tf_op jit(solution)/shard_map/place/pallas_call | solution.py:590
  57.5 0.8 %collective-permute-done.9 = f32[104,128]{1,0:T(8,128)S(1)} collective-permute-done((f32[104,128]{1,0:T(8,128)S(1)}, f32[104,128]{1,0:T(8,128)S(1)}, u32[]{:S(2)}, u32[]{:S(2)}) %collective-permute-start.9) | collective-permute-done | bytes 53280 | tf_op jit(solution)/shard_map/ppermute | solution.py:478
  58.3 1.3 %collective-permute-done.8 = f32[104,128]{1,0:T(8,128)S(1)} collective-permute-done((f32[104,128]{1,0:T(8,128)S(1)}, f32[104,128]{1,0:T(8,128)S(1)}, u32[]{:S(2)}, u32[]{:S(2)}) %collective-permute-start.8) | collective-permute-done | bytes 53280 | tf_op jit(solution)/shard_map/ppermute | solution.py:478
  59.6 0.5 collective-permute-done.7
  60.3 1.2 %collective-permute-done.11.other = f32[104,128]{1,0:T(8,128)S(1)} collective-permute-done((f32[104,128]{1,0:T(8,128)S(1)}, f32[104,128]{1,0:T(8,128)S(1)}, u32[]{:S(2)}, u32[]{:S(2)}) %collective-permute-start.11) | collective-permute-done | bytes 53280 | tf_op jit(solution)/shard_map/ppermute | solution.py:478
  61.5 0.8 %taps.1 = (f32[3,3,32,64]{3,2,1,0:T(8,128)}, f32[3,3,16,32]{3,2,1,0:T(8,128)}) custom-call(f32[104,128]{1,0:T(8,128)S(1)} %add_add_fusion.mine, f32[104,128]{1,0:T(8,128)S(1)} %collective-permute-done.11.other), custom_call_target="tpu_custom_call" | custom-call | tf_op jit(solution)/shard_map/taps/pallas_call | solution.py:601
  (31 shorter events, 0.6 us)
Async XLA Ops:
  0.6 1.4 %copy-start = (bf16[1,32,23040]{2,1,0:T(8,128)(2,1)S(1)}, bf16[1,32,23040]{2,1,0:T(8,128)(2,1)}, u32[]{:S(2)}) copy-start(bf16[1,32,23040]{2,1,0:T(8,128)(2,1)} %targets.3) | copy-start | bytes 4423684
  2.0 1.0 %copy-start.2 = (bf16[1,8,23040]{2,1,0:T(8,128)(2,1)S(1)}, bf16[1,8,23040]{2,1,0:T(8,128)(2,1)}, u32[]{:S(2)}) copy-start(bf16[1,8,23040]{2,1,0:T(8,128)(2,1)} %latent.3) | copy-start | bytes 1105924
  3.0 0.7 %copy-start.5 = (s32[32,48]{1,0:T(8,128)S(1)}, s32[32,48]{1,0:T(8,128)}, u32[]{:S(2)}) copy-start(s32[32,48]{1,0:T(8,128)} %land.3) | copy-start | bytes 18436
  3.7 4.1 %copy-start.3 = (bf16[1,8,23040]{2,1,0:T(8,128)(2,1)S(1)}, bf16[1,8,23040]{2,1,0:T(8,128)(2,1)}, u32[]{:S(2)}) copy-start(bf16[1,8,23040]{2,1,0:T(8,128)(2,1)} %latent.3) | copy-start | bytes 1105924
  3.7 4.1 %copy-start.8 = (s32[8]{0:T(128)S(1)}, s32[8]{0:T(128)}, u32[]{:S(2)}) copy-start(s32[8]{0:T(128)} %seeds.3) | copy-start | bytes 100
  3.7 4.1 %copy-start.9 = (f32[64]{0:T(128)S(1)}, f32[64]{0:T(128)}, u32[]{:S(2)}) copy-start(f32[64]{0:T(128)} %scale.3) | copy-start | bytes 772
  3.7 8.0 %copy-start.1 = (bf16[1,32,23040]{2,1,0:T(8,128)(2,1)S(1)}, bf16[1,32,23040]{2,1,0:T(8,128)(2,1)}, u32[]{:S(2)}) copy-start(bf16[1,32,23040]{2,1,0:T(8,128)(2,1)} %targets.3) | copy-start | bytes 4423684
  3.7 8.0 %copy-start.6 = (s32[32,48]{1,0:T(8,128)S(1)}, s32[32,48]{1,0:T(8,128)}, u32[]{:S(2)}) copy-start(s32[32,48]{1,0:T(8,128)} %land.3) | copy-start | bytes 18436
  3.7 8.0 %copy-start.10 = (f32[16]{0:T(128)S(1)}, f32[16]{0:T(128)}, u32[]{:S(2)}) copy-start(f32[16]{0:T(128)} %channel_weight.1) | copy-start | bytes 196
  4.0 7.7 %collective-permute-start = (bf16[50,8,128]{2,1,0:T(8,128)(2,1)S(1)}, bf16[50,8,128]{2,1,0:T(8,128)(2,1)S(1)}, u32[]{:S(2)}, u32[]{:S(2)}) collective-permute-start(bf16[50,8,128]{2,1,0:T(8,128)(2,1)S(1)} %get-tuple-element.22), channel_id=1, source_target_pairs={{0,4},{4,8},{8,12},{12,16},{16,20},{20,24},{24,28},{1,5},{5,9},{9,... | collective-permute-start | bytes 307208 | tf_op jit(solution)/shard_map/ppermute | solution.py:24
  6.5 5.2 %collective-permute-start.1 = (bf16[1,6400]{1,0:T(2,128)(2,1)S(1)}, bf16[1,6400]{1,0:T(2,128)(2,1)S(1)}, u32[]{:S(2)}, u32[]{:S(2)}) collective-permute-start(bf16[1,6400]{1,0:T(2,128)(2,1)S(1)} %get-tuple-element.23), channel_id=1, source_target_pairs={{4,0},{8,4},{12,8},{16,12},{20,16},{24,20},{28,24},{5,1},{9,5},{13... | collective-permute-start | bytes 38408 | tf_op jit(solution)/shard_map/ppermute | solution.py:24
  7.8 0.9 %copy-start.4 = (bf16[3,3,64,32]{2,3,1,0:T(8,128)(2,1)S(1)}, bf16[3,3,64,32]{2,3,1,0:T(8,128)(2,1)}, u32[]{:S(2)}) copy-start(bf16[3,3,64,32]{2,3,1,0:T(8,128)(2,1)} %param.11) | copy-start | bytes 110596
  8.7 0.8 %copy-start.7 = (bf16[3,3,32,16]{2,3,1,0:T(8,128)(2,1)S(1)}, bf16[3,3,32,16]{2,3,1,0:T(8,128)(2,1)}, u32[]{:S(2)}) copy-start(bf16[3,3,32,16]{2,3,1,0:T(8,128)(2,1)} %param.12) | copy-start | bytes 27652
  35.2 6.8 %collective-permute-start.2 = (f32[104,128]{1,0:T(8,128)S(1)}, f32[104,128]{1,0:T(8,128)S(1)}, u32[]{:S(2)}, u32[]{:S(2)}) collective-permute-start(f32[104,128]{1,0:T(8,128)S(1)} %get-tuple-element.29), channel_id=1, source_target_pairs={{0,4},{4,0},{8,12},{12,8},{16,20},{20,16},{24,28},{28,24},{1,5},{5... | collective-permute-start | bytes 159752 | tf_op jit(solution)/shard_map/ppermute | solution.py:478
  38.5 7.8 %collective-permute-start.4 = (bf16[8,5760]{1,0:T(8,128)(2,1)S(1)}, bf16[8,5760]{1,0:T(8,128)(2,1)S(1)}, u32[]{:S(2)}, u32[]{:S(2)}) collective-permute-start(bf16[8,5760]{1,0:T(8,128)(2,1)S(1)} %get-tuple-element.30.part0), channel_id=1, source_target_pairs={{0,3},{1,2},{2,1},{3,0},{4,7},{5,6},{6,5},{7,4},{8,11},{9,10},{10,... | collective-permute-start | bytes 276488 | tf_op jit(solution)/shard_map/ppermute | solution.py:478
  42.1 4.2 %collective-permute-start.3 = (f32[104,128]{1,0:T(8,128)S(1)}, f32[104,128]{1,0:T(8,128)S(1)}, u32[]{:S(2)}, u32[]{:S(2)}) collective-permute-start(f32[104,128]{1,0:T(8,128)S(1)} %add.18), channel_id=1, source_target_pairs={{0,8},{4,12},{8,0},{12,4},{16,24},{20,28},{24,16},{28,20},{1,9},{5... | collective-permute-start | bytes 159752 | tf_op jit(solution)/shard_map/ppermute | solution.py:478
  43.9 8.2 %collective-permute-start.6 = (bf16[8,5760]{1,0:T(8,128)(2,1)S(1)}, bf16[8,5760]{1,0:T(8,128)(2,1)S(1)}, u32[]{:S(2)}, u32[]{:S(2)}) collective-permute-start(bf16[8,5760]{1,0:T(8,128)(2,1)S(1)} %get-tuple-element.30.part0), channel_id=1, source_target_pairs={{0,2},{1,3},{2,0},{3,1},{4,6},{5,7},{6,4},{7,5},{8,10},{9,11},{10,... | collective-permute-start | bytes 276488 | tf_op jit(solution)/shard_map/ppermute | solution.py:478
  46.3 5.8 %collective-permute-start.5 = (f32[104,128]{1,0:T(8,128)S(1)}, f32[104,128]{1,0:T(8,128)S(1)}, u32[]{:S(2)}, u32[]{:S(2)}) collective-permute-start(f32[104,128]{1,0:T(8,128)S(1)} %add.19), channel_id=1, source_target_pairs={{0,16},{4,20},{8,24},{12,28},{16,0},{20,4},{24,8},{28,12},{1,17},{... | collective-permute-start | bytes 159752 | tf_op jit(solution)/shard_map/ppermute | solution.py:478
  49.0 7.6 %collective-permute-start.10 = (bf16[8,5760]{1,0:T(8,128)(2,1)S(1)}, bf16[8,5760]{1,0:T(8,128)(2,1)S(1)}, u32[]{:S(2)}, u32[]{:S(2)}) collective-permute-start(bf16[8,5760]{1,0:T(8,128)(2,1)S(1)} %get-tuple-element.30.part0), channel_id=1, source_target_pairs={{0,1},{1,0},{2,3},{3,2},{4,5},{5,4},{6,7},{7,6},{8,9},{9,8},{10,11... | collective-permute-start | bytes 276488 | tf_op jit(solution)/shard_map/ppermute | solution.py:478
  52.1 6.2 %collective-permute-start.9 = (f32[104,128]{1,0:T(8,128)S(1)}, f32[104,128]{1,0:T(8,128)S(1)}, u32[]{:S(2)}, u32[]{:S(2)}) collective-permute-start(f32[104,128]{1,0:T(8,128)S(1)} %add.20), channel_id=1, source_target_pairs={{0,3},{1,2},{2,1},{3,0},{4,7},{5,6},{6,5},{7,4},{8,11},{9,10},{10,... | collective-permute-start | bytes 159752 | tf_op jit(solution)/shard_map/ppermute | solution.py:478
  54.3 5.3 %collective-permute-start.8 = (f32[104,128]{1,0:T(8,128)S(1)}, f32[104,128]{1,0:T(8,128)S(1)}, u32[]{:S(2)}, u32[]{:S(2)}) collective-permute-start(f32[104,128]{1,0:T(8,128)S(1)} %add.20), channel_id=1, source_target_pairs={{0,2},{1,3},{2,0},{3,1},{4,6},{5,7},{6,4},{7,5},{8,10},{9,11},{10,... | collective-permute-start | bytes 159752 | tf_op jit(solution)/shard_map/ppermute | solution.py:478
  55.8 4.4 %collective-permute-start.7 = (f32[104,128]{1,0:T(8,128)S(1)}, f32[104,128]{1,0:T(8,128)S(1)}, u32[]{:S(2)}, u32[]{:S(2)}) collective-permute-start(f32[104,128]{1,0:T(8,128)S(1)} %add.20), channel_id=1, source_target_pairs={{0,1},{1,0},{2,3},{3,2},{4,5},{5,4},{6,7},{7,6},{8,9},{9,8},{10,11... | collective-permute-start | bytes 159752 | tf_op jit(solution)/shard_map/ppermute | solution.py:478
  60.2 1.3 %collective-permute-start.11 = (f32[104,128]{1,0:T(8,128)S(1)}, f32[104,128]{1,0:T(8,128)S(1)}, u32[]{:S(2)}, u32[]{:S(2)}) collective-permute-start(f32[104,128]{1,0:T(8,128)S(1)} %add_add_fusion.mine), channel_id=1, source_target_pairs={{0,4},{4,0},{8,12},{12,8},{16,20},{20,16},{24,28},{28,24},{1,5},{5... | collective-permute-start | bytes 159752 | tf_op jit(solution)/shard_map/ppermute | solution.py:478

commit v6 on v5

--- a/solution.py
+++ b/solution.py
@@ -377,6 +377,8 @@
     pick_prev = ((group // 2 < half) & (place == owner)).astype(bf16)
     pick = jnp.concatenate([pick_own, pick_prev], axis=0)
 
+    unit = (iota((256, 256), 0) == iota((256, 256), 1)).astype(bf16)
+
     def second_product(n, cast):
         taken = jnp.concatenate([operand(act, 2 * n + k, 0, front) for k in range(2)], axis=0)
         out = jnp.dot(taken, band_two[...], preferred_element_type=f32).astype(bf16)
@@ -419,7 +421,8 @@
             return fgrad[line, start : start + count].reshape(count * 16, LANES)
 
         def product(g, x):
-            return lax.dot_general(g, x, (((0,), (0,)), ((), ())), preferred_element_type=f32)
+            turned = lax.dot_general(unit, g, (((1,), (1,)), ((), ())), preferred_element_type=f32)
+            return jnp.dot(turned.astype(bf16), x, preferred_element_type=f32)
 
         g = [
             jnp.concatenate(
@@ -518,7 +521,7 @@
             jax.ShapeDtypeStruct((1, 2 * wide * LANES), bf16),
         ],
         scratch_shapes=[pltpu.VMEM((8, LANES), jnp.int32)],
-        compiler_params=small,
+        compiler_params=pltpu.CompilerParams(vmem_limit_bytes=56 * 1024 * 1024),
         name="edges",
     )(latent, targets, land_words)
     above = shifted(down, "lat", 1)

time: 62.6 us -> 63.7 us (1.018)
  Pallas kernels: 27.6 us -> 31.9 us
  local copies, waits for them, and re-layouts: 4.74 us -> 1.67 us
    unnamed x22 -> x16, local copies, waits for them, and re-layouts: 4.74 us -> 1.67 us
    pallas_call x1, Pallas kernels: 23.5 us -> 26 us  [local(): pl.pallas_call(functools.partial(band_kernel, half, (chan0, chan1, chan2)...]
    pallas_call x1, Pallas kernels: 0.24 us -> 2.1 us  [local(): pl.pallas_call(functools.partial(edge_kernel, half, chan2), grid=(1,), in...]
where the time goes in v6:
time: 63.7 us; the launch traced here: 63.4 us
  Pallas kernels  31.9 us (50%)
  starting transfers between devices  22.6 us (35%)
  waiting for transfers between devices  6.33 us (10%)
  local copies, waits for them, and re-layouts  1.67 us (3%)
  between operations  0.79 us (1%)
    pallas_call x1, Pallas kernels, local(): pl.pallas_call(functools.partial(band_kernel, half, (chan0, chan1, chan2)...  26 us
    ppermute x10, starting transfers between devices, swapped(): lax.ppermute(array, axis, [(i, i ^ bit) for i in range(lax.axis_size(axis...  19 us
    ppermute x10, waiting for transfers between devices, swapped(): lax.ppermute(array, axis, [(i, i ^ bit) for i in range(lax.axis_size(axis...  6.05 us
    ppermute x2, starting transfers between devices, shifted(): return lax.ppermute(array, axis, pairs)  3.64 us
    pallas_call x1, Pallas kernels, local(): pl.pallas_call(functools.partial(prepare_kernel, half), in_specs=[smem] *...  2.14 us
    pallas_call x1, Pallas kernels, local(): pl.pallas_call(functools.partial(edge_kernel, half, chan2), grid=(1,), in...  2.1 us
    unnamed x16, local copies, waits for them, and re-layouts  1.67 us
  transfers between devices with their start and end apart: 12, of which 6 were waited for; matrix products, arithmetic and copies ran while one was open for 0% of the time, Pallas kernels for 5%

profile of v6, /device:TPU:0, one launch (start us, length us, event | category | flops | bytes accessed | tf_op | source)
XLA Modules:
  0.0 63.4 jit_solution(3633986997121874253)
XLA Ops:
  0.7 2.1 %edges.1 = (bf16[50,8,128]{2,1,0:T(8,128)(2,1)}, bf16[1,6400]{1,0:T(2,128)(2,1)}) custom-call(bf16[1,8,23040]{2,1,0:T(8,128)(2,1)} %latent.3, bf16[1,32,23040]{2,1,0:T(8,128)(2,1)} %targets.3, s32[32,48]{1,0:T(8,128)} %land.3), custom_call_target="tpu_custom_call" | custom-call | tf_op jit(solution)/shard_map/edges/pallas_call | solution.py:507
  2.8 2.4 %collective-permute-start = (bf16[50,8,128]{2,1,0:T(8,128)(2,1)}, bf16[50,8,128]{2,1,0:T(8,128)(2,1)S(1)}, u32[]{:S(2)}, u32[]{:S(2)}) collective-permute-start(bf16[50,8,128]{2,1,0:T(8,128)(2,1)} %get-tuple-element.22), channel_id=1, source_target_pairs={{0,4},{4,8},{8,12},{12,16},{16,20},{20,24},{24,28},{1,5},{5,9},{9,... | collective-permute-start | bytes 307208 | tf_op jit(solution)/shard_map/ppermute | solution.py:24
  5.2 1.3 %collective-permute-start.1 = (bf16[1,6400]{1,0:T(2,128)(2,1)}, bf16[1,6400]{1,0:T(2,128)(2,1)S(1)}, u32[]{:S(2)}, u32[]{:S(2)}) collective-permute-start(bf16[1,6400]{1,0:T(2,128)(2,1)} %get-tuple-element.23), channel_id=1, source_target_pairs={{4,0},{8,4},{12,8},{16,12},{20,16},{24,20},{28,24},{5,1},{9,5},{13... | collective-permute-start | bytes 38408 | tf_op jit(solution)/shard_map/ppermute | solution.py:24
  6.5 0.9 %copy-done.2 = bf16[3,3,64,32]{2,3,1,0:T(8,128)(2,1)S(1)} copy-done((bf16[3,3,64,32]{2,3,1,0:T(8,128)(2,1)S(1)}, bf16[3,3,64,32]{2,3,1,0:T(8,128)(2,1)}, u32[]{:S(2)}) %copy-start.2) | copy-done | bytes 36888
  7.4 0.8 %copy-done.4 = bf16[3,3,32,16]{2,3,1,0:T(8,128)(2,1)S(1)} copy-done((bf16[3,3,32,16]{2,3,1,0:T(8,128)(2,1)S(1)}, bf16[3,3,32,16]{2,3,1,0:T(8,128)(2,1)}, u32[]{:S(2)}) %copy-start.4) | copy-done | bytes 9240
  8.1 2.1 %prepare.1 = (bf16[8,25,16,128]{3,2,1,0:T(8,128)(2,1)S(1)}, bf16[512,256]{1,0:T(8,128)(2,1)S(1)}, bf16[512,256]{1,0:T(8,128)(2,1)S(1)}, bf16[512,256]{1,0:T(8,128)(2,1)S(1)}, bf16[512,256]{1,0:T(8,128)(2,1)S(1)}) custom-call(s32[8]{0:T(128)S(1)} %copy-done.5, f32[64]{0:T(128)S(1)} %copy-done.6, bf16[1,8,23040]{2,1,0:T(8,128)(2,1)S(1)} %copy-done.1, ...), custom_call_target="tpu_custom_call" | custom-call | flops 100000000 | bytes 10000000 | tf_op jit(solution)/shard_map/prepare/pallas_call | solution.py:530
  10.3 0.3 collective-permute-done.1.below
  10.6 26.0 %band.1 = (bf16[8,5760]{1,0:T(8,128)(2,1)S(1)}, f32[104,128]{1,0:T(8,128)S(1)}, f32[104,128]{1,0:T(8,128)S(1)}) custom-call(s32[8]{0:T(128)S(1)} %copy-done.5, f32[64]{0:T(128)S(1)} %copy-done.6, f32[16]{0:T(128)S(1)} %copy-done.7, bf16[8,25,16,128]{3,2,1,0:T(8,128)(2,1)S(1)} %get-tuple-element.21.own_source, ...), custom_call_target="tpu_custom_call" | custom-call | tf_op jit(solution)/shard_map/band/pallas_call | solution.py:542
  36.6 3.1 %collective-permute-start.2 = (f32[104,128]{1,0:T(8,128)S(1)}, f32[104,128]{1,0:T(8,128)S(1)}, u32[]{:S(2)}, u32[]{:S(2)}) collective-permute-start(f32[104,128]{1,0:T(8,128)S(1)} %get-tuple-element.29), channel_id=1, source_target_pairs={{0,4},{4,0},{8,12},{12,8},{16,20},{20,16},{24,28},{28,24},{1,5},{5... | collective-permute-start | bytes 159752 | tf_op jit(solution)/shard_map/ppermute | solution.py:481
  39.6 3.6 %collective-permute-start.4 = (bf16[8,5760]{1,0:T(8,128)(2,1)S(1)}, bf16[8,5760]{1,0:T(8,128)(2,1)S(1)}, u32[]{:S(2)}, u32[]{:S(2)}) collective-permute-start(bf16[8,5760]{1,0:T(8,128)(2,1)S(1)} %get-tuple-element.30.part0), channel_id=1, source_target_pairs={{0,3},{1,2},{2,1},{3,0},{4,7},{5,6},{6,5},{7,4},{8,11},{9,10},{10,... | collective-permute-start | bytes 276488 | tf_op jit(solution)/shard_map/ppermute | solution.py:481
  43.2 2.0 %collective-permute-start.3 = (f32[104,128]{1,0:T(8,128)S(1)}, f32[104,128]{1,0:T(8,128)S(1)}, u32[]{:S(2)}, u32[]{:S(2)}) collective-permute-start(f32[104,128]{1,0:T(8,128)S(1)} %add.18), channel_id=1, source_target_pairs={{0,8},{4,12},{8,0},{12,4},{16,24},{20,28},{24,16},{28,20},{1,9},{5... | collective-permute-start | bytes 159752 | tf_op jit(solution)/shard_map/ppermute | solution.py:481
  45.3 2.2 %collective-permute-done.3 = f32[104,128]{1,0:T(8,128)S(1)} collective-permute-done((f32[104,128]{1,0:T(8,128)S(1)}, f32[104,128]{1,0:T(8,128)S(1)}, u32[]{:S(2)}, u32[]{:S(2)}) %collective-permute-start.3) | collective-permute-done | bytes 53280 | tf_op jit(solution)/shard_map/ppermute | solution.py:481
  47.5 2.7 %collective-permute-start.5 = (f32[104,128]{1,0:T(8,128)S(1)}, f32[104,128]{1,0:T(8,128)S(1)}, u32[]{:S(2)}, u32[]{:S(2)}) collective-permute-start(f32[104,128]{1,0:T(8,128)S(1)} %add.19), channel_id=1, source_target_pairs={{0,16},{4,20},{8,24},{12,28},{16,0},{20,4},{24,8},{28,12},{1,17},{... | collective-permute-start | bytes 159752 | tf_op jit(solution)/shard_map/ppermute | solution.py:481
  50.1 3.1 %collective-permute-start.10 = (bf16[8,5760]{1,0:T(8,128)(2,1)S(1)}, bf16[8,5760]{1,0:T(8,128)(2,1)S(1)}, u32[]{:S(2)}, u32[]{:S(2)}) collective-permute-start(bf16[8,5760]{1,0:T(8,128)(2,1)S(1)} %get-tuple-element.30.part0), channel_id=1, source_target_pairs={{0,1},{1,0},{2,3},{3,2},{4,5},{5,4},{6,7},{7,6},{8,9},{9,8},{10,11... | collective-permute-start | bytes 276488 | tf_op jit(solution)/shard_map/ppermute | solution.py:481
  53.3 2.1 %collective-permute-start.9 = (f32[104,128]{1,0:T(8,128)S(1)}, f32[104,128]{1,0:T(8,128)S(1)}, u32[]{:S(2)}, u32[]{:S(2)}) collective-permute-start(f32[104,128]{1,0:T(8,128)S(1)} %add.20), channel_id=1, source_target_pairs={{0,3},{1,2},{2,1},{3,0},{4,7},{5,6},{6,5},{7,4},{8,11},{9,10},{10,... | collective-permute-start | bytes 159752 | tf_op jit(solution)/shard_map/ppermute | solution.py:481
  55.4 1.5 %collective-permute-start.8 = (f32[104,128]{1,0:T(8,128)S(1)}, f32[104,128]{1,0:T(8,128)S(1)}, u32[]{:S(2)}, u32[]{:S(2)}) collective-permute-start(f32[104,128]{1,0:T(8,128)S(1)} %add.20), channel_id=1, source_target_pairs={{0,2},{1,3},{2,0},{3,1},{4,6},{5,7},{6,4},{7,5},{8,10},{9,11},{10,... | collective-permute-start | bytes 159752 | tf_op jit(solution)/shard_map/ppermute | solution.py:481
  56.9 0.8 %collective-permute-start.7 = (f32[104,128]{1,0:T(8,128)S(1)}, f32[104,128]{1,0:T(8,128)S(1)}, u32[]{:S(2)}, u32[]{:S(2)}) collective-permute-start(f32[104,128]{1,0:T(8,128)S(1)} %add.20), channel_id=1, source_target_pairs={{0,1},{1,0},{2,3},{3,2},{4,5},{5,4},{6,7},{7,6},{8,9},{9,8},{10,11... | collective-permute-start | bytes 159752 | tf_op jit(solution)/shard_map/ppermute | solution.py:481
  57.7 0.9 %place.1 = f32[1,8,23040]{2,1,0:T(8,128)} custom-call(bf16[8,5760]{1,0:T(8,128)(2,1)S(1)} %get-tuple-element.30.part0, bf16[8,5760]{1,0:T(8,128)(2,1)S(1)} %collective-permute-done.10.part1, bf16[8,5760]{1,0:T(8,128)(2,1)S(1)} %collective-permute-done.6.part2, bf16[8,5760]{1,0:T(8,128)(2,1)S(1)} %collective-permute-done.4.part3), custom_call_target="tpu_custom_call" | custom-call | tf_op jit(solution)/shard_map/place/pallas_call | solution.py:593
  58.6 0.8 %collective-permute-done.9 = f32[104,128]{1,0:T(8,128)S(1)} collective-permute-done((f32[104,128]{1,0:T(8,128)S(1)}, f32[104,128]{1,0:T(8,128)S(1)}, u32[]{:S(2)}, u32[]{:S(2)}) %collective-permute-start.9) | collective-permute-done | bytes 53280 | tf_op jit(solution)/shard_map/ppermute | solution.py:481
  59.5 1.3 %collective-permute-done.8 = f32[104,128]{1,0:T(8,128)S(1)} collective-permute-done((f32[104,128]{1,0:T(8,128)S(1)}, f32[104,128]{1,0:T(8,128)S(1)}, u32[]{:S(2)}, u32[]{:S(2)}) %collective-permute-start.8) | collective-permute-done | bytes 53280 | tf_op jit(solution)/shard_map/ppermute | solution.py:481
  60.7 0.5 collective-permute-done.7
  61.3 0.1 collective-permute-start.11
  61.4 1.2 %collective-permute-done.11.other = f32[104,128]{1,0:T(8,128)S(1)} collective-permute-done((f32[104,128]{1,0:T(8,128)S(1)}, f32[104,128]{1,0:T(8,128)S(1)}, u32[]{:S(2)}, u32[]{:S(2)}) %collective-permute-start.11) | collective-permute-done | bytes 53280 | tf_op jit(solution)/shard_map/ppermute | solution.py:481
  62.6 0.8 %taps.1 = (f32[3,3,32,64]{3,2,1,0:T(8,128)}, f32[3,3,16,32]{3,2,1,0:T(8,128)}) custom-call(f32[104,128]{1,0:T(8,128)S(1)} %add_add_fusion.mine, f32[104,128]{1,0:T(8,128)S(1)} %collective-permute-done.11.other), custom_call_target="tpu_custom_call" | custom-call | tf_op jit(solution)/shard_map/taps/pallas_call | solution.py:604
  (25 shorter events, 0.1 us)
Async XLA Ops:
  0.6 9.9 %copy-start.3 = (s32[32,48]{1,0:T(8,128)S(1)}, s32[32,48]{1,0:T(8,128)}, u32[]{:S(2)}) copy-start(s32[32,48]{1,0:T(8,128)} %land.3) | copy-start | bytes 18436
  0.6 9.9 %copy-start = (bf16[1,32,23040]{2,1,0:T(8,128)(2,1)S(1)}, bf16[1,32,23040]{2,1,0:T(8,128)(2,1)}, u32[]{:S(2)}) copy-start(bf16[1,32,23040]{2,1,0:T(8,128)(2,1)} %targets.3) | copy-start | bytes 4423684
  0.7 5.8 %copy-start.1 = (bf16[1,8,23040]{2,1,0:T(8,128)(2,1)S(1)}, bf16[1,8,23040]{2,1,0:T(8,128)(2,1)}, u32[]{:S(2)}) copy-start(bf16[1,8,23040]{2,1,0:T(8,128)(2,1)} %latent.3) | copy-start | bytes 1105924
  0.7 5.8 %copy-start.6 = (f32[64]{0:T(128)S(1)}, f32[64]{0:T(128)}, u32[]{:S(2)}) copy-start(f32[64]{0:T(128)} %scale.3) | copy-start | bytes 772
  0.7 5.8 %copy-start.5 = (s32[8]{0:T(128)S(1)}, s32[8]{0:T(128)}, u32[]{:S(2)}) copy-start(s32[8]{0:T(128)} %seeds.3) | copy-start | bytes 100
  0.7 9.9 %copy-start.7 = (f32[16]{0:T(128)S(1)}, f32[16]{0:T(128)}, u32[]{:S(2)}) copy-start(f32[16]{0:T(128)} %channel_weight.1) | copy-start | bytes 196
  2.8 7.8 %collective-permute-start = (bf16[50,8,128]{2,1,0:T(8,128)(2,1)}, bf16[50,8,128]{2,1,0:T(8,128)(2,1)S(1)}, u32[]{:S(2)}, u32[]{:S(2)}) collective-permute-start(bf16[50,8,128]{2,1,0:T(8,128)(2,1)} %get-tuple-element.22), channel_id=1, source_target_pairs={{0,4},{4,8},{8,12},{12,16},{16,20},{20,24},{24,28},{1,5},{5,9},{9,... | collective-permute-start | bytes 307208 | tf_op jit(solution)/shard_map/ppermute | solution.py:24
  5.2 5.4 %collective-permute-start.1 = (bf16[1,6400]{1,0:T(2,128)(2,1)}, bf16[1,6400]{1,0:T(2,128)(2,1)S(1)}, u32[]{:S(2)}, u32[]{:S(2)}) collective-permute-start(bf16[1,6400]{1,0:T(2,128)(2,1)} %get-tuple-element.23), channel_id=1, source_target_pairs={{4,0},{8,4},{12,8},{16,12},{20,16},{24,20},{28,24},{5,1},{9,5},{13... | collective-permute-start | bytes 38408 | tf_op jit(solution)/shard_map/ppermute | solution.py:24
  6.5 0.9 %copy-start.2 = (bf16[3,3,64,32]{2,3,1,0:T(8,128)(2,1)S(1)}, bf16[3,3,64,32]{2,3,1,0:T(8,128)(2,1)}, u32[]{:S(2)}) copy-start(bf16[3,3,64,32]{2,3,1,0:T(8,128)(2,1)} %param.11) | copy-start | bytes 110596
  7.4 0.8 %copy-start.4 = (bf16[3,3,32,16]{2,3,1,0:T(8,128)(2,1)S(1)}, bf16[3,3,32,16]{2,3,1,0:T(8,128)(2,1)}, u32[]{:S(2)}) copy-start(bf16[3,3,32,16]{2,3,1,0:T(8,128)(2,1)} %param.12) | copy-start | bytes 27652
  36.6 6.7 %collective-permute-start.2 = (f32[104,128]{1,0:T(8,128)S(1)}, f32[104,128]{1,0:T(8,128)S(1)}, u32[]{:S(2)}, u32[]{:S(2)}) collective-permute-start(f32[104,128]{1,0:T(8,128)S(1)} %get-tuple-element.29), channel_id=1, source_target_pairs={{0,4},{4,0},{8,12},{12,8},{16,20},{20,16},{24,28},{28,24},{1,5},{5... | collective-permute-start | bytes 159752 | tf_op jit(solution)/shard_map/ppermute | solution.py:481
  39.6 7.8 %collective-permute-start.4 = (bf16[8,5760]{1,0:T(8,128)(2,1)S(1)}, bf16[8,5760]{1,0:T(8,128)(2,1)S(1)}, u32[]{:S(2)}, u32[]{:S(2)}) collective-permute-start(bf16[8,5760]{1,0:T(8,128)(2,1)S(1)} %get-tuple-element.30.part0), channel_id=1, source_target_pairs={{0,3},{1,2},{2,1},{3,0},{4,7},{5,6},{6,5},{7,4},{8,11},{9,10},{10,... | collective-permute-start | bytes 276488 | tf_op jit(solution)/shard_map/ppermute | solution.py:481
  43.2 4.2 %collective-permute-start.3 = (f32[104,128]{1,0:T(8,128)S(1)}, f32[104,128]{1,0:T(8,128)S(1)}, u32[]{:S(2)}, u32[]{:S(2)}) collective-permute-start(f32[104,128]{1,0:T(8,128)S(1)} %add.18), channel_id=1, source_target_pairs={{0,8},{4,12},{8,0},{12,4},{16,24},{20,28},{24,16},{28,20},{1,9},{5... | collective-permute-start | bytes 159752 | tf_op jit(solution)/shard_map/ppermute | solution.py:481
  45.3 8.0 %collective-permute-start.6 = (bf16[8,5760]{1,0:T(8,128)(2,1)S(1)}, bf16[8,5760]{1,0:T(8,128)(2,1)S(1)}, u32[]{:S(2)}, u32[]{:S(2)}) collective-permute-start(bf16[8,5760]{1,0:T(8,128)(2,1)S(1)} %get-tuple-element.30.part0), channel_id=1, source_target_pairs={{0,2},{1,3},{2,0},{3,1},{4,6},{5,7},{6,4},{7,5},{8,10},{9,11},{10,... | collective-permute-start | bytes 276488 | tf_op jit(solution)/shard_map/ppermute | solution.py:481
  47.5 5.8 %collective-permute-start.5 = (f32[104,128]{1,0:T(8,128)S(1)}, f32[104,128]{1,0:T(8,128)S(1)}, u32[]{:S(2)}, u32[]{:S(2)}) collective-permute-start(f32[104,128]{1,0:T(8,128)S(1)} %add.19), channel_id=1, source_target_pairs={{0,16},{4,20},{8,24},{12,28},{16,0},{20,4},{24,8},{28,12},{1,17},{... | collective-permute-start | bytes 159752 | tf_op jit(solution)/shard_map/ppermute | solution.py:481
  50.1 7.6 %collective-permute-start.10 = (bf16[8,5760]{1,0:T(8,128)(2,1)S(1)}, bf16[8,5760]{1,0:T(8,128)(2,1)S(1)}, u32[]{:S(2)}, u32[]{:S(2)}) collective-permute-start(bf16[8,5760]{1,0:T(8,128)(2,1)S(1)} %get-tuple-element.30.part0), channel_id=1, source_target_pairs={{0,1},{1,0},{2,3},{3,2},{4,5},{5,4},{6,7},{7,6},{8,9},{9,8},{10,11... | collective-permute-start | bytes 276488 | tf_op jit(solution)/shard_map/ppermute | solution.py:481
  53.3 6.2 %collective-permute-start.9 = (f32[104,128]{1,0:T(8,128)S(1)}, f32[104,128]{1,0:T(8,128)S(1)}, u32[]{:S(2)}, u32[]{:S(2)}) collective-permute-start(f32[104,128]{1,0:T(8,128)S(1)} %add.20), channel_id=1, source_target_pairs={{0,3},{1,2},{2,1},{3,0},{4,7},{5,6},{6,5},{7,4},{8,11},{9,10},{10,... | collective-permute-start | bytes 159752 | tf_op jit(solution)/shard_map/ppermute | solution.py:481
  55.4 5.3 %collective-permute-start.8 = (f32[104,128]{1,0:T(8,128)S(1)}, f32[104,128]{1,0:T(8,128)S(1)}, u32[]{:S(2)}, u32[]{:S(2)}) collective-permute-start(f32[104,128]{1,0:T(8,128)S(1)} %add.20), channel_id=1, source_target_pairs={{0,2},{1,3},{2,0},{3,1},{4,6},{5,7},{6,4},{7,5},{8,10},{9,11},{10,... | collective-permute-start | bytes 159752 | tf_op jit(solution)/shard_map/ppermute | solution.py:481
  56.9 4.4 %collective-permute-start.7 = (f32[104,128]{1,0:T(8,128)S(1)}, f32[104,128]{1,0:T(8,128)S(1)}, u32[]{:S(2)}, u32[]{:S(2)}) collective-permute-start(f32[104,128]{1,0:T(8,128)S(1)} %add.20), channel_id=1, source_target_pairs={{0,1},{1,0},{2,3},{3,2},{4,5},{5,4},{6,7},{7,6},{8,9},{9,8},{10,11... | collective-permute-start | bytes 159752 | tf_op jit(solution)/shard_map/ppermute | solution.py:481
  61.3 1.3 %collective-permute-start.11 = (f32[104,128]{1,0:T(8,128)S(1)}, f32[104,128]{1,0:T(8,128)S(1)}, u32[]{:S(2)}, u32[]{:S(2)}) collective-permute-start(f32[104,128]{1,0:T(8,128)S(1)} %add_add_fusion.mine), channel_id=1, source_target_pairs={{0,4},{4,0},{8,12},{12,8},{16,20},{20,16},{24,28},{28,24},{1,5},{5... | collective-permute-start | bytes 159752 | tf_op jit(solution)/shard_map/ppermute | solution.py:481

commit v7 on v6

--- a/solution.py
+++ b/solution.py
@@ -85,7 +85,7 @@
                     back_ref[at : at + chan_out, row * LANES : (row + 1) * LANES] = part.astype(jnp.bfloat16)
 
 
-def pack_taps(acc_ref, out_ref, first, chan_in, chan_out, norm):
+def pack_taps(acc_ref, next_ref, out_ref, first, chan_in, chan_out, norm):
     cells = LANES // chan_in
     group = iota((chan_out, LANES), 1) // chan_in
     packed = None
@@ -98,9 +98,9 @@
             q = 2 * reach + b - 1
             if 0 <= q < 2 * cells:
                 block, cell = reach // cells, reach % cells
-                lines = sub * LANES + q * chan_out
-                lanes = block * 256 + row * LANES
-                piece = acc_ref[lines : lines + chan_out, lanes : lanes + LANES]
+                lines = sub * LANES + q * chan_out if block == 0 else sub * chan_out
+                ref = acc_ref if block == 0 else next_ref
+                piece = ref[lines : lines + chan_out, row * LANES : (row + 1) * LANES]
                 turn = (slot - cell) % cells * chan_in
                 piece = pltpu.roll(piece, turn, 1) if turn else piece
                 part = piece if part is None else part + piece
@@ -266,7 +266,9 @@
     lat_lines,
     taps,
     acc_one,
+    acc_one_next,
     acc_two,
+    acc_two_next,
 ):
     rows = own_source.shape[0]
     span = targets.shape[2]
@@ -316,8 +318,8 @@
     fgrad_odd[...] = jnp.zeros(fgrad_odd.shape, bf16)
     carry[...] = jnp.zeros(carry.shape, f32)
     carry_lat[...] = jnp.zeros(carry_lat.shape, f32)
-    acc_one[...] = jnp.zeros(acc_one.shape, f32)
-    acc_two[...] = jnp.zeros(acc_two.shape, f32)
+    for acc in (acc_one, acc_one_next, acc_two, acc_two_next):
+        acc[...] = jnp.zeros(acc.shape, f32)
 
     def line(slot, i):
         return spread_line(lat_rows, slot, i)
@@ -376,8 +378,6 @@
     pick_own = (real & (place - 1 == owner)).astype(bf16)
     pick_prev = ((group // 2 < half) & (place == owner)).astype(bf16)
     pick = jnp.concatenate([pick_own, pick_prev], axis=0)
-
-    unit = (iota((256, 256), 0) == iota((256, 256), 1)).astype(bf16)
 
     def second_product(n, cast):
         taken = jnp.concatenate([operand(act, 2 * n + k, 0, front) for k in range(2)], axis=0)
@@ -420,9 +420,12 @@
         def flat(line, start, count):
             return fgrad[line, start : start + count].reshape(count * 16, LANES)
 
-        def product(g, x):
-            turned = lax.dot_general(unit, g, (((1,), (1,)), ((), ())), preferred_element_type=f32)
-            return jnp.dot(turned.astype(bf16), x, preferred_element_type=f32)
+        def add_taps(g, x, acc, acc_next, chan_out):
+            turned = g.T
+            acc[...] += jnp.dot(turned, x[:, :256], preferred_element_type=f32)
+            last = [turned[k * LANES - chan_out : k * LANES] for k in (1, 2)]
+            last = jnp.concatenate(last, axis=0)
+            acc_next[...] += jnp.dot(last, x[:, 256:], preferred_element_type=f32)
 
         g = [
             jnp.concatenate(
@@ -434,7 +437,7 @@
         pulled = jnp.dot(jnp.concatenate(g, axis=0), back_two[...], preferred_element_type=f32)
         g = [jnp.concatenate([flat(2 * k, 2, half), flat(2 * k + 1, 2, half)], axis=1) for k in range(2)]
         x = [operand(act, 2 * at + k, 1, half) for k in range(2)]
-        acc_two[...] += product(jnp.concatenate(g, axis=0) * keep, jnp.concatenate(x, axis=0))
+        add_taps(jnp.concatenate(g, axis=0) * keep, jnp.concatenate(x, axis=0), acc_two, acc_two_next, chan2)
         grads = [
             pulled[:members, :LANES] + carry[...],
             pulled[members:, :LANES] + pulled[:members, LANES:],
@@ -450,7 +453,7 @@
         z = z[:48] + z[48:]
         lat_lines[pl.ds(jnp.maximum(n - 1, 0), 48, stride=rows), :] = z[:, :LANES] + carry_lat[...]
         carry_lat[...] = z[:, LANES:]
-        acc_one[...] += product(grads[16:] * keep, operand(source, at, 1, half))
+        add_taps(grads[16:] * keep, operand(source, at, 1, half), acc_one, acc_one_next, chan1)
 
     def second_segment(m, _):
         second_product(2 * m + 1, cast_odd)
@@ -469,8 +472,8 @@
 
     for t in range(own):
         out_lat[:, t * LANES : (t + 1) * LANES] = lat_lines[t * rows : (t + 1) * rows].astype(bf16)
-    pack_taps(acc_one, taps, 0, chan0, chan1, norm)
-    pack_taps(acc_two, taps, -(-9 // (LANES // chan0)) * chan1, chan1, chan2, norm)
+    pack_taps(acc_one, acc_one_next, taps, 0, chan0, chan1, norm)
+    pack_taps(acc_two, acc_two_next, taps, -(-9 // (LANES // chan0)) * chan1, chan1, chan2, norm)
     count = taps_keep.shape[0]
     odd = jnp.bitwise_and(lat_pos, 1)
     taps_keep[...] = taps[pl.ds(pl.multiple_of(odd * count, 8), count), :]
@@ -566,8 +569,10 @@
             pltpu.VMEM((48, LANES), f32),
             pltpu.VMEM((48 * rows, LANES), f32),
             pltpu.VMEM((tap_rows, LANES), f32),
-            pltpu.VMEM((256, 512), f32),
-            pltpu.VMEM((256, 512), f32),
+            pltpu.VMEM((256, 256), f32),
+            pltpu.VMEM((2 * chan1, 256), f32),
+            pltpu.VMEM((256, 256), f32),
+            pltpu.VMEM((2 * chan2, 256), f32),
         ],
         compiler_params=params,
         name="band",

time: 63.7 us -> 59.9 us (0.940)
  Pallas kernels: 31.9 us -> 28.2 us
    pallas_call x1, Pallas kernels: 26 us -> 22.3 us  [local(): pl.pallas_call(functools.partial(band_kernel, half, (chan0, chan1, chan2)...]
where the time goes in v7:
time: 59.9 us; the launch traced here: 59.7 us
  Pallas kernels  28.2 us (47%)
  starting transfers between devices  22.6 us (38%)
  waiting for transfers between devices  6.33 us (11%)
  local copies, waits for them, and re-layouts  1.67 us (3%)
  between operations  0.79 us (1%)
    pallas_call x1, Pallas kernels, local(): pl.pallas_call(functools.partial(band_kernel, half, (chan0, chan1, chan2)...  22.3 us
    ppermute x10, starting transfers between devices, swapped(): lax.ppermute(array, axis, [(i, i ^ bit) for i in range(lax.axis_size(axis...  19 us
    ppermute x10, waiting for transfers between devices, swapped(): lax.ppermute(array, axis, [(i, i ^ bit) for i in range(lax.axis_size(axis...  6.05 us
    ppermute x2, starting transfers between devices, shifted(): return lax.ppermute(array, axis, pairs)  3.64 us
    pallas_call x1, Pallas kernels, local(): pl.pallas_call(functools.partial(prepare_kernel, half), in_specs=[smem] *...  2.14 us
    pallas_call x1, Pallas kernels, local(): pl.pallas_call(functools.partial(edge_kernel, half, chan2), grid=(1,), in...  2.1 us
    unnamed x16, local copies, waits for them, and re-layouts  1.67 us
  transfers between devices with their start and end apart: 12, of which 6 were waited for; matrix products, arithmetic and copies ran while one was open for 0% of the time, Pallas kernels for 5%

profile of v7, /device:TPU:0, one launch (start us, length us, event | category | flops | bytes accessed | tf_op | source)
XLA Modules:
  0.0 59.7 jit_solution(4154746689641834557)
XLA Ops:
  0.7 2.1 %edges.1 = (bf16[50,8,128]{2,1,0:T(8,128)(2,1)}, bf16[1,6400]{1,0:T(2,128)(2,1)}) custom-call(bf16[1,8,23040]{2,1,0:T(8,128)(2,1)} %latent.3, bf16[1,32,23040]{2,1,0:T(8,128)(2,1)} %targets.3, s32[32,48]{1,0:T(8,128)} %land.3), custom_call_target="tpu_custom_call" | custom-call | tf_op jit(solution)/shard_map/edges/pallas_call | solution.py:510
  2.8 2.4 %collective-permute-start = (bf16[50,8,128]{2,1,0:T(8,128)(2,1)}, bf16[50,8,128]{2,1,0:T(8,128)(2,1)S(1)}, u32[]{:S(2)}, u32[]{:S(2)}) collective-permute-start(bf16[50,8,128]{2,1,0:T(8,128)(2,1)} %get-tuple-element.22), channel_id=1, source_target_pairs={{0,4},{4,8},{8,12},{12,16},{16,20},{20,24},{24,28},{1,5},{5,9},{9,... | collective-permute-start | bytes 307208 | tf_op jit(solution)/shard_map/ppermute | solution.py:24
  5.2 1.3 %collective-permute-start.1 = (bf16[1,6400]{1,0:T(2,128)(2,1)}, bf16[1,6400]{1,0:T(2,128)(2,1)S(1)}, u32[]{:S(2)}, u32[]{:S(2)}) collective-permute-start(bf16[1,6400]{1,0:T(2,128)(2,1)} %get-tuple-element.23), channel_id=1, source_target_pairs={{4,0},{8,4},{12,8},{16,12},{20,16},{24,20},{28,24},{5,1},{9,5},{13... | collective-permute-start | bytes 38408 | tf_op jit(solution)/shard_map/ppermute | solution.py:24
  6.5 0.9 %copy-done.2 = bf16[3,3,64,32]{2,3,1,0:T(8,128)(2,1)S(1)} copy-done((bf16[3,3,64,32]{2,3,1,0:T(8,128)(2,1)S(1)}, bf16[3,3,64,32]{2,3,1,0:T(8,128)(2,1)}, u32[]{:S(2)}) %copy-start.2) | copy-done | bytes 36888
  7.4 0.8 %copy-done.4 = bf16[3,3,32,16]{2,3,1,0:T(8,128)(2,1)S(1)} copy-done((bf16[3,3,32,16]{2,3,1,0:T(8,128)(2,1)S(1)}, bf16[3,3,32,16]{2,3,1,0:T(8,128)(2,1)}, u32[]{:S(2)}) %copy-start.4) | copy-done | bytes 9240
  8.1 2.1 %prepare.1 = (bf16[8,25,16,128]{3,2,1,0:T(8,128)(2,1)S(1)}, bf16[512,256]{1,0:T(8,128)(2,1)S(1)}, bf16[512,256]{1,0:T(8,128)(2,1)S(1)}, bf16[512,256]{1,0:T(8,128)(2,1)S(1)}, bf16[512,256]{1,0:T(8,128)(2,1)S(1)}) custom-call(s32[8]{0:T(128)S(1)} %copy-done.5, f32[64]{0:T(128)S(1)} %copy-done.6, bf16[1,8,23040]{2,1,0:T(8,128)(2,1)S(1)} %copy-done.1, ...), custom_call_target="tpu_custom_call" | custom-call | flops 100000000 | bytes 10000000 | tf_op jit(solution)/shard_map/prepare/pallas_call | solution.py:533
  10.3 0.3 collective-permute-done.1.below
  10.6 22.3 %band.1 = (bf16[8,5760]{1,0:T(8,128)(2,1)S(1)}, f32[104,128]{1,0:T(8,128)S(1)}, f32[104,128]{1,0:T(8,128)S(1)}) custom-call(s32[8]{0:T(128)S(1)} %copy-done.5, f32[64]{0:T(128)S(1)} %copy-done.6, f32[16]{0:T(128)S(1)} %copy-done.7, bf16[8,25,16,128]{3,2,1,0:T(8,128)(2,1)S(1)} %get-tuple-element.21.own_source, ...), custom_call_target="tpu_custom_call" | custom-call | tf_op jit(solution)/shard_map/band/pallas_call | solution.py:545
  32.8 3.1 %collective-permute-start.2 = (f32[104,128]{1,0:T(8,128)S(1)}, f32[104,128]{1,0:T(8,128)S(1)}, u32[]{:S(2)}, u32[]{:S(2)}) collective-permute-start(f32[104,128]{1,0:T(8,128)S(1)} %get-tuple-element.29), channel_id=1, source_target_pairs={{0,4},{4,0},{8,12},{12,8},{16,20},{20,16},{24,28},{28,24},{1,5},{5... | collective-permute-start | bytes 159752 | tf_op jit(solution)/shard_map/ppermute | solution.py:484
  35.9 3.6 %collective-permute-start.4 = (bf16[8,5760]{1,0:T(8,128)(2,1)S(1)}, bf16[8,5760]{1,0:T(8,128)(2,1)S(1)}, u32[]{:S(2)}, u32[]{:S(2)}) collective-permute-start(bf16[8,5760]{1,0:T(8,128)(2,1)S(1)} %get-tuple-element.30.part0), channel_id=1, source_target_pairs={{0,3},{1,2},{2,1},{3,0},{4,7},{5,6},{6,5},{7,4},{8,11},{9,10},{10,... | collective-permute-start | bytes 276488 | tf_op jit(solution)/shard_map/ppermute | solution.py:484
  39.5 2.0 %collective-permute-start.3 = (f32[104,128]{1,0:T(8,128)S(1)}, f32[104,128]{1,0:T(8,128)S(1)}, u32[]{:S(2)}, u32[]{:S(2)}) collective-permute-start(f32[104,128]{1,0:T(8,128)S(1)} %add.18), channel_id=1, source_target_pairs={{0,8},{4,12},{8,0},{12,4},{16,24},{20,28},{24,16},{28,20},{1,9},{5... | collective-permute-start | bytes 159752 | tf_op jit(solution)/shard_map/ppermute | solution.py:484
  41.5 2.2 %collective-permute-done.3 = f32[104,128]{1,0:T(8,128)S(1)} collective-permute-done((f32[104,128]{1,0:T(8,128)S(1)}, f32[104,128]{1,0:T(8,128)S(1)}, u32[]{:S(2)}, u32[]{:S(2)}) %collective-permute-start.3) | collective-permute-done | bytes 53280 | tf_op jit(solution)/shard_map/ppermute | solution.py:484
  43.7 2.7 %collective-permute-start.5 = (f32[104,128]{1,0:T(8,128)S(1)}, f32[104,128]{1,0:T(8,128)S(1)}, u32[]{:S(2)}, u32[]{:S(2)}) collective-permute-start(f32[104,128]{1,0:T(8,128)S(1)} %add.19), channel_id=1, source_target_pairs={{0,16},{4,20},{8,24},{12,28},{16,0},{20,4},{24,8},{28,12},{1,17},{... | collective-permute-start | bytes 159752 | tf_op jit(solution)/shard_map/ppermute | solution.py:484
  46.4 3.1 %collective-permute-start.10 = (bf16[8,5760]{1,0:T(8,128)(2,1)S(1)}, bf16[8,5760]{1,0:T(8,128)(2,1)S(1)}, u32[]{:S(2)}, u32[]{:S(2)}) collective-permute-start(bf16[8,5760]{1,0:T(8,128)(2,1)S(1)} %get-tuple-element.30.part0), channel_id=1, source_target_pairs={{0,1},{1,0},{2,3},{3,2},{4,5},{5,4},{6,7},{7,6},{8,9},{9,8},{10,11... | collective-permute-start | bytes 276488 | tf_op jit(solution)/shard_map/ppermute | solution.py:484
  49.5 2.1 %collective-permute-start.9 = (f32[104,128]{1,0:T(8,128)S(1)}, f32[104,128]{1,0:T(8,128)S(1)}, u32[]{:S(2)}, u32[]{:S(2)}) collective-permute-start(f32[104,128]{1,0:T(8,128)S(1)} %add.20), channel_id=1, source_target_pairs={{0,3},{1,2},{2,1},{3,0},{4,7},{5,6},{6,5},{7,4},{8,11},{9,10},{10,... | collective-permute-start | bytes 159752 | tf_op jit(solution)/shard_map/ppermute | solution.py:484
  51.7 1.5 %collective-permute-start.8 = (f32[104,128]{1,0:T(8,128)S(1)}, f32[104,128]{1,0:T(8,128)S(1)}, u32[]{:S(2)}, u32[]{:S(2)}) collective-permute-start(f32[104,128]{1,0:T(8,128)S(1)} %add.20), channel_id=1, source_target_pairs={{0,2},{1,3},{2,0},{3,1},{4,6},{5,7},{6,4},{7,5},{8,10},{9,11},{10,... | collective-permute-start | bytes 159752 | tf_op jit(solution)/shard_map/ppermute | solution.py:484
  53.2 0.8 %collective-permute-start.7 = (f32[104,128]{1,0:T(8,128)S(1)}, f32[104,128]{1,0:T(8,128)S(1)}, u32[]{:S(2)}, u32[]{:S(2)}) collective-permute-start(f32[104,128]{1,0:T(8,128)S(1)} %add.20), channel_id=1, source_target_pairs={{0,1},{1,0},{2,3},{3,2},{4,5},{5,4},{6,7},{7,6},{8,9},{9,8},{10,11... | collective-permute-start | bytes 159752 | tf_op jit(solution)/shard_map/ppermute | solution.py:484
  54.0 0.9 %place.1 = f32[1,8,23040]{2,1,0:T(8,128)} custom-call(bf16[8,5760]{1,0:T(8,128)(2,1)S(1)} %get-tuple-element.30.part0, bf16[8,5760]{1,0:T(8,128)(2,1)S(1)} %collective-permute-done.10.part1, bf16[8,5760]{1,0:T(8,128)(2,1)S(1)} %collective-permute-done.6.part2, bf16[8,5760]{1,0:T(8,128)(2,1)S(1)} %collective-permute-done.4.part3), custom_call_target="tpu_custom_call" | custom-call | tf_op jit(solution)/shard_map/place/pallas_call | solution.py:598
  54.9 0.8 %collective-permute-done.9 = f32[104,128]{1,0:T(8,128)S(1)} collective-permute-done((f32[104,128]{1,0:T(8,128)S(1)}, f32[104,128]{1,0:T(8,128)S(1)}, u32[]{:S(2)}, u32[]{:S(2)}) %collective-permute-start.9) | collective-permute-done | bytes 53280 | tf_op jit(solution)/shard_map/ppermute | solution.py:484
  55.7 1.3 %collective-permute-done.8 = f32[104,128]{1,0:T(8,128)S(1)} collective-permute-done((f32[104,128]{1,0:T(8,128)S(1)}, f32[104,128]{1,0:T(8,128)S(1)}, u32[]{:S(2)}, u32[]{:S(2)}) %collective-permute-start.8) | collective-permute-done | bytes 53280 | tf_op jit(solution)/shard_map/ppermute | solution.py:484
  57.0 0.5 collective-permute-done.7
  57.6 0.1 collective-permute-start.11
  57.7 1.2 %collective-permute-done.11.other = f32[104,128]{1,0:T(8,128)S(1)} collective-permute-done((f32[104,128]{1,0:T(8,128)S(1)}, f32[104,128]{1,0:T(8,128)S(1)}, u32[]{:S(2)}, u32[]{:S(2)}) %collective-permute-start.11) | collective-permute-done | bytes 53280 | tf_op jit(solution)/shard_map/ppermute | solution.py:484
  58.9 0.8 %taps.1 = (f32[3,3,32,64]{3,2,1,0:T(8,128)}, f32[3,3,16,32]{3,2,1,0:T(8,128)}) custom-call(f32[104,128]{1,0:T(8,128)S(1)} %add_add_fusion.mine, f32[104,128]{1,0:T(8,128)S(1)} %collective-permute-done.11.other), custom_call_target="tpu_custom_call" | custom-call | tf_op jit(solution)/shard_map/taps/pallas_call | solution.py:609
  (25 shorter events, 0.1 us)
Async XLA Ops:
  0.6 9.9 %copy-start.3 = (s32[32,48]{1,0:T(8,128)S(1)}, s32[32,48]{1,0:T(8,128)}, u32[]{:S(2)}) copy-start(s32[32,48]{1,0:T(8,128)} %land.3) | copy-start | bytes 18436
  0.6 9.9 %copy-start = (bf16[1,32,23040]{2,1,0:T(8,128)(2,1)S(1)}, bf16[1,32,23040]{2,1,0:T(8,128)(2,1)}, u32[]{:S(2)}) copy-start(bf16[1,32,23040]{2,1,0:T(8,128)(2,1)} %targets.3) | copy-start | bytes 4423684
  0.7 5.8 %copy-start.1 = (bf16[1,8,23040]{2,1,0:T(8,128)(2,1)S(1)}, bf16[1,8,23040]{2,1,0:T(8,128)(2,1)}, u32[]{:S(2)}) copy-start(bf16[1,8,23040]{2,1,0:T(8,128)(2,1)} %latent.3) | copy-start | bytes 1105924
  0.7 5.8 %copy-start.6 = (f32[64]{0:T(128)S(1)}, f32[64]{0:T(128)}, u32[]{:S(2)}) copy-start(f32[64]{0:T(128)} %scale.3) | copy-start | bytes 772
  0.7 5.8 %copy-start.5 = (s32[8]{0:T(128)S(1)}, s32[8]{0:T(128)}, u32[]{:S(2)}) copy-start(s32[8]{0:T(128)} %seeds.3) | copy-start | bytes 100
  0.7 9.9 %copy-start.7 = (f32[16]{0:T(128)S(1)}, f32[16]{0:T(128)}, u32[]{:S(2)}) copy-start(f32[16]{0:T(128)} %channel_weight.1) | copy-start | bytes 196
  2.8 7.8 %collective-permute-start = (bf16[50,8,128]{2,1,0:T(8,128)(2,1)}, bf16[50,8,128]{2,1,0:T(8,128)(2,1)S(1)}, u32[]{:S(2)}, u32[]{:S(2)}) collective-permute-start(bf16[50,8,128]{2,1,0:T(8,128)(2,1)} %get-tuple-element.22), channel_id=1, source_target_pairs={{0,4},{4,8},{8,12},{12,16},{16,20},{20,24},{24,28},{1,5},{5,9},{9,... | collective-permute-start | bytes 307208 | tf_op jit(solution)/shard_map/ppermute | solution.py:24
  5.2 5.4 %collective-permute-start.1 = (bf16[1,6400]{1,0:T(2,128)(2,1)}, bf16[1,6400]{1,0:T(2,128)(2,1)S(1)}, u32[]{:S(2)}, u32[]{:S(2)}) collective-permute-start(bf16[1,6400]{1,0:T(2,128)(2,1)} %get-tuple-element.23), channel_id=1, source_target_pairs={{4,0},{8,4},{12,8},{16,12},{20,16},{24,20},{28,24},{5,1},{9,5},{13... | collective-permute-start | bytes 38408 | tf_op jit(solution)/shard_map/ppermute | solution.py:24
  6.5 0.9 %copy-start.2 = (bf16[3,3,64,32]{2,3,1,0:T(8,128)(2,1)S(1)}, bf16[3,3,64,32]{2,3,1,0:T(8,128)(2,1)}, u32[]{:S(2)}) copy-start(bf16[3,3,64,32]{2,3,1,0:T(8,128)(2,1)} %param.11) | copy-start | bytes 110596
  7.4 0.8 %copy-start.4 = (bf16[3,3,32,16]{2,3,1,0:T(8,128)(2,1)S(1)}, bf16[3,3,32,16]{2,3,1,0:T(8,128)(2,1)}, u32[]{:S(2)}) copy-start(bf16[3,3,32,16]{2,3,1,0:T(8,128)(2,1)} %param.12) | copy-start | bytes 27652
  32.8 6.7 %collective-permute-start.2 = (f32[104,128]{1,0:T(8,128)S(1)}, f32[104,128]{1,0:T(8,128)S(1)}, u32[]{:S(2)}, u32[]{:S(2)}) collective-permute-start(f32[104,128]{1,0:T(8,128)S(1)} %get-tuple-element.29), channel_id=1, source_target_pairs={{0,4},{4,0},{8,12},{12,8},{16,20},{20,16},{24,28},{28,24},{1,5},{5... | collective-permute-start | bytes 159752 | tf_op jit(solution)/shard_map/ppermute | solution.py:484
  35.9 7.8 %collective-permute-start.4 = (bf16[8,5760]{1,0:T(8,128)(2,1)S(1)}, bf16[8,5760]{1,0:T(8,128)(2,1)S(1)}, u32[]{:S(2)}, u32[]{:S(2)}) collective-permute-start(bf16[8,5760]{1,0:T(8,128)(2,1)S(1)} %get-tuple-element.30.part0), channel_id=1, source_target_pairs={{0,3},{1,2},{2,1},{3,0},{4,7},{5,6},{6,5},{7,4},{8,11},{9,10},{10,... | collective-permute-start | bytes 276488 | tf_op jit(solution)/shard_map/ppermute | solution.py:484
  39.5 4.2 %collective-permute-start.3 = (f32[104,128]{1,0:T(8,128)S(1)}, f32[104,128]{1,0:T(8,128)S(1)}, u32[]{:S(2)}, u32[]{:S(2)}) collective-permute-start(f32[104,128]{1,0:T(8,128)S(1)} %add.18), channel_id=1, source_target_pairs={{0,8},{4,12},{8,0},{12,4},{16,24},{20,28},{24,16},{28,20},{1,9},{5... | collective-permute-start | bytes 159752 | tf_op jit(solution)/shard_map/ppermute | solution.py:484
  41.5 8.0 %collective-permute-start.6 = (bf16[8,5760]{1,0:T(8,128)(2,1)S(1)}, bf16[8,5760]{1,0:T(8,128)(2,1)S(1)}, u32[]{:S(2)}, u32[]{:S(2)}) collective-permute-start(bf16[8,5760]{1,0:T(8,128)(2,1)S(1)} %get-tuple-element.30.part0), channel_id=1, source_target_pairs={{0,2},{1,3},{2,0},{3,1},{4,6},{5,7},{6,4},{7,5},{8,10},{9,11},{10,... | collective-permute-start | bytes 276488 | tf_op jit(solution)/shard_map/ppermute | solution.py:484
  43.7 5.8 %collective-permute-start.5 = (f32[104,128]{1,0:T(8,128)S(1)}, f32[104,128]{1,0:T(8,128)S(1)}, u32[]{:S(2)}, u32[]{:S(2)}) collective-permute-start(f32[104,128]{1,0:T(8,128)S(1)} %add.19), channel_id=1, source_target_pairs={{0,16},{4,20},{8,24},{12,28},{16,0},{20,4},{24,8},{28,12},{1,17},{... | collective-permute-start | bytes 159752 | tf_op jit(solution)/shard_map/ppermute | solution.py:484
  46.4 7.6 %collective-permute-start.10 = (bf16[8,5760]{1,0:T(8,128)(2,1)S(1)}, bf16[8,5760]{1,0:T(8,128)(2,1)S(1)}, u32[]{:S(2)}, u32[]{:S(2)}) collective-permute-start(bf16[8,5760]{1,0:T(8,128)(2,1)S(1)} %get-tuple-element.30.part0), channel_id=1, source_target_pairs={{0,1},{1,0},{2,3},{3,2},{4,5},{5,4},{6,7},{7,6},{8,9},{9,8},{10,11... | collective-permute-start | bytes 276488 | tf_op jit(solution)/shard_map/ppermute | solution.py:484
  49.5 6.2 %collective-permute-start.9 = (f32[104,128]{1,0:T(8,128)S(1)}, f32[104,128]{1,0:T(8,128)S(1)}, u32[]{:S(2)}, u32[]{:S(2)}) collective-permute-start(f32[104,128]{1,0:T(8,128)S(1)} %add.20), channel_id=1, source_target_pairs={{0,3},{1,2},{2,1},{3,0},{4,7},{5,6},{6,5},{7,4},{8,11},{9,10},{10,... | collective-permute-start | bytes 159752 | tf_op jit(solution)/shard_map/ppermute | solution.py:484
  51.7 5.3 %collective-permute-start.8 = (f32[104,128]{1,0:T(8,128)S(1)}, f32[104,128]{1,0:T(8,128)S(1)}, u32[]{:S(2)}, u32[]{:S(2)}) collective-permute-start(f32[104,128]{1,0:T(8,128)S(1)} %add.20), channel_id=1, source_target_pairs={{0,2},{1,3},{2,0},{3,1},{4,6},{5,7},{6,4},{7,5},{8,10},{9,11},{10,... | collective-permute-start | bytes 159752 | tf_op jit(solution)/shard_map/ppermute | solution.py:484
  53.2 4.4 %collective-permute-start.7 = (f32[104,128]{1,0:T(8,128)S(1)}, f32[104,128]{1,0:T(8,128)S(1)}, u32[]{:S(2)}, u32[]{:S(2)}) collective-permute-start(f32[104,128]{1,0:T(8,128)S(1)} %add.20), channel_id=1, source_target_pairs={{0,1},{1,0},{2,3},{3,2},{4,5},{5,4},{6,7},{7,6},{8,9},{9,8},{10,11... | collective-permute-start | bytes 159752 | tf_op jit(solution)/shard_map/ppermute | solution.py:484
  57.6 1.3 %collective-permute-start.11 = (f32[104,128]{1,0:T(8,128)S(1)}, f32[104,128]{1,0:T(8,128)S(1)}, u32[]{:S(2)}, u32[]{:S(2)}) collective-permute-start(f32[104,128]{1,0:T(8,128)S(1)} %add_add_fusion.mine), channel_id=1, source_target_pairs={{0,4},{4,0},{8,12},{12,8},{16,20},{20,16},{24,28},{28,24},{1,5},{5... | collective-permute-start | bytes 159752 | tf_op jit(solution)/shard_map/ppermute | solution.py:484

commit v8 on v7

--- a/solution.py
+++ b/solution.py
@@ -85,14 +85,20 @@
                     back_ref[at : at + chan_out, row * LANES : (row + 1) * LANES] = part.astype(jnp.bfloat16)
 
 
+def tap_place(k, first, chan_in, chan_out):
+    cells = LANES // chan_in
+    if k == 8 and first > 0:
+        return 4 * 2 * chan_out, 2 * chan_in
+    return first + k // cells * chan_out, k % cells * chan_in
+
+
 def pack_taps(acc_ref, next_ref, out_ref, first, chan_in, chan_out, norm):
     cells = LANES // chan_in
     group = iota((chan_out, LANES), 1) // chan_in
-    packed = None
     for k in range(9):
         a, b = divmod(k, 3)
         row, sub = ((1, 1), (0, 0), (0, 1))[a]
-        slot = k % cells
+        at, lane = tap_place(k, first, chan_in, chan_out)
         part = None
         for reach in range(cells + 1):
             q = 2 * reach + b - 1
@@ -101,13 +107,13 @@
                 lines = sub * LANES + q * chan_out if block == 0 else sub * chan_out
                 ref = acc_ref if block == 0 else next_ref
                 piece = ref[lines : lines + chan_out, row * LANES : (row + 1) * LANES]
-                turn = (slot - cell) % cells * chan_in
+                turn = (lane - cell * chan_in) % LANES
                 piece = pltpu.roll(piece, turn, 1) if turn else piece
                 part = piece if part is None else part + piece
-        packed = part if slot == 0 else jnp.where(group == slot, part, packed)
-        if slot == cells - 1 or k == 8:
-            at = first + k // cells * chan_out
-            out_ref[at : at + chan_out, :] = packed * norm
+        part = part * norm
+        if lane:
+            part = jnp.where(group == lane // chan_in, part, out_ref[at : at + chan_out, :])
+        out_ref[at : at + chan_out, :] = part
 
 
 def spread_line(ref, slot, at):
@@ -157,22 +163,16 @@
         latent_grad[0, :, pl.ds(off, own * LANES)] = part[...].astype(jnp.float32)
 
 
-def taps_kernel(mine, other, grad_one, grad_two, taps):
-    count = mine.shape[0]
-    odd = jnp.bitwise_and(lax.axis_index("lat"), 1)
-    taps[pl.ds(pl.multiple_of(odd * count, 8), count), :] = mine[...]
-    taps[pl.ds(pl.multiple_of((1 - odd) * count, 8), count), :] = other[...]
+def taps_kernel(taps, grad_one, grad_two):
     first = 0
     for out in (grad_one, grad_two):
         chan_out, chan_in = out.shape[2], out.shape[3]
-        cells = LANES // chan_in
         for k in range(9):
-            at = first + k // cells * chan_out
+            at, lane = tap_place(k, first, chan_in, chan_out)
             block = taps[at : at + chan_out, :]
-            turn = (-(k % cells)) % cells * chan_in
-            block = pltpu.roll(block, turn, 1) if turn else block
+            block = pltpu.roll(block, LANES - lane, 1) if lane else block
             out[k // 3, k % 3] = block[:, :chan_in]
-        first += -(-9 // cells) * chan_out
+        first += 5 * chan_out
 
 
 def make_source(i, row, total_rows, span, own, half, seeds, scale, chan, line, store):
@@ -246,8 +246,7 @@
     back_one,
     back_two,
     out_lat,
-    taps_keep,
-    taps_send,
+    taps,
     lat_rows,
     tgt_rows,
     weight_rows,
@@ -264,7 +263,6 @@
     carry,
     carry_lat,
     lat_lines,
-    taps,
     acc_one,
     acc_one_next,
     acc_two,
@@ -473,20 +471,11 @@
     for t in range(own):
         out_lat[:, t * LANES : (t + 1) * LANES] = lat_lines[t * rows : (t + 1) * rows].astype(bf16)
     pack_taps(acc_one, acc_one_next, taps, 0, chan0, chan1, norm)
-    pack_taps(acc_two, acc_two_next, taps, -(-9 // (LANES // chan0)) * chan1, chan1, chan2, norm)
-    count = taps_keep.shape[0]
-    odd = jnp.bitwise_and(lat_pos, 1)
-    taps_keep[...] = taps[pl.ds(pl.multiple_of(odd * count, 8), count), :]
-    taps_send[...] = taps[pl.ds(pl.multiple_of((1 - odd) * count, 8), count), :]
+    pack_taps(acc_two, acc_two_next, taps, 5 * chan1, chan1, chan2, norm)
 
 
 def swapped(array, axis, bit):
     return lax.ppermute(array, axis, [(i, i ^ bit) for i in range(lax.axis_size(axis))])
-
-
-def total(array, axis, first, second):
-    one, two, three = (swapped(array, axis, k) for k in (first, second, first ^ second))
-    return (array + one) + (two + three)
 
 
 def local(
@@ -541,15 +530,14 @@
         name="prepare",
     )(member_seeds, noise_scale, latent, kernel_one, kernel_two)
     norm = 1.0 / math.sqrt(sample_count * 4 * rows * lat_count * targets.shape[2])
-    tap_rows = 5 * chan1 + 3 * chan2
-    lat_grad, taps, taps_send = pl.pallas_call(
+    tap_rows = 5 * chan1 + 2 * chan2
+    lat_grad, taps = pl.pallas_call(
         functools.partial(band_kernel, half, (chan0, chan1, chan2), norm),
         in_specs=[smem] * 3 + [vmem] * 9,
-        out_specs=[vmem] * 3,
+        out_specs=[vmem] * 2,
         out_shape=[
             jax.ShapeDtypeStruct((rows, own * LANES), bf16),
-            jax.ShapeDtypeStruct((tap_rows // 2, LANES), f32),
-            jax.ShapeDtypeStruct((tap_rows // 2, LANES), f32),
+            jax.ShapeDtypeStruct((tap_rows, LANES), f32),
         ],
         scratch_shapes=[
             pltpu.VMEM((2 * wide, 8, LANES), f32),
@@ -568,7 +556,6 @@
             pltpu.VMEM((front * 16, LANES), f32),
             pltpu.VMEM((48, LANES), f32),
             pltpu.VMEM((48 * rows, LANES), f32),
-            pltpu.VMEM((tap_rows, LANES), f32),
             pltpu.VMEM((256, 256), f32),
             pltpu.VMEM((2 * chan1, 256), f32),
             pltpu.VMEM((256, 256), f32),
@@ -588,13 +575,12 @@
         *bands,
     )
     one, two, three = (swapped(lat_grad, "mem", k) for k in range(1, 4))
-    taps = taps + swapped(taps_send, "lat", 1)
-    bits = [1 << k for k in range(1, lat_count.bit_length() - 1)]
-    for bit in bits:
-        if bit == bits[-1]:
-            taps, three = lax.optimization_barrier((taps, three))
-        taps = taps + swapped(taps, "lat", bit)
-    taps, two = lax.optimization_barrier((taps, two))
+    taps = taps.reshape(lat_count, tap_rows // lat_count, LANES)
+    share = jnp.sum(lax.all_to_all(taps, "lat", 0, 0, tiled=True), axis=0)
+    share = jnp.broadcast_to(share, (lax.axis_size("mem"),) + share.shape)
+    share = jnp.sum(lax.all_to_all(share, "mem", 0, 0, tiled=True), axis=0)
+    share = jnp.broadcast_to(share, (lat_count,) + share.shape)
+    taps = lax.all_to_all(share, "lat", 0, 0, tiled=True).reshape(tap_rows, LANES)
     latent_grad = pl.pallas_call(
         functools.partial(place_kernel, own),
         in_specs=[vmem] * 4,
@@ -603,21 +589,17 @@
         compiler_params=small,
         name="place",
     )(lat_grad, one, two, three)
-    taps = total(taps, "mem", 1, 2)
-    taps, latent_grad = lax.optimization_barrier((taps, latent_grad))
-    other = swapped(taps, "lat", 1)
     one, two = pl.pallas_call(
         taps_kernel,
-        in_specs=[vmem] * 2,
+        in_specs=[vmem],
         out_specs=[vmem] * 2,
         out_shape=[
             jax.ShapeDtypeStruct(kernel_one.shape, f32),
             jax.ShapeDtypeStruct(kernel_two.shape, f32),
         ],
-        scratch_shapes=[pltpu.VMEM((tap_rows, LANES), f32)],
         compiler_params=small,
         name="taps",
-    )(taps, other)
+    )(taps)
     return (latent_grad, one.transpose(0, 1, 3, 2), two.transpose(0, 1, 3, 2))
 
 

time: 59.9 us -> 68.9 us (1.15)
  blocking collectives: 0 us -> 11.8 us
  starting transfers between devices: 22.6 us -> 16.3 us
  waiting for transfers between devices: 6.33 us -> 8.34 us
  local copies, waits for them, and re-layouts: 1.67 us -> 2.95 us
    ppermute x10 -> x3, starting transfers between devices: 19 us -> 4.42 us  [swapped(): lax.ppermute(array, axis, [(i, i ^ bit) for i in range(lax.axis_size(axis...]
    all_to_all x0 -> x1, blocking collectives: none -> 11.8 us  [local(): share = jnp.sum(lax.all_to_all(taps, 'lat', 0, 0, tiled=True), axis=0)]
    all_to_all x0 -> x2, starting transfers between devices: none -> 8.23 us  [the longest x1 4.87 us: local(): share = jnp.sum(lax.all_to_all(share, 'mem', 0, 0, tiled=True), axis=0)]
    all_to_all x0 -> x2, waiting for transfers between devices: none -> 8.06 us  [the longest x1 4.17 us: local(): lax.all_to_all(share, 'lat', 0, 0, tiled=True).reshape(tap_rows, LANES)]
    ppermute x10 -> x3, waiting for transfers between devices: 6.05 us -> 0.01 us  [swapped(): lax.ppermute(array, axis, [(i, i ^ bit) for i in range(lax.axis_size(axis...]
    broadcast_in_dim x0 -> x2, local copies, waits for them, and re-layouts: none -> 1.27 us  [the longest x1 0.65 us: local(): share = jnp.broadcast_to(share, (lat_count,) + share.shape)]
  transfers between devices with their start and end apart: 12 -> 7, of which waited for: 6 -> 3; matrix products, arithmetic and copies ran while one was open for 0% -> 1% of each run, Pallas kernels for 5% -> 4%
where the time goes in v8:
time: 68.9 us; the launch traced here: 68.4 us
  Pallas kernels  28.2 us (41%)
  starting transfers between devices  16.3 us (24%)
  blocking collectives  11.8 us (17%)
  waiting for transfers between devices  8.34 us (12%)
  local copies, waits for them, and re-layouts  2.95 us (4%)
  between operations  0.8 us (1%)
    pallas_call x1, Pallas kernels, local(): pl.pallas_call(functools.partial(band_kernel, half, (chan0, chan1, chan2)...  22.3 us
    all_to_all x1, blocking collectives, local(): share = jnp.sum(lax.all_to_all(taps, 'lat', 0, 0, tiled=True), axis=0)  11.8 us
    all_to_all x1, starting transfers between devices, local(): share = jnp.sum(lax.all_to_all(share, 'mem', 0, 0, tiled=True), axis=0)  4.87 us
    ppermute x3, starting transfers between devices, swapped(): lax.ppermute(array, axis, [(i, i ^ bit) for i in range(lax.axis_size(axis...  4.42 us
    all_to_all x1, waiting for transfers between devices, local(): lax.all_to_all(share, 'lat', 0, 0, tiled=True).reshape(tap_rows, LANES)  4.17 us
    all_to_all x1, waiting for transfers between devices, local(): share = jnp.sum(lax.all_to_all(share, 'mem', 0, 0, tiled=True), axis=0)  3.89 us
    ppermute x2, starting transfers between devices, shifted(): return lax.ppermute(array, axis, pairs)  3.64 us
    all_to_all x1, starting transfers between devices, local(): lax.all_to_all(share, 'lat', 0, 0, tiled=True).reshape(tap_rows, LANES)  3.36 us
  transfers between devices with their start and end apart: 7, of which 3 were waited for; matrix products, arithmetic and copies ran while one was open for 1% of the time, Pallas kernels for 4%

profile of v8, /device:TPU:0, one launch (start us, length us, event | category | flops | bytes accessed | tf_op | source)
XLA Modules:
  0.0 68.4 jit_solution(1353962969777544935)
XLA Ops:
  0.7 2.1 %edges.1 = (bf16[50,8,128]{2,1,0:T(8,128)(2,1)}, bf16[1,6400]{1,0:T(2,128)(2,1)}) custom-call(bf16[1,8,23040]{2,1,0:T(8,128)(2,1)} %latent.3, bf16[1,32,23040]{2,1,0:T(8,128)(2,1)} %targets.3, s32[32,48]{1,0:T(8,128)} %land.3), custom_call_target="tpu_custom_call" | custom-call | tf_op jit(solution)/shard_map/edges/pallas_call | solution.py:499
  2.8 2.4 %collective-permute-start = (bf16[50,8,128]{2,1,0:T(8,128)(2,1)}, bf16[50,8,128]{2,1,0:T(8,128)(2,1)S(1)}, u32[]{:S(2)}, u32[]{:S(2)}) collective-permute-start(bf16[50,8,128]{2,1,0:T(8,128)(2,1)} %get-tuple-element.15), channel_id=1, source_target_pairs={{0,4},{4,8},{8,12},{12,16},{16,20},{20,24},{24,28},{1,5},{5,9},{9,... | collective-permute-start | bytes 307208 | tf_op jit(solution)/shard_map/ppermute | solution.py:24
  5.2 1.3 %collective-permute-start.1 = (bf16[1,6400]{1,0:T(2,128)(2,1)}, bf16[1,6400]{1,0:T(2,128)(2,1)S(1)}, u32[]{:S(2)}, u32[]{:S(2)}) collective-permute-start(bf16[1,6400]{1,0:T(2,128)(2,1)} %get-tuple-element.16), channel_id=1, source_target_pairs={{4,0},{8,4},{12,8},{16,12},{20,16},{24,20},{28,24},{5,1},{9,5},{13... | collective-permute-start | bytes 38408 | tf_op jit(solution)/shard_map/ppermute | solution.py:24
  6.5 0.0 copy-start.2
  6.5 0.9 %copy-done.2 = bf16[3,3,64,32]{2,3,1,0:T(8,128)(2,1)S(1)} copy-done((bf16[3,3,64,32]{2,3,1,0:T(8,128)(2,1)S(1)}, bf16[3,3,64,32]{2,3,1,0:T(8,128)(2,1)}, u32[]{:S(2)}) %copy-start.2) | copy-done | bytes 36888
  7.4 0.8 %copy-done.4 = bf16[3,3,32,16]{2,3,1,0:T(8,128)(2,1)S(1)} copy-done((bf16[3,3,32,16]{2,3,1,0:T(8,128)(2,1)S(1)}, bf16[3,3,32,16]{2,3,1,0:T(8,128)(2,1)}, u32[]{:S(2)}) %copy-start.4) | copy-done | bytes 9240
  8.1 2.1 %prepare.1 = (bf16[8,25,16,128]{3,2,1,0:T(8,128)(2,1)S(1)}, bf16[512,256]{1,0:T(8,128)(2,1)S(1)}, bf16[512,256]{1,0:T(8,128)(2,1)S(1)}, bf16[512,256]{1,0:T(8,128)(2,1)S(1)}, bf16[512,256]{1,0:T(8,128)(2,1)S(1)}) custom-call(s32[8]{0:T(128)S(1)} %copy-done.5, f32[64]{0:T(128)S(1)} %copy-done.6, bf16[1,8,23040]{2,1,0:T(8,128)(2,1)S(1)} %copy-done.1, ...), custom_call_target="tpu_custom_call" | custom-call | flops 100000000 | bytes 10000000 | tf_op jit(solution)/shard_map/prepare/pallas_call | solution.py:522
  10.3 0.3 collective-permute-done.1.below
  10.6 0.0 collective-permute-done.above
  10.6 22.3 %band.1 = (bf16[8,5760]{1,0:T(8,128)(2,1)S(1)}, f32[192,128]{1,0:T(8,128)S(1)}) custom-call(s32[8]{0:T(128)S(1)} %copy-done.5, f32[64]{0:T(128)S(1)} %copy-done.6, f32[16]{0:T(128)S(1)} %copy-done.7, bf16[8,25,16,128]{3,2,1,0:T(8,128)(2,1)S(1)} %get-tuple-element.14.own_source, bf16[50,8,128]{2,1,0:T(8,128)(2,1)S(1)} %collective-permute-done.above, ...), custom_call_target="tpu_custom_call" | custom-call | tf_op jit(solution)/shard_map/band/pallas_call | solution.py:534
  32.8 11.8 %all_to_all.15 = f32[8,24,128]{2,1,0:T(8,128)S(1)} all-to-all(f32[8,24,128]{2,1,0:T(8,128)S(1)} %bitcast.7), channel_id=1, replica_groups=mesh['lat'=8,'mem'=4] {'lat'}, dimensions={0} | all-to-all | bytes 196608 | tf_op jit(solution)/shard_map/all_to_all | solution.py:579
  44.7 0.6 broadcast_in_dim.6
  45.3 4.9 %all-to-all-start.1 = ((f32[4,24,128]{2,1,0:T(8,128)}), f32[4,24,128]{2,1,0:T(8,128)S(1)}, u32[]{:S(2)}, u32[]{:S(2)}) async-start(f32[4,24,128]{2,1,0:T(8,128)} %broadcast_in_dim.6), calls=%async_computation.1 | async-start | bytes 98304 | tf_op jit(solution)/shard_map/all_to_all | solution.py:581
  50.2 3.8 %collective-permute-start.4 = (bf16[8,5760]{1,0:T(8,128)(2,1)S(1)}, bf16[8,5760]{1,0:T(8,128)(2,1)S(1)}, u32[]{:S(2)}, u32[]{:S(2)}) collective-permute-start(bf16[8,5760]{1,0:T(8,128)(2,1)S(1)} %get-tuple-element.21.part0), channel_id=1, source_target_pairs={{0,3},{1,2},{2,1},{3,0},{4,7},{5,6},{6,5},{7,4},{8,11},{9,10},{10,... | collective-permute-start | bytes 276488 | tf_op jit(solution)/shard_map/ppermute | solution.py:478
  54.0 0.0 collective-permute-start.3
  54.0 0.6 collective-permute-start.2
  54.6 3.9 %all-to-all-done.1 = f32[4,24,128]{2,1,0:T(8,128)S(1)} async-done(((f32[4,24,128]{2,1,0:T(8,128)}), f32[4,24,128]{2,1,0:T(8,128)S(1)}, u32[]{:S(2)}, u32[]{:S(2)}) %all-to-all-start.1) | async-done | bytes 49184 | tf_op jit(solution)/shard_map/all_to_all | solution.py:581
  58.5 0.7 broadcast_in_dim.7
  59.1 3.4 %all-to-all-start.2 = ((f32[8,24,128]{2,1,0:T(8,128)}), f32[8,24,128]{2,1,0:T(8,128)S(1)}, u32[]{:S(2)}, u32[]{:S(2)}) async-start(f32[8,24,128]{2,1,0:T(8,128)} %broadcast_in_dim.7), calls=%async_computation.2 | async-start | bytes 196608 | tf_op jit(solution)/shard_map/all_to_all | solution.py:583
  62.5 0.0 collective-permute-done.3.part2
  62.5 0.0 collective-permute-done.2.part1
  62.5 0.9 %place.1 = f32[1,8,23040]{2,1,0:T(8,128)} custom-call(bf16[8,5760]{1,0:T(8,128)(2,1)S(1)} %get-tuple-element.21.part0, bf16[8,5760]{1,0:T(8,128)(2,1)S(1)} %collective-permute-done.2.part1, bf16[8,5760]{1,0:T(8,128)(2,1)S(1)} %collective-permute-done.3.part2, bf16[8,5760]{1,0:T(8,128)(2,1)S(1)} %collective-permute-done.4.part3), custom_call_target="tpu_custom_call" | custom-call | tf_op jit(solution)/shard_map/place/pallas_call | solution.py:584
  63.5 4.2 %all-to-all-done.2 = f32[8,24,128]{2,1,0:T(8,128)S(1)} async-done(((f32[8,24,128]{2,1,0:T(8,128)}), f32[8,24,128]{2,1,0:T(8,128)S(1)}, u32[]{:S(2)}, u32[]{:S(2)}) %all-to-all-start.2) | async-done | bytes 98336 | tf_op jit(solution)/shard_map/all_to_all | solution.py:583
  67.6 0.8 %taps.1 = (f32[3,3,32,64]{3,2,1,0:T(8,128)}, f32[3,3,16,32]{3,2,1,0:T(8,128)}) custom-call(f32[192,128]{1,0:T(8,128)S(1)} %bitcast.6), custom_call_target="tpu_custom_call" | custom-call | tf_op jit(solution)/shard_map/taps/pallas_call | solution.py:592
  (16 shorter events, 0.0 us)
Async XLA Ops:
  0.6 9.9 %copy-start.3 = (s32[32,48]{1,0:T(8,128)S(1)}, s32[32,48]{1,0:T(8,128)}, u32[]{:S(2)}) copy-start(s32[32,48]{1,0:T(8,128)} %land.3) | copy-start | bytes 18436
  0.6 9.9 %copy-start = (bf16[1,32,23040]{2,1,0:T(8,128)(2,1)S(1)}, bf16[1,32,23040]{2,1,0:T(8,128)(2,1)}, u32[]{:S(2)}) copy-start(bf16[1,32,23040]{2,1,0:T(8,128)(2,1)} %targets.3) | copy-start | bytes 4423684
  0.7 5.8 %copy-start.1 = (bf16[1,8,23040]{2,1,0:T(8,128)(2,1)S(1)}, bf16[1,8,23040]{2,1,0:T(8,128)(2,1)}, u32[]{:S(2)}) copy-start(bf16[1,8,23040]{2,1,0:T(8,128)(2,1)} %latent.3) | copy-start | bytes 1105924
  0.7 5.8 %copy-start.6 = (f32[64]{0:T(128)S(1)}, f32[64]{0:T(128)}, u32[]{:S(2)}) copy-start(f32[64]{0:T(128)} %scale.3) | copy-start | bytes 772
  0.7 5.8 %copy-start.5 = (s32[8]{0:T(128)S(1)}, s32[8]{0:T(128)}, u32[]{:S(2)}) copy-start(s32[8]{0:T(128)} %seeds.3) | copy-start | bytes 100
  0.7 9.9 %copy-start.7 = (f32[16]{0:T(128)S(1)}, f32[16]{0:T(128)}, u32[]{:S(2)}) copy-start(f32[16]{0:T(128)} %channel_weight.1) | copy-start | bytes 196
  2.8 7.8 %collective-permute-start = (bf16[50,8,128]{2,1,0:T(8,128)(2,1)}, bf16[50,8,128]{2,1,0:T(8,128)(2,1)S(1)}, u32[]{:S(2)}, u32[]{:S(2)}) collective-permute-start(bf16[50,8,128]{2,1,0:T(8,128)(2,1)} %get-tuple-element.15), channel_id=1, source_target_pairs={{0,4},{4,8},{8,12},{12,16},{16,20},{20,24},{24,28},{1,5},{5,9},{9,... | collective-permute-start | bytes 307208 | tf_op jit(solution)/shard_map/ppermute | solution.py:24
  5.2 5.4 %collective-permute-start.1 = (bf16[1,6400]{1,0:T(2,128)(2,1)}, bf16[1,6400]{1,0:T(2,128)(2,1)S(1)}, u32[]{:S(2)}, u32[]{:S(2)}) collective-permute-start(bf16[1,6400]{1,0:T(2,128)(2,1)} %get-tuple-element.16), channel_id=1, source_target_pairs={{4,0},{8,4},{12,8},{16,12},{20,16},{24,20},{28,24},{5,1},{9,5},{13... | collective-permute-start | bytes 38408 | tf_op jit(solution)/shard_map/ppermute | solution.py:24
  6.5 0.9 %copy-start.2 = (bf16[3,3,64,32]{2,3,1,0:T(8,128)(2,1)S(1)}, bf16[3,3,64,32]{2,3,1,0:T(8,128)(2,1)}, u32[]{:S(2)}) copy-start(bf16[3,3,64,32]{2,3,1,0:T(8,128)(2,1)} %param.11) | copy-start | bytes 110596
  7.4 0.8 %copy-start.4 = (bf16[3,3,32,16]{2,3,1,0:T(8,128)(2,1)S(1)}, bf16[3,3,32,16]{2,3,1,0:T(8,128)(2,1)}, u32[]{:S(2)}) copy-start(bf16[3,3,32,16]{2,3,1,0:T(8,128)(2,1)} %param.12) | copy-start | bytes 27652
  45.3 13.2 %all-to-all-start.1 = ((f32[4,24,128]{2,1,0:T(8,128)}), f32[4,24,128]{2,1,0:T(8,128)S(1)}, u32[]{:S(2)}, u32[]{:S(2)}) async-start(f32[4,24,128]{2,1,0:T(8,128)} %broadcast_in_dim.6), calls=%async_computation.1 | async-start | bytes 98304 | tf_op jit(solution)/shard_map/all_to_all | solution.py:581
  50.2 12.3 %collective-permute-start.4 = (bf16[8,5760]{1,0:T(8,128)(2,1)S(1)}, bf16[8,5760]{1,0:T(8,128)(2,1)S(1)}, u32[]{:S(2)}, u32[]{:S(2)}) collective-permute-start(bf16[8,5760]{1,0:T(8,128)(2,1)S(1)} %get-tuple-element.21.part0), channel_id=1, source_target_pairs={{0,3},{1,2},{2,1},{3,0},{4,7},{5,6},{6,5},{7,4},{8,11},{9,10},{10,... | collective-permute-start | bytes 276488 | tf_op jit(solution)/shard_map/ppermute | solution.py:478
  54.0 8.5 %collective-permute-start.3 = (bf16[8,5760]{1,0:T(8,128)(2,1)S(1)}, bf16[8,5760]{1,0:T(8,128)(2,1)S(1)}, u32[]{:S(2)}, u32[]{:S(2)}) collective-permute-start(bf16[8,5760]{1,0:T(8,128)(2,1)S(1)} %get-tuple-element.21.part0), channel_id=1, source_target_pairs={{0,2},{1,3},{2,0},{3,1},{4,6},{5,7},{6,4},{7,5},{8,10},{9,11},{10,... | collective-permute-start | bytes 276488 | tf_op jit(solution)/shard_map/ppermute | solution.py:478
  54.0 8.5 %collective-permute-start.2 = (bf16[8,5760]{1,0:T(8,128)(2,1)S(1)}, bf16[8,5760]{1,0:T(8,128)(2,1)S(1)}, u32[]{:S(2)}, u32[]{:S(2)}) collective-permute-start(bf16[8,5760]{1,0:T(8,128)(2,1)S(1)} %get-tuple-element.21.part0), channel_id=1, source_target_pairs={{0,1},{1,0},{2,3},{3,2},{4,5},{5,4},{6,7},{7,6},{8,9},{9,8},{10,11... | collective-permute-start | bytes 276488 | tf_op jit(solution)/shard_map/ppermute | solution.py:478
  59.1 8.5 %all-to-all-start.2 = ((f32[8,24,128]{2,1,0:T(8,128)}), f32[8,24,128]{2,1,0:T(8,128)S(1)}, u32[]{:S(2)}, u32[]{:S(2)}) async-start(f32[8,24,128]{2,1,0:T(8,128)} %broadcast_in_dim.7), calls=%async_computation.2 | async-start | bytes 196608 | tf_op jit(solution)/shard_map/all_to_all | solution.py:583

commit v9 on v7

--- a/solution.py
+++ b/solution.py
@@ -111,7 +111,7 @@
 
 
 def spread_line(ref, slot, at):
-    return ref[slot, pl.ds(at, 8, stride=0), :]
+    return jnp.broadcast_to(ref[slot, pl.ds(at, 1), :], (8, LANES))
 
 
 def window_block(mem_pos, own, half, blocks, part, t):
@@ -587,14 +587,17 @@
         land_words,
         *bands,
     )
+    taps = taps + swapped(taps_send, "lat", 1)
+    taps = total(taps, "mem", 1, 2)
     one, two, three = (swapped(lat_grad, "mem", k) for k in range(1, 4))
-    taps = taps + swapped(taps_send, "lat", 1)
     bits = [1 << k for k in range(1, lat_count.bit_length() - 1)]
+    taps, one = lax.optimization_barrier((taps, one))
     for bit in bits:
         if bit == bits[-1]:
             taps, three = lax.optimization_barrier((taps, three))
         taps = taps + swapped(taps, "lat", bit)
     taps, two = lax.optimization_barrier((taps, two))
+    other = swapped(taps, "lat", 1)
     latent_grad = pl.pallas_call(
         functools.partial(place_kernel, own),
         in_specs=[vmem] * 4,
@@ -603,9 +606,6 @@
         compiler_params=small,
         name="place",
     )(lat_grad, one, two, three)
-    taps = total(taps, "mem", 1, 2)
-    taps, latent_grad = lax.optimization_barrier((taps, latent_grad))
-    other = swapped(taps, "lat", 1)
     one, two = pl.pallas_call(
         taps_kernel,
         in_specs=[vmem] * 2,

time: 59.9 us -> 61.6 us (1.028)
  waiting for transfers between devices: 6.33 us -> 9.93 us
  starting transfers between devices: 22.6 us -> 20.7 us
    ppermute x10, waiting for transfers between devices: 6.05 us -> 9.66 us  [swapped(): lax.ppermute(array, axis, [(i, i ^ bit) for i in range(lax.axis_size(axis...]
    ppermute x10, starting transfers between devices: 19 us -> 17 us  [swapped(): lax.ppermute(array, axis, [(i, i ^ bit) for i in range(lax.axis_size(axis...]
  transfers between devices with their start and end apart: 12 -> 12, of which waited for: 6 -> 7; matrix products, arithmetic and copies ran while one was open for 0% -> 0% of each run, Pallas kernels for 5% -> 5%
where the time goes in v9:
time: 61.6 us; the launch traced here: 61.3 us
  Pallas kernels  28.2 us (46%)
  starting transfers between devices  20.7 us (34%)
  waiting for transfers between devices  9.93 us (16%)
  local copies, waits for them, and re-layouts  1.67 us (3%)
  between operations  0.79 us (1%)
    pallas_call x1, Pallas kernels, local(): pl.pallas_call(functools.partial(band_kernel, half, (chan0, chan1, chan2)...  22.2 us
    ppermute x10, starting transfers between devices, swapped(): lax.ppermute(array, axis, [(i, i ^ bit) for i in range(lax.axis_size(axis...  17 us
    ppermute x10, waiting for transfers between devices, swapped(): lax.ppermute(array, axis, [(i, i ^ bit) for i in range(lax.axis_size(axis...  9.66 us
    ppermute x2, starting transfers between devices, shifted(): return lax.ppermute(array, axis, pairs)  3.64 us
    pallas_call x1, Pallas kernels, local(): pl.pallas_call(functools.partial(prepare_kernel, half), in_specs=[smem] *...  2.14 us
    pallas_call x1, Pallas kernels, local(): pl.pallas_call(functools.partial(edge_kernel, half, chan2), grid=(1,), in...  2.1 us
    unnamed x16, local copies, waits for them, and re-layouts  1.67 us
  transfers between devices with their start and end apart: 12, of which 7 were waited for; matrix products, arithmetic and copies ran while one was open for 0% of the time, Pallas kernels for 5%

profile of v9, /device:TPU:0, one launch (start us, length us, event | category | flops | bytes accessed | tf_op | source)
XLA Modules:
  0.0 61.3 jit_solution(8339357635857721180)
XLA Ops:
  0.7 2.1 %edges.1 = (bf16[50,8,128]{2,1,0:T(8,128)(2,1)}, bf16[1,6400]{1,0:T(2,128)(2,1)}) custom-call(bf16[1,8,23040]{2,1,0:T(8,128)(2,1)} %latent.3, bf16[1,32,23040]{2,1,0:T(8,128)(2,1)} %targets.3, s32[32,48]{1,0:T(8,128)} %land.3), custom_call_target="tpu_custom_call" | custom-call | tf_op jit(solution)/shard_map/edges/pallas_call | solution.py:510
  2.8 2.4 %collective-permute-start = (bf16[50,8,128]{2,1,0:T(8,128)(2,1)}, bf16[50,8,128]{2,1,0:T(8,128)(2,1)S(1)}, u32[]{:S(2)}, u32[]{:S(2)}) collective-permute-start(bf16[50,8,128]{2,1,0:T(8,128)(2,1)} %get-tuple-element.22), channel_id=1, source_target_pairs={{0,4},{4,8},{8,12},{12,16},{16,20},{20,24},{24,28},{1,5},{5,9},{9,... | collective-permute-start | bytes 307208 | tf_op jit(solution)/shard_map/ppermute | solution.py:24
  5.2 1.3 %collective-permute-start.1 = (bf16[1,6400]{1,0:T(2,128)(2,1)}, bf16[1,6400]{1,0:T(2,128)(2,1)S(1)}, u32[]{:S(2)}, u32[]{:S(2)}) collective-permute-start(bf16[1,6400]{1,0:T(2,128)(2,1)} %get-tuple-element.23), channel_id=1, source_target_pairs={{4,0},{8,4},{12,8},{16,12},{20,16},{24,20},{28,24},{5,1},{9,5},{13... | collective-permute-start | bytes 38408 | tf_op jit(solution)/shard_map/ppermute | solution.py:24
  6.5 0.9 %copy-done.2 = bf16[3,3,64,32]{2,3,1,0:T(8,128)(2,1)S(1)} copy-done((bf16[3,3,64,32]{2,3,1,0:T(8,128)(2,1)S(1)}, bf16[3,3,64,32]{2,3,1,0:T(8,128)(2,1)}, u32[]{:S(2)}) %copy-start.2) | copy-done | bytes 36888
  7.4 0.8 %copy-done.4 = bf16[3,3,32,16]{2,3,1,0:T(8,128)(2,1)S(1)} copy-done((bf16[3,3,32,16]{2,3,1,0:T(8,128)(2,1)S(1)}, bf16[3,3,32,16]{2,3,1,0:T(8,128)(2,1)}, u32[]{:S(2)}) %copy-start.4) | copy-done | bytes 9240
  8.1 2.1 %prepare.1 = (bf16[8,25,16,128]{3,2,1,0:T(8,128)(2,1)S(1)}, bf16[512,256]{1,0:T(8,128)(2,1)S(1)}, bf16[512,256]{1,0:T(8,128)(2,1)S(1)}, bf16[512,256]{1,0:T(8,128)(2,1)S(1)}, bf16[512,256]{1,0:T(8,128)(2,1)S(1)}) custom-call(s32[8]{0:T(128)S(1)} %copy-done.5, f32[64]{0:T(128)S(1)} %copy-done.6, bf16[1,8,23040]{2,1,0:T(8,128)(2,1)S(1)} %copy-done.1, ...), custom_call_target="tpu_custom_call" | custom-call | flops 100000000 | bytes 10000000 | tf_op jit(solution)/shard_map/prepare/pallas_call | solution.py:533
  10.3 0.3 collective-permute-done.1.below
  10.6 22.2 %band.1 = (bf16[8,5760]{1,0:T(8,128)(2,1)S(1)}, f32[104,128]{1,0:T(8,128)S(1)}, f32[104,128]{1,0:T(8,128)S(1)}) custom-call(s32[8]{0:T(128)S(1)} %copy-done.5, f32[64]{0:T(128)S(1)} %copy-done.6, f32[16]{0:T(128)S(1)} %copy-done.7, bf16[8,25,16,128]{3,2,1,0:T(8,128)(2,1)S(1)} %get-tuple-element.21.own_source, ...), custom_call_target="tpu_custom_call" | custom-call | tf_op jit(solution)/shard_map/band/pallas_call | solution.py:545
  32.8 3.1 %collective-permute-start.2 = (f32[104,128]{1,0:T(8,128)S(1)}, f32[104,128]{1,0:T(8,128)S(1)}, u32[]{:S(2)}, u32[]{:S(2)}) collective-permute-start(f32[104,128]{1,0:T(8,128)S(1)} %get-tuple-element.30), channel_id=1, source_target_pairs={{0,4},{4,0},{8,12},{12,8},{16,20},{20,16},{24,28},{28,24},{1,5},{5... | collective-permute-start | bytes 159752 | tf_op jit(solution)/shard_map/ppermute | solution.py:484
  35.9 0.9 %collective-permute-done.2 = f32[104,128]{1,0:T(8,128)S(1)} collective-permute-done((f32[104,128]{1,0:T(8,128)S(1)}, f32[104,128]{1,0:T(8,128)S(1)}, u32[]{:S(2)}, u32[]{:S(2)}) %collective-permute-start.2) | collective-permute-done | bytes 53280 | tf_op jit(solution)/shard_map/ppermute | solution.py:484
  36.8 3.6 %collective-permute-start.5 = (f32[104,128]{1,0:T(8,128)S(1)}, f32[104,128]{1,0:T(8,128)S(1)}, u32[]{:S(2)}, u32[]{:S(2)}) collective-permute-start(f32[104,128]{1,0:T(8,128)S(1)} %add.18), channel_id=1, source_target_pairs={{0,3},{1,2},{2,1},{3,0},{4,7},{5,6},{6,5},{7,4},{8,11},{9,10},{10,... | collective-permute-start | bytes 159752 | tf_op jit(solution)/shard_map/ppermute | solution.py:484
  40.4 0.8 %collective-permute-start.3 = (f32[104,128]{1,0:T(8,128)S(1)}, f32[104,128]{1,0:T(8,128)S(1)}, u32[]{:S(2)}, u32[]{:S(2)}) collective-permute-start(f32[104,128]{1,0:T(8,128)S(1)} %add.18), channel_id=1, source_target_pairs={{0,1},{1,0},{2,3},{3,2},{4,5},{5,4},{6,7},{7,6},{8,9},{9,8},{10,11... | collective-permute-start | bytes 159752 | tf_op jit(solution)/shard_map/ppermute | solution.py:484
  41.2 3.6 %collective-permute-start.8 = (bf16[8,5760]{1,0:T(8,128)(2,1)S(1)}, bf16[8,5760]{1,0:T(8,128)(2,1)S(1)}, u32[]{:S(2)}, u32[]{:S(2)}) collective-permute-start(bf16[8,5760]{1,0:T(8,128)(2,1)S(1)} %get-tuple-element.28.part0), channel_id=1, source_target_pairs={{0,3},{1,2},{2,1},{3,0},{4,7},{5,6},{6,5},{7,4},{8,11},{9,10},{10,... | collective-permute-start | bytes 276488 | tf_op jit(solution)/shard_map/ppermute | solution.py:484
  44.8 1.9 %collective-permute-done.4 = f32[104,128]{1,0:T(8,128)S(1)} collective-permute-done((f32[104,128]{1,0:T(8,128)S(1)}, f32[104,128]{1,0:T(8,128)S(1)}, u32[]{:S(2)}, u32[]{:S(2)}) %collective-permute-start.4) | collective-permute-done | bytes 53280 | tf_op jit(solution)/shard_map/ppermute | solution.py:484
  46.7 3.2 %collective-permute-done.6.part1 = bf16[8,5760]{1,0:T(8,128)(2,1)S(1)} collective-permute-done((bf16[8,5760]{1,0:T(8,128)(2,1)S(1)}, bf16[8,5760]{1,0:T(8,128)(2,1)S(1)}, u32[]{:S(2)}, u32[]{:S(2)}) %collective-permute-start.6) | collective-permute-done | bytes 92192 | tf_op jit(solution)/shard_map/ppermute | solution.py:484
  49.9 2.0 %collective-permute-start.7 = (f32[104,128]{1,0:T(8,128)S(1)}, f32[104,128]{1,0:T(8,128)S(1)}, u32[]{:S(2)}, u32[]{:S(2)}) collective-permute-start(f32[104,128]{1,0:T(8,128)S(1)} %add_add_fusion), channel_id=1, source_target_pairs={{0,8},{4,12},{8,0},{12,4},{16,24},{20,28},{24,16},{28,20},{1,9},{5... | collective-permute-start | bytes 159752 | tf_op jit(solution)/shard_map/ppermute | solution.py:484
  51.9 0.9 %collective-permute-start.10 = (bf16[8,5760]{1,0:T(8,128)(2,1)S(1)}, bf16[8,5760]{1,0:T(8,128)(2,1)S(1)}, u32[]{:S(2)}, u32[]{:S(2)}) collective-permute-start(bf16[8,5760]{1,0:T(8,128)(2,1)S(1)} %get-tuple-element.28.part0), channel_id=1, source_target_pairs={{0,2},{1,3},{2,0},{3,1},{4,6},{5,7},{6,4},{7,5},{8,10},{9,11},{10,... | collective-permute-start | bytes 276488 | tf_op jit(solution)/shard_map/ppermute | solution.py:484
  52.8 1.2 %collective-permute-done.7 = f32[104,128]{1,0:T(8,128)S(1)} collective-permute-done((f32[104,128]{1,0:T(8,128)S(1)}, f32[104,128]{1,0:T(8,128)S(1)}, u32[]{:S(2)}, u32[]{:S(2)}) %collective-permute-start.7) | collective-permute-done | bytes 53280 | tf_op jit(solution)/shard_map/ppermute | solution.py:484
  54.1 3.0 %collective-permute-start.9 = (f32[104,128]{1,0:T(8,128)S(1)}, f32[104,128]{1,0:T(8,128)S(1)}, u32[]{:S(2)}, u32[]{:S(2)}) collective-permute-start(f32[104,128]{1,0:T(8,128)S(1)} %add.22), channel_id=1, source_target_pairs={{0,16},{4,20},{8,24},{12,28},{16,0},{20,4},{24,8},{28,12},{1,17},{... | collective-permute-start | bytes 159752 | tf_op jit(solution)/shard_map/ppermute | solution.py:484
  57.1 2.1 %collective-permute-done.9 = f32[104,128]{1,0:T(8,128)S(1)} collective-permute-done((f32[104,128]{1,0:T(8,128)S(1)}, f32[104,128]{1,0:T(8,128)S(1)}, u32[]{:S(2)}, u32[]{:S(2)}) %collective-permute-start.9) | collective-permute-done | bytes 53280 | tf_op jit(solution)/shard_map/ppermute | solution.py:484
  59.2 0.1 collective-permute-start.11
  59.3 0.9 %place.1 = f32[1,8,23040]{2,1,0:T(8,128)} custom-call(bf16[8,5760]{1,0:T(8,128)(2,1)S(1)} %get-tuple-element.28.part0, bf16[8,5760]{1,0:T(8,128)(2,1)S(1)} %collective-permute-done.6.part1, bf16[8,5760]{1,0:T(8,128)(2,1)S(1)} %collective-permute-done.10.part2, bf16[8,5760]{1,0:T(8,128)(2,1)S(1)} %collective-permute-done.8.part3), custom_call_target="tpu_custom_call" | custom-call | tf_op jit(solution)/shard_map/place/pallas_call | solution.py:601
  60.2 0.3 collective-permute-done.11.other
  60.5 0.8 %taps.1 = (f32[3,3,32,64]{3,2,1,0:T(8,128)}, f32[3,3,16,32]{3,2,1,0:T(8,128)}) custom-call(f32[104,128]{1,0:T(8,128)S(1)} %add.23.mine, f32[104,128]{1,0:T(8,128)S(1)} %collective-permute-done.11.other), custom_call_target="tpu_custom_call" | custom-call | tf_op jit(solution)/shard_map/taps/pallas_call | solution.py:609
  (25 shorter events, 0.1 us)
Async XLA Ops:
  0.6 9.9 %copy-start.3 = (s32[32,48]{1,0:T(8,128)S(1)}, s32[32,48]{1,0:T(8,128)}, u32[]{:S(2)}) copy-start(s32[32,48]{1,0:T(8,128)} %land.3) | copy-start | bytes 18436
  0.6 9.9 %copy-start = (bf16[1,32,23040]{2,1,0:T(8,128)(2,1)S(1)}, bf16[1,32,23040]{2,1,0:T(8,128)(2,1)}, u32[]{:S(2)}) copy-start(bf16[1,32,23040]{2,1,0:T(8,128)(2,1)} %targets.3) | copy-start | bytes 4423684
  0.7 5.8 %copy-start.1 = (bf16[1,8,23040]{2,1,0:T(8,128)(2,1)S(1)}, bf16[1,8,23040]{2,1,0:T(8,128)(2,1)}, u32[]{:S(2)}) copy-start(bf16[1,8,23040]{2,1,0:T(8,128)(2,1)} %latent.3) | copy-start | bytes 1105924
  0.7 5.8 %copy-start.6 = (f32[64]{0:T(128)S(1)}, f32[64]{0:T(128)}, u32[]{:S(2)}) copy-start(f32[64]{0:T(128)} %scale.3) | copy-start | bytes 772
  0.7 5.8 %copy-start.5 = (s32[8]{0:T(128)S(1)}, s32[8]{0:T(128)}, u32[]{:S(2)}) copy-start(s32[8]{0:T(128)} %seeds.3) | copy-start | bytes 100
  0.7 9.9 %copy-start.7 = (f32[16]{0:T(128)S(1)}, f32[16]{0:T(128)}, u32[]{:S(2)}) copy-start(f32[16]{0:T(128)} %channel_weight.1) | copy-start | bytes 196
  2.8 7.8 %collective-permute-start = (bf16[50,8,128]{2,1,0:T(8,128)(2,1)}, bf16[50,8,128]{2,1,0:T(8,128)(2,1)S(1)}, u32[]{:S(2)}, u32[]{:S(2)}) collective-permute-start(bf16[50,8,128]{2,1,0:T(8,128)(2,1)} %get-tuple-element.22), channel_id=1, source_target_pairs={{0,4},{4,8},{8,12},{12,16},{16,20},{20,24},{24,28},{1,5},{5,9},{9,... | collective-permute-start | bytes 307208 | tf_op jit(solution)/shard_map/ppermute | solution.py:24
  5.2 5.4 %collective-permute-start.1 = (bf16[1,6400]{1,0:T(2,128)(2,1)}, bf16[1,6400]{1,0:T(2,128)(2,1)S(1)}, u32[]{:S(2)}, u32[]{:S(2)}) collective-permute-start(bf16[1,6400]{1,0:T(2,128)(2,1)} %get-tuple-element.23), channel_id=1, source_target_pairs={{4,0},{8,4},{12,8},{16,12},{20,16},{24,20},{28,24},{5,1},{9,5},{13... | collective-permute-start | bytes 38408 | tf_op jit(solution)/shard_map/ppermute | solution.py:24
  6.5 0.9 %copy-start.2 = (bf16[3,3,64,32]{2,3,1,0:T(8,128)(2,1)S(1)}, bf16[3,3,64,32]{2,3,1,0:T(8,128)(2,1)}, u32[]{:S(2)}) copy-start(bf16[3,3,64,32]{2,3,1,0:T(8,128)(2,1)} %param.11) | copy-start | bytes 110596
  7.4 0.8 %copy-start.4 = (bf16[3,3,32,16]{2,3,1,0:T(8,128)(2,1)S(1)}, bf16[3,3,32,16]{2,3,1,0:T(8,128)(2,1)}, u32[]{:S(2)}) copy-start(bf16[3,3,32,16]{2,3,1,0:T(8,128)(2,1)} %param.12) | copy-start | bytes 27652
  32.8 3.9 %collective-permute-start.2 = (f32[104,128]{1,0:T(8,128)S(1)}, f32[104,128]{1,0:T(8,128)S(1)}, u32[]{:S(2)}, u32[]{:S(2)}) collective-permute-start(f32[104,128]{1,0:T(8,128)S(1)} %get-tuple-element.30), channel_id=1, source_target_pairs={{0,4},{4,0},{8,12},{12,8},{16,20},{20,16},{24,28},{28,24},{1,5},{5... | collective-permute-start | bytes 159752 | tf_op jit(solution)/shard_map/ppermute | solution.py:484
  36.8 8.0 %collective-permute-start.5 = (f32[104,128]{1,0:T(8,128)S(1)}, f32[104,128]{1,0:T(8,128)S(1)}, u32[]{:S(2)}, u32[]{:S(2)}) collective-permute-start(f32[104,128]{1,0:T(8,128)S(1)} %add.18), channel_id=1, source_target_pairs={{0,3},{1,2},{2,1},{3,0},{4,7},{5,6},{6,5},{7,4},{8,11},{9,10},{10,... | collective-permute-start | bytes 159752 | tf_op jit(solution)/shard_map/ppermute | solution.py:484
  40.4 6.3 %collective-permute-start.4 = (f32[104,128]{1,0:T(8,128)S(1)}, f32[104,128]{1,0:T(8,128)S(1)}, u32[]{:S(2)}, u32[]{:S(2)}) collective-permute-start(f32[104,128]{1,0:T(8,128)S(1)} %add.18), channel_id=1, source_target_pairs={{0,2},{1,3},{2,0},{3,1},{4,6},{5,7},{6,4},{7,5},{8,10},{9,11},{10,... | collective-permute-start | bytes 159752 | tf_op jit(solution)/shard_map/ppermute | solution.py:484
  40.4 6.3 %collective-permute-start.3 = (f32[104,128]{1,0:T(8,128)S(1)}, f32[104,128]{1,0:T(8,128)S(1)}, u32[]{:S(2)}, u32[]{:S(2)}) collective-permute-start(f32[104,128]{1,0:T(8,128)S(1)} %add.18), channel_id=1, source_target_pairs={{0,1},{1,0},{2,3},{3,2},{4,5},{5,4},{6,7},{7,6},{8,9},{9,8},{10,11... | collective-permute-start | bytes 159752 | tf_op jit(solution)/shard_map/ppermute | solution.py:484
  41.2 12.9 %collective-permute-start.8 = (bf16[8,5760]{1,0:T(8,128)(2,1)S(1)}, bf16[8,5760]{1,0:T(8,128)(2,1)S(1)}, u32[]{:S(2)}, u32[]{:S(2)}) collective-permute-start(bf16[8,5760]{1,0:T(8,128)(2,1)S(1)} %get-tuple-element.28.part0), channel_id=1, source_target_pairs={{0,3},{1,2},{2,1},{3,0},{4,7},{5,6},{6,5},{7,4},{8,11},{9,10},{10,... | collective-permute-start | bytes 276488 | tf_op jit(solution)/shard_map/ppermute | solution.py:484
  44.8 5.1 %collective-permute-start.6 = (bf16[8,5760]{1,0:T(8,128)(2,1)S(1)}, bf16[8,5760]{1,0:T(8,128)(2,1)S(1)}, u32[]{:S(2)}, u32[]{:S(2)}) collective-permute-start(bf16[8,5760]{1,0:T(8,128)(2,1)S(1)} %get-tuple-element.28.part0), channel_id=1, source_target_pairs={{0,1},{1,0},{2,3},{3,2},{4,5},{5,4},{6,7},{7,6},{8,9},{9,8},{10,11... | collective-permute-start | bytes 276488 | tf_op jit(solution)/shard_map/ppermute | solution.py:484
  49.9 4.1 %collective-permute-start.7 = (f32[104,128]{1,0:T(8,128)S(1)}, f32[104,128]{1,0:T(8,128)S(1)}, u32[]{:S(2)}, u32[]{:S(2)}) collective-permute-start(f32[104,128]{1,0:T(8,128)S(1)} %add_add_fusion), channel_id=1, source_target_pairs={{0,8},{4,12},{8,0},{12,4},{16,24},{20,28},{24,16},{28,20},{1,9},{5... | collective-permute-start | bytes 159752 | tf_op jit(solution)/shard_map/ppermute | solution.py:484
  51.9 7.3 %collective-permute-start.10 = (bf16[8,5760]{1,0:T(8,128)(2,1)S(1)}, bf16[8,5760]{1,0:T(8,128)(2,1)S(1)}, u32[]{:S(2)}, u32[]{:S(2)}) collective-permute-start(bf16[8,5760]{1,0:T(8,128)(2,1)S(1)} %get-tuple-element.28.part0), channel_id=1, source_target_pairs={{0,2},{1,3},{2,0},{3,1},{4,6},{5,7},{6,4},{7,5},{8,10},{9,11},{10,... | collective-permute-start | bytes 276488 | tf_op jit(solution)/shard_map/ppermute | solution.py:484
  54.1 5.1 %collective-permute-start.9 = (f32[104,128]{1,0:T(8,128)S(1)}, f32[104,128]{1,0:T(8,128)S(1)}, u32[]{:S(2)}, u32[]{:S(2)}) collective-permute-start(f32[104,128]{1,0:T(8,128)S(1)} %add.22), channel_id=1, source_target_pairs={{0,16},{4,20},{8,24},{12,28},{16,0},{20,4},{24,8},{28,12},{1,17},{... | collective-permute-start | bytes 159752 | tf_op jit(solution)/shard_map/ppermute | solution.py:484
  59.2 1.3 %collective-permute-start.11 = (f32[104,128]{1,0:T(8,128)S(1)}, f32[104,128]{1,0:T(8,128)S(1)}, u32[]{:S(2)}, u32[]{:S(2)}) collective-permute-start(f32[104,128]{1,0:T(8,128)S(1)} %add.23.mine), channel_id=1, source_target_pairs={{0,4},{4,0},{8,12},{12,8},{16,20},{20,16},{24,28},{28,24},{1,5},{5... | collective-permute-start | bytes 159752 | tf_op jit(solution)/shard_map/ppermute | solution.py:484

commit v10 on v9

--- a/solution.py
+++ b/solution.py
@@ -127,9 +127,32 @@
     return jnp.bitwise_and(jnp.right_shift(picked, cell - 30 * word), 1).astype(jnp.float32)
 
 
-def edge_kernel(half, chan, latent, targets, land, down, up, words):
+def edge_kernel(
+    half,
+    chan,
+    latent_hbm,
+    targets_hbm,
+    land_hbm,
+    down,
+    up,
+    latent,
+    targets,
+    land,
+    words,
+    sems,
+):
     rows = latent.shape[1]
     blocks = latent.shape[2] // LANES
+    edge = pl.ds(targets_hbm.shape[1] - 8, 8)
+    copies = [
+        pltpu.make_async_copy(latent_hbm, latent, sems.at[0]),
+        pltpu.make_async_copy(targets_hbm.at[:, edge], targets, sems.at[1]),
+        pltpu.make_async_copy(land_hbm.at[edge], land, sems.at[2]),
+    ]
+    for copy in copies:
+        copy.start()
+    for copy in copies:
+        copy.wait()
     own = blocks // lax.axis_size("mem")
     mem_pos = lax.axis_index("mem")
     words[...] = jnp.zeros(words.shape, jnp.int32)
@@ -199,7 +222,7 @@
         store(i, t, jnp.concatenate(parts, axis=0).astype(jnp.bfloat16))
 
 
-def prepare_kernel(half, seeds, scale, latent, kernel_one, kernel_two, source, band_one, band_two, back_one, back_two, lines):
+def prepare_kernel(half, chan, seeds, scale, latent, source, lines):
     rows, span = latent.shape[1], latent.shape[2]
     blocks = span // LANES
     own = blocks // lax.axis_size("mem")
@@ -218,11 +241,14 @@
 
     def step(i, _):
         make_source(
-            i, lat_pos * rows + i, total_rows, span, own, half, seeds, scale, kernel_one.shape[3], line, store
+            i, lat_pos * rows + i, total_rows, span, own, half, seeds, scale, chan, line, store
         )
         return 0
 
     lax.fori_loop(0, rows, step, 0)
+
+
+def bands_kernel(kernel_one, kernel_two, band_one, band_two, back_one, back_two):
     build_band(kernel_one, band_one)
     build_band(kernel_two, band_two)
     build_back(kernel_one, back_one)
@@ -501,6 +527,7 @@
     assert 4 * chan2 == 2 * chan1 == chan0 and chan0 == 64
     vmem = pl.BlockSpec(memory_space=pltpu.VMEM)
     smem = pl.BlockSpec(memory_space=pltpu.SMEM)
+    hbm = pl.BlockSpec(memory_space=pltpu.HBM)
     f32, bf16 = jnp.float32, jnp.bfloat16
     wide, front = half + 2, half + 1
     params = pltpu.CompilerParams(vmem_limit_bytes=32 * 1024 * 1024)
@@ -509,37 +536,43 @@
     kernel_two = kernel_two.transpose(0, 1, 3, 2)
     down, up = pl.pallas_call(
         functools.partial(edge_kernel, half, chan2),
-        grid=(1,),
-        in_specs=[
-            pl.BlockSpec((1, 8, span), lambda i: (0, 0, 0)),
-            pl.BlockSpec((1, 8, span), lambda i: (0, rows // 2 - 1, 0)),
-            pl.BlockSpec((8, land_words.shape[1]), lambda i: (rows // 2 - 1, 0)),
-        ],
-        out_specs=[
-            pl.BlockSpec((2 * wide, 8, LANES), lambda i: (0, 0, 0)),
-            pl.BlockSpec((1, 2 * wide * LANES), lambda i: (0, 0)),
-        ],
+        in_specs=[hbm] * 3,
+        out_specs=[vmem] * 2,
         out_shape=[
             jax.ShapeDtypeStruct((2 * wide, 8, LANES), bf16),
             jax.ShapeDtypeStruct((1, 2 * wide * LANES), bf16),
         ],
-        scratch_shapes=[pltpu.VMEM((8, LANES), jnp.int32)],
+        scratch_shapes=[
+            pltpu.VMEM((1, 8, span), bf16),
+            pltpu.VMEM((1, 8, span), bf16),
+            pltpu.VMEM((8, land_words.shape[1]), jnp.int32),
+            pltpu.VMEM((8, LANES), jnp.int32),
+            pltpu.SemaphoreType.DMA((3,)),
+        ],
         compiler_params=pltpu.CompilerParams(vmem_limit_bytes=56 * 1024 * 1024),
         name="edges",
     )(latent, targets, land_words)
     above = shifted(down, "lat", 1)
     below = shifted(up, "lat", -1)
-    band = jax.ShapeDtypeStruct((512, 256), bf16)
-    source, *bands = pl.pallas_call(
-        functools.partial(prepare_kernel, half),
-        in_specs=[smem] * 2 + [vmem] * 3,
-        out_specs=[vmem] * 5,
-        out_shape=[jax.ShapeDtypeStruct((rows, wide, 16, LANES), bf16)] + [band] * 4,
+    source = pl.pallas_call(
+        functools.partial(prepare_kernel, half, chan0),
+        in_specs=[smem] * 2 + [vmem],
+        out_specs=vmem,
+        out_shape=jax.ShapeDtypeStruct((rows, wide, 16, LANES), bf16),
         scratch_shapes=[pltpu.VMEM((2 * wide, rows, LANES), f32)],
         compiler_params=small,
         cost_estimate=pl.CostEstimate(flops=10**8, bytes_accessed=10**7, transcendentals=0),
         name="prepare",
-    )(member_seeds, noise_scale, latent, kernel_one, kernel_two)
+    )(member_seeds, noise_scale, latent)
+    bands = pl.pallas_call(
+        bands_kernel,
+        in_specs=[vmem] * 2,
+        out_specs=[vmem] * 4,
+        out_shape=[jax.ShapeDtypeStruct((512, 256), bf16)] * 4,
+        compiler_params=small,
+        cost_estimate=pl.CostEstimate(flops=10**8, bytes_accessed=10**7, transcendentals=0),
+        name="bands",
+    )(kernel_one, kernel_two)
     norm = 1.0 / math.sqrt(sample_count * 4 * rows * lat_count * targets.shape[2])
     tap_rows = 5 * chan1 + 3 * chan2
     lat_grad, taps, taps_send = pl.pallas_call(
@@ -591,12 +624,11 @@
     taps = total(taps, "mem", 1, 2)
     one, two, three = (swapped(lat_grad, "mem", k) for k in range(1, 4))
     bits = [1 << k for k in range(1, lat_count.bit_length() - 1)]
-    taps, one = lax.optimization_barrier((taps, one))
     for bit in bits:
         if bit == bits[-1]:
             taps, three = lax.optimization_barrier((taps, three))
         taps = taps + swapped(taps, "lat", bit)
-    taps, two = lax.optimization_barrier((taps, two))
+    taps, one, two = lax.optimization_barrier((taps, one, two))
     other = swapped(taps, "lat", 1)
     latent_grad = pl.pallas_call(
         functools.partial(place_kernel, own),

time: 61.6 us -> 57.6 us (0.935)
  waiting for transfers between devices: 9.93 us -> 7.74 us
  local copies, waits for them, and re-layouts: 1.67 us -> 0.03 us
    ppermute x10, waiting for transfers between devices: 9.66 us -> 5.83 us  [swapped(): lax.ppermute(array, axis, [(i, i ^ bit) for i in range(lax.axis_size(axis...]
    ppermute x2, waiting for transfers between devices: 0.27 us -> 1.92 us  [shifted(): return lax.ppermute(array, axis, pairs)]
    unnamed x16, local copies, waits for them, and re-layouts: 1.67 us -> 0.03 us
    pallas_call x2 -> x3, Pallas kernels: 4.25 us -> 4.26 us  [the longest x1 2.13 us: local(): pl.pallas_call(functools.partial(edge_kernel, half, chan2), in_specs=[hbm...]
  transfers between devices with their start and end apart: 12 -> 12, of which waited for: 7 -> 6; matrix products, arithmetic and copies ran while one was open for 0% -> 0% of each run, Pallas kernels for 5% -> 5%
where the time goes in v10:
time: 57.6 us; the launch traced here: 57.4 us
  Pallas kernels  28.2 us (49%)
  starting transfers between devices  20.6 us (36%)
  waiting for transfers between devices  7.74 us (13%)
  between operations  0.81 us (1%)
    pallas_call x1, Pallas kernels, local(): pl.pallas_call(functools.partial(band_kernel, half, (chan0, chan1, chan2)...  22.2 us
    ppermute x10, starting transfers between devices, swapped(): lax.ppermute(array, axis, [(i, i ^ bit) for i in range(lax.axis_size(axis...  16.9 us
    ppermute x10, waiting for transfers between devices, swapped(): lax.ppermute(array, axis, [(i, i ^ bit) for i in range(lax.axis_size(axis...  5.83 us
    ppermute x2, starting transfers between devices, shifted(): return lax.ppermute(array, axis, pairs)  3.65 us
    pallas_call x1, Pallas kernels, local(): pl.pallas_call(functools.partial(edge_kernel, half, chan2), in_specs=[hbm...  2.13 us
    ppermute x2, waiting for transfers between devices, shifted(): return lax.ppermute(array, axis, pairs)  1.92 us
    pallas_call x1, Pallas kernels, local(): pl.pallas_call(functools.partial(prepare_kernel, half, chan0), in_specs=[...  1.83 us
  transfers between devices with their start and end apart: 12, of which 6 were waited for; matrix products, arithmetic and copies ran while one was open for 0% of the time, Pallas kernels for 5%

profile of v10, /device:TPU:0, one launch (start us, length us, event | category | flops | bytes accessed | tf_op | source)
XLA Modules:
  0.0 57.4 jit_solution(11258849511272566667)
XLA Ops:
  0.7 2.1 %edges.1 = (bf16[50,8,128]{2,1,0:T(8,128)(2,1)}, bf16[1,6400]{1,0:T(2,128)(2,1)}) custom-call(bf16[1,8,23040]{2,1,0:T(8,128)(2,1)} %latent_hbm.1, bf16[1,32,23040]{2,1,0:T(8,128)(2,1)} %targets.1, s32[32,48]{1,0:T(8,128)} %land.1), custom_call_target="tpu_custom_call" | custom-call | tf_op jit(solution)/shard_map/edges/pallas_call | solution.py:537
  2.9 2.4 %collective-permute-start = (bf16[50,8,128]{2,1,0:T(8,128)(2,1)}, bf16[50,8,128]{2,1,0:T(8,128)(2,1)S(1)}, u32[]{:S(2)}, u32[]{:S(2)}) collective-permute-start(bf16[50,8,128]{2,1,0:T(8,128)(2,1)} %get-tuple-element.19), channel_id=1, source_target_pairs={{0,4},{4,8},{8,12},{12,16},{16,20},{20,24},{24,28},{1,5},{5,9},{9,... | collective-permute-start | bytes 307208 | tf_op jit(solution)/shard_map/ppermute | solution.py:24
  5.2 1.3 %collective-permute-start.1 = (bf16[1,6400]{1,0:T(2,128)(2,1)}, bf16[1,6400]{1,0:T(2,128)(2,1)S(1)}, u32[]{:S(2)}, u32[]{:S(2)}) collective-permute-start(bf16[1,6400]{1,0:T(2,128)(2,1)} %get-tuple-element.20), channel_id=1, source_target_pairs={{4,0},{8,4},{12,8},{16,12},{20,16},{24,20},{28,24},{5,1},{9,5},{13... | collective-permute-start | bytes 38408 | tf_op jit(solution)/shard_map/ppermute | solution.py:24
  6.6 1.8 %prepare.1.own_source = bf16[8,25,16,128]{3,2,1,0:T(8,128)(2,1)S(1)} custom-call(s32[8]{0:T(128)S(1)} %copy-done.3, f32[64]{0:T(128)S(1)} %copy-done.4, bf16[1,8,23040]{2,1,0:T(8,128)(2,1)S(1)} %copy-done.1), custom_call_target="tpu_custom_call" | custom-call | flops 100000000 | bytes 10000000 | tf_op jit(solution)/shard_map/prepare/pallas_call | solution.py:557
  8.4 0.3 bands.1
  8.7 1.9 %collective-permute-done.1.below = bf16[1,6400]{1,0:T(2,128)(2,1)S(1)} collective-permute-done((bf16[1,6400]{1,0:T(2,128)(2,1)}, bf16[1,6400]{1,0:T(2,128)(2,1)S(1)}, u32[]{:S(2)}, u32[]{:S(2)}) %collective-permute-start.1) | collective-permute-done | bytes 12832 | tf_op jit(solution)/shard_map/ppermute | solution.py:24
  10.6 0.0 collective-permute-done.above
  10.6 22.2 %band.1 = (bf16[8,5760]{1,0:T(8,128)(2,1)S(1)}, f32[104,128]{1,0:T(8,128)S(1)}, f32[104,128]{1,0:T(8,128)S(1)}) custom-call(s32[8]{0:T(128)S(1)} %copy-done.3, f32[64]{0:T(128)S(1)} %copy-done.4, f32[16]{0:T(128)S(1)} %copy-done.5, bf16[8,25,16,128]{3,2,1,0:T(8,128)(2,1)S(1)} %prepare.1.own_source, bf16[50,8,128]{2,1,0:T(8,128)(2,1)S(1)} %collective-permute-done.above, ...), custom_call_target="tpu_custom_call" | custom-call | tf_op jit(solution)/shard_map/band/pallas_call | solution.py:578
  32.9 2.6 %collective-permute-start.2 = (f32[104,128]{1,0:T(8,128)S(1)}, f32[104,128]{1,0:T(8,128)S(1)}, u32[]{:S(2)}, u32[]{:S(2)}) collective-permute-start(f32[104,128]{1,0:T(8,128)S(1)} %get-tuple-element.27), channel_id=1, source_target_pairs={{0,4},{4,0},{8,12},{12,8},{16,20},{20,16},{24,28},{28,24},{1,5},{5... | collective-permute-start | bytes 159752 | tf_op jit(solution)/shard_map/ppermute | solution.py:510
  35.5 0.9 %collective-permute-done.2 = f32[104,128]{1,0:T(8,128)S(1)} collective-permute-done((f32[104,128]{1,0:T(8,128)S(1)}, f32[104,128]{1,0:T(8,128)S(1)}, u32[]{:S(2)}, u32[]{:S(2)}) %collective-permute-start.2) | collective-permute-done | bytes 53280 | tf_op jit(solution)/shard_map/ppermute | solution.py:510
  36.4 3.6 %collective-permute-start.5 = (f32[104,128]{1,0:T(8,128)S(1)}, f32[104,128]{1,0:T(8,128)S(1)}, u32[]{:S(2)}, u32[]{:S(2)}) collective-permute-start(f32[104,128]{1,0:T(8,128)S(1)} %add.18), channel_id=1, source_target_pairs={{0,3},{1,2},{2,1},{3,0},{4,7},{5,6},{6,5},{7,4},{8,11},{9,10},{10,... | collective-permute-start | bytes 159752 | tf_op jit(solution)/shard_map/ppermute | solution.py:510
  40.0 0.8 %collective-permute-start.3 = (f32[104,128]{1,0:T(8,128)S(1)}, f32[104,128]{1,0:T(8,128)S(1)}, u32[]{:S(2)}, u32[]{:S(2)}) collective-permute-start(f32[104,128]{1,0:T(8,128)S(1)} %add.18), channel_id=1, source_target_pairs={{0,1},{1,0},{2,3},{3,2},{4,5},{5,4},{6,7},{7,6},{8,9},{9,8},{10,11... | collective-permute-start | bytes 159752 | tf_op jit(solution)/shard_map/ppermute | solution.py:510
  40.8 3.6 %collective-permute-start.7 = (bf16[8,5760]{1,0:T(8,128)(2,1)S(1)}, bf16[8,5760]{1,0:T(8,128)(2,1)S(1)}, u32[]{:S(2)}, u32[]{:S(2)}) collective-permute-start(bf16[8,5760]{1,0:T(8,128)(2,1)S(1)} %get-tuple-element.25.part0), channel_id=1, source_target_pairs={{0,3},{1,2},{2,1},{3,0},{4,7},{5,6},{6,5},{7,4},{8,11},{9,10},{10,... | collective-permute-start | bytes 276488 | tf_op jit(solution)/shard_map/ppermute | solution.py:510
  44.4 1.9 %collective-permute-done.4 = f32[104,128]{1,0:T(8,128)S(1)} collective-permute-done((f32[104,128]{1,0:T(8,128)S(1)}, f32[104,128]{1,0:T(8,128)S(1)}, u32[]{:S(2)}, u32[]{:S(2)}) %collective-permute-start.4) | collective-permute-done | bytes 53280 | tf_op jit(solution)/shard_map/ppermute | solution.py:510
  46.3 2.5 %collective-permute-start.6 = (f32[104,128]{1,0:T(8,128)S(1)}, f32[104,128]{1,0:T(8,128)S(1)}, u32[]{:S(2)}, u32[]{:S(2)}) collective-permute-start(f32[104,128]{1,0:T(8,128)S(1)} %add_add_fusion), channel_id=1, source_target_pairs={{0,8},{4,12},{8,0},{12,4},{16,24},{20,28},{24,16},{28,20},{1,9},{5... | collective-permute-start | bytes 159752 | tf_op jit(solution)/shard_map/ppermute | solution.py:510
  48.8 1.2 %collective-permute-start.10 = (bf16[8,5760]{1,0:T(8,128)(2,1)S(1)}, bf16[8,5760]{1,0:T(8,128)(2,1)S(1)}, u32[]{:S(2)}, u32[]{:S(2)}) collective-permute-start(bf16[8,5760]{1,0:T(8,128)(2,1)S(1)} %get-tuple-element.25.part0), channel_id=1, source_target_pairs={{0,2},{1,3},{2,0},{3,1},{4,6},{5,7},{6,4},{7,5},{8,10},{9,11},{10,... | collective-permute-start | bytes 276488 | tf_op jit(solution)/shard_map/ppermute | solution.py:510
  50.0 0.9 %collective-permute-start.9 = (bf16[8,5760]{1,0:T(8,128)(2,1)S(1)}, bf16[8,5760]{1,0:T(8,128)(2,1)S(1)}, u32[]{:S(2)}, u32[]{:S(2)}) collective-permute-start(bf16[8,5760]{1,0:T(8,128)(2,1)S(1)} %get-tuple-element.25.part0), channel_id=1, source_target_pairs={{0,1},{1,0},{2,3},{3,2},{4,5},{5,4},{6,7},{7,6},{8,9},{9,8},{10,11... | collective-permute-start | bytes 276488 | tf_op jit(solution)/shard_map/ppermute | solution.py:510
  51.0 0.0 collective-permute-done.7.part3
  51.0 1.7 %collective-permute-start.8 = (f32[104,128]{1,0:T(8,128)S(1)}, f32[104,128]{1,0:T(8,128)S(1)}, u32[]{:S(2)}, u32[]{:S(2)}) collective-permute-start(f32[104,128]{1,0:T(8,128)S(1)} %add.22), channel_id=1, source_target_pairs={{0,16},{4,20},{8,24},{12,28},{16,0},{20,4},{24,8},{28,12},{1,17},{... | collective-permute-start | bytes 159752 | tf_op jit(solution)/shard_map/ppermute | solution.py:510
  52.7 2.5 %collective-permute-done.8 = f32[104,128]{1,0:T(8,128)S(1)} collective-permute-done((f32[104,128]{1,0:T(8,128)S(1)}, f32[104,128]{1,0:T(8,128)S(1)}, u32[]{:S(2)}, u32[]{:S(2)}) %collective-permute-start.8) | collective-permute-done | bytes 53280 | tf_op jit(solution)/shard_map/ppermute | solution.py:510
  55.2 0.2 collective-permute-done.9.part1
  55.4 0.9 %place.1 = f32[1,8,23040]{2,1,0:T(8,128)} custom-call(bf16[8,5760]{1,0:T(8,128)(2,1)S(1)} %get-tuple-element.25.part0, bf16[8,5760]{1,0:T(8,128)(2,1)S(1)} %collective-permute-done.9.part1, bf16[8,5760]{1,0:T(8,128)(2,1)S(1)} %collective-permute-done.10.part2, bf16[8,5760]{1,0:T(8,128)(2,1)S(1)} %collective-permute-done.7.part3), custom_call_target="tpu_custom_call" | custom-call | tf_op jit(solution)/shard_map/place/pallas_call | solution.py:633
  56.3 0.3 collective-permute-done.11.other
  56.6 0.8 %taps.1 = (f32[3,3,32,64]{3,2,1,0:T(8,128)}, f32[3,3,16,32]{3,2,1,0:T(8,128)}) custom-call(f32[104,128]{1,0:T(8,128)S(1)} %add.23.mine, f32[104,128]{1,0:T(8,128)S(1)} %collective-permute-done.11.other), custom_call_target="tpu_custom_call" | custom-call | tf_op jit(solution)/shard_map/taps/pallas_call | solution.py:641
  (26 shorter events, 0.1 us)
Async XLA Ops:
  0.6 10.0 %copy-start.2 = (s32[32,48]{1,0:T(8,128)S(1)}, s32[32,48]{1,0:T(8,128)}, u32[]{:S(2)}) copy-start(s32[32,48]{1,0:T(8,128)} %land.1) | copy-start | bytes 18436
  0.6 10.0 %copy-start = (bf16[1,32,23040]{2,1,0:T(8,128)(2,1)S(1)}, bf16[1,32,23040]{2,1,0:T(8,128)(2,1)}, u32[]{:S(2)}) copy-start(bf16[1,32,23040]{2,1,0:T(8,128)(2,1)} %targets.1) | copy-start | bytes 4423684
  0.7 5.9 %copy-start.1 = (bf16[1,8,23040]{2,1,0:T(8,128)(2,1)S(1)}, bf16[1,8,23040]{2,1,0:T(8,128)(2,1)}, u32[]{:S(2)}) copy-start(bf16[1,8,23040]{2,1,0:T(8,128)(2,1)} %latent_hbm.1) | copy-start | bytes 1105924
  0.7 5.9 %copy-start.4 = (f32[64]{0:T(128)S(1)}, f32[64]{0:T(128)}, u32[]{:S(2)}) copy-start(f32[64]{0:T(128)} %scale.3) | copy-start | bytes 772
  0.7 5.9 %copy-start.3 = (s32[8]{0:T(128)S(1)}, s32[8]{0:T(128)}, u32[]{:S(2)}) copy-start(s32[8]{0:T(128)} %seeds.3) | copy-start | bytes 100
  0.7 7.7 %copy-start.7 = (bf16[3,3,32,16]{2,3,1,0:T(8,128)(2,1)S(1)}, bf16[3,3,32,16]{2,3,1,0:T(8,128)(2,1)}, u32[]{:S(2)}) copy-start(bf16[3,3,32,16]{2,3,1,0:T(8,128)(2,1)} %param.12) | copy-start | bytes 27652
  0.7 7.7 %copy-start.6 = (bf16[3,3,64,32]{2,3,1,0:T(8,128)(2,1)S(1)}, bf16[3,3,64,32]{2,3,1,0:T(8,128)(2,1)}, u32[]{:S(2)}) copy-start(bf16[3,3,64,32]{2,3,1,0:T(8,128)(2,1)} %param.11) | copy-start | bytes 110596
  0.7 9.9 %copy-start.5 = (f32[16]{0:T(128)S(1)}, f32[16]{0:T(128)}, u32[]{:S(2)}) copy-start(f32[16]{0:T(128)} %channel_weight.1) | copy-start | bytes 196
  2.9 7.8 %collective-permute-start = (bf16[50,8,128]{2,1,0:T(8,128)(2,1)}, bf16[50,8,128]{2,1,0:T(8,128)(2,1)S(1)}, u32[]{:S(2)}, u32[]{:S(2)}) collective-permute-start(bf16[50,8,128]{2,1,0:T(8,128)(2,1)} %get-tuple-element.19), channel_id=1, source_target_pairs={{0,4},{4,8},{8,12},{12,16},{16,20},{20,24},{24,28},{1,5},{5,9},{9,... | collective-permute-start | bytes 307208 | tf_op jit(solution)/shard_map/ppermute | solution.py:24
  5.2 5.4 %collective-permute-start.1 = (bf16[1,6400]{1,0:T(2,128)(2,1)}, bf16[1,6400]{1,0:T(2,128)(2,1)S(1)}, u32[]{:S(2)}, u32[]{:S(2)}) collective-permute-start(bf16[1,6400]{1,0:T(2,128)(2,1)} %get-tuple-element.20), channel_id=1, source_target_pairs={{4,0},{8,4},{12,8},{16,12},{20,16},{24,20},{28,24},{5,1},{9,5},{13... | collective-permute-start | bytes 38408 | tf_op jit(solution)/shard_map/ppermute | solution.py:24
  32.9 3.5 %collective-permute-start.2 = (f32[104,128]{1,0:T(8,128)S(1)}, f32[104,128]{1,0:T(8,128)S(1)}, u32[]{:S(2)}, u32[]{:S(2)}) collective-permute-start(f32[104,128]{1,0:T(8,128)S(1)} %get-tuple-element.27), channel_id=1, source_target_pairs={{0,4},{4,0},{8,12},{12,8},{16,20},{20,16},{24,28},{28,24},{1,5},{5... | collective-permute-start | bytes 159752 | tf_op jit(solution)/shard_map/ppermute | solution.py:510
  36.4 8.0 %collective-permute-start.5 = (f32[104,128]{1,0:T(8,128)S(1)}, f32[104,128]{1,0:T(8,128)S(1)}, u32[]{:S(2)}, u32[]{:S(2)}) collective-permute-start(f32[104,128]{1,0:T(8,128)S(1)} %add.18), channel_id=1, source_target_pairs={{0,3},{1,2},{2,1},{3,0},{4,7},{5,6},{6,5},{7,4},{8,11},{9,10},{10,... | collective-permute-start | bytes 159752 | tf_op jit(solution)/shard_map/ppermute | solution.py:510
  40.0 6.3 %collective-permute-start.4 = (f32[104,128]{1,0:T(8,128)S(1)}, f32[104,128]{1,0:T(8,128)S(1)}, u32[]{:S(2)}, u32[]{:S(2)}) collective-permute-start(f32[104,128]{1,0:T(8,128)S(1)} %add.18), channel_id=1, source_target_pairs={{0,2},{1,3},{2,0},{3,1},{4,6},{5,7},{6,4},{7,5},{8,10},{9,11},{10,... | collective-permute-start | bytes 159752 | tf_op jit(solution)/shard_map/ppermute | solution.py:510
  40.0 6.3 %collective-permute-start.3 = (f32[104,128]{1,0:T(8,128)S(1)}, f32[104,128]{1,0:T(8,128)S(1)}, u32[]{:S(2)}, u32[]{:S(2)}) collective-permute-start(f32[104,128]{1,0:T(8,128)S(1)} %add.18), channel_id=1, source_target_pairs={{0,1},{1,0},{2,3},{3,2},{4,5},{5,4},{6,7},{7,6},{8,9},{9,8},{10,11... | collective-permute-start | bytes 159752 | tf_op jit(solution)/shard_map/ppermute | solution.py:510
  40.8 10.1 %collective-permute-start.7 = (bf16[8,5760]{1,0:T(8,128)(2,1)S(1)}, bf16[8,5760]{1,0:T(8,128)(2,1)S(1)}, u32[]{:S(2)}, u32[]{:S(2)}) collective-permute-start(bf16[8,5760]{1,0:T(8,128)(2,1)S(1)} %get-tuple-element.25.part0), channel_id=1, source_target_pairs={{0,3},{1,2},{2,1},{3,0},{4,7},{5,6},{6,5},{7,4},{8,11},{9,10},{10,... | collective-permute-start | bytes 276488 | tf_op jit(solution)/shard_map/ppermute | solution.py:510
  46.3 4.6 %collective-permute-start.6 = (f32[104,128]{1,0:T(8,128)S(1)}, f32[104,128]{1,0:T(8,128)S(1)}, u32[]{:S(2)}, u32[]{:S(2)}) collective-permute-start(f32[104,128]{1,0:T(8,128)S(1)} %add_add_fusion), channel_id=1, source_target_pairs={{0,8},{4,12},{8,0},{12,4},{16,24},{20,28},{24,16},{28,20},{1,9},{5... | collective-permute-start | bytes 159752 | tf_op jit(solution)/shard_map/ppermute | solution.py:510
  48.8 6.4 %collective-permute-start.10 = (bf16[8,5760]{1,0:T(8,128)(2,1)S(1)}, bf16[8,5760]{1,0:T(8,128)(2,1)S(1)}, u32[]{:S(2)}, u32[]{:S(2)}) collective-permute-start(bf16[8,5760]{1,0:T(8,128)(2,1)S(1)} %get-tuple-element.25.part0), channel_id=1, source_target_pairs={{0,2},{1,3},{2,0},{3,1},{4,6},{5,7},{6,4},{7,5},{8,10},{9,11},{10,... | collective-permute-start | bytes 276488 | tf_op jit(solution)/shard_map/ppermute | solution.py:510
  50.0 5.4 %collective-permute-start.9 = (bf16[8,5760]{1,0:T(8,128)(2,1)S(1)}, bf16[8,5760]{1,0:T(8,128)(2,1)S(1)}, u32[]{:S(2)}, u32[]{:S(2)}) collective-permute-start(bf16[8,5760]{1,0:T(8,128)(2,1)S(1)} %get-tuple-element.25.part0), channel_id=1, source_target_pairs={{0,1},{1,0},{2,3},{3,2},{4,5},{5,4},{6,7},{7,6},{8,9},{9,8},{10,11... | collective-permute-start | bytes 276488 | tf_op jit(solution)/shard_map/ppermute | solution.py:510
  51.0 4.2 %collective-permute-start.8 = (f32[104,128]{1,0:T(8,128)S(1)}, f32[104,128]{1,0:T(8,128)S(1)}, u32[]{:S(2)}, u32[]{:S(2)}) collective-permute-start(f32[104,128]{1,0:T(8,128)S(1)} %add.22), channel_id=1, source_target_pairs={{0,16},{4,20},{8,24},{12,28},{16,0},{20,4},{24,8},{28,12},{1,17},{... | collective-permute-start | bytes 159752 | tf_op jit(solution)/shard_map/ppermute | solution.py:510
  55.4 1.2 %collective-permute-start.11 = (f32[104,128]{1,0:T(8,128)S(1)}, f32[104,128]{1,0:T(8,128)S(1)}, u32[]{:S(2)}, u32[]{:S(2)}) collective-permute-start(f32[104,128]{1,0:T(8,128)S(1)} %add.23.mine), channel_id=1, source_target_pairs={{0,4},{4,0},{8,12},{12,8},{16,20},{20,16},{24,28},{28,24},{1,5},{5... | collective-permute-start | bytes 159752 | tf_op jit(solution)/shard_map/ppermute | solution.py:510

commit v11 on v10

--- a/solution.py
+++ b/solution.py
@@ -222,16 +222,34 @@
         store(i, t, jnp.concatenate(parts, axis=0).astype(jnp.bfloat16))
 
 
-def prepare_kernel(half, chan, seeds, scale, latent, source, lines):
+def weight_lines(grid_row, channel_weight, chan, grid_total):
+    latitude = math.pi / 2 - math.pi * (grid_row.astype(jnp.float32) + 0.5) / grid_total
+    cosine = jnp.where(grid_row >= 0, jnp.cos(latitude), 0.0)
+    channels = jnp.tile(lane_table(channel_weight, chan), (grid_row.shape[0] // 8, 1))
+    return cosine * (channels * (1.0 / (MEM * (MEM - 1))))
+
+
+def prepare_kernel(
+    half, chan, chan2, seeds, scale, channel_weight, latent, targets, land, source, aims, weights, lines, words
+):
     rows, span = latent.shape[1], latent.shape[2]
     blocks = span // LANES
     own = blocks // lax.axis_size("mem")
     total_rows = rows * lax.axis_size("lat")
     lat_pos, mem_pos = lax.axis_index("lat"), lax.axis_index("mem")
+    grid_row = iota((4 * rows, LANES), 0) + lat_pos * 4 * rows
+    base = weight_lines(grid_row, channel_weight, chan2, 4 * total_rows)
+    words[...] = jnp.zeros(words.shape, jnp.int32)
+    words[:, : land.shape[1]] = land[...]
     for t in range(half + 2):
         for part in range(2):
-            off = pl.multiple_of(window_block(mem_pos, own, half, blocks, part, t) * LANES, LANES)
-            lines[t * 2 + part] = latent[0, :, pl.ds(off, LANES)].astype(jnp.float32)
+            block = window_block(mem_pos, own, half, blocks, part, t)
+            off = pl.multiple_of(block * LANES, LANES)
+            slot = t * 2 + part
+            lines[slot] = latent[0, :, pl.ds(off, LANES)].astype(jnp.float32)
+            if t < half + 1:
+                aims[slot] = targets[0, :, pl.ds(off, LANES)].astype(jnp.float32)
+                weights[slot] = base + base * land_of(words[...], block, chan2)
 
     def line(slot, i):
         return spread_line(lines, slot, i)
@@ -255,18 +273,27 @@
     build_back(kernel_two, back_two)
 
 
+def take_turns(*parts):
+    parts = list(parts)
+    while parts:
+        for part in tuple(parts):
+            if next(part, part) is part:
+                parts.remove(part)
+
+
 def band_kernel(
     half,
     chans,
+    span,
     norm,
     seeds,
     scale,
     channel_weight,
     own_source,
+    aims,
+    weights,
     above,
     below,
-    targets,
-    land,
     band_one,
     band_two,
     back_one,
@@ -275,9 +302,8 @@
     taps_keep,
     taps_send,
     lat_rows,
-    tgt_rows,
-    weight_rows,
-    words,
+    edge_aims,
+    edge_weights,
     source,
     pre_even,
     pre_odd,
@@ -297,51 +323,30 @@
     acc_two_next,
 ):
     rows = own_source.shape[0]
-    span = targets.shape[2]
     blocks = span // LANES
-    lat_count = lax.axis_size("lat")
     own = blocks // lax.axis_size("mem")
-    total_rows = rows * lat_count
-    grid_rows = 4 * rows
-    grid_total = grid_rows * lat_count
+    total_rows = rows * lax.axis_size("lat")
     lat_pos = lax.axis_index("lat")
-    mem_pos = lax.axis_index("mem")
     wide = half + 2
     front = half + 1
     chan0, chan1, chan2 = chans
     f32, bf16 = jnp.float32, jnp.bfloat16
 
-    def block_of(part, t):
-        return window_block(mem_pos, own, half, blocks, part, t)
-
-    pad_rows = grid_rows + 8
-    grid_row = iota((pad_rows, LANES), 0)
-    grid_row = jnp.where(grid_row < grid_rows, grid_row, grid_row - (grid_rows + 4)) + lat_pos * grid_rows
-    latitude = math.pi / 2 - math.pi * (grid_row.astype(f32) + 0.5) / grid_total
-    channels = lane_table(channel_weight, chan2)
-    cosine = jnp.where(grid_row >= 0, jnp.cos(latitude), 0.0)
-    base_rows = cosine * (jnp.tile(channels, (pad_rows // 8, 1)) * (1.0 / (MEM * (MEM - 1))))
-
-    words[...] = jnp.zeros(words.shape, jnp.int32)
-    words[:, : land.shape[1]] = land[...]
-    for t in range(wide):
-        for part in range(2):
-            block = block_of(part, t)
-            off = pl.multiple_of(block * LANES, LANES)
-            slot = t * 2 + part
-            edge = above[slot].astype(f32)
-            lat_rows[slot, 0:1] = edge[0:1]
-            lat_rows[slot, 1:2] = below[:, slot * LANES : (slot + 1) * LANES].astype(f32)
-            if t < front:
-                tgt_rows[slot, 0:grid_rows] = targets[0, :, pl.ds(off, LANES)].astype(f32)
-                tgt_rows[slot, grid_rows:] = edge
-                mask = jnp.concatenate([land_of(words[...], block, chan2), pltpu.roll(edge, 5, 0)], axis=0)
-                weight_rows[slot] = base_rows + base_rows * mask
+    grid_row = iota((8, LANES), 0) + (lat_pos * 4 * rows - 4)
+    base = weight_lines(grid_row, channel_weight, chan2, 4 * total_rows)
+    for slot in range(2 * wide):
+        edge = above[slot].astype(f32)
+        lat_rows[slot, 0:1] = edge[0:1]
+        lat_rows[slot, 1:2] = below[:, slot * LANES : (slot + 1) * LANES].astype(f32)
+        if slot < 2 * front:
+            edge_aims[slot] = edge
+            edge_weights[slot] = base + base * pltpu.roll(edge, 5, 0)
 
     source[rows + 2 :] = jnp.zeros((2,) + source.shape[1:], bf16)
     source[:, wide] = jnp.zeros((source.shape[0],) + source.shape[2:], bf16)
-    fgrad_even[:, 0] = jnp.zeros((4,) + fgrad_even.shape[2:], bf16)
-    fgrad_odd[...] = jnp.zeros(fgrad_odd.shape, bf16)
+    fgrad_even[0] = jnp.zeros(fgrad_even.shape[1:], bf16)
+    for fgrad in (fgrad_even, fgrad_odd):
+        fgrad[:, 0] = jnp.zeros((4,) + fgrad.shape[2:], bf16)
     carry[...] = jnp.zeros(carry.shape, f32)
     carry_lat[...] = jnp.zeros(carry_lat.shape, f32)
     for acc in (acc_one, acc_one_next, acc_two, acc_two_next):
@@ -406,16 +411,14 @@
     pick = jnp.concatenate([pick_own, pick_prev], axis=0)
 
     def second_product(n, cast):
-        taken = jnp.concatenate([operand(act, 2 * n + k, 0, front) for k in range(2)], axis=0)
-        out = jnp.dot(taken, band_two[...], preferred_element_type=f32).astype(bf16)
         for k in range(2):
+            out = jnp.dot(operand(act, 2 * n + k, 0, front), band_two[...], preferred_element_type=f32).astype(bf16)
             for sub in range(2):
-                part = out[k * members : (k + 1) * members, sub * LANES : (sub + 1) * LANES]
-                cast[2 * k + sub] = part.reshape(front, 16, LANES)
-
-    def loss_gradient(n, cast, fgrad):
-        first = jnp.where(n >= 1, 4 * (n - 1), grid_rows)
-        for line in range(4):
+                cast[2 * k + sub] = out[:, sub * LANES : (sub + 1) * LANES].reshape(front, 16, LANES)
+            yield
+
+    def loss_gradient(cast, fgrad, aim_ref, weight_ref, first, lines):
+        for line in lines:
             for t in range(front):
                 both = cast[line, t].astype(f32)
                 parts = []
@@ -424,7 +427,7 @@
                         parts.append(jnp.zeros((8, LANES), f32))
                         continue
                     f = both[part * 8 : part * 8 + 8]
-                    d = f - spread_line(tgt_rows, t * 2 + part, first + line)
+                    d = f - spread_line(aim_ref, t * 2 + part, first + line)
                     goal = d * lax.rsqrt(d * d + SMOOTH)
                     gs = []
                     for k in range(1, 5):
@@ -435,12 +438,12 @@
                         back = gs[k] + pltpu.roll(back, MEM - 1, 0)
                     back = pltpu.roll(back, MEM - 1, 0)
                     spread = (gs[0] + gs[1]) + (gs[2] + gs[3]) - back
-                    weight = spread_line(weight_rows, t * 2 + part, first + line)
+                    weight = spread_line(weight_ref, t * 2 + part, first + line)
                     parts.append(weight * ((MEM - 1.0) * goal - spread))
                 fgrad[line, t + 1] = jnp.concatenate(parts, axis=0).astype(bf16)
+            yield
 
     def pull_back(n, fgrad):
-        at = jnp.maximum(n, 0)
         keep = jnp.where(n >= 1, 1.0, 0.0).astype(bf16)
 
         def flat(line, start, count):
@@ -453,24 +456,21 @@
             last = jnp.concatenate(last, axis=0)
             acc_next[...] += jnp.dot(last, x[:, 256:], preferred_element_type=f32)
 
-        g = [
-            jnp.concatenate(
-                [flat(2 * k, 1, front), flat(2 * k + 1, 1, front), flat(2 * k, 0, front), flat(2 * k + 1, 0, front)],
-                axis=1,
-            )
-            for k in range(2)
-        ]
-        pulled = jnp.dot(jnp.concatenate(g, axis=0), back_two[...], preferred_element_type=f32)
+        grads = []
+        for k in range(2):
+            g = [flat(2 * k, 1, front), flat(2 * k + 1, 1, front), flat(2 * k, 0, front), flat(2 * k + 1, 0, front)]
+            pulled = jnp.dot(jnp.concatenate(g, axis=1), back_two[...], preferred_element_type=f32)
+            grad = pulled[:, :LANES] + carry[...]
+            carry[...] = pulled[:, LANES:]
+            grads.append((grad * slope[2 * n + k].reshape(members, LANES)).astype(bf16))
+            yield
+        grads = jnp.concatenate(grads, axis=1)
         g = [jnp.concatenate([flat(2 * k, 2, half), flat(2 * k + 1, 2, half)], axis=1) for k in range(2)]
-        x = [operand(act, 2 * at + k, 1, half) for k in range(2)]
+        x = [operand(act, 2 * n + k, 1, half) for k in range(2)]
         add_taps(jnp.concatenate(g, axis=0) * keep, jnp.concatenate(x, axis=0), acc_two, acc_two_next, chan2)
-        grads = [
-            pulled[:members, :LANES] + carry[...],
-            pulled[members:, :LANES] + pulled[:members, LANES:],
-        ]
-        carry[...] = pulled[members:, LANES:]
-        grads = [(grads[k] * slope[2 * at + k].reshape(members, LANES)).astype(bf16) for k in range(2)]
-        grads = jnp.concatenate(grads, axis=1)
+        yield
+        add_taps(grads[16:] * keep, operand(source, n, 1, half), acc_one, acc_one_next, chan1)
+        yield
         z = jnp.dot(pick, grads, preferred_element_type=f32)
         z = jnp.concatenate([z[:48], z[48:]], axis=1)
         high = z.astype(bf16)
@@ -479,22 +479,31 @@
         z = z[:48] + z[48:]
         lat_lines[pl.ds(jnp.maximum(n - 1, 0), 48, stride=rows), :] = z[:, :LANES] + carry_lat[...]
         carry_lat[...] = z[:, LANES:]
-        add_taps(grads[16:] * keep, operand(source, at, 1, half), acc_one, acc_one_next, chan1)
+        yield
+
+    def own_gradient(n, cast, fgrad):
+        return loss_gradient(cast, fgrad, aims, weights, 4 * (n - 1), range(4))
 
     def second_segment(m, _):
-        second_product(2 * m + 1, cast_odd)
-        loss_gradient(2 * m, cast_even, fgrad_even)
-        pull_back(2 * m - 1, fgrad_odd)
-        second_product(2 * m + 2, cast_even)
-        loss_gradient(2 * m + 1, cast_odd, fgrad_odd)
-        pull_back(2 * m, fgrad_even)
+        take_turns(
+            second_product(2 * m + 2, cast_even),
+            own_gradient(2 * m + 1, cast_odd, fgrad_odd),
+            pull_back(2 * m, fgrad_even),
+        )
+        take_turns(
+            second_product(jnp.minimum(2 * m + 3, rows), cast_odd),
+            own_gradient(2 * m + 2, cast_even, fgrad_even),
+            pull_back(2 * m + 1, fgrad_odd),
+        )
         return 0
 
-    second_product(0, cast_even)
+    take_turns(second_product(0, cast_even))
+    take_turns(
+        second_product(1, cast_odd),
+        loss_gradient(cast_even, fgrad_even, edge_aims, edge_weights, 0, range(1, 4)),
+    )
     lax.fori_loop(0, rows // 2, second_segment, 0)
-    loss_gradient(rows, cast_even, fgrad_even)
-    pull_back(rows - 1, fgrad_odd)
-    pull_back(rows, fgrad_even)
+    take_turns(pull_back(rows, fgrad_even))
 
     for t in range(own):
         out_lat[:, t * LANES : (t + 1) * LANES] = lat_lines[t * rows : (t + 1) * rows].astype(bf16)
@@ -554,16 +563,18 @@
     )(latent, targets, land_words)
     above = shifted(down, "lat", 1)
     below = shifted(up, "lat", -1)
-    source = pl.pallas_call(
-        functools.partial(prepare_kernel, half, chan0),
-        in_specs=[smem] * 2 + [vmem],
-        out_specs=vmem,
-        out_shape=jax.ShapeDtypeStruct((rows, wide, 16, LANES), bf16),
-        scratch_shapes=[pltpu.VMEM((2 * wide, rows, LANES), f32)],
+    source, aims, weights = pl.pallas_call(
+        functools.partial(prepare_kernel, half, chan0, chan2),
+        in_specs=[smem] * 3 + [vmem] * 3,
+        out_specs=[vmem] * 3,
+        out_shape=[jax.ShapeDtypeStruct((rows, wide, 16, LANES), bf16)]
+        + [jax.ShapeDtypeStruct((2 * front, 4 * rows, LANES), f32)] * 2,
+        scratch_shapes=[pltpu.VMEM((2 * wide, rows, LANES), f32), pltpu.VMEM((4 * rows, LANES), jnp.int32)],
         compiler_params=small,
         cost_estimate=pl.CostEstimate(flops=10**8, bytes_accessed=10**7, transcendentals=0),
         name="prepare",
-    )(member_seeds, noise_scale, latent)
+    )(member_seeds, noise_scale, channel_weight, latent, targets, land_words)
+    one_late, two_late, source = lax.optimization_barrier((kernel_one, kernel_two, source))
     bands = pl.pallas_call(
         bands_kernel,
         in_specs=[vmem] * 2,
@@ -572,11 +583,11 @@
         compiler_params=small,
         cost_estimate=pl.CostEstimate(flops=10**8, bytes_accessed=10**7, transcendentals=0),
         name="bands",
-    )(kernel_one, kernel_two)
+    )(one_late, two_late)
     norm = 1.0 / math.sqrt(sample_count * 4 * rows * lat_count * targets.shape[2])
     tap_rows = 5 * chan1 + 3 * chan2
     lat_grad, taps, taps_send = pl.pallas_call(
-        functools.partial(band_kernel, half, (chan0, chan1, chan2), norm),
+        functools.partial(band_kernel, half, (chan0, chan1, chan2), span, norm),
         in_specs=[smem] * 3 + [vmem] * 9,
         out_specs=[vmem] * 3,
         out_shape=[
@@ -586,9 +597,8 @@
         ],
         scratch_shapes=[
             pltpu.VMEM((2 * wide, 8, LANES), f32),
-            pltpu.VMEM((2 * front, 4 * rows + 8, LANES), f32),
-            pltpu.VMEM((2 * front, 4 * rows + 8, LANES), f32),
-            pltpu.VMEM((4 * rows, LANES), jnp.int32),
+            pltpu.VMEM((2 * front, 8, LANES), f32),
+            pltpu.VMEM((2 * front, 8, LANES), f32),
             pltpu.VMEM((rows + 4, wide + 1, 16, LANES), bf16),
             pltpu.VMEM((wide * 16, 2 * LANES), f32),
             pltpu.VMEM((wide * 16, 2 * LANES), f32),
@@ -614,10 +624,10 @@
         noise_scale,
         channel_weight,
         source,
+        aims,
+        weights,
         above,
         below,
-        targets,
-        land_words,
         *bands,
     )
     taps = taps + swapped(taps_send, "lat", 1)

time: 57.6 us -> 56.5 us (0.981)
  Pallas kernels: 28.2 us -> 27.4 us
  waiting for transfers between devices: 7.74 us -> 7.06 us
    pallas_call x1, Pallas kernels: 22.2 us -> 21.1 us  [local(): pl.pallas_call(functools.partial(band_kernel, half, (chan0, chan1, chan2)...]
  transfers between devices with their start and end apart: 12 -> 12, of which waited for: 6 -> 6; matrix products, arithmetic and copies ran while one was open for 0% -> 0% of each run, Pallas kernels for 5% -> 6%
where the time goes in v11:
time: 56.5 us; the launch traced here: 56.3 us
  Pallas kernels  27.4 us (48%)
  starting transfers between devices  20.9 us (37%)
  waiting for transfers between devices  7.06 us (12%)
  between operations  0.83 us (1%)
    pallas_call x1, Pallas kernels, local(): pl.pallas_call(functools.partial(band_kernel, half, (chan0, chan1, chan2)...  21.1 us
    ppermute x10, starting transfers between devices, swapped(): lax.ppermute(array, axis, [(i, i ^ bit) for i in range(lax.axis_size(axis...  17.3 us
    ppermute x10, waiting for transfers between devices, swapped(): lax.ppermute(array, axis, [(i, i ^ bit) for i in range(lax.axis_size(axis...  5.48 us
    ppermute x2, starting transfers between devices, shifted(): return lax.ppermute(array, axis, pairs)  3.65 us
    pallas_call x1, Pallas kernels, local(): pl.pallas_call(functools.partial(prepare_kernel, half, chan0, chan2), in_...  2.13 us
    pallas_call x1, Pallas kernels, local(): pl.pallas_call(functools.partial(edge_kernel, half, chan2), in_specs=[hbm...  2.13 us
    ppermute x2, waiting for transfers between devices, shifted(): return lax.ppermute(array, axis, pairs)  1.58 us
  transfers between devices with their start and end apart: 12, of which 6 were waited for; matrix products, arithmetic and copies ran while one was open for 0% of the time, Pallas kernels for 6%

profile of v11, /device:TPU:0, one launch (start us, length us, event | category | flops | bytes accessed | tf_op | source)
XLA Modules:
  0.0 56.3 jit_solution(14131894845849437713)
XLA Ops:
  0.7 2.1 %edges.1 = (bf16[50,8,128]{2,1,0:T(8,128)(2,1)}, bf16[1,6400]{1,0:T(2,128)(2,1)}) custom-call(bf16[1,8,23040]{2,1,0:T(8,128)(2,1)} %latent_hbm.1, bf16[1,32,23040]{2,1,0:T(8,128)(2,1)} %targets_hbm.1, s32[32,48]{1,0:T(8,128)} %land_hbm.1), custom_call_target="tpu_custom_call" | custom-call | tf_op jit(solution)/shard_map/edges/pallas_call | solution.py:546
  2.9 2.4 %collective-permute-start = (bf16[50,8,128]{2,1,0:T(8,128)(2,1)}, bf16[50,8,128]{2,1,0:T(8,128)(2,1)S(1)}, u32[]{:S(2)}, u32[]{:S(2)}) collective-permute-start(bf16[50,8,128]{2,1,0:T(8,128)(2,1)} %get-tuple-element.29), channel_id=1, source_target_pairs={{0,4},{4,8},{8,12},{12,16},{16,20},{20,24},{24,28},{1,5},{5,9},{9,... | collective-permute-start | bytes 307208 | tf_op jit(solution)/shard_map/ppermute | solution.py:24
  5.2 1.3 %collective-permute-start.1 = (bf16[1,6400]{1,0:T(2,128)(2,1)}, bf16[1,6400]{1,0:T(2,128)(2,1)S(1)}, u32[]{:S(2)}, u32[]{:S(2)}) collective-permute-start(bf16[1,6400]{1,0:T(2,128)(2,1)} %get-tuple-element.30), channel_id=1, source_target_pairs={{4,0},{8,4},{12,8},{16,12},{20,16},{24,20},{28,24},{5,1},{9,5},{13... | collective-permute-start | bytes 38408 | tf_op jit(solution)/shard_map/ppermute | solution.py:24
  6.6 2.1 %prepare.1 = (bf16[8,25,16,128]{3,2,1,0:T(8,128)(2,1)S(1)}, f32[48,32,128]{2,1,0:T(8,128)S(1)}, f32[48,32,128]{2,1,0:T(8,128)S(1)}) custom-call(s32[8]{0:T(128)S(1)} %copy-done.3, f32[64]{0:T(128)S(1)} %copy-done.4, f32[16]{0:T(128)S(1)} %copy-done.5, bf16[1,8,23040]{2,1,0:T(8,128)(2,1)S(1)} %copy-done.1, bf16[1,32,23040]{2,1,0:T(8,128)(2,1)S(1)} %copy-done, ...), custom_call_target="tpu_custom_call" | custom-call | flops 100000000 | bytes 10000000 | tf_op jit(solution)/shard_map/prepare/pallas_call | solution.py:566
  8.7 0.3 bands.1
  9.0 1.6 %collective-permute-done.1.below = bf16[1,6400]{1,0:T(2,128)(2,1)S(1)} collective-permute-done((bf16[1,6400]{1,0:T(2,128)(2,1)}, bf16[1,6400]{1,0:T(2,128)(2,1)S(1)}, u32[]{:S(2)}, u32[]{:S(2)}) %collective-permute-start.1) | collective-permute-done | bytes 12832 | tf_op jit(solution)/shard_map/ppermute | solution.py:24
  10.6 0.0 collective-permute-done.above
  10.6 21.1 %band.1 = (bf16[8,5760]{1,0:T(8,128)(2,1)S(1)}, f32[104,128]{1,0:T(8,128)S(1)}, f32[104,128]{1,0:T(8,128)S(1)}) custom-call(s32[8]{0:T(128)S(1)} %copy-done.3, f32[64]{0:T(128)S(1)} %copy-done.4, f32[16]{0:T(128)S(1)} %copy-done.5, bf16[8,25,16,128]{3,2,1,0:T(8,128)(2,1)S(1)} %get-tuple-element.26.own_source, f32[48,32,128]{2,1,0:T(8,128)S(1)} %get-tuple-element.27.aims, ...), custom_call_target="tpu_custom_call" | custom-call | tf_op jit(solution)/shard_map/band/pallas_call | solution.py:589
  31.8 2.6 %collective-permute-start.2 = (f32[104,128]{1,0:T(8,128)S(1)}, f32[104,128]{1,0:T(8,128)S(1)}, u32[]{:S(2)}, u32[]{:S(2)}) collective-permute-start(f32[104,128]{1,0:T(8,128)S(1)} %get-tuple-element.39), channel_id=1, source_target_pairs={{0,4},{4,0},{8,12},{12,8},{16,20},{20,16},{24,28},{28,24},{1,5},{5... | collective-permute-start | bytes 159752 | tf_op jit(solution)/shard_map/ppermute | solution.py:519
  34.4 0.9 %collective-permute-done.2 = f32[104,128]{1,0:T(8,128)S(1)} collective-permute-done((f32[104,128]{1,0:T(8,128)S(1)}, f32[104,128]{1,0:T(8,128)S(1)}, u32[]{:S(2)}, u32[]{:S(2)}) %collective-permute-start.2) | collective-permute-done | bytes 53280 | tf_op jit(solution)/shard_map/ppermute | solution.py:519
  35.3 3.6 %collective-permute-start.5 = (f32[104,128]{1,0:T(8,128)S(1)}, f32[104,128]{1,0:T(8,128)S(1)}, u32[]{:S(2)}, u32[]{:S(2)}) collective-permute-start(f32[104,128]{1,0:T(8,128)S(1)} %add.18), channel_id=1, source_target_pairs={{0,3},{1,2},{2,1},{3,0},{4,7},{5,6},{6,5},{7,4},{8,11},{9,10},{10,... | collective-permute-start | bytes 159752 | tf_op jit(solution)/shard_map/ppermute | solution.py:519
  38.9 0.8 %collective-permute-start.3 = (f32[104,128]{1,0:T(8,128)S(1)}, f32[104,128]{1,0:T(8,128)S(1)}, u32[]{:S(2)}, u32[]{:S(2)}) collective-permute-start(f32[104,128]{1,0:T(8,128)S(1)} %add.18), channel_id=1, source_target_pairs={{0,1},{1,0},{2,3},{3,2},{4,5},{5,4},{6,7},{7,6},{8,9},{9,8},{10,11... | collective-permute-start | bytes 159752 | tf_op jit(solution)/shard_map/ppermute | solution.py:519
  39.7 3.6 %collective-permute-start.7 = (bf16[8,5760]{1,0:T(8,128)(2,1)S(1)}, bf16[8,5760]{1,0:T(8,128)(2,1)S(1)}, u32[]{:S(2)}, u32[]{:S(2)}) collective-permute-start(bf16[8,5760]{1,0:T(8,128)(2,1)S(1)} %get-tuple-element.37.part0), channel_id=1, source_target_pairs={{0,3},{1,2},{2,1},{3,0},{4,7},{5,6},{6,5},{7,4},{8,11},{9,10},{10,... | collective-permute-start | bytes 276488 | tf_op jit(solution)/shard_map/ppermute | solution.py:519
  43.3 1.9 %collective-permute-done.4 = f32[104,128]{1,0:T(8,128)S(1)} collective-permute-done((f32[104,128]{1,0:T(8,128)S(1)}, f32[104,128]{1,0:T(8,128)S(1)}, u32[]{:S(2)}, u32[]{:S(2)}) %collective-permute-start.4) | collective-permute-done | bytes 53280 | tf_op jit(solution)/shard_map/ppermute | solution.py:519
  45.2 2.5 %collective-permute-start.6 = (f32[104,128]{1,0:T(8,128)S(1)}, f32[104,128]{1,0:T(8,128)S(1)}, u32[]{:S(2)}, u32[]{:S(2)}) collective-permute-start(f32[104,128]{1,0:T(8,128)S(1)} %add_add_fusion), channel_id=1, source_target_pairs={{0,8},{4,12},{8,0},{12,4},{16,24},{20,28},{24,16},{28,20},{1,9},{5... | collective-permute-start | bytes 159752 | tf_op jit(solution)/shard_map/ppermute | solution.py:519
  47.7 1.2 %collective-permute-start.10 = (bf16[8,5760]{1,0:T(8,128)(2,1)S(1)}, bf16[8,5760]{1,0:T(8,128)(2,1)S(1)}, u32[]{:S(2)}, u32[]{:S(2)}) collective-permute-start(bf16[8,5760]{1,0:T(8,128)(2,1)S(1)} %get-tuple-element.37.part0), channel_id=1, source_target_pairs={{0,2},{1,3},{2,0},{3,1},{4,6},{5,7},{6,4},{7,5},{8,10},{9,11},{10,... | collective-permute-start | bytes 276488 | tf_op jit(solution)/shard_map/ppermute | solution.py:519
  48.9 0.9 %collective-permute-start.9 = (bf16[8,5760]{1,0:T(8,128)(2,1)S(1)}, bf16[8,5760]{1,0:T(8,128)(2,1)S(1)}, u32[]{:S(2)}, u32[]{:S(2)}) collective-permute-start(bf16[8,5760]{1,0:T(8,128)(2,1)S(1)} %get-tuple-element.37.part0), channel_id=1, source_target_pairs={{0,1},{1,0},{2,3},{3,2},{4,5},{5,4},{6,7},{7,6},{8,9},{9,8},{10,11... | collective-permute-start | bytes 276488 | tf_op jit(solution)/shard_map/ppermute | solution.py:519
  49.8 0.0 collective-permute-done.6
  49.9 2.0 %collective-permute-start.8 = (f32[104,128]{1,0:T(8,128)S(1)}, f32[104,128]{1,0:T(8,128)S(1)}, u32[]{:S(2)}, u32[]{:S(2)}) collective-permute-start(f32[104,128]{1,0:T(8,128)S(1)} %add.22), channel_id=1, source_target_pairs={{0,16},{4,20},{8,24},{12,28},{16,0},{20,4},{24,8},{28,12},{1,17},{... | collective-permute-start | bytes 159752 | tf_op jit(solution)/shard_map/ppermute | solution.py:519
  51.9 2.2 %collective-permute-done.8 = f32[104,128]{1,0:T(8,128)S(1)} collective-permute-done((f32[104,128]{1,0:T(8,128)S(1)}, f32[104,128]{1,0:T(8,128)S(1)}, u32[]{:S(2)}, u32[]{:S(2)}) %collective-permute-start.8) | collective-permute-done | bytes 53280 | tf_op jit(solution)/shard_map/ppermute | solution.py:519
  54.1 0.2 collective-permute-done.9.part1
  54.3 0.9 %place.1 = f32[1,8,23040]{2,1,0:T(8,128)} custom-call(bf16[8,5760]{1,0:T(8,128)(2,1)S(1)} %get-tuple-element.37.part0, bf16[8,5760]{1,0:T(8,128)(2,1)S(1)} %collective-permute-done.9.part1, bf16[8,5760]{1,0:T(8,128)(2,1)S(1)} %collective-permute-done.10.part2, bf16[8,5760]{1,0:T(8,128)(2,1)S(1)} %collective-permute-done.7.part3), custom_call_target="tpu_custom_call" | custom-call | tf_op jit(solution)/shard_map/place/pallas_call | solution.py:643
  55.2 0.3 collective-permute-done.11.other
  55.5 0.8 %taps.1 = (f32[3,3,32,64]{3,2,1,0:T(8,128)}, f32[3,3,16,32]{3,2,1,0:T(8,128)}) custom-call(f32[104,128]{1,0:T(8,128)S(1)} %add.23.mine, f32[104,128]{1,0:T(8,128)S(1)} %collective-permute-done.11.other), custom_call_target="tpu_custom_call" | custom-call | tf_op jit(solution)/shard_map/taps/pallas_call | solution.py:651
  (26 shorter events, 0.1 us)
Async XLA Ops:
  0.6 5.9 %copy-start.2 = (s32[32,48]{1,0:T(8,128)S(1)}, s32[32,48]{1,0:T(8,128)}, u32[]{:S(2)}) copy-start(s32[32,48]{1,0:T(8,128)} %land_hbm.1) | copy-start | bytes 18436
  0.6 5.9 %copy-start = (bf16[1,32,23040]{2,1,0:T(8,128)(2,1)S(1)}, bf16[1,32,23040]{2,1,0:T(8,128)(2,1)}, u32[]{:S(2)}) copy-start(bf16[1,32,23040]{2,1,0:T(8,128)(2,1)} %targets_hbm.1) | copy-start | bytes 4423684
  0.7 5.9 %copy-start.1 = (bf16[1,8,23040]{2,1,0:T(8,128)(2,1)S(1)}, bf16[1,8,23040]{2,1,0:T(8,128)(2,1)}, u32[]{:S(2)}) copy-start(bf16[1,8,23040]{2,1,0:T(8,128)(2,1)} %latent_hbm.1) | copy-start | bytes 1105924
  0.7 5.9 %copy-start.5 = (f32[16]{0:T(128)S(1)}, f32[16]{0:T(128)}, u32[]{:S(2)}) copy-start(f32[16]{0:T(128)} %channel_weight.3) | copy-start | bytes 196
  0.7 5.9 %copy-start.4 = (f32[64]{0:T(128)S(1)}, f32[64]{0:T(128)}, u32[]{:S(2)}) copy-start(f32[64]{0:T(128)} %scale.3) | copy-start | bytes 772
  0.7 5.9 %copy-start.3 = (s32[8]{0:T(128)S(1)}, s32[8]{0:T(128)}, u32[]{:S(2)}) copy-start(s32[8]{0:T(128)} %seeds.3) | copy-start | bytes 100
  0.7 8.0 %copy-start.7 = (bf16[3,3,32,16]{2,3,1,0:T(8,128)(2,1)S(1)}, bf16[3,3,32,16]{2,3,1,0:T(8,128)(2,1)}, u32[]{:S(2)}) copy-start(bf16[3,3,32,16]{2,3,1,0:T(8,128)(2,1)} %param.12) | copy-start | bytes 27652
  0.7 8.0 %copy-start.6 = (bf16[3,3,64,32]{2,3,1,0:T(8,128)(2,1)S(1)}, bf16[3,3,64,32]{2,3,1,0:T(8,128)(2,1)}, u32[]{:S(2)}) copy-start(bf16[3,3,64,32]{2,3,1,0:T(8,128)(2,1)} %param.11) | copy-start | bytes 110596
  2.9 7.8 %collective-permute-start = (bf16[50,8,128]{2,1,0:T(8,128)(2,1)}, bf16[50,8,128]{2,1,0:T(8,128)(2,1)S(1)}, u32[]{:S(2)}, u32[]{:S(2)}) collective-permute-start(bf16[50,8,128]{2,1,0:T(8,128)(2,1)} %get-tuple-element.29), channel_id=1, source_target_pairs={{0,4},{4,8},{8,12},{12,16},{16,20},{20,24},{24,28},{1,5},{5,9},{9,... | collective-permute-start | bytes 307208 | tf_op jit(solution)/shard_map/ppermute | solution.py:24
  5.2 5.4 %collective-permute-start.1 = (bf16[1,6400]{1,0:T(2,128)(2,1)}, bf16[1,6400]{1,0:T(2,128)(2,1)S(1)}, u32[]{:S(2)}, u32[]{:S(2)}) collective-permute-start(bf16[1,6400]{1,0:T(2,128)(2,1)} %get-tuple-element.30), channel_id=1, source_target_pairs={{4,0},{8,4},{12,8},{16,12},{20,16},{24,20},{28,24},{5,1},{9,5},{13... | collective-permute-start | bytes 38408 | tf_op jit(solution)/shard_map/ppermute | solution.py:24
  31.8 3.5 %collective-permute-start.2 = (f32[104,128]{1,0:T(8,128)S(1)}, f32[104,128]{1,0:T(8,128)S(1)}, u32[]{:S(2)}, u32[]{:S(2)}) collective-permute-start(f32[104,128]{1,0:T(8,128)S(1)} %get-tuple-element.39), channel_id=1, source_target_pairs={{0,4},{4,0},{8,12},{12,8},{16,20},{20,16},{24,28},{28,24},{1,5},{5... | collective-permute-start | bytes 159752 | tf_op jit(solution)/shard_map/ppermute | solution.py:519
  35.3 8.0 %collective-permute-start.5 = (f32[104,128]{1,0:T(8,128)S(1)}, f32[104,128]{1,0:T(8,128)S(1)}, u32[]{:S(2)}, u32[]{:S(2)}) collective-permute-start(f32[104,128]{1,0:T(8,128)S(1)} %add.18), channel_id=1, source_target_pairs={{0,3},{1,2},{2,1},{3,0},{4,7},{5,6},{6,5},{7,4},{8,11},{9,10},{10,... | collective-permute-start | bytes 159752 | tf_op jit(solution)/shard_map/ppermute | solution.py:519
  38.9 6.3 %collective-permute-start.4 = (f32[104,128]{1,0:T(8,128)S(1)}, f32[104,128]{1,0:T(8,128)S(1)}, u32[]{:S(2)}, u32[]{:S(2)}) collective-permute-start(f32[104,128]{1,0:T(8,128)S(1)} %add.18), channel_id=1, source_target_pairs={{0,2},{1,3},{2,0},{3,1},{4,6},{5,7},{6,4},{7,5},{8,10},{9,11},{10,... | collective-permute-start | bytes 159752 | tf_op jit(solution)/shard_map/ppermute | solution.py:519
  38.9 6.3 %collective-permute-start.3 = (f32[104,128]{1,0:T(8,128)S(1)}, f32[104,128]{1,0:T(8,128)S(1)}, u32[]{:S(2)}, u32[]{:S(2)}) collective-permute-start(f32[104,128]{1,0:T(8,128)S(1)} %add.18), channel_id=1, source_target_pairs={{0,1},{1,0},{2,3},{3,2},{4,5},{5,4},{6,7},{7,6},{8,9},{9,8},{10,11... | collective-permute-start | bytes 159752 | tf_op jit(solution)/shard_map/ppermute | solution.py:519
  39.7 10.1 %collective-permute-start.7 = (bf16[8,5760]{1,0:T(8,128)(2,1)S(1)}, bf16[8,5760]{1,0:T(8,128)(2,1)S(1)}, u32[]{:S(2)}, u32[]{:S(2)}) collective-permute-start(bf16[8,5760]{1,0:T(8,128)(2,1)S(1)} %get-tuple-element.37.part0), channel_id=1, source_target_pairs={{0,3},{1,2},{2,1},{3,0},{4,7},{5,6},{6,5},{7,4},{8,11},{9,10},{10,... | collective-permute-start | bytes 276488 | tf_op jit(solution)/shard_map/ppermute | solution.py:519
  45.2 4.6 %collective-permute-start.6 = (f32[104,128]{1,0:T(8,128)S(1)}, f32[104,128]{1,0:T(8,128)S(1)}, u32[]{:S(2)}, u32[]{:S(2)}) collective-permute-start(f32[104,128]{1,0:T(8,128)S(1)} %add_add_fusion), channel_id=1, source_target_pairs={{0,8},{4,12},{8,0},{12,4},{16,24},{20,28},{24,16},{28,20},{1,9},{5... | collective-permute-start | bytes 159752 | tf_op jit(solution)/shard_map/ppermute | solution.py:519
  47.7 6.4 %collective-permute-start.10 = (bf16[8,5760]{1,0:T(8,128)(2,1)S(1)}, bf16[8,5760]{1,0:T(8,128)(2,1)S(1)}, u32[]{:S(2)}, u32[]{:S(2)}) collective-permute-start(bf16[8,5760]{1,0:T(8,128)(2,1)S(1)} %get-tuple-element.37.part0), channel_id=1, source_target_pairs={{0,2},{1,3},{2,0},{3,1},{4,6},{5,7},{6,4},{7,5},{8,10},{9,11},{10,... | collective-permute-start | bytes 276488 | tf_op jit(solution)/shard_map/ppermute | solution.py:519
  48.9 5.4 %collective-permute-start.9 = (bf16[8,5760]{1,0:T(8,128)(2,1)S(1)}, bf16[8,5760]{1,0:T(8,128)(2,1)S(1)}, u32[]{:S(2)}, u32[]{:S(2)}) collective-permute-start(bf16[8,5760]{1,0:T(8,128)(2,1)S(1)} %get-tuple-element.37.part0), channel_id=1, source_target_pairs={{0,1},{1,0},{2,3},{3,2},{4,5},{5,4},{6,7},{7,6},{8,9},{9,8},{10,11... | collective-permute-start | bytes 276488 | tf_op jit(solution)/shard_map/ppermute | solution.py:519
  49.9 4.2 %collective-permute-start.8 = (f32[104,128]{1,0:T(8,128)S(1)}, f32[104,128]{1,0:T(8,128)S(1)}, u32[]{:S(2)}, u32[]{:S(2)}) collective-permute-start(f32[104,128]{1,0:T(8,128)S(1)} %add.22), channel_id=1, source_target_pairs={{0,16},{4,20},{8,24},{12,28},{16,0},{20,4},{24,8},{28,12},{1,17},{... | collective-permute-start | bytes 159752 | tf_op jit(solution)/shard_map/ppermute | solution.py:519
  54.3 1.2 %collective-permute-start.11 = (f32[104,128]{1,0:T(8,128)S(1)}, f32[104,128]{1,0:T(8,128)S(1)}, u32[]{:S(2)}, u32[]{:S(2)}) collective-permute-start(f32[104,128]{1,0:T(8,128)S(1)} %add.23.mine), channel_id=1, source_target_pairs={{0,4},{4,0},{8,12},{12,8},{16,20},{20,16},{24,28},{28,24},{1,5},{5... | collective-permute-start | bytes 159752 | tf_op jit(solution)/shard_map/ppermute | solution.py:519

commit v12 on v11

--- a/solution.py
+++ b/solution.py
@@ -374,22 +374,25 @@
             [piece(i, start), piece(i + 1, start), piece(i, start + 1), piece(i + 1, start + 1)], axis=1
         )
 
-    def first_product(i, pre):
-        pre[...] = jnp.dot(operand(source, i, 0, wide), band_one[...], preferred_element_type=f32)
-
-    def first_gelu(i, pre):
-        for t in range(wide):
-            for sub in range(2):
-                x = pre[t * 16 : (t + 1) * 16, sub * LANES : (sub + 1) * LANES]
-                square = x * x
-                th = jnp.tanh(x * (GELU_A + (GELU_A * GELU_B) * square))
-                plus = 0.5 + 0.5 * th
-                act[2 * i + sub, t] = (x * plus).astype(bf16)
-                if t < front:
-                    d = plus + (x * plus) * (1.0 - th) * (GELU_A + (3.0 * GELU_A * GELU_B) * square)
-                    if t == half:
-                        d = jnp.where(iota((16, LANES), 0) < 8, d, 0.0)
-                    slope[2 * i + sub, t] = d
+    def first_product(pair, pre):
+        taken = jnp.concatenate([operand(source, 2 * pair + k, 0, wide) for k in range(2)], axis=0)
+        pre[...] = jnp.dot(taken, band_one[...], preferred_element_type=f32)
+
+    def first_gelu(pair, pre):
+        for k in range(2):
+            for t in range(wide):
+                for sub in range(2):
+                    at = (k * wide + t) * 16
+                    x = pre[at : at + 16, sub * LANES : (sub + 1) * LANES]
+                    square = x * x
+                    th = jnp.tanh(x * (GELU_A + (GELU_A * GELU_B) * square))
+                    plus = 0.5 + 0.5 * th
+                    act[4 * pair + 2 * k + sub, t] = (x * plus).astype(bf16)
+                    if t < front:
+                        d = plus + (x * plus) * (1.0 - th) * (GELU_A + (3.0 * GELU_A * GELU_B) * square)
+                        if t == half:
+                            d = jnp.where(iota((16, LANES), 0) < 8, d, 0.0)
+                        slope[4 * pair + 2 * k + sub, t] = d
 
     def first_segment(m, _):
         first_product(2 * m + 1, pre_odd)
@@ -399,7 +402,8 @@
         return 0
 
     first_product(0, pre_even)
-    lax.fori_loop(0, rows // 2 + 1, first_segment, 0)
+    lax.fori_loop(0, rows // 4, first_segment, 0)
+    first_gelu(rows // 2, pre_even)
 
     members = front * 16
     owner = iota((48, members), 0)
@@ -411,11 +415,13 @@
     pick = jnp.concatenate([pick_own, pick_prev], axis=0)
 
     def second_product(n, cast):
+        taken = jnp.concatenate([operand(act, 2 * n + k, 0, front) for k in range(2)], axis=0)
+        out = jnp.dot(taken, band_two[...], preferred_element_type=f32).astype(bf16)
         for k in range(2):
-            out = jnp.dot(operand(act, 2 * n + k, 0, front), band_two[...], preferred_element_type=f32).astype(bf16)
             for sub in range(2):
-                cast[2 * k + sub] = out[:, sub * LANES : (sub + 1) * LANES].reshape(front, 16, LANES)
-            yield
+                part = out[k * members : (k + 1) * members, sub * LANES : (sub + 1) * LANES]
+                cast[2 * k + sub] = part.reshape(front, 16, LANES)
+        yield
 
     def loss_gradient(cast, fgrad, aim_ref, weight_ref, first, lines):
         for line in lines:
@@ -456,14 +462,21 @@
             last = jnp.concatenate(last, axis=0)
             acc_next[...] += jnp.dot(last, x[:, 256:], preferred_element_type=f32)
 
-        grads = []
-        for k in range(2):
-            g = [flat(2 * k, 1, front), flat(2 * k + 1, 1, front), flat(2 * k, 0, front), flat(2 * k + 1, 0, front)]
-            pulled = jnp.dot(jnp.concatenate(g, axis=1), back_two[...], preferred_element_type=f32)
-            grad = pulled[:, :LANES] + carry[...]
-            carry[...] = pulled[:, LANES:]
-            grads.append((grad * slope[2 * n + k].reshape(members, LANES)).astype(bf16))
-            yield
+        g = [
+            jnp.concatenate(
+                [flat(2 * k, 1, front), flat(2 * k + 1, 1, front), flat(2 * k, 0, front), flat(2 * k + 1, 0, front)],
+                axis=1,
+            )
+            for k in range(2)
+        ]
+        pulled = jnp.dot(jnp.concatenate(g, axis=0), back_two[...], preferred_element_type=f32)
+        grads = [
+            pulled[:members, :LANES] + carry[...],
+            pulled[members:, :LANES] + pulled[:members, LANES:],
+        ]
+        carry[...] = pulled[members:, LANES:]
+        grads = [(grads[k] * slope[2 * n + k].reshape(members, LANES)).astype(bf16) for k in range(2)]
+        yield
         grads = jnp.concatenate(grads, axis=1)
         g = [jnp.concatenate([flat(2 * k, 2, half), flat(2 * k + 1, 2, half)], axis=1) for k in range(2)]
         x = [operand(act, 2 * n + k, 1, half) for k in range(2)]
@@ -520,8 +533,8 @@
 
 
 def total(array, axis, first, second):
-    one, two, three = (swapped(array, axis, k) for k in (first, second, first ^ second))
-    return (array + one) + (two + three)
+    one, two, three = (swapped(array, axis, k).astype(jnp.float32) for k in (first, second, first ^ second))
+    return (array.astype(jnp.float32) + one) + (two + three)
 
 
 def local(
@@ -532,7 +545,7 @@
     lat_count = lax.axis_size("lat")
     own = span // LANES // lax.axis_size("mem")
     half = (own + 1) // 2
-    assert sample_count == 1 and member_seeds.shape[0] == MEM and rows % 2 == 0 and own % 2 == 1 and lax.axis_size("mem") == 4
+    assert sample_count == 1 and member_seeds.shape[0] == MEM and rows % 4 == 0 and own % 2 == 1 and lax.axis_size("mem") == 4
     assert 4 * chan2 == 2 * chan1 == chan0 and chan0 == 64
     vmem = pl.BlockSpec(memory_space=pltpu.VMEM)
     smem = pl.BlockSpec(memory_space=pltpu.SMEM)
@@ -600,8 +613,8 @@
             pltpu.VMEM((2 * front, 8, LANES), f32),
             pltpu.VMEM((2 * front, 8, LANES), f32),
             pltpu.VMEM((rows + 4, wide + 1, 16, LANES), bf16),
-            pltpu.VMEM((wide * 16, 2 * LANES), f32),
-            pltpu.VMEM((wide * 16, 2 * LANES), f32),
+            pltpu.VMEM((wide * 32, 2 * LANES), f32),
+            pltpu.VMEM((wide * 32, 2 * LANES), f32),
             pltpu.VMEM((2 * rows + 4, wide, 16, LANES), bf16),
             pltpu.VMEM((2 * rows + 4, front, 16, LANES), f32),
             pltpu.VMEM((4, front, 16, LANES), bf16),
@@ -630,7 +643,7 @@
         below,
         *bands,
     )
-    taps = taps + swapped(taps_send, "lat", 1)
+    taps = (taps + swapped(taps_send, "lat", 1)).astype(bf16)
     taps = total(taps, "mem", 1, 2)
     one, two, three = (swapped(lat_grad, "mem", k) for k in range(1, 4))
     bits = [1 << k for k in range(1, lat_count.bit_length() - 1)]

time: 56.5 us -> 55.7 us (0.986)
  waiting for transfers between devices: 7.06 us -> 5.78 us
    ppermute x10, waiting for transfers between devices: 5.48 us -> 4.19 us  [swapped(): lax.ppermute(array, axis, [(i, i ^ bit) for i in range(lax.axis_size(axis...]
where the time goes in v12:
time: 55.7 us; the launch traced here: 55.5 us
  Pallas kernels  27.4 us (49%)
  starting transfers between devices  21.4 us (38%)
  waiting for transfers between devices  5.78 us (10%)
  between operations  0.85 us (2%)
    pallas_call x1, Pallas kernels, local(): pl.pallas_call(functools.partial(band_kernel, half, (chan0, chan1, chan2)...  21.1 us
    ppermute x10, starting transfers between devices, swapped(): lax.ppermute(array, axis, [(i, i ^ bit) for i in range(lax.axis_size(axis...  17.8 us
    ppermute x10, waiting for transfers between devices, swapped(): lax.ppermute(array, axis, [(i, i ^ bit) for i in range(lax.axis_size(axis...  4.19 us
    ppermute x2, starting transfers between devices, shifted(): return lax.ppermute(array, axis, pairs)  3.65 us
    pallas_call x1, Pallas kernels, local(): pl.pallas_call(functools.partial(prepare_kernel, half, chan0, chan2), in_...  2.13 us
    pallas_call x1, Pallas kernels, local(): pl.pallas_call(functools.partial(edge_kernel, half, chan2), in_specs=[hbm...  2.13 us
    ppermute x2, waiting for transfers between devices, shifted(): return lax.ppermute(array, axis, pairs)  1.58 us
  transfers between devices with their start and end apart: 12, of which 6 were waited for; matrix products, arithmetic and copies ran while one was open for 0% of the time, Pallas kernels for 6%

profile of v12, /device:TPU:0, one launch (start us, length us, event | category | flops | bytes accessed | tf_op | source)
XLA Modules:
  0.0 55.5 jit_solution(13431287119650293485)
XLA Ops:
  0.7 2.1 %edges.1 = (bf16[50,8,128]{2,1,0:T(8,128)(2,1)}, bf16[1,6400]{1,0:T(2,128)(2,1)}) custom-call(bf16[1,8,23040]{2,1,0:T(8,128)(2,1)} %latent_hbm.1, bf16[1,32,23040]{2,1,0:T(8,128)(2,1)} %targets_hbm.1, s32[32,48]{1,0:T(8,128)} %land_hbm.1), custom_call_target="tpu_custom_call" | custom-call | tf_op jit(solution)/shard_map/edges/pallas_call | solution.py:559
  2.9 2.4 %collective-permute-start = (bf16[50,8,128]{2,1,0:T(8,128)(2,1)}, bf16[50,8,128]{2,1,0:T(8,128)(2,1)S(1)}, u32[]{:S(2)}, u32[]{:S(2)}) collective-permute-start(bf16[50,8,128]{2,1,0:T(8,128)(2,1)} %get-tuple-element.29), channel_id=1, source_target_pairs={{0,4},{4,8},{8,12},{12,16},{16,20},{20,24},{24,28},{1,5},{5,9},{9,... | collective-permute-start | bytes 307208 | tf_op jit(solution)/shard_map/ppermute | solution.py:24
  5.2 1.3 %collective-permute-start.1 = (bf16[1,6400]{1,0:T(2,128)(2,1)}, bf16[1,6400]{1,0:T(2,128)(2,1)S(1)}, u32[]{:S(2)}, u32[]{:S(2)}) collective-permute-start(bf16[1,6400]{1,0:T(2,128)(2,1)} %get-tuple-element.30), channel_id=1, source_target_pairs={{4,0},{8,4},{12,8},{16,12},{20,16},{24,20},{28,24},{5,1},{9,5},{13... | collective-permute-start | bytes 38408 | tf_op jit(solution)/shard_map/ppermute | solution.py:24
  6.6 2.1 %prepare.1 = (bf16[8,25,16,128]{3,2,1,0:T(8,128)(2,1)S(1)}, f32[48,32,128]{2,1,0:T(8,128)S(1)}, f32[48,32,128]{2,1,0:T(8,128)S(1)}) custom-call(s32[8]{0:T(128)S(1)} %copy-done.3, f32[64]{0:T(128)S(1)} %copy-done.4, f32[16]{0:T(128)S(1)} %copy-done.5, bf16[1,8,23040]{2,1,0:T(8,128)(2,1)S(1)} %copy-done.1, bf16[1,32,23040]{2,1,0:T(8,128)(2,1)S(1)} %copy-done, ...), custom_call_target="tpu_custom_call" | custom-call | flops 100000000 | bytes 10000000 | tf_op jit(solution)/shard_map/prepare/pallas_call | solution.py:579
  8.7 0.3 bands.1
  9.0 1.6 %collective-permute-done.1.below = bf16[1,6400]{1,0:T(2,128)(2,1)S(1)} collective-permute-done((bf16[1,6400]{1,0:T(2,128)(2,1)}, bf16[1,6400]{1,0:T(2,128)(2,1)S(1)}, u32[]{:S(2)}, u32[]{:S(2)}) %collective-permute-start.1) | collective-permute-done | bytes 12832 | tf_op jit(solution)/shard_map/ppermute | solution.py:24
  10.6 0.0 collective-permute-done.above
  10.6 21.1 %band.1 = (bf16[8,5760]{1,0:T(8,128)(2,1)S(1)}, f32[104,128]{1,0:T(8,128)S(1)}, f32[104,128]{1,0:T(8,128)S(1)}) custom-call(s32[8]{0:T(128)S(1)} %copy-done.3, f32[64]{0:T(128)S(1)} %copy-done.4, f32[16]{0:T(128)S(1)} %copy-done.5, bf16[8,25,16,128]{3,2,1,0:T(8,128)(2,1)S(1)} %get-tuple-element.26.own_source, f32[48,32,128]{2,1,0:T(8,128)S(1)} %get-tuple-element.27.aims, ...), custom_call_target="tpu_custom_call" | custom-call | tf_op jit(solution)/shard_map/band/pallas_call | solution.py:602
  31.7 2.6 %collective-permute-start.2 = (f32[104,128]{1,0:T(8,128)S(1)}, f32[104,128]{1,0:T(8,128)S(1)}, u32[]{:S(2)}, u32[]{:S(2)}) collective-permute-start(f32[104,128]{1,0:T(8,128)S(1)} %get-tuple-element.39), channel_id=1, source_target_pairs={{0,4},{4,0},{8,12},{12,8},{16,20},{20,16},{24,28},{28,24},{1,5},{5... | collective-permute-start | bytes 159752 | tf_op jit(solution)/shard_map/ppermute | solution.py:532
  34.4 0.9 %collective-permute-done.2 = f32[104,128]{1,0:T(8,128)S(1)} collective-permute-done((f32[104,128]{1,0:T(8,128)S(1)}, f32[104,128]{1,0:T(8,128)S(1)}, u32[]{:S(2)}, u32[]{:S(2)}) %collective-permute-start.2) | collective-permute-done | bytes 53280 | tf_op jit(solution)/shard_map/ppermute | solution.py:532
  35.3 3.7 %collective-permute-start.5 = (bf16[104,128]{1,0:T(8,128)(2,1)S(1)}, bf16[104,128]{1,0:T(8,128)(2,1)S(1)}, u32[]{:S(2)}, u32[]{:S(2)}) collective-permute-start(bf16[104,128]{1,0:T(8,128)(2,1)S(1)} %add_convert_fusion), channel_id=1, source_target_pairs={{0,3},{1,2},{2,1},{3,0},{4,7},{5,6},{6,5},{7,4},{8,11},{9,10},{10,... | collective-permute-start | bytes 79880 | tf_op jit(solution)/shard_map/ppermute | solution.py:532
  38.9 0.8 %collective-permute-start.3 = (bf16[104,128]{1,0:T(8,128)(2,1)S(1)}, bf16[104,128]{1,0:T(8,128)(2,1)S(1)}, u32[]{:S(2)}, u32[]{:S(2)}) collective-permute-start(bf16[104,128]{1,0:T(8,128)(2,1)S(1)} %add_convert_fusion), channel_id=1, source_target_pairs={{0,1},{1,0},{2,3},{3,2},{4,5},{5,4},{6,7},{7,6},{8,9},{9,8},{10,11... | collective-permute-start | bytes 79880 | tf_op jit(solution)/shard_map/ppermute | solution.py:532
  39.7 3.6 %collective-permute-start.7 = (bf16[8,5760]{1,0:T(8,128)(2,1)S(1)}, bf16[8,5760]{1,0:T(8,128)(2,1)S(1)}, u32[]{:S(2)}, u32[]{:S(2)}) collective-permute-start(bf16[8,5760]{1,0:T(8,128)(2,1)S(1)} %get-tuple-element.37.part0), channel_id=1, source_target_pairs={{0,3},{1,2},{2,1},{3,0},{4,7},{5,6},{6,5},{7,4},{8,11},{9,10},{10,... | collective-permute-start | bytes 276488 | tf_op jit(solution)/shard_map/ppermute | solution.py:532
  43.3 0.6 %collective-permute-done.4 = bf16[104,128]{1,0:T(8,128)(2,1)S(1)} collective-permute-done((bf16[104,128]{1,0:T(8,128)(2,1)S(1)}, bf16[104,128]{1,0:T(8,128)(2,1)S(1)}, u32[]{:S(2)}, u32[]{:S(2)}) %collective-permute-start.4) | collective-permute-done | bytes 26656 | tf_op jit(solution)/shard_map/ppermute | solution.py:532
  43.9 0.0 collective-permute-done.3
  44.0 2.5 %collective-permute-start.6 = (f32[104,128]{1,0:T(8,128)S(1)}, f32[104,128]{1,0:T(8,128)S(1)}, u32[]{:S(2)}, u32[]{:S(2)}) collective-permute-start(f32[104,128]{1,0:T(8,128)S(1)} %add_add_fusion), channel_id=1, source_target_pairs={{0,8},{4,12},{8,0},{12,4},{16,24},{20,28},{24,16},{28,20},{1,9},{5... | collective-permute-start | bytes 159752 | tf_op jit(solution)/shard_map/ppermute | solution.py:532
  46.4 1.9 %collective-permute-start.10 = (bf16[8,5760]{1,0:T(8,128)(2,1)S(1)}, bf16[8,5760]{1,0:T(8,128)(2,1)S(1)}, u32[]{:S(2)}, u32[]{:S(2)}) collective-permute-start(bf16[8,5760]{1,0:T(8,128)(2,1)S(1)} %get-tuple-element.37.part0), channel_id=1, source_target_pairs={{0,2},{1,3},{2,0},{3,1},{4,6},{5,7},{6,4},{7,5},{8,10},{9,11},{10,... | collective-permute-start | bytes 276488 | tf_op jit(solution)/shard_map/ppermute | solution.py:532
  48.3 0.3 collective-permute-done.6
  48.6 2.7 %collective-permute-start.8 = (f32[104,128]{1,0:T(8,128)S(1)}, f32[104,128]{1,0:T(8,128)S(1)}, u32[]{:S(2)}, u32[]{:S(2)}) collective-permute-start(f32[104,128]{1,0:T(8,128)S(1)} %add.22), channel_id=1, source_target_pairs={{0,16},{4,20},{8,24},{12,28},{16,0},{20,4},{24,8},{28,12},{1,17},{... | collective-permute-start | bytes 159752 | tf_op jit(solution)/shard_map/ppermute | solution.py:532
  51.3 2.1 %collective-permute-done.8 = f32[104,128]{1,0:T(8,128)S(1)} collective-permute-done((f32[104,128]{1,0:T(8,128)S(1)}, f32[104,128]{1,0:T(8,128)S(1)}, u32[]{:S(2)}, u32[]{:S(2)}) %collective-permute-start.8) | collective-permute-done | bytes 53280 | tf_op jit(solution)/shard_map/ppermute | solution.py:532
  53.4 0.1 collective-permute-start.11
  53.5 0.9 %place.1 = f32[1,8,23040]{2,1,0:T(8,128)} custom-call(bf16[8,5760]{1,0:T(8,128)(2,1)S(1)} %get-tuple-element.37.part0, bf16[8,5760]{1,0:T(8,128)(2,1)S(1)} %collective-permute-done.9.part1, bf16[8,5760]{1,0:T(8,128)(2,1)S(1)} %collective-permute-done.10.part2, bf16[8,5760]{1,0:T(8,128)(2,1)S(1)} %collective-permute-done.7.part3), custom_call_target="tpu_custom_call" | custom-call | tf_op jit(solution)/shard_map/place/pallas_call | solution.py:656
  54.4 0.3 collective-permute-done.11.other
  54.7 0.8 %taps.1 = (f32[3,3,32,64]{3,2,1,0:T(8,128)}, f32[3,3,16,32]{3,2,1,0:T(8,128)}) custom-call(f32[104,128]{1,0:T(8,128)S(1)} %add.23.mine, f32[104,128]{1,0:T(8,128)S(1)} %collective-permute-done.11.other), custom_call_target="tpu_custom_call" | custom-call | tf_op jit(solution)/shard_map/taps/pallas_call | solution.py:664
  (26 shorter events, 0.1 us)
Async XLA Ops:
  0.6 5.9 %copy-start.2 = (s32[32,48]{1,0:T(8,128)S(1)}, s32[32,48]{1,0:T(8,128)}, u32[]{:S(2)}) copy-start(s32[32,48]{1,0:T(8,128)} %land_hbm.1) | copy-start | bytes 18436
  0.6 5.9 %copy-start = (bf16[1,32,23040]{2,1,0:T(8,128)(2,1)S(1)}, bf16[1,32,23040]{2,1,0:T(8,128)(2,1)}, u32[]{:S(2)}) copy-start(bf16[1,32,23040]{2,1,0:T(8,128)(2,1)} %targets_hbm.1) | copy-start | bytes 4423684
  0.7 5.9 %copy-start.1 = (bf16[1,8,23040]{2,1,0:T(8,128)(2,1)S(1)}, bf16[1,8,23040]{2,1,0:T(8,128)(2,1)}, u32[]{:S(2)}) copy-start(bf16[1,8,23040]{2,1,0:T(8,128)(2,1)} %latent_hbm.1) | copy-start | bytes 1105924
  0.7 5.9 %copy-start.5 = (f32[16]{0:T(128)S(1)}, f32[16]{0:T(128)}, u32[]{:S(2)}) copy-start(f32[16]{0:T(128)} %channel_weight.3) | copy-start | bytes 196
  0.7 5.9 %copy-start.4 = (f32[64]{0:T(128)S(1)}, f32[64]{0:T(128)}, u32[]{:S(2)}) copy-start(f32[64]{0:T(128)} %scale.3) | copy-start | bytes 772
  0.7 5.9 %copy-start.3 = (s32[8]{0:T(128)S(1)}, s32[8]{0:T(128)}, u32[]{:S(2)}) copy-start(s32[8]{0:T(128)} %seeds.3) | copy-start | bytes 100
  0.7 8.0 %copy-start.7 = (bf16[3,3,32,16]{2,3,1,0:T(8,128)(2,1)S(1)}, bf16[3,3,32,16]{2,3,1,0:T(8,128)(2,1)}, u32[]{:S(2)}) copy-start(bf16[3,3,32,16]{2,3,1,0:T(8,128)(2,1)} %param.12) | copy-start | bytes 27652
  0.7 8.0 %copy-start.6 = (bf16[3,3,64,32]{2,3,1,0:T(8,128)(2,1)S(1)}, bf16[3,3,64,32]{2,3,1,0:T(8,128)(2,1)}, u32[]{:S(2)}) copy-start(bf16[3,3,64,32]{2,3,1,0:T(8,128)(2,1)} %param.11) | copy-start | bytes 110596
  2.9 7.8 %collective-permute-start = (bf16[50,8,128]{2,1,0:T(8,128)(2,1)}, bf16[50,8,128]{2,1,0:T(8,128)(2,1)S(1)}, u32[]{:S(2)}, u32[]{:S(2)}) collective-permute-start(bf16[50,8,128]{2,1,0:T(8,128)(2,1)} %get-tuple-element.29), channel_id=1, source_target_pairs={{0,4},{4,8},{8,12},{12,16},{16,20},{20,24},{24,28},{1,5},{5,9},{9,... | collective-permute-start | bytes 307208 | tf_op jit(solution)/shard_map/ppermute | solution.py:24
  5.2 5.4 %collective-permute-start.1 = (bf16[1,6400]{1,0:T(2,128)(2,1)}, bf16[1,6400]{1,0:T(2,128)(2,1)S(1)}, u32[]{:S(2)}, u32[]{:S(2)}) collective-permute-start(bf16[1,6400]{1,0:T(2,128)(2,1)} %get-tuple-element.30), channel_id=1, source_target_pairs={{4,0},{8,4},{12,8},{16,12},{20,16},{24,20},{28,24},{5,1},{9,5},{13... | collective-permute-start | bytes 38408 | tf_op jit(solution)/shard_map/ppermute | solution.py:24
  31.7 3.5 %collective-permute-start.2 = (f32[104,128]{1,0:T(8,128)S(1)}, f32[104,128]{1,0:T(8,128)S(1)}, u32[]{:S(2)}, u32[]{:S(2)}) collective-permute-start(f32[104,128]{1,0:T(8,128)S(1)} %get-tuple-element.39), channel_id=1, source_target_pairs={{0,4},{4,0},{8,12},{12,8},{16,20},{20,16},{24,28},{28,24},{1,5},{5... | collective-permute-start | bytes 159752 | tf_op jit(solution)/shard_map/ppermute | solution.py:532
  35.3 8.1 %collective-permute-start.5 = (bf16[104,128]{1,0:T(8,128)(2,1)S(1)}, bf16[104,128]{1,0:T(8,128)(2,1)S(1)}, u32[]{:S(2)}, u32[]{:S(2)}) collective-permute-start(bf16[104,128]{1,0:T(8,128)(2,1)S(1)} %add_convert_fusion), channel_id=1, source_target_pairs={{0,3},{1,2},{2,1},{3,0},{4,7},{5,6},{6,5},{7,4},{8,11},{9,10},{10,... | collective-permute-start | bytes 79880 | tf_op jit(solution)/shard_map/ppermute | solution.py:532
  38.9 5.0 %collective-permute-start.4 = (bf16[104,128]{1,0:T(8,128)(2,1)S(1)}, bf16[104,128]{1,0:T(8,128)(2,1)S(1)}, u32[]{:S(2)}, u32[]{:S(2)}) collective-permute-start(bf16[104,128]{1,0:T(8,128)(2,1)S(1)} %add_convert_fusion), channel_id=1, source_target_pairs={{0,2},{1,3},{2,0},{3,1},{4,6},{5,7},{6,4},{7,5},{8,10},{9,11},{10,... | collective-permute-start | bytes 79880 | tf_op jit(solution)/shard_map/ppermute | solution.py:532
  38.9 5.0 %collective-permute-start.3 = (bf16[104,128]{1,0:T(8,128)(2,1)S(1)}, bf16[104,128]{1,0:T(8,128)(2,1)S(1)}, u32[]{:S(2)}, u32[]{:S(2)}) collective-permute-start(bf16[104,128]{1,0:T(8,128)(2,1)S(1)} %add_convert_fusion), channel_id=1, source_target_pairs={{0,1},{1,0},{2,3},{3,2},{4,5},{5,4},{6,7},{7,6},{8,9},{9,8},{10,11... | collective-permute-start | bytes 79880 | tf_op jit(solution)/shard_map/ppermute | solution.py:532
  39.7 8.8 %collective-permute-start.7 = (bf16[8,5760]{1,0:T(8,128)(2,1)S(1)}, bf16[8,5760]{1,0:T(8,128)(2,1)S(1)}, u32[]{:S(2)}, u32[]{:S(2)}) collective-permute-start(bf16[8,5760]{1,0:T(8,128)(2,1)S(1)} %get-tuple-element.37.part0), channel_id=1, source_target_pairs={{0,3},{1,2},{2,1},{3,0},{4,7},{5,6},{6,5},{7,4},{8,11},{9,10},{10,... | collective-permute-start | bytes 276488 | tf_op jit(solution)/shard_map/ppermute | solution.py:532
  44.0 4.6 %collective-permute-start.6 = (f32[104,128]{1,0:T(8,128)S(1)}, f32[104,128]{1,0:T(8,128)S(1)}, u32[]{:S(2)}, u32[]{:S(2)}) collective-permute-start(f32[104,128]{1,0:T(8,128)S(1)} %add_add_fusion), channel_id=1, source_target_pairs={{0,8},{4,12},{8,0},{12,4},{16,24},{20,28},{24,16},{28,20},{1,9},{5... | collective-permute-start | bytes 159752 | tf_op jit(solution)/shard_map/ppermute | solution.py:532
  46.4 7.0 %collective-permute-start.10 = (bf16[8,5760]{1,0:T(8,128)(2,1)S(1)}, bf16[8,5760]{1,0:T(8,128)(2,1)S(1)}, u32[]{:S(2)}, u32[]{:S(2)}) collective-permute-start(bf16[8,5760]{1,0:T(8,128)(2,1)S(1)} %get-tuple-element.37.part0), channel_id=1, source_target_pairs={{0,2},{1,3},{2,0},{3,1},{4,6},{5,7},{6,4},{7,5},{8,10},{9,11},{10,... | collective-permute-start | bytes 276488 | tf_op jit(solution)/shard_map/ppermute | solution.py:532
  48.3 5.1 %collective-permute-start.9 = (bf16[8,5760]{1,0:T(8,128)(2,1)S(1)}, bf16[8,5760]{1,0:T(8,128)(2,1)S(1)}, u32[]{:S(2)}, u32[]{:S(2)}) collective-permute-start(bf16[8,5760]{1,0:T(8,128)(2,1)S(1)} %get-tuple-element.37.part0), channel_id=1, source_target_pairs={{0,1},{1,0},{2,3},{3,2},{4,5},{5,4},{6,7},{7,6},{8,9},{9,8},{10,11... | collective-permute-start | bytes 276488 | tf_op jit(solution)/shard_map/ppermute | solution.py:532
  48.6 4.8 %collective-permute-start.8 = (f32[104,128]{1,0:T(8,128)S(1)}, f32[104,128]{1,0:T(8,128)S(1)}, u32[]{:S(2)}, u32[]{:S(2)}) collective-permute-start(f32[104,128]{1,0:T(8,128)S(1)} %add.22), channel_id=1, source_target_pairs={{0,16},{4,20},{8,24},{12,28},{16,0},{20,4},{24,8},{28,12},{1,17},{... | collective-permute-start | bytes 159752 | tf_op jit(solution)/shard_map/ppermute | solution.py:532
  53.4 1.3 %collective-permute-start.11 = (f32[104,128]{1,0:T(8,128)S(1)}, f32[104,128]{1,0:T(8,128)S(1)}, u32[]{:S(2)}, u32[]{:S(2)}) collective-permute-start(f32[104,128]{1,0:T(8,128)S(1)} %add.23.mine), channel_id=1, source_target_pairs={{0,4},{4,0},{8,12},{12,8},{16,20},{20,16},{24,28},{28,24},{1,5},{5... | collective-permute-start | bytes 159752 | tf_op jit(solution)/shard_map/ppermute | solution.py:532

commit v13 on v11

--- a/solution.py
+++ b/solution.py
@@ -309,10 +309,10 @@
     pre_odd,
     act,
     slope,
-    cast_even,
-    cast_odd,
-    fgrad_even,
-    fgrad_odd,
+    cast_now,
+    cast_next,
+    fgrad_now,
+    fgrad_next,
     carry,
     carry_lat,
     lat_lines,
@@ -344,9 +344,8 @@
 
     source[rows + 2 :] = jnp.zeros((2,) + source.shape[1:], bf16)
     source[:, wide] = jnp.zeros((source.shape[0],) + source.shape[2:], bf16)
-    fgrad_even[0] = jnp.zeros(fgrad_even.shape[1:], bf16)
-    for fgrad in (fgrad_even, fgrad_odd):
-        fgrad[:, 0] = jnp.zeros((4,) + fgrad.shape[2:], bf16)
+    fgrad_next[0] = jnp.zeros(fgrad_next.shape[1:], bf16)
+    fgrad_next[:, 0] = jnp.zeros((4,) + fgrad_next.shape[2:], bf16)
     carry[...] = jnp.zeros(carry.shape, f32)
     carry_lat[...] = jnp.zeros(carry_lat.shape, f32)
     for acc in (acc_one, acc_one_next, acc_two, acc_two_next):
@@ -411,11 +410,13 @@
     pick = jnp.concatenate([pick_own, pick_prev], axis=0)
 
     def second_product(n, cast):
+        taken = jnp.concatenate([operand(act, 2 * n + k, 0, front) for k in range(2)], axis=0)
+        out = jnp.dot(taken, band_two[...], preferred_element_type=f32).astype(bf16)
         for k in range(2):
-            out = jnp.dot(operand(act, 2 * n + k, 0, front), band_two[...], preferred_element_type=f32).astype(bf16)
             for sub in range(2):
-                cast[2 * k + sub] = out[:, sub * LANES : (sub + 1) * LANES].reshape(front, 16, LANES)
-            yield
+                part = out[k * members : (k + 1) * members, sub * LANES : (sub + 1) * LANES]
+                cast[2 * k + sub] = part.reshape(front, 16, LANES)
+        yield
 
     def loss_gradient(cast, fgrad, aim_ref, weight_ref, first, lines):
         for line in lines:
@@ -456,14 +457,21 @@
             last = jnp.concatenate(last, axis=0)
             acc_next[...] += jnp.dot(last, x[:, 256:], preferred_element_type=f32)
 
-        grads = []
-        for k in range(2):
-            g = [flat(2 * k, 1, front), flat(2 * k + 1, 1, front), flat(2 * k, 0, front), flat(2 * k + 1, 0, front)]
-            pulled = jnp.dot(jnp.concatenate(g, axis=1), back_two[...], preferred_element_type=f32)
-            grad = pulled[:, :LANES] + carry[...]
-            carry[...] = pulled[:, LANES:]
-            grads.append((grad * slope[2 * n + k].reshape(members, LANES)).astype(bf16))
-            yield
+        g = [
+            jnp.concatenate(
+                [flat(2 * k, 1, front), flat(2 * k + 1, 1, front), flat(2 * k, 0, front), flat(2 * k + 1, 0, front)],
+                axis=1,
+            )
+            for k in range(2)
+        ]
+        pulled = jnp.dot(jnp.concatenate(g, axis=0), back_two[...], preferred_element_type=f32)
+        grads = [
+            pulled[:members, :LANES] + carry[...],
+            pulled[members:, :LANES] + pulled[:members, LANES:],
+        ]
+        carry[...] = pulled[members:, LANES:]
+        grads = [(grads[k] * slope[2 * n + k].reshape(members, LANES)).astype(bf16) for k in range(2)]
+        yield
         grads = jnp.concatenate(grads, axis=1)
         g = [jnp.concatenate([flat(2 * k, 2, half), flat(2 * k + 1, 2, half)], axis=1) for k in range(2)]
         x = [operand(act, 2 * n + k, 1, half) for k in range(2)]
@@ -481,29 +489,23 @@
         carry_lat[...] = z[:, LANES:]
         yield
 
-    def own_gradient(n, cast, fgrad):
-        return loss_gradient(cast, fgrad, aims, weights, 4 * (n - 1), range(4))
-
-    def second_segment(m, _):
+    def second_segment(k, _):
+        cast_now[...] = cast_next[...]
+        fgrad_now[...] = fgrad_next[...]
         take_turns(
-            second_product(2 * m + 2, cast_even),
-            own_gradient(2 * m + 1, cast_odd, fgrad_odd),
-            pull_back(2 * m, fgrad_even),
-        )
-        take_turns(
-            second_product(jnp.minimum(2 * m + 3, rows), cast_odd),
-            own_gradient(2 * m + 2, cast_even, fgrad_even),
-            pull_back(2 * m + 1, fgrad_odd),
+            second_product(jnp.minimum(k + 1, rows), cast_next),
+            loss_gradient(cast_now, fgrad_next, aims, weights, 4 * (k - 1), range(4)),
+            pull_back(k - 1, fgrad_now),
         )
         return 0
 
-    take_turns(second_product(0, cast_even))
+    take_turns(second_product(0, cast_now))
     take_turns(
-        second_product(1, cast_odd),
-        loss_gradient(cast_even, fgrad_even, edge_aims, edge_weights, 0, range(1, 4)),
+        second_product(1, cast_next),
+        loss_gradient(cast_now, fgrad_next, edge_aims, edge_weights, 0, range(1, 4)),
     )
-    lax.fori_loop(0, rows // 2, second_segment, 0)
-    take_turns(pull_back(rows, fgrad_even))
+    lax.fori_loop(1, rows + 1, second_segment, 0)
+    take_turns(pull_back(rows, fgrad_next))
 
     for t in range(own):
         out_lat[:, t * LANES : (t + 1) * LANES] = lat_lines[t * rows : (t + 1) * rows].astype(bf16)
@@ -520,8 +522,8 @@
 
 
 def total(array, axis, first, second):
-    one, two, three = (swapped(array, axis, k) for k in (first, second, first ^ second))
-    return (array + one) + (two + three)
+    one, two, three = (swapped(array, axis, k).astype(jnp.float32) for k in (first, second, first ^ second))
+    return (array.astype(jnp.float32) + one) + (two + three)
 
 
 def local(
@@ -532,7 +534,7 @@
     lat_count = lax.axis_size("lat")
     own = span // LANES // lax.axis_size("mem")
     half = (own + 1) // 2
-    assert sample_count == 1 and member_seeds.shape[0] == MEM and rows % 2 == 0 and own % 2 == 1 and lax.axis_size("mem") == 4
+    assert sample_count == 1 and member_seeds.shape[0] == MEM and rows % 4 == 0 and own % 2 == 1 and lax.axis_size("mem") == 4
     assert 4 * chan2 == 2 * chan1 == chan0 and chan0 == 64
     vmem = pl.BlockSpec(memory_space=pltpu.VMEM)
     smem = pl.BlockSpec(memory_space=pltpu.SMEM)
@@ -630,7 +632,7 @@
         below,
         *bands,
     )
-    taps = taps + swapped(taps_send, "lat", 1)
+    taps = (taps + swapped(taps_send, "lat", 1)).astype(bf16)
     taps = total(taps, "mem", 1, 2)
     one, two, three = (swapped(lat_grad, "mem", k) for k in range(1, 4))
     bits = [1 << k for k in range(1, lat_count.bit_length() - 1)]

time: 56.5 us -> 56.2 us (level)
  waiting for transfers between devices: 7.06 us -> 5.78 us
    ppermute x10, waiting for transfers between devices: 5.48 us -> 4.19 us  [swapped(): lax.ppermute(array, axis, [(i, i ^ bit) for i in range(lax.axis_size(axis...]
where the time goes in v13:
time: 56.2 us; the launch traced here: 56 us
  Pallas kernels  27.8 us (49%)
  starting transfers between devices  21.4 us (38%)
  waiting for transfers between devices  5.78 us (10%)
  between operations  0.85 us (2%)
    pallas_call x1, Pallas kernels, local(): pl.pallas_call(functools.partial(band_kernel, half, (chan0, chan1, chan2)...  21.6 us
    ppermute x10, starting transfers between devices, swapped(): lax.ppermute(array, axis, [(i, i ^ bit) for i in range(lax.axis_size(axis...  17.8 us
    ppermute x10, waiting for transfers between devices, swapped(): lax.ppermute(array, axis, [(i, i ^ bit) for i in range(lax.axis_size(axis...  4.19 us
    ppermute x2, starting transfers between devices, shifted(): return lax.ppermute(array, axis, pairs)  3.65 us
    pallas_call x1, Pallas kernels, local(): pl.pallas_call(functools.partial(prepare_kernel, half, chan0, chan2), in_...  2.13 us
    pallas_call x1, Pallas kernels, local(): pl.pallas_call(functools.partial(edge_kernel, half, chan2), in_specs=[hbm...  2.13 us
    ppermute x2, waiting for transfers between devices, shifted(): return lax.ppermute(array, axis, pairs)  1.58 us
  transfers between devices with their start and end apart: 12, of which 6 were waited for; matrix products, arithmetic and copies ran while one was open for 0% of the time, Pallas kernels for 6%

profile of v13, /device:TPU:0, one launch (start us, length us, event | category | flops | bytes accessed | tf_op | source)
XLA Modules:
  0.0 56.0 jit_solution(8118785061998779225)
XLA Ops:
  0.7 2.1 %edges.1 = (bf16[50,8,128]{2,1,0:T(8,128)(2,1)}, bf16[1,6400]{1,0:T(2,128)(2,1)}) custom-call(bf16[1,8,23040]{2,1,0:T(8,128)(2,1)} %latent_hbm.1, bf16[1,32,23040]{2,1,0:T(8,128)(2,1)} %targets_hbm.1, s32[32,48]{1,0:T(8,128)} %land_hbm.1), custom_call_target="tpu_custom_call" | custom-call | tf_op jit(solution)/shard_map/edges/pallas_call | solution.py:548
  2.9 2.4 %collective-permute-start = (bf16[50,8,128]{2,1,0:T(8,128)(2,1)}, bf16[50,8,128]{2,1,0:T(8,128)(2,1)S(1)}, u32[]{:S(2)}, u32[]{:S(2)}) collective-permute-start(bf16[50,8,128]{2,1,0:T(8,128)(2,1)} %get-tuple-element.29), channel_id=1, source_target_pairs={{0,4},{4,8},{8,12},{12,16},{16,20},{20,24},{24,28},{1,5},{5,9},{9,... | collective-permute-start | bytes 307208 | tf_op jit(solution)/shard_map/ppermute | solution.py:24
  5.2 1.3 %collective-permute-start.1 = (bf16[1,6400]{1,0:T(2,128)(2,1)}, bf16[1,6400]{1,0:T(2,128)(2,1)S(1)}, u32[]{:S(2)}, u32[]{:S(2)}) collective-permute-start(bf16[1,6400]{1,0:T(2,128)(2,1)} %get-tuple-element.30), channel_id=1, source_target_pairs={{4,0},{8,4},{12,8},{16,12},{20,16},{24,20},{28,24},{5,1},{9,5},{13... | collective-permute-start | bytes 38408 | tf_op jit(solution)/shard_map/ppermute | solution.py:24
  6.6 2.1 %prepare.1 = (bf16[8,25,16,128]{3,2,1,0:T(8,128)(2,1)S(1)}, f32[48,32,128]{2,1,0:T(8,128)S(1)}, f32[48,32,128]{2,1,0:T(8,128)S(1)}) custom-call(s32[8]{0:T(128)S(1)} %copy-done.3, f32[64]{0:T(128)S(1)} %copy-done.4, f32[16]{0:T(128)S(1)} %copy-done.5, bf16[1,8,23040]{2,1,0:T(8,128)(2,1)S(1)} %copy-done.1, bf16[1,32,23040]{2,1,0:T(8,128)(2,1)S(1)} %copy-done, ...), custom_call_target="tpu_custom_call" | custom-call | flops 100000000 | bytes 10000000 | tf_op jit(solution)/shard_map/prepare/pallas_call | solution.py:568
  8.7 0.3 bands.1
  9.0 1.6 %collective-permute-done.1.below = bf16[1,6400]{1,0:T(2,128)(2,1)S(1)} collective-permute-done((bf16[1,6400]{1,0:T(2,128)(2,1)}, bf16[1,6400]{1,0:T(2,128)(2,1)S(1)}, u32[]{:S(2)}, u32[]{:S(2)}) %collective-permute-start.1) | collective-permute-done | bytes 12832 | tf_op jit(solution)/shard_map/ppermute | solution.py:24
  10.6 0.0 collective-permute-done.above
  10.6 21.6 %band.1 = (bf16[8,5760]{1,0:T(8,128)(2,1)S(1)}, f32[104,128]{1,0:T(8,128)S(1)}, f32[104,128]{1,0:T(8,128)S(1)}) custom-call(s32[8]{0:T(128)S(1)} %copy-done.3, f32[64]{0:T(128)S(1)} %copy-done.4, f32[16]{0:T(128)S(1)} %copy-done.5, bf16[8,25,16,128]{3,2,1,0:T(8,128)(2,1)S(1)} %get-tuple-element.26.own_source, f32[48,32,128]{2,1,0:T(8,128)S(1)} %get-tuple-element.27.aims, ...), custom_call_target="tpu_custom_call" | custom-call | tf_op jit(solution)/shard_map/band/pallas_call | solution.py:591
  32.2 2.6 %collective-permute-start.2 = (f32[104,128]{1,0:T(8,128)S(1)}, f32[104,128]{1,0:T(8,128)S(1)}, u32[]{:S(2)}, u32[]{:S(2)}) collective-permute-start(f32[104,128]{1,0:T(8,128)S(1)} %get-tuple-element.39), channel_id=1, source_target_pairs={{0,4},{4,0},{8,12},{12,8},{16,20},{20,16},{24,28},{28,24},{1,5},{5... | collective-permute-start | bytes 159752 | tf_op jit(solution)/shard_map/ppermute | solution.py:521
  34.8 0.9 %collective-permute-done.2 = f32[104,128]{1,0:T(8,128)S(1)} collective-permute-done((f32[104,128]{1,0:T(8,128)S(1)}, f32[104,128]{1,0:T(8,128)S(1)}, u32[]{:S(2)}, u32[]{:S(2)}) %collective-permute-start.2) | collective-permute-done | bytes 53280 | tf_op jit(solution)/shard_map/ppermute | solution.py:521
  35.7 3.7 %collective-permute-start.5 = (bf16[104,128]{1,0:T(8,128)(2,1)S(1)}, bf16[104,128]{1,0:T(8,128)(2,1)S(1)}, u32[]{:S(2)}, u32[]{:S(2)}) collective-permute-start(bf16[104,128]{1,0:T(8,128)(2,1)S(1)} %add_convert_fusion), channel_id=1, source_target_pairs={{0,3},{1,2},{2,1},{3,0},{4,7},{5,6},{6,5},{7,4},{8,11},{9,10},{10,... | collective-permute-start | bytes 79880 | tf_op jit(solution)/shard_map/ppermute | solution.py:521
  39.4 0.8 %collective-permute-start.3 = (bf16[104,128]{1,0:T(8,128)(2,1)S(1)}, bf16[104,128]{1,0:T(8,128)(2,1)S(1)}, u32[]{:S(2)}, u32[]{:S(2)}) collective-permute-start(bf16[104,128]{1,0:T(8,128)(2,1)S(1)} %add_convert_fusion), channel_id=1, source_target_pairs={{0,1},{1,0},{2,3},{3,2},{4,5},{5,4},{6,7},{7,6},{8,9},{9,8},{10,11... | collective-permute-start | bytes 79880 | tf_op jit(solution)/shard_map/ppermute | solution.py:521
  40.2 3.6 %collective-permute-start.7 = (bf16[8,5760]{1,0:T(8,128)(2,1)S(1)}, bf16[8,5760]{1,0:T(8,128)(2,1)S(1)}, u32[]{:S(2)}, u32[]{:S(2)}) collective-permute-start(bf16[8,5760]{1,0:T(8,128)(2,1)S(1)} %get-tuple-element.37.part0), channel_id=1, source_target_pairs={{0,3},{1,2},{2,1},{3,0},{4,7},{5,6},{6,5},{7,4},{8,11},{9,10},{10,... | collective-permute-start | bytes 276488 | tf_op jit(solution)/shard_map/ppermute | solution.py:521
  43.8 0.6 %collective-permute-done.4 = bf16[104,128]{1,0:T(8,128)(2,1)S(1)} collective-permute-done((bf16[104,128]{1,0:T(8,128)(2,1)S(1)}, bf16[104,128]{1,0:T(8,128)(2,1)S(1)}, u32[]{:S(2)}, u32[]{:S(2)}) %collective-permute-start.4) | collective-permute-done | bytes 26656 | tf_op jit(solution)/shard_map/ppermute | solution.py:521
  44.4 0.0 collective-permute-done.3
  44.4 2.5 %collective-permute-start.6 = (f32[104,128]{1,0:T(8,128)S(1)}, f32[104,128]{1,0:T(8,128)S(1)}, u32[]{:S(2)}, u32[]{:S(2)}) collective-permute-start(f32[104,128]{1,0:T(8,128)S(1)} %add_add_fusion), channel_id=1, source_target_pairs={{0,8},{4,12},{8,0},{12,4},{16,24},{20,28},{24,16},{28,20},{1,9},{5... | collective-permute-start | bytes 159752 | tf_op jit(solution)/shard_map/ppermute | solution.py:521
  46.9 1.9 %collective-permute-start.10 = (bf16[8,5760]{1,0:T(8,128)(2,1)S(1)}, bf16[8,5760]{1,0:T(8,128)(2,1)S(1)}, u32[]{:S(2)}, u32[]{:S(2)}) collective-permute-start(bf16[8,5760]{1,0:T(8,128)(2,1)S(1)} %get-tuple-element.37.part0), channel_id=1, source_target_pairs={{0,2},{1,3},{2,0},{3,1},{4,6},{5,7},{6,4},{7,5},{8,10},{9,11},{10,... | collective-permute-start | bytes 276488 | tf_op jit(solution)/shard_map/ppermute | solution.py:521
  48.8 0.3 collective-permute-done.6
  49.0 2.7 %collective-permute-start.8 = (f32[104,128]{1,0:T(8,128)S(1)}, f32[104,128]{1,0:T(8,128)S(1)}, u32[]{:S(2)}, u32[]{:S(2)}) collective-permute-start(f32[104,128]{1,0:T(8,128)S(1)} %add.22), channel_id=1, source_target_pairs={{0,16},{4,20},{8,24},{12,28},{16,0},{20,4},{24,8},{28,12},{1,17},{... | collective-permute-start | bytes 159752 | tf_op jit(solution)/shard_map/ppermute | solution.py:521
  51.8 2.1 %collective-permute-done.8 = f32[104,128]{1,0:T(8,128)S(1)} collective-permute-done((f32[104,128]{1,0:T(8,128)S(1)}, f32[104,128]{1,0:T(8,128)S(1)}, u32[]{:S(2)}, u32[]{:S(2)}) %collective-permute-start.8) | collective-permute-done | bytes 53280 | tf_op jit(solution)/shard_map/ppermute | solution.py:521
  53.9 0.1 collective-permute-start.11
  54.0 0.9 %place.1 = f32[1,8,23040]{2,1,0:T(8,128)} custom-call(bf16[8,5760]{1,0:T(8,128)(2,1)S(1)} %get-tuple-element.37.part0, bf16[8,5760]{1,0:T(8,128)(2,1)S(1)} %collective-permute-done.9.part1, bf16[8,5760]{1,0:T(8,128)(2,1)S(1)} %collective-permute-done.10.part2, bf16[8,5760]{1,0:T(8,128)(2,1)S(1)} %collective-permute-done.7.part3), custom_call_target="tpu_custom_call" | custom-call | tf_op jit(solution)/shard_map/place/pallas_call | solution.py:645
  54.9 0.3 collective-permute-done.11.other
  55.2 0.8 %taps.1 = (f32[3,3,32,64]{3,2,1,0:T(8,128)}, f32[3,3,16,32]{3,2,1,0:T(8,128)}) custom-call(f32[104,128]{1,0:T(8,128)S(1)} %add.23.mine, f32[104,128]{1,0:T(8,128)S(1)} %collective-permute-done.11.other), custom_call_target="tpu_custom_call" | custom-call | tf_op jit(solution)/shard_map/taps/pallas_call | solution.py:653
  (26 shorter events, 0.1 us)
Async XLA Ops:
  0.6 5.9 %copy-start.2 = (s32[32,48]{1,0:T(8,128)S(1)}, s32[32,48]{1,0:T(8,128)}, u32[]{:S(2)}) copy-start(s32[32,48]{1,0:T(8,128)} %land_hbm.1) | copy-start | bytes 18436
  0.6 5.9 %copy-start = (bf16[1,32,23040]{2,1,0:T(8,128)(2,1)S(1)}, bf16[1,32,23040]{2,1,0:T(8,128)(2,1)}, u32[]{:S(2)}) copy-start(bf16[1,32,23040]{2,1,0:T(8,128)(2,1)} %targets_hbm.1) | copy-start | bytes 4423684
  0.7 5.9 %copy-start.1 = (bf16[1,8,23040]{2,1,0:T(8,128)(2,1)S(1)}, bf16[1,8,23040]{2,1,0:T(8,128)(2,1)}, u32[]{:S(2)}) copy-start(bf16[1,8,23040]{2,1,0:T(8,128)(2,1)} %latent_hbm.1) | copy-start | bytes 1105924
  0.7 5.9 %copy-start.5 = (f32[16]{0:T(128)S(1)}, f32[16]{0:T(128)}, u32[]{:S(2)}) copy-start(f32[16]{0:T(128)} %channel_weight.3) | copy-start | bytes 196
  0.7 5.9 %copy-start.4 = (f32[64]{0:T(128)S(1)}, f32[64]{0:T(128)}, u32[]{:S(2)}) copy-start(f32[64]{0:T(128)} %scale.3) | copy-start | bytes 772
  0.7 5.9 %copy-start.3 = (s32[8]{0:T(128)S(1)}, s32[8]{0:T(128)}, u32[]{:S(2)}) copy-start(s32[8]{0:T(128)} %seeds.3) | copy-start | bytes 100
  0.7 8.0 %copy-start.7 = (bf16[3,3,32,16]{2,3,1,0:T(8,128)(2,1)S(1)}, bf16[3,3,32,16]{2,3,1,0:T(8,128)(2,1)}, u32[]{:S(2)}) copy-start(bf16[3,3,32,16]{2,3,1,0:T(8,128)(2,1)} %param.12) | copy-start | bytes 27652
  0.7 8.0 %copy-start.6 = (bf16[3,3,64,32]{2,3,1,0:T(8,128)(2,1)S(1)}, bf16[3,3,64,32]{2,3,1,0:T(8,128)(2,1)}, u32[]{:S(2)}) copy-start(bf16[3,3,64,32]{2,3,1,0:T(8,128)(2,1)} %param.11) | copy-start | bytes 110596
  2.9 7.8 %collective-permute-start = (bf16[50,8,128]{2,1,0:T(8,128)(2,1)}, bf16[50,8,128]{2,1,0:T(8,128)(2,1)S(1)}, u32[]{:S(2)}, u32[]{:S(2)}) collective-permute-start(bf16[50,8,128]{2,1,0:T(8,128)(2,1)} %get-tuple-element.29), channel_id=1, source_target_pairs={{0,4},{4,8},{8,12},{12,16},{16,20},{20,24},{24,28},{1,5},{5,9},{9,... | collective-permute-start | bytes 307208 | tf_op jit(solution)/shard_map/ppermute | solution.py:24
  5.2 5.4 %collective-permute-start.1 = (bf16[1,6400]{1,0:T(2,128)(2,1)}, bf16[1,6400]{1,0:T(2,128)(2,1)S(1)}, u32[]{:S(2)}, u32[]{:S(2)}) collective-permute-start(bf16[1,6400]{1,0:T(2,128)(2,1)} %get-tuple-element.30), channel_id=1, source_target_pairs={{4,0},{8,4},{12,8},{16,12},{20,16},{24,20},{28,24},{5,1},{9,5},{13... | collective-permute-start | bytes 38408 | tf_op jit(solution)/shard_map/ppermute | solution.py:24
  32.2 3.5 %collective-permute-start.2 = (f32[104,128]{1,0:T(8,128)S(1)}, f32[104,128]{1,0:T(8,128)S(1)}, u32[]{:S(2)}, u32[]{:S(2)}) collective-permute-start(f32[104,128]{1,0:T(8,128)S(1)} %get-tuple-element.39), channel_id=1, source_target_pairs={{0,4},{4,0},{8,12},{12,8},{16,20},{20,16},{24,28},{28,24},{1,5},{5... | collective-permute-start | bytes 159752 | tf_op jit(solution)/shard_map/ppermute | solution.py:521
  35.7 8.1 %collective-permute-start.5 = (bf16[104,128]{1,0:T(8,128)(2,1)S(1)}, bf16[104,128]{1,0:T(8,128)(2,1)S(1)}, u32[]{:S(2)}, u32[]{:S(2)}) collective-permute-start(bf16[104,128]{1,0:T(8,128)(2,1)S(1)} %add_convert_fusion), channel_id=1, source_target_pairs={{0,3},{1,2},{2,1},{3,0},{4,7},{5,6},{6,5},{7,4},{8,11},{9,10},{10,... | collective-permute-start | bytes 79880 | tf_op jit(solution)/shard_map/ppermute | solution.py:521
  39.4 5.0 %collective-permute-start.4 = (bf16[104,128]{1,0:T(8,128)(2,1)S(1)}, bf16[104,128]{1,0:T(8,128)(2,1)S(1)}, u32[]{:S(2)}, u32[]{:S(2)}) collective-permute-start(bf16[104,128]{1,0:T(8,128)(2,1)S(1)} %add_convert_fusion), channel_id=1, source_target_pairs={{0,2},{1,3},{2,0},{3,1},{4,6},{5,7},{6,4},{7,5},{8,10},{9,11},{10,... | collective-permute-start | bytes 79880 | tf_op jit(solution)/shard_map/ppermute | solution.py:521
  39.4 5.0 %collective-permute-start.3 = (bf16[104,128]{1,0:T(8,128)(2,1)S(1)}, bf16[104,128]{1,0:T(8,128)(2,1)S(1)}, u32[]{:S(2)}, u32[]{:S(2)}) collective-permute-start(bf16[104,128]{1,0:T(8,128)(2,1)S(1)} %add_convert_fusion), channel_id=1, source_target_pairs={{0,1},{1,0},{2,3},{3,2},{4,5},{5,4},{6,7},{7,6},{8,9},{9,8},{10,11... | collective-permute-start | bytes 79880 | tf_op jit(solution)/shard_map/ppermute | solution.py:521
  40.2 8.8 %collective-permute-start.7 = (bf16[8,5760]{1,0:T(8,128)(2,1)S(1)}, bf16[8,5760]{1,0:T(8,128)(2,1)S(1)}, u32[]{:S(2)}, u32[]{:S(2)}) collective-permute-start(bf16[8,5760]{1,0:T(8,128)(2,1)S(1)} %get-tuple-element.37.part0), channel_id=1, source_target_pairs={{0,3},{1,2},{2,1},{3,0},{4,7},{5,6},{6,5},{7,4},{8,11},{9,10},{10,... | collective-permute-start | bytes 276488 | tf_op jit(solution)/shard_map/ppermute | solution.py:521
  44.4 4.6 %collective-permute-start.6 = (f32[104,128]{1,0:T(8,128)S(1)}, f32[104,128]{1,0:T(8,128)S(1)}, u32[]{:S(2)}, u32[]{:S(2)}) collective-permute-start(f32[104,128]{1,0:T(8,128)S(1)} %add_add_fusion), channel_id=1, source_target_pairs={{0,8},{4,12},{8,0},{12,4},{16,24},{20,28},{24,16},{28,20},{1,9},{5... | collective-permute-start | bytes 159752 | tf_op jit(solution)/shard_map/ppermute | solution.py:521
  46.9 7.0 %collective-permute-start.10 = (bf16[8,5760]{1,0:T(8,128)(2,1)S(1)}, bf16[8,5760]{1,0:T(8,128)(2,1)S(1)}, u32[]{:S(2)}, u32[]{:S(2)}) collective-permute-start(bf16[8,5760]{1,0:T(8,128)(2,1)S(1)} %get-tuple-element.37.part0), channel_id=1, source_target_pairs={{0,2},{1,3},{2,0},{3,1},{4,6},{5,7},{6,4},{7,5},{8,10},{9,11},{10,... | collective-permute-start | bytes 276488 | tf_op jit(solution)/shard_map/ppermute | solution.py:521
  48.7 5.1 %collective-permute-start.9 = (bf16[8,5760]{1,0:T(8,128)(2,1)S(1)}, bf16[8,5760]{1,0:T(8,128)(2,1)S(1)}, u32[]{:S(2)}, u32[]{:S(2)}) collective-permute-start(bf16[8,5760]{1,0:T(8,128)(2,1)S(1)} %get-tuple-element.37.part0), channel_id=1, source_target_pairs={{0,1},{1,0},{2,3},{3,2},{4,5},{5,4},{6,7},{7,6},{8,9},{9,8},{10,11... | collective-permute-start | bytes 276488 | tf_op jit(solution)/shard_map/ppermute | solution.py:521
  49.0 4.8 %collective-permute-start.8 = (f32[104,128]{1,0:T(8,128)S(1)}, f32[104,128]{1,0:T(8,128)S(1)}, u32[]{:S(2)}, u32[]{:S(2)}) collective-permute-start(f32[104,128]{1,0:T(8,128)S(1)} %add.22), channel_id=1, source_target_pairs={{0,16},{4,20},{8,24},{12,28},{16,0},{20,4},{24,8},{28,12},{1,17},{... | collective-permute-start | bytes 159752 | tf_op jit(solution)/shard_map/ppermute | solution.py:521
  53.9 1.3 %collective-permute-start.11 = (f32[104,128]{1,0:T(8,128)S(1)}, f32[104,128]{1,0:T(8,128)S(1)}, u32[]{:S(2)}, u32[]{:S(2)}) collective-permute-start(f32[104,128]{1,0:T(8,128)S(1)} %add.23.mine), channel_id=1, source_target_pairs={{0,4},{4,0},{8,12},{12,8},{16,20},{20,16},{24,28},{28,24},{1,5},{5... | collective-permute-start | bytes 159752 | tf_op jit(solution)/shard_map/ppermute | solution.py:521

commit v14 on v12

--- a/solution.py
+++ b/solution.py
@@ -449,9 +449,7 @@
                 fgrad[line, t + 1] = jnp.concatenate(parts, axis=0).astype(bf16)
             yield
 
-    def pull_back(n, fgrad):
-        keep = jnp.where(n >= 1, 1.0, 0.0).astype(bf16)
-
+    def pull_back(n, fgrad, with_taps=True):
         def flat(line, start, count):
             return fgrad[line, start : start + count].reshape(count * 16, LANES)
 
@@ -480,10 +478,11 @@
         grads = jnp.concatenate(grads, axis=1)
         g = [jnp.concatenate([flat(2 * k, 2, half), flat(2 * k + 1, 2, half)], axis=1) for k in range(2)]
         x = [operand(act, 2 * n + k, 1, half) for k in range(2)]
-        add_taps(jnp.concatenate(g, axis=0) * keep, jnp.concatenate(x, axis=0), acc_two, acc_two_next, chan2)
-        yield
-        add_taps(grads[16:] * keep, operand(source, n, 1, half), acc_one, acc_one_next, chan1)
-        yield
+        if with_taps:
+            add_taps(jnp.concatenate(g, axis=0), jnp.concatenate(x, axis=0), acc_two, acc_two_next, chan2)
+            yield
+            add_taps(grads[16:], operand(source, n, 1, half), acc_one, acc_one_next, chan1)
+            yield
         z = jnp.dot(pick, grads, preferred_element_type=f32)
         z = jnp.concatenate([z[:48], z[48:]], axis=1)
         high = z.astype(bf16)
@@ -499,14 +498,14 @@
 
     def second_segment(m, _):
         take_turns(
-            second_product(2 * m + 2, cast_even),
-            own_gradient(2 * m + 1, cast_odd, fgrad_odd),
-            pull_back(2 * m, fgrad_even),
+            second_product(2 * m + 3, cast_odd),
+            own_gradient(2 * m + 2, cast_even, fgrad_even),
+            pull_back(2 * m + 1, fgrad_odd),
         )
         take_turns(
-            second_product(jnp.minimum(2 * m + 3, rows), cast_odd),
-            own_gradient(2 * m + 2, cast_even, fgrad_even),
-            pull_back(2 * m + 1, fgrad_odd),
+            second_product(2 * m + 4, cast_even),
+            own_gradient(2 * m + 3, cast_odd, fgrad_odd),
+            pull_back(2 * m + 2, fgrad_even),
         )
         return 0
 
@@ -515,7 +514,13 @@
         second_product(1, cast_odd),
         loss_gradient(cast_even, fgrad_even, edge_aims, edge_weights, 0, range(1, 4)),
     )
-    lax.fori_loop(0, rows // 2, second_segment, 0)
+    take_turns(
+        second_product(2, cast_even),
+        own_gradient(1, cast_odd, fgrad_odd),
+        pull_back(0, fgrad_even, with_taps=False),
+    )
+    lax.fori_loop(0, rows // 2 - 1, second_segment, 0)
+    take_turns(own_gradient(rows, cast_even, fgrad_even), pull_back(rows - 1, fgrad_odd))
     take_turns(pull_back(rows, fgrad_even))
 
     for t in range(own):
@@ -649,9 +654,9 @@
     bits = [1 << k for k in range(1, lat_count.bit_length() - 1)]
     for bit in bits:
         if bit == bits[-1]:
-            taps, three = lax.optimization_barrier((taps, three))
+            taps, one, three = lax.optimization_barrier((taps, one, three))
         taps = taps + swapped(taps, "lat", bit)
-    taps, one, two = lax.optimization_barrier((taps, one, two))
+    taps, two = lax.optimization_barrier((taps, two))
     other = swapped(taps, "lat", 1)
     latent_grad = pl.pallas_call(
         functools.partial(place_kernel, own),

time: 55.7 us -> 55.3 us (level)
  no operation moved by 1% of the time
where the time goes in v14:
time: 55.3 us; the launch traced here: 55.1 us
  Pallas kernels  27 us (49%)
  starting transfers between devices  21.7 us (39%)
  waiting for transfers between devices  5.57 us (10%)
  between operations  0.85 us (2%)
    pallas_call x1, Pallas kernels, local(): pl.pallas_call(functools.partial(band_kernel, half, (chan0, chan1, chan2)...  20.7 us
    ppermute x10, starting transfers between devices, swapped(): lax.ppermute(array, axis, [(i, i ^ bit) for i in range(lax.axis_size(axis...  18 us
    ppermute x10, waiting for transfers between devices, swapped(): lax.ppermute(array, axis, [(i, i ^ bit) for i in range(lax.axis_size(axis...  3.98 us
    ppermute x2, starting transfers between devices, shifted(): return lax.ppermute(array, axis, pairs)  3.65 us
    pallas_call x1, Pallas kernels, local(): pl.pallas_call(functools.partial(prepare_kernel, half, chan0, chan2), in_...  2.13 us
    pallas_call x1, Pallas kernels, local(): pl.pallas_call(functools.partial(edge_kernel, half, chan2), in_specs=[hbm...  2.13 us
    ppermute x2, waiting for transfers between devices, shifted(): return lax.ppermute(array, axis, pairs)  1.58 us
  transfers between devices with their start and end apart: 12, of which 6 were waited for; matrix products, arithmetic and copies ran while one was open for 0% of the time, Pallas kernels for 6%

profile of v14, /device:TPU:0, one launch (start us, length us, event | category | flops | bytes accessed | tf_op | source)
XLA Modules:
  0.0 55.1 jit_solution(9731271224516051136)
XLA Ops:
  0.7 2.1 %edges.1 = (bf16[50,8,128]{2,1,0:T(8,128)(2,1)}, bf16[1,6400]{1,0:T(2,128)(2,1)}) custom-call(bf16[1,8,23040]{2,1,0:T(8,128)(2,1)} %latent_hbm.1, bf16[1,32,23040]{2,1,0:T(8,128)(2,1)} %targets_hbm.1, s32[32,48]{1,0:T(8,128)} %land_hbm.1), custom_call_target="tpu_custom_call" | custom-call | tf_op jit(solution)/shard_map/edges/pallas_call | solution.py:564
  2.9 2.4 %collective-permute-start = (bf16[50,8,128]{2,1,0:T(8,128)(2,1)}, bf16[50,8,128]{2,1,0:T(8,128)(2,1)S(1)}, u32[]{:S(2)}, u32[]{:S(2)}) collective-permute-start(bf16[50,8,128]{2,1,0:T(8,128)(2,1)} %get-tuple-element.29), channel_id=1, source_target_pairs={{0,4},{4,8},{8,12},{12,16},{16,20},{20,24},{24,28},{1,5},{5,9},{9,... | collective-permute-start | bytes 307208 | tf_op jit(solution)/shard_map/ppermute | solution.py:24
  5.2 1.3 %collective-permute-start.1 = (bf16[1,6400]{1,0:T(2,128)(2,1)}, bf16[1,6400]{1,0:T(2,128)(2,1)S(1)}, u32[]{:S(2)}, u32[]{:S(2)}) collective-permute-start(bf16[1,6400]{1,0:T(2,128)(2,1)} %get-tuple-element.30), channel_id=1, source_target_pairs={{4,0},{8,4},{12,8},{16,12},{20,16},{24,20},{28,24},{5,1},{9,5},{13... | collective-permute-start | bytes 38408 | tf_op jit(solution)/shard_map/ppermute | solution.py:24
  6.6 2.1 %prepare.1 = (bf16[8,25,16,128]{3,2,1,0:T(8,128)(2,1)S(1)}, f32[48,32,128]{2,1,0:T(8,128)S(1)}, f32[48,32,128]{2,1,0:T(8,128)S(1)}) custom-call(s32[8]{0:T(128)S(1)} %copy-done.3, f32[64]{0:T(128)S(1)} %copy-done.4, f32[16]{0:T(128)S(1)} %copy-done.5, bf16[1,8,23040]{2,1,0:T(8,128)(2,1)S(1)} %copy-done.1, bf16[1,32,23040]{2,1,0:T(8,128)(2,1)S(1)} %copy-done, ...), custom_call_target="tpu_custom_call" | custom-call | flops 100000000 | bytes 10000000 | tf_op jit(solution)/shard_map/prepare/pallas_call | solution.py:584
  8.7 0.3 bands.1
  9.0 1.6 %collective-permute-done.1.below = bf16[1,6400]{1,0:T(2,128)(2,1)S(1)} collective-permute-done((bf16[1,6400]{1,0:T(2,128)(2,1)}, bf16[1,6400]{1,0:T(2,128)(2,1)S(1)}, u32[]{:S(2)}, u32[]{:S(2)}) %collective-permute-start.1) | collective-permute-done | bytes 12832 | tf_op jit(solution)/shard_map/ppermute | solution.py:24
  10.6 20.7 %band.1 = (bf16[8,5760]{1,0:T(8,128)(2,1)S(1)}, f32[104,128]{1,0:T(8,128)S(1)}, f32[104,128]{1,0:T(8,128)S(1)}) custom-call(s32[8]{0:T(128)S(1)} %copy-done.3, f32[64]{0:T(128)S(1)} %copy-done.4, f32[16]{0:T(128)S(1)} %copy-done.5, bf16[8,25,16,128]{3,2,1,0:T(8,128)(2,1)S(1)} %get-tuple-element.26.own_source, f32[48,32,128]{2,1,0:T(8,128)S(1)} %get-tuple-element.27.aims, ...), custom_call_target="tpu_custom_call" | custom-call | tf_op jit(solution)/shard_map/band/pallas_call | solution.py:607
  31.4 2.6 %collective-permute-start.2 = (f32[104,128]{1,0:T(8,128)S(1)}, f32[104,128]{1,0:T(8,128)S(1)}, u32[]{:S(2)}, u32[]{:S(2)}) collective-permute-start(f32[104,128]{1,0:T(8,128)S(1)} %get-tuple-element.39), channel_id=1, source_target_pairs={{0,4},{4,0},{8,12},{12,8},{16,20},{20,16},{24,28},{28,24},{1,5},{5... | collective-permute-start | bytes 159752 | tf_op jit(solution)/shard_map/ppermute | solution.py:537
  34.0 0.9 %collective-permute-done.2 = f32[104,128]{1,0:T(8,128)S(1)} collective-permute-done((f32[104,128]{1,0:T(8,128)S(1)}, f32[104,128]{1,0:T(8,128)S(1)}, u32[]{:S(2)}, u32[]{:S(2)}) %collective-permute-start.2) | collective-permute-done | bytes 53280 | tf_op jit(solution)/shard_map/ppermute | solution.py:537
  34.9 3.7 %collective-permute-start.5 = (bf16[104,128]{1,0:T(8,128)(2,1)S(1)}, bf16[104,128]{1,0:T(8,128)(2,1)S(1)}, u32[]{:S(2)}, u32[]{:S(2)}) collective-permute-start(bf16[104,128]{1,0:T(8,128)(2,1)S(1)} %add_convert_fusion), channel_id=1, source_target_pairs={{0,3},{1,2},{2,1},{3,0},{4,7},{5,6},{6,5},{7,4},{8,11},{9,10},{10,... | collective-permute-start | bytes 79880 | tf_op jit(solution)/shard_map/ppermute | solution.py:537
  38.6 0.0 collective-permute-start.4
  38.6 0.8 %collective-permute-start.3 = (bf16[104,128]{1,0:T(8,128)(2,1)S(1)}, bf16[104,128]{1,0:T(8,128)(2,1)S(1)}, u32[]{:S(2)}, u32[]{:S(2)}) collective-permute-start(bf16[104,128]{1,0:T(8,128)(2,1)S(1)} %add_convert_fusion), channel_id=1, source_target_pairs={{0,1},{1,0},{2,3},{3,2},{4,5},{5,4},{6,7},{7,6},{8,9},{9,8},{10,11... | collective-permute-start | bytes 79880 | tf_op jit(solution)/shard_map/ppermute | solution.py:537
  39.3 3.6 %collective-permute-start.8 = (bf16[8,5760]{1,0:T(8,128)(2,1)S(1)}, bf16[8,5760]{1,0:T(8,128)(2,1)S(1)}, u32[]{:S(2)}, u32[]{:S(2)}) collective-permute-start(bf16[8,5760]{1,0:T(8,128)(2,1)S(1)} %get-tuple-element.37.part0), channel_id=1, source_target_pairs={{0,3},{1,2},{2,1},{3,0},{4,7},{5,6},{6,5},{7,4},{8,11},{9,10},{10,... | collective-permute-start | bytes 276488 | tf_op jit(solution)/shard_map/ppermute | solution.py:537
  43.0 0.0 collective-permute-start.7
  43.0 0.6 %collective-permute-done.4 = bf16[104,128]{1,0:T(8,128)(2,1)S(1)} collective-permute-done((bf16[104,128]{1,0:T(8,128)(2,1)S(1)}, bf16[104,128]{1,0:T(8,128)(2,1)S(1)}, u32[]{:S(2)}, u32[]{:S(2)}) %collective-permute-start.4) | collective-permute-done | bytes 26656 | tf_op jit(solution)/shard_map/ppermute | solution.py:537
  43.6 2.5 %collective-permute-start.6 = (f32[104,128]{1,0:T(8,128)S(1)}, f32[104,128]{1,0:T(8,128)S(1)}, u32[]{:S(2)}, u32[]{:S(2)}) collective-permute-start(f32[104,128]{1,0:T(8,128)S(1)} %add_add_fusion), channel_id=1, source_target_pairs={{0,8},{4,12},{8,0},{12,4},{16,24},{20,28},{24,16},{28,20},{1,9},{5... | collective-permute-start | bytes 159752 | tf_op jit(solution)/shard_map/ppermute | solution.py:537
  46.1 2.1 %collective-permute-start.10 = (bf16[8,5760]{1,0:T(8,128)(2,1)S(1)}, bf16[8,5760]{1,0:T(8,128)(2,1)S(1)}, u32[]{:S(2)}, u32[]{:S(2)}) collective-permute-start(bf16[8,5760]{1,0:T(8,128)(2,1)S(1)} %get-tuple-element.37.part0), channel_id=1, source_target_pairs={{0,2},{1,3},{2,0},{3,1},{4,6},{5,7},{6,4},{7,5},{8,10},{9,11},{10,... | collective-permute-start | bytes 276488 | tf_op jit(solution)/shard_map/ppermute | solution.py:537
  48.1 0.1 collective-permute-done.6
  48.2 2.7 %collective-permute-start.9 = (f32[104,128]{1,0:T(8,128)S(1)}, f32[104,128]{1,0:T(8,128)S(1)}, u32[]{:S(2)}, u32[]{:S(2)}) collective-permute-start(f32[104,128]{1,0:T(8,128)S(1)} %add.22), channel_id=1, source_target_pairs={{0,16},{4,20},{8,24},{12,28},{16,0},{20,4},{24,8},{28,12},{1,17},{... | collective-permute-start | bytes 159752 | tf_op jit(solution)/shard_map/ppermute | solution.py:537
  50.9 2.1 %collective-permute-done.9 = f32[104,128]{1,0:T(8,128)S(1)} collective-permute-done((f32[104,128]{1,0:T(8,128)S(1)}, f32[104,128]{1,0:T(8,128)S(1)}, u32[]{:S(2)}, u32[]{:S(2)}) %collective-permute-start.9) | collective-permute-done | bytes 53280 | tf_op jit(solution)/shard_map/ppermute | solution.py:537
  53.1 0.1 collective-permute-start.11
  53.1 0.9 %place.1 = f32[1,8,23040]{2,1,0:T(8,128)} custom-call(bf16[8,5760]{1,0:T(8,128)(2,1)S(1)} %get-tuple-element.37.part0, bf16[8,5760]{1,0:T(8,128)(2,1)S(1)} %collective-permute-done.7.part1, bf16[8,5760]{1,0:T(8,128)(2,1)S(1)} %collective-permute-done.10.part2, bf16[8,5760]{1,0:T(8,128)(2,1)S(1)} %collective-permute-done.8.part3), custom_call_target="tpu_custom_call" | custom-call | tf_op jit(solution)/shard_map/place/pallas_call | solution.py:661
  54.1 0.3 collective-permute-done.11.other
  54.4 0.8 %taps.1 = (f32[3,3,32,64]{3,2,1,0:T(8,128)}, f32[3,3,16,32]{3,2,1,0:T(8,128)}) custom-call(f32[104,128]{1,0:T(8,128)S(1)} %add.23.mine, f32[104,128]{1,0:T(8,128)S(1)} %collective-permute-done.11.other), custom_call_target="tpu_custom_call" | custom-call | tf_op jit(solution)/shard_map/taps/pallas_call | solution.py:669
  (26 shorter events, 0.1 us)
Async XLA Ops:
  0.6 5.9 %copy-start.2 = (s32[32,48]{1,0:T(8,128)S(1)}, s32[32,48]{1,0:T(8,128)}, u32[]{:S(2)}) copy-start(s32[32,48]{1,0:T(8,128)} %land_hbm.1) | copy-start | bytes 18436
  0.6 5.9 %copy-start = (bf16[1,32,23040]{2,1,0:T(8,128)(2,1)S(1)}, bf16[1,32,23040]{2,1,0:T(8,128)(2,1)}, u32[]{:S(2)}) copy-start(bf16[1,32,23040]{2,1,0:T(8,128)(2,1)} %targets_hbm.1) | copy-start | bytes 4423684
  0.7 5.9 %copy-start.1 = (bf16[1,8,23040]{2,1,0:T(8,128)(2,1)S(1)}, bf16[1,8,23040]{2,1,0:T(8,128)(2,1)}, u32[]{:S(2)}) copy-start(bf16[1,8,23040]{2,1,0:T(8,128)(2,1)} %latent_hbm.1) | copy-start | bytes 1105924
  0.7 5.9 %copy-start.5 = (f32[16]{0:T(128)S(1)}, f32[16]{0:T(128)}, u32[]{:S(2)}) copy-start(f32[16]{0:T(128)} %channel_weight.3) | copy-start | bytes 196
  0.7 5.9 %copy-start.4 = (f32[64]{0:T(128)S(1)}, f32[64]{0:T(128)}, u32[]{:S(2)}) copy-start(f32[64]{0:T(128)} %scale.3) | copy-start | bytes 772
  0.7 5.9 %copy-start.3 = (s32[8]{0:T(128)S(1)}, s32[8]{0:T(128)}, u32[]{:S(2)}) copy-start(s32[8]{0:T(128)} %seeds.3) | copy-start | bytes 100
  0.7 8.0 %copy-start.7 = (bf16[3,3,32,16]{2,3,1,0:T(8,128)(2,1)S(1)}, bf16[3,3,32,16]{2,3,1,0:T(8,128)(2,1)}, u32[]{:S(2)}) copy-start(bf16[3,3,32,16]{2,3,1,0:T(8,128)(2,1)} %param.12) | copy-start | bytes 27652
  0.7 8.0 %copy-start.6 = (bf16[3,3,64,32]{2,3,1,0:T(8,128)(2,1)S(1)}, bf16[3,3,64,32]{2,3,1,0:T(8,128)(2,1)}, u32[]{:S(2)}) copy-start(bf16[3,3,64,32]{2,3,1,0:T(8,128)(2,1)} %param.11) | copy-start | bytes 110596
  2.9 7.8 %collective-permute-start = (bf16[50,8,128]{2,1,0:T(8,128)(2,1)}, bf16[50,8,128]{2,1,0:T(8,128)(2,1)S(1)}, u32[]{:S(2)}, u32[]{:S(2)}) collective-permute-start(bf16[50,8,128]{2,1,0:T(8,128)(2,1)} %get-tuple-element.29), channel_id=1, source_target_pairs={{0,4},{4,8},{8,12},{12,16},{16,20},{20,24},{24,28},{1,5},{5,9},{9,... | collective-permute-start | bytes 307208 | tf_op jit(solution)/shard_map/ppermute | solution.py:24
  5.2 5.4 %collective-permute-start.1 = (bf16[1,6400]{1,0:T(2,128)(2,1)}, bf16[1,6400]{1,0:T(2,128)(2,1)S(1)}, u32[]{:S(2)}, u32[]{:S(2)}) collective-permute-start(bf16[1,6400]{1,0:T(2,128)(2,1)} %get-tuple-element.30), channel_id=1, source_target_pairs={{4,0},{8,4},{12,8},{16,12},{20,16},{24,20},{28,24},{5,1},{9,5},{13... | collective-permute-start | bytes 38408 | tf_op jit(solution)/shard_map/ppermute | solution.py:24
  31.4 3.5 %collective-permute-start.2 = (f32[104,128]{1,0:T(8,128)S(1)}, f32[104,128]{1,0:T(8,128)S(1)}, u32[]{:S(2)}, u32[]{:S(2)}) collective-permute-start(f32[104,128]{1,0:T(8,128)S(1)} %get-tuple-element.39), channel_id=1, source_target_pairs={{0,4},{4,0},{8,12},{12,8},{16,20},{20,16},{24,28},{28,24},{1,5},{5... | collective-permute-start | bytes 159752 | tf_op jit(solution)/shard_map/ppermute | solution.py:537
  34.9 8.1 %collective-permute-start.5 = (bf16[104,128]{1,0:T(8,128)(2,1)S(1)}, bf16[104,128]{1,0:T(8,128)(2,1)S(1)}, u32[]{:S(2)}, u32[]{:S(2)}) collective-permute-start(bf16[104,128]{1,0:T(8,128)(2,1)S(1)} %add_convert_fusion), channel_id=1, source_target_pairs={{0,3},{1,2},{2,1},{3,0},{4,7},{5,6},{6,5},{7,4},{8,11},{9,10},{10,... | collective-permute-start | bytes 79880 | tf_op jit(solution)/shard_map/ppermute | solution.py:537
  38.6 5.0 %collective-permute-start.4 = (bf16[104,128]{1,0:T(8,128)(2,1)S(1)}, bf16[104,128]{1,0:T(8,128)(2,1)S(1)}, u32[]{:S(2)}, u32[]{:S(2)}) collective-permute-start(bf16[104,128]{1,0:T(8,128)(2,1)S(1)} %add_convert_fusion), channel_id=1, source_target_pairs={{0,2},{1,3},{2,0},{3,1},{4,6},{5,7},{6,4},{7,5},{8,10},{9,11},{10,... | collective-permute-start | bytes 79880 | tf_op jit(solution)/shard_map/ppermute | solution.py:537
  38.6 5.0 %collective-permute-start.3 = (bf16[104,128]{1,0:T(8,128)(2,1)S(1)}, bf16[104,128]{1,0:T(8,128)(2,1)S(1)}, u32[]{:S(2)}, u32[]{:S(2)}) collective-permute-start(bf16[104,128]{1,0:T(8,128)(2,1)S(1)} %add_convert_fusion), channel_id=1, source_target_pairs={{0,1},{1,0},{2,3},{3,2},{4,5},{5,4},{6,7},{7,6},{8,9},{9,8},{10,11... | collective-permute-start | bytes 79880 | tf_op jit(solution)/shard_map/ppermute | solution.py:537
  39.3 8.8 %collective-permute-start.8 = (bf16[8,5760]{1,0:T(8,128)(2,1)S(1)}, bf16[8,5760]{1,0:T(8,128)(2,1)S(1)}, u32[]{:S(2)}, u32[]{:S(2)}) collective-permute-start(bf16[8,5760]{1,0:T(8,128)(2,1)S(1)} %get-tuple-element.37.part0), channel_id=1, source_target_pairs={{0,3},{1,2},{2,1},{3,0},{4,7},{5,6},{6,5},{7,4},{8,11},{9,10},{10,... | collective-permute-start | bytes 276488 | tf_op jit(solution)/shard_map/ppermute | solution.py:537
  43.0 5.2 %collective-permute-start.7 = (bf16[8,5760]{1,0:T(8,128)(2,1)S(1)}, bf16[8,5760]{1,0:T(8,128)(2,1)S(1)}, u32[]{:S(2)}, u32[]{:S(2)}) collective-permute-start(bf16[8,5760]{1,0:T(8,128)(2,1)S(1)} %get-tuple-element.37.part0), channel_id=1, source_target_pairs={{0,1},{1,0},{2,3},{3,2},{4,5},{5,4},{6,7},{7,6},{8,9},{9,8},{10,11... | collective-permute-start | bytes 276488 | tf_op jit(solution)/shard_map/ppermute | solution.py:537
  43.6 4.6 %collective-permute-start.6 = (f32[104,128]{1,0:T(8,128)S(1)}, f32[104,128]{1,0:T(8,128)S(1)}, u32[]{:S(2)}, u32[]{:S(2)}) collective-permute-start(f32[104,128]{1,0:T(8,128)S(1)} %add_add_fusion), channel_id=1, source_target_pairs={{0,8},{4,12},{8,0},{12,4},{16,24},{20,28},{24,16},{28,20},{1,9},{5... | collective-permute-start | bytes 159752 | tf_op jit(solution)/shard_map/ppermute | solution.py:537
  46.1 7.0 %collective-permute-start.10 = (bf16[8,5760]{1,0:T(8,128)(2,1)S(1)}, bf16[8,5760]{1,0:T(8,128)(2,1)S(1)}, u32[]{:S(2)}, u32[]{:S(2)}) collective-permute-start(bf16[8,5760]{1,0:T(8,128)(2,1)S(1)} %get-tuple-element.37.part0), channel_id=1, source_target_pairs={{0,2},{1,3},{2,0},{3,1},{4,6},{5,7},{6,4},{7,5},{8,10},{9,11},{10,... | collective-permute-start | bytes 276488 | tf_op jit(solution)/shard_map/ppermute | solution.py:537
  48.2 4.8 %collective-permute-start.9 = (f32[104,128]{1,0:T(8,128)S(1)}, f32[104,128]{1,0:T(8,128)S(1)}, u32[]{:S(2)}, u32[]{:S(2)}) collective-permute-start(f32[104,128]{1,0:T(8,128)S(1)} %add.22), channel_id=1, source_target_pairs={{0,16},{4,20},{8,24},{12,28},{16,0},{20,4},{24,8},{28,12},{1,17},{... | collective-permute-start | bytes 159752 | tf_op jit(solution)/shard_map/ppermute | solution.py:537
  53.1 1.3 %collective-permute-start.11 = (f32[104,128]{1,0:T(8,128)S(1)}, f32[104,128]{1,0:T(8,128)S(1)}, u32[]{:S(2)}, u32[]{:S(2)}) collective-permute-start(f32[104,128]{1,0:T(8,128)S(1)} %add.23.mine), channel_id=1, source_target_pairs={{0,4},{4,0},{8,12},{12,8},{16,20},{20,16},{24,28},{28,24},{1,5},{5... | collective-permute-start | bytes 159752 | tf_op jit(solution)/shard_map/ppermute | solution.py:537

commit v15 on v14

--- a/solution.py
+++ b/solution.py
@@ -314,7 +314,7 @@
     fgrad_even,
     fgrad_odd,
     carry,
-    carry_lat,
+    sums,
     lat_lines,
     taps,
     acc_one,
@@ -348,7 +348,6 @@
     for fgrad in (fgrad_even, fgrad_odd):
         fgrad[:, 0] = jnp.zeros((4,) + fgrad.shape[2:], bf16)
     carry[...] = jnp.zeros(carry.shape, f32)
-    carry_lat[...] = jnp.zeros(carry_lat.shape, f32)
     for acc in (acc_one, acc_one_next, acc_two, acc_two_next):
         acc[...] = jnp.zeros(acc.shape, f32)
 
@@ -486,11 +485,8 @@
         z = jnp.dot(pick, grads, preferred_element_type=f32)
         z = jnp.concatenate([z[:48], z[48:]], axis=1)
         high = z.astype(bf16)
-        z = jnp.concatenate([high, (z - high.astype(f32)).astype(bf16)], axis=0)
-        z = jnp.dot(z, back_one[...], preferred_element_type=f32)
-        z = z[:48] + z[48:]
-        lat_lines[pl.ds(jnp.maximum(n - 1, 0), 48, stride=rows), :] = z[:, :LANES] + carry_lat[...]
-        carry_lat[...] = z[:, LANES:]
+        sums[0, n] = high
+        sums[1, n] = (z - high.astype(f32)).astype(bf16)
         yield
 
     def own_gradient(n, cast, fgrad):
@@ -523,6 +519,11 @@
     take_turns(own_gradient(rows, cast_even, fgrad_even), pull_back(rows - 1, fgrad_odd))
     take_turns(pull_back(rows, fgrad_even))
 
+    z = jnp.dot(sums[...].reshape(2 * (rows + 1) * 48, 512), back_one[...], preferred_element_type=f32)
+    z = z.reshape(2, rows + 1, 48, 2 * LANES)
+    z = z[0] + z[1]
+    for n in range(rows):
+        lat_lines[pl.ds(n, 48, stride=rows), :] = z[n + 1, :, :LANES] + z[n, :, LANES:]
     for t in range(own):
         out_lat[:, t * LANES : (t + 1) * LANES] = lat_lines[t * rows : (t + 1) * rows].astype(bf16)
     pack_taps(acc_one, acc_one_next, taps, 0, chan0, chan1, norm)
@@ -627,7 +628,7 @@
             pltpu.VMEM((4, front + 1, 16, LANES), bf16),
             pltpu.VMEM((4, front + 1, 16, LANES), bf16),
             pltpu.VMEM((front * 16, LANES), f32),
-            pltpu.VMEM((48, LANES), f32),
+            pltpu.VMEM((2, rows + 1, 48, 512), bf16),
             pltpu.VMEM((48 * rows, LANES), f32),
             pltpu.VMEM((tap_rows, LANES), f32),
             pltpu.VMEM((256, 256), f32),
@@ -650,13 +651,13 @@
     )
     taps = (taps + swapped(taps_send, "lat", 1)).astype(bf16)
     taps = total(taps, "mem", 1, 2)
-    one, two, three = (swapped(lat_grad, "mem", k) for k in range(1, 4))
+    one, three = (swapped(lat_grad, "mem", k) for k in (1, 3))
     bits = [1 << k for k in range(1, lat_count.bit_length() - 1)]
     for bit in bits:
         if bit == bits[-1]:
-            taps, one, three = lax.optimization_barrier((taps, one, three))
+            taps, one, three, late = lax.optimization_barrier((taps, one, three, lat_grad))
+            two = swapped(late, "mem", 2)
         taps = taps + swapped(taps, "lat", bit)
-    taps, two = lax.optimization_barrier((taps, two))
     other = swapped(taps, "lat", 1)
     latent_grad = pl.pallas_call(
         functools.partial(place_kernel, own),
@@ -666,6 +667,7 @@
         compiler_params=small,
         name="place",
     )(lat_grad, one, two, three)
+    other, latent_grad = lax.optimization_barrier((other, latent_grad))
     one, two = pl.pallas_call(
         taps_kernel,
         in_specs=[vmem] * 2,

time: 55.3 us -> 57.7 us (1.043)
  waiting for transfers between devices: 5.57 us -> 10.3 us
  Pallas kernels: 27 us -> 25.7 us
  starting transfers between devices: 21.7 us -> 20.7 us
    ppermute x10, waiting for transfers between devices: 3.98 us -> 8.74 us  [swapped(): lax.ppermute(array, axis, [(i, i ^ bit) for i in range(lax.axis_size(axis...]
    pallas_call x1, Pallas kernels: 20.7 us -> 19.4 us  [local(): pl.pallas_call(functools.partial(band_kernel, half, (chan0, chan1, chan2)...]
    ppermute x10, starting transfers between devices: 18 us -> 17 us  [swapped(): lax.ppermute(array, axis, [(i, i ^ bit) for i in range(lax.axis_size(axis...]
where the time goes in v15:
time: 57.7 us; the launch traced here: 57.6 us
  Pallas kernels  25.7 us (45%)
  starting transfers between devices  20.7 us (36%)
  waiting for transfers between devices  10.3 us (18%)
  between operations  0.84 us (1%)
    pallas_call x1, Pallas kernels, local(): pl.pallas_call(functools.partial(band_kernel, half, (chan0, chan1, chan2)...  19.4 us
    ppermute x10, starting transfers between devices, swapped(): lax.ppermute(array, axis, [(i, i ^ bit) for i in range(lax.axis_size(axis...  17 us
    ppermute x10, waiting for transfers between devices, swapped(): lax.ppermute(array, axis, [(i, i ^ bit) for i in range(lax.axis_size(axis...  8.74 us
    ppermute x2, starting transfers between devices, shifted(): return lax.ppermute(array, axis, pairs)  3.65 us
    pallas_call x1, Pallas kernels, local(): pl.pallas_call(functools.partial(prepare_kernel, half, chan0, chan2), in_...  2.13 us
    pallas_call x1, Pallas kernels, local(): pl.pallas_call(functools.partial(edge_kernel, half, chan2), in_specs=[hbm...  2.13 us
    ppermute x2, waiting for transfers between devices, shifted(): return lax.ppermute(array, axis, pairs)  1.58 us
  transfers between devices with their start and end apart: 12, of which 6 were waited for; matrix products, arithmetic and copies ran while one was open for 0% of the time, Pallas kernels for 6%

profile of v15, /device:TPU:0, one launch (start us, length us, event | category | flops | bytes accessed | tf_op | source)
XLA Modules:
  0.0 57.6 jit_solution(18321271594757554758)
XLA Ops:
  0.7 2.1 %edges.1 = (bf16[50,8,128]{2,1,0:T(8,128)(2,1)}, bf16[1,6400]{1,0:T(2,128)(2,1)}) custom-call(bf16[1,8,23040]{2,1,0:T(8,128)(2,1)} %latent_hbm.1, bf16[1,32,23040]{2,1,0:T(8,128)(2,1)} %targets_hbm.1, s32[32,48]{1,0:T(8,128)} %land_hbm.1), custom_call_target="tpu_custom_call" | custom-call | tf_op jit(solution)/shard_map/edges/pallas_call | solution.py:565
  2.9 2.4 %collective-permute-start = (bf16[50,8,128]{2,1,0:T(8,128)(2,1)}, bf16[50,8,128]{2,1,0:T(8,128)(2,1)S(1)}, u32[]{:S(2)}, u32[]{:S(2)}) collective-permute-start(bf16[50,8,128]{2,1,0:T(8,128)(2,1)} %get-tuple-element.30), channel_id=1, source_target_pairs={{0,4},{4,8},{8,12},{12,16},{16,20},{20,24},{24,28},{1,5},{5,9},{9,... | collective-permute-start | bytes 307208 | tf_op jit(solution)/shard_map/ppermute | solution.py:24
  5.2 1.3 %collective-permute-start.1 = (bf16[1,6400]{1,0:T(2,128)(2,1)}, bf16[1,6400]{1,0:T(2,128)(2,1)S(1)}, u32[]{:S(2)}, u32[]{:S(2)}) collective-permute-start(bf16[1,6400]{1,0:T(2,128)(2,1)} %get-tuple-element.31), channel_id=1, source_target_pairs={{4,0},{8,4},{12,8},{16,12},{20,16},{24,20},{28,24},{5,1},{9,5},{13... | collective-permute-start | bytes 38408 | tf_op jit(solution)/shard_map/ppermute | solution.py:24
  6.6 2.1 %prepare.1 = (bf16[8,25,16,128]{3,2,1,0:T(8,128)(2,1)S(1)}, f32[48,32,128]{2,1,0:T(8,128)S(1)}, f32[48,32,128]{2,1,0:T(8,128)S(1)}) custom-call(s32[8]{0:T(128)S(1)} %copy-done.3, f32[64]{0:T(128)S(1)} %copy-done.4, f32[16]{0:T(128)S(1)} %copy-done.5, bf16[1,8,23040]{2,1,0:T(8,128)(2,1)S(1)} %copy-done.1, bf16[1,32,23040]{2,1,0:T(8,128)(2,1)S(1)} %copy-done, ...), custom_call_target="tpu_custom_call" | custom-call | flops 100000000 | bytes 10000000 | tf_op jit(solution)/shard_map/prepare/pallas_call | solution.py:585
  8.7 0.3 bands.1
  9.0 1.6 %collective-permute-done.1.below = bf16[1,6400]{1,0:T(2,128)(2,1)S(1)} collective-permute-done((bf16[1,6400]{1,0:T(2,128)(2,1)}, bf16[1,6400]{1,0:T(2,128)(2,1)S(1)}, u32[]{:S(2)}, u32[]{:S(2)}) %collective-permute-start.1) | collective-permute-done | bytes 12832 | tf_op jit(solution)/shard_map/ppermute | solution.py:24
  10.6 0.0 collective-permute-done.above
  10.6 19.4 %band.1 = (bf16[8,5760]{1,0:T(8,128)(2,1)S(1)}, f32[104,128]{1,0:T(8,128)S(1)}, f32[104,128]{1,0:T(8,128)S(1)}) custom-call(s32[8]{0:T(128)S(1)} %copy-done.3, f32[64]{0:T(128)S(1)} %copy-done.4, f32[16]{0:T(128)S(1)} %copy-done.5, bf16[8,25,16,128]{3,2,1,0:T(8,128)(2,1)S(1)} %get-tuple-element.27.own_source, f32[48,32,128]{2,1,0:T(8,128)S(1)} %get-tuple-element.28.aims, ...), custom_call_target="tpu_custom_call" | custom-call | tf_op jit(solution)/shard_map/band/pallas_call | solution.py:608
  30.0 2.6 %collective-permute-start.2 = (f32[104,128]{1,0:T(8,128)S(1)}, f32[104,128]{1,0:T(8,128)S(1)}, u32[]{:S(2)}, u32[]{:S(2)}) collective-permute-start(f32[104,128]{1,0:T(8,128)S(1)} %get-tuple-element.39), channel_id=1, source_target_pairs={{0,4},{4,0},{8,12},{12,8},{16,20},{20,16},{24,28},{28,24},{1,5},{5... | collective-permute-start | bytes 159752 | tf_op jit(solution)/shard_map/ppermute | solution.py:538
  32.7 0.9 %collective-permute-done.2 = f32[104,128]{1,0:T(8,128)S(1)} collective-permute-done((f32[104,128]{1,0:T(8,128)S(1)}, f32[104,128]{1,0:T(8,128)S(1)}, u32[]{:S(2)}, u32[]{:S(2)}) %collective-permute-start.2) | collective-permute-done | bytes 53280 | tf_op jit(solution)/shard_map/ppermute | solution.py:538
  33.6 3.7 %collective-permute-start.5 = (bf16[104,128]{1,0:T(8,128)(2,1)S(1)}, bf16[104,128]{1,0:T(8,128)(2,1)S(1)}, u32[]{:S(2)}, u32[]{:S(2)}) collective-permute-start(bf16[104,128]{1,0:T(8,128)(2,1)S(1)} %add_convert_fusion), channel_id=1, source_target_pairs={{0,3},{1,2},{2,1},{3,0},{4,7},{5,6},{6,5},{7,4},{8,11},{9,10},{10,... | collective-permute-start | bytes 79880 | tf_op jit(solution)/shard_map/ppermute | solution.py:538
  37.2 0.8 %collective-permute-start.3 = (bf16[104,128]{1,0:T(8,128)(2,1)S(1)}, bf16[104,128]{1,0:T(8,128)(2,1)S(1)}, u32[]{:S(2)}, u32[]{:S(2)}) collective-permute-start(bf16[104,128]{1,0:T(8,128)(2,1)S(1)} %add_convert_fusion), channel_id=1, source_target_pairs={{0,1},{1,0},{2,3},{3,2},{4,5},{5,4},{6,7},{7,6},{8,9},{9,8},{10,11... | collective-permute-start | bytes 79880 | tf_op jit(solution)/shard_map/ppermute | solution.py:538
  38.0 3.6 %collective-permute-start.8 = (bf16[8,5760]{1,0:T(8,128)(2,1)S(1)}, bf16[8,5760]{1,0:T(8,128)(2,1)S(1)}, u32[]{:S(2)}, u32[]{:S(2)}) collective-permute-start(bf16[8,5760]{1,0:T(8,128)(2,1)S(1)} %get-tuple-element.43.part0), channel_id=1, source_target_pairs={{0,3},{1,2},{2,1},{3,0},{4,7},{5,6},{6,5},{7,4},{8,11},{9,10},{10,... | collective-permute-start | bytes 276488 | tf_op jit(solution)/shard_map/ppermute | solution.py:538
  41.6 0.6 %collective-permute-done.4 = bf16[104,128]{1,0:T(8,128)(2,1)S(1)} collective-permute-done((bf16[104,128]{1,0:T(8,128)(2,1)S(1)}, bf16[104,128]{1,0:T(8,128)(2,1)S(1)}, u32[]{:S(2)}, u32[]{:S(2)}) %collective-permute-start.4) | collective-permute-done | bytes 26656 | tf_op jit(solution)/shard_map/ppermute | solution.py:538
  42.2 0.0 collective-permute-done.3
  42.3 2.5 %collective-permute-start.6 = (f32[104,128]{1,0:T(8,128)S(1)}, f32[104,128]{1,0:T(8,128)S(1)}, u32[]{:S(2)}, u32[]{:S(2)}) collective-permute-start(f32[104,128]{1,0:T(8,128)S(1)} %add_add_fusion), channel_id=1, source_target_pairs={{0,8},{4,12},{8,0},{12,4},{16,24},{20,28},{24,16},{28,20},{1,9},{5... | collective-permute-start | bytes 159752 | tf_op jit(solution)/shard_map/ppermute | solution.py:538
  44.7 2.1 %collective-permute-done.6 = f32[104,128]{1,0:T(8,128)S(1)} collective-permute-done((f32[104,128]{1,0:T(8,128)S(1)}, f32[104,128]{1,0:T(8,128)S(1)}, u32[]{:S(2)}, u32[]{:S(2)}) %collective-permute-start.6) | collective-permute-done | bytes 53280 | tf_op jit(solution)/shard_map/ppermute | solution.py:538
  46.9 2.7 %collective-permute-start.9 = (f32[104,128]{1,0:T(8,128)S(1)}, f32[104,128]{1,0:T(8,128)S(1)}, u32[]{:S(2)}, u32[]{:S(2)}) collective-permute-start(f32[104,128]{1,0:T(8,128)S(1)} %add.22), channel_id=1, source_target_pairs={{0,16},{4,20},{8,24},{12,28},{16,0},{20,4},{24,8},{28,12},{1,17},{... | collective-permute-start | bytes 159752 | tf_op jit(solution)/shard_map/ppermute | solution.py:538
  49.6 1.1 %collective-permute-start.11 = (bf16[8,5760]{1,0:T(8,128)(2,1)S(1)}, bf16[8,5760]{1,0:T(8,128)(2,1)S(1)}, u32[]{:S(2)}, u32[]{:S(2)}) collective-permute-start(bf16[8,5760]{1,0:T(8,128)(2,1)S(1)} %get-tuple-element.43.part0), channel_id=1, source_target_pairs={{0,2},{1,3},{2,0},{3,1},{4,6},{5,7},{6,4},{7,5},{8,10},{9,11},{10,... | collective-permute-start | bytes 276488 | tf_op jit(solution)/shard_map/ppermute | solution.py:538
  50.7 1.0 %collective-permute-done.9 = f32[104,128]{1,0:T(8,128)S(1)} collective-permute-done((f32[104,128]{1,0:T(8,128)S(1)}, f32[104,128]{1,0:T(8,128)S(1)}, u32[]{:S(2)}, u32[]{:S(2)}) %collective-permute-start.9) | collective-permute-done | bytes 53280 | tf_op jit(solution)/shard_map/ppermute | solution.py:538
  51.7 0.1 collective-permute-start.10
  51.8 4.1 %collective-permute-done.11.part2 = bf16[8,5760]{1,0:T(8,128)(2,1)S(1)} collective-permute-done((bf16[8,5760]{1,0:T(8,128)(2,1)S(1)}, bf16[8,5760]{1,0:T(8,128)(2,1)S(1)}, u32[]{:S(2)}, u32[]{:S(2)}) %collective-permute-start.11) | collective-permute-done | bytes 92192 | tf_op jit(solution)/shard_map/ppermute | solution.py:538
  55.9 0.9 %place.1 = f32[1,8,23040]{2,1,0:T(8,128)} custom-call(bf16[8,5760]{1,0:T(8,128)(2,1)S(1)} %get-tuple-element.43.part0, bf16[8,5760]{1,0:T(8,128)(2,1)S(1)} %collective-permute-done.7.part1, bf16[8,5760]{1,0:T(8,128)(2,1)S(1)} %collective-permute-done.11.part2, bf16[8,5760]{1,0:T(8,128)(2,1)S(1)} %collective-permute-done.8.part3), custom_call_target="tpu_custom_call" | custom-call | tf_op jit(solution)/shard_map/place/pallas_call | solution.py:662
  56.8 0.8 %taps.1 = (f32[3,3,32,64]{3,2,1,0:T(8,128)}, f32[3,3,16,32]{3,2,1,0:T(8,128)}) custom-call(f32[104,128]{1,0:T(8,128)S(1)} %add.23.mine, f32[104,128]{1,0:T(8,128)S(1)} %collective-permute-done.10.other), custom_call_target="tpu_custom_call" | custom-call | tf_op jit(solution)/shard_map/taps/pallas_call | solution.py:671
  (26 shorter events, 0.1 us)
Async XLA Ops:
  0.6 5.9 %copy-start.2 = (s32[32,48]{1,0:T(8,128)S(1)}, s32[32,48]{1,0:T(8,128)}, u32[]{:S(2)}) copy-start(s32[32,48]{1,0:T(8,128)} %land_hbm.1) | copy-start | bytes 18436
  0.6 5.9 %copy-start = (bf16[1,32,23040]{2,1,0:T(8,128)(2,1)S(1)}, bf16[1,32,23040]{2,1,0:T(8,128)(2,1)}, u32[]{:S(2)}) copy-start(bf16[1,32,23040]{2,1,0:T(8,128)(2,1)} %targets_hbm.1) | copy-start | bytes 4423684
  0.7 5.9 %copy-start.1 = (bf16[1,8,23040]{2,1,0:T(8,128)(2,1)S(1)}, bf16[1,8,23040]{2,1,0:T(8,128)(2,1)}, u32[]{:S(2)}) copy-start(bf16[1,8,23040]{2,1,0:T(8,128)(2,1)} %latent_hbm.1) | copy-start | bytes 1105924
  0.7 5.9 %copy-start.5 = (f32[16]{0:T(128)S(1)}, f32[16]{0:T(128)}, u32[]{:S(2)}) copy-start(f32[16]{0:T(128)} %channel_weight.3) | copy-start | bytes 196
  0.7 5.9 %copy-start.4 = (f32[64]{0:T(128)S(1)}, f32[64]{0:T(128)}, u32[]{:S(2)}) copy-start(f32[64]{0:T(128)} %scale.3) | copy-start | bytes 772
  0.7 5.9 %copy-start.3 = (s32[8]{0:T(128)S(1)}, s32[8]{0:T(128)}, u32[]{:S(2)}) copy-start(s32[8]{0:T(128)} %seeds.3) | copy-start | bytes 100
  0.7 8.0 %copy-start.7 = (bf16[3,3,32,16]{2,3,1,0:T(8,128)(2,1)S(1)}, bf16[3,3,32,16]{2,3,1,0:T(8,128)(2,1)}, u32[]{:S(2)}) copy-start(bf16[3,3,32,16]{2,3,1,0:T(8,128)(2,1)} %param.12) | copy-start | bytes 27652
  0.7 8.0 %copy-start.6 = (bf16[3,3,64,32]{2,3,1,0:T(8,128)(2,1)S(1)}, bf16[3,3,64,32]{2,3,1,0:T(8,128)(2,1)}, u32[]{:S(2)}) copy-start(bf16[3,3,64,32]{2,3,1,0:T(8,128)(2,1)} %param.11) | copy-start | bytes 110596
  2.9 7.8 %collective-permute-start = (bf16[50,8,128]{2,1,0:T(8,128)(2,1)}, bf16[50,8,128]{2,1,0:T(8,128)(2,1)S(1)}, u32[]{:S(2)}, u32[]{:S(2)}) collective-permute-start(bf16[50,8,128]{2,1,0:T(8,128)(2,1)} %get-tuple-element.30), channel_id=1, source_target_pairs={{0,4},{4,8},{8,12},{12,16},{16,20},{20,24},{24,28},{1,5},{5,9},{9,... | collective-permute-start | bytes 307208 | tf_op jit(solution)/shard_map/ppermute | solution.py:24
  5.2 5.4 %collective-permute-start.1 = (bf16[1,6400]{1,0:T(2,128)(2,1)}, bf16[1,6400]{1,0:T(2,128)(2,1)S(1)}, u32[]{:S(2)}, u32[]{:S(2)}) collective-permute-start(bf16[1,6400]{1,0:T(2,128)(2,1)} %get-tuple-element.31), channel_id=1, source_target_pairs={{4,0},{8,4},{12,8},{16,12},{20,16},{24,20},{28,24},{5,1},{9,5},{13... | collective-permute-start | bytes 38408 | tf_op jit(solution)/shard_map/ppermute | solution.py:24
  30.0 3.5 %collective-permute-start.2 = (f32[104,128]{1,0:T(8,128)S(1)}, f32[104,128]{1,0:T(8,128)S(1)}, u32[]{:S(2)}, u32[]{:S(2)}) collective-permute-start(f32[104,128]{1,0:T(8,128)S(1)} %get-tuple-element.39), channel_id=1, source_target_pairs={{0,4},{4,0},{8,12},{12,8},{16,20},{20,16},{24,28},{28,24},{1,5},{5... | collective-permute-start | bytes 159752 | tf_op jit(solution)/shard_map/ppermute | solution.py:538
  33.6 8.1 %collective-permute-start.5 = (bf16[104,128]{1,0:T(8,128)(2,1)S(1)}, bf16[104,128]{1,0:T(8,128)(2,1)S(1)}, u32[]{:S(2)}, u32[]{:S(2)}) collective-permute-start(bf16[104,128]{1,0:T(8,128)(2,1)S(1)} %add_convert_fusion), channel_id=1, source_target_pairs={{0,3},{1,2},{2,1},{3,0},{4,7},{5,6},{6,5},{7,4},{8,11},{9,10},{10,... | collective-permute-start | bytes 79880 | tf_op jit(solution)/shard_map/ppermute | solution.py:538
  37.2 5.0 %collective-permute-start.4 = (bf16[104,128]{1,0:T(8,128)(2,1)S(1)}, bf16[104,128]{1,0:T(8,128)(2,1)S(1)}, u32[]{:S(2)}, u32[]{:S(2)}) collective-permute-start(bf16[104,128]{1,0:T(8,128)(2,1)S(1)} %add_convert_fusion), channel_id=1, source_target_pairs={{0,2},{1,3},{2,0},{3,1},{4,6},{5,7},{6,4},{7,5},{8,10},{9,11},{10,... | collective-permute-start | bytes 79880 | tf_op jit(solution)/shard_map/ppermute | solution.py:538
  37.2 5.0 %collective-permute-start.3 = (bf16[104,128]{1,0:T(8,128)(2,1)S(1)}, bf16[104,128]{1,0:T(8,128)(2,1)S(1)}, u32[]{:S(2)}, u32[]{:S(2)}) collective-permute-start(bf16[104,128]{1,0:T(8,128)(2,1)S(1)} %add_convert_fusion), channel_id=1, source_target_pairs={{0,1},{1,0},{2,3},{3,2},{4,5},{5,4},{6,7},{7,6},{8,9},{9,8},{10,11... | collective-permute-start | bytes 79880 | tf_op jit(solution)/shard_map/ppermute | solution.py:538
  38.0 8.8 %collective-permute-start.8 = (bf16[8,5760]{1,0:T(8,128)(2,1)S(1)}, bf16[8,5760]{1,0:T(8,128)(2,1)S(1)}, u32[]{:S(2)}, u32[]{:S(2)}) collective-permute-start(bf16[8,5760]{1,0:T(8,128)(2,1)S(1)} %get-tuple-element.43.part0), channel_id=1, source_target_pairs={{0,3},{1,2},{2,1},{3,0},{4,7},{5,6},{6,5},{7,4},{8,11},{9,10},{10,... | collective-permute-start | bytes 276488 | tf_op jit(solution)/shard_map/ppermute | solution.py:538
  41.6 5.2 %collective-permute-start.7 = (bf16[8,5760]{1,0:T(8,128)(2,1)S(1)}, bf16[8,5760]{1,0:T(8,128)(2,1)S(1)}, u32[]{:S(2)}, u32[]{:S(2)}) collective-permute-start(bf16[8,5760]{1,0:T(8,128)(2,1)S(1)} %get-tuple-element.43.part0), channel_id=1, source_target_pairs={{0,1},{1,0},{2,3},{3,2},{4,5},{5,4},{6,7},{7,6},{8,9},{9,8},{10,11... | collective-permute-start | bytes 276488 | tf_op jit(solution)/shard_map/ppermute | solution.py:538
  42.3 4.6 %collective-permute-start.6 = (f32[104,128]{1,0:T(8,128)S(1)}, f32[104,128]{1,0:T(8,128)S(1)}, u32[]{:S(2)}, u32[]{:S(2)}) collective-permute-start(f32[104,128]{1,0:T(8,128)S(1)} %add_add_fusion), channel_id=1, source_target_pairs={{0,8},{4,12},{8,0},{12,4},{16,24},{20,28},{24,16},{28,20},{1,9},{5... | collective-permute-start | bytes 159752 | tf_op jit(solution)/shard_map/ppermute | solution.py:538
  46.9 4.8 %collective-permute-start.9 = (f32[104,128]{1,0:T(8,128)S(1)}, f32[104,128]{1,0:T(8,128)S(1)}, u32[]{:S(2)}, u32[]{:S(2)}) collective-permute-start(f32[104,128]{1,0:T(8,128)S(1)} %add.22), channel_id=1, source_target_pairs={{0,16},{4,20},{8,24},{12,28},{16,0},{20,4},{24,8},{28,12},{1,17},{... | collective-permute-start | bytes 159752 | tf_op jit(solution)/shard_map/ppermute | solution.py:538
  49.6 6.3 %collective-permute-start.11 = (bf16[8,5760]{1,0:T(8,128)(2,1)S(1)}, bf16[8,5760]{1,0:T(8,128)(2,1)S(1)}, u32[]{:S(2)}, u32[]{:S(2)}) collective-permute-start(bf16[8,5760]{1,0:T(8,128)(2,1)S(1)} %get-tuple-element.43.part0), channel_id=1, source_target_pairs={{0,2},{1,3},{2,0},{3,1},{4,6},{5,7},{6,4},{7,5},{8,10},{9,11},{10,... | collective-permute-start | bytes 276488 | tf_op jit(solution)/shard_map/ppermute | solution.py:538
  51.7 5.1 %collective-permute-start.10 = (f32[104,128]{1,0:T(8,128)S(1)}, f32[104,128]{1,0:T(8,128)S(1)}, u32[]{:S(2)}, u32[]{:S(2)}) collective-permute-start(f32[104,128]{1,0:T(8,128)S(1)} %add.23.mine), channel_id=1, source_target_pairs={{0,4},{4,0},{8,12},{12,8},{16,20},{20,16},{24,28},{28,24},{1,5},{5... | collective-permute-start | bytes 159752 | tf_op jit(solution)/shard_map/ppermute | solution.py:538

commit v16 on v15

--- a/solution.py
+++ b/solution.py
@@ -85,7 +85,8 @@
                     back_ref[at : at + chan_out, row * LANES : (row + 1) * LANES] = part.astype(jnp.bfloat16)
 
 
-def pack_taps(acc_ref, next_ref, out_ref, first, chan_in, chan_out, norm):
+def pack_taps(acc_ref, out_ref, first, chan_in, chan_out, norm):
+    acc = acc_ref[...].T
     cells = LANES // chan_in
     group = iota((chan_out, LANES), 1) // chan_in
     packed = None
@@ -98,10 +99,10 @@
             q = 2 * reach + b - 1
             if 0 <= q < 2 * cells:
                 block, cell = reach // cells, reach % cells
-                lines = sub * LANES + q * chan_out if block == 0 else sub * chan_out
-                ref = acc_ref if block == 0 else next_ref
-                piece = ref[lines : lines + chan_out, row * LANES : (row + 1) * LANES]
-                turn = (slot - cell) % cells * chan_in
+                lines = sub * LANES + q * chan_out
+                lanes = row * LANES if block == 0 else 256
+                piece = acc[lines : lines + chan_out, lanes : lanes + LANES]
+                turn = (slot - (cell if block == 0 else row)) % cells * chan_in
                 piece = pltpu.roll(piece, turn, 1) if turn else piece
                 part = piece if part is None else part + piece
         packed = part if slot == 0 else jnp.where(group == slot, part, packed)
@@ -318,9 +319,7 @@
     lat_lines,
     taps,
     acc_one,
-    acc_one_next,
     acc_two,
-    acc_two_next,
 ):
     rows = own_source.shape[0]
     blocks = span // LANES
@@ -348,7 +347,7 @@
     for fgrad in (fgrad_even, fgrad_odd):
         fgrad[:, 0] = jnp.zeros((4,) + fgrad.shape[2:], bf16)
     carry[...] = jnp.zeros(carry.shape, f32)
-    for acc in (acc_one, acc_one_next, acc_two, acc_two_next):
+    for acc in (acc_one, acc_two):
         acc[...] = jnp.zeros(acc.shape, f32)
 
     def line(slot, i):
@@ -452,12 +451,11 @@
         def flat(line, start, count):
             return fgrad[line, start : start + count].reshape(count * 16, LANES)
 
-        def add_taps(g, x, acc, acc_next, chan_out):
-            turned = g.T
-            acc[...] += jnp.dot(turned, x[:, :256], preferred_element_type=f32)
-            last = [turned[k * LANES - chan_out : k * LANES] for k in (1, 2)]
-            last = jnp.concatenate(last, axis=0)
-            acc_next[...] += jnp.dot(last, x[:, 256:], preferred_element_type=f32)
+        def add_taps(g, x, acc, chan_in):
+            beside = pltpu.roll(x[:, 384:], chan_in, 1)
+            after = jnp.where(iota((x.shape[0], LANES), 1) < chan_in, x[:, 256:384], beside)
+            turned = jnp.concatenate([x[:, :256].T, after.T[: 2 * chan_in]], axis=0)
+            acc[: 256 + 2 * chan_in] += jnp.dot(turned, g, preferred_element_type=f32)
 
         g = [
             jnp.concatenate(
@@ -478,9 +476,9 @@
         g = [jnp.concatenate([flat(2 * k, 2, half), flat(2 * k + 1, 2, half)], axis=1) for k in range(2)]
         x = [operand(act, 2 * n + k, 1, half) for k in range(2)]
         if with_taps:
-            add_taps(jnp.concatenate(g, axis=0), jnp.concatenate(x, axis=0), acc_two, acc_two_next, chan2)
+            add_taps(jnp.concatenate(g, axis=0), jnp.concatenate(x, axis=0), acc_two, chan1)
             yield
-            add_taps(grads[16:], operand(source, n, 1, half), acc_one, acc_one_next, chan1)
+            add_taps(grads[16:], operand(source, n, 1, half), acc_one, chan0)
             yield
         z = jnp.dot(pick, grads, preferred_element_type=f32)
         z = jnp.concatenate([z[:48], z[48:]], axis=1)
@@ -526,8 +524,8 @@
         lat_lines[pl.ds(n, 48, stride=rows), :] = z[n + 1, :, :LANES] + z[n, :, LANES:]
     for t in range(own):
         out_lat[:, t * LANES : (t + 1) * LANES] = lat_lines[t * rows : (t + 1) * rows].astype(bf16)
-    pack_taps(acc_one, acc_one_next, taps, 0, chan0, chan1, norm)
-    pack_taps(acc_two, acc_two_next, taps, -(-9 // (LANES // chan0)) * chan1, chan1, chan2, norm)
+    pack_taps(acc_one, taps, 0, chan0, chan1, norm)
+    pack_taps(acc_two, taps, -(-9 // (LANES // chan0)) * chan1, chan1, chan2, norm)
     count = taps_keep.shape[0]
     odd = jnp.bitwise_and(lat_pos, 1)
     taps_keep[...] = taps[pl.ds(pl.multiple_of(odd * count, 8), count), :]
@@ -631,10 +629,8 @@
             pltpu.VMEM((2, rows + 1, 48, 512), bf16),
             pltpu.VMEM((48 * rows, LANES), f32),
             pltpu.VMEM((tap_rows, LANES), f32),
-            pltpu.VMEM((256, 256), f32),
-            pltpu.VMEM((2 * chan1, 256), f32),
-            pltpu.VMEM((256, 256), f32),
-            pltpu.VMEM((2 * chan2, 256), f32),
+            pltpu.VMEM((384, 256), f32),
+            pltpu.VMEM((384, 256), f32),
         ],
         compiler_params=params,
         name="band",
@@ -651,13 +647,13 @@
     )
     taps = (taps + swapped(taps_send, "lat", 1)).astype(bf16)
     taps = total(taps, "mem", 1, 2)
-    one, three = (swapped(lat_grad, "mem", k) for k in (1, 3))
+    one, two, three = (swapped(lat_grad, "mem", k) for k in range(1, 4))
     bits = [1 << k for k in range(1, lat_count.bit_length() - 1)]
     for bit in bits:
         if bit == bits[-1]:
-            taps, one, three, late = lax.optimization_barrier((taps, one, three, lat_grad))
-            two = swapped(late, "mem", 2)
+            taps, one, three = lax.optimization_barrier((taps, one, three))
         taps = taps + swapped(taps, "lat", bit)
+    taps, two = lax.optimization_barrier((taps, two))
     other = swapped(taps, "lat", 1)
     latent_grad = pl.pallas_call(
         functools.partial(place_kernel, own),
@@ -667,7 +663,6 @@
         compiler_params=small,
         name="place",
     )(lat_grad, one, two, three)
-    other, latent_grad = lax.optimization_barrier((other, latent_grad))
     one, two = pl.pallas_call(
         taps_kernel,
         in_specs=[vmem] * 2,

time: 57.7 us -> 54.6 us (0.946)
  waiting for transfers between devices: 10.3 us -> 5.57 us
  starting transfers between devices: 20.7 us -> 21.6 us
  Pallas kernels: 25.7 us -> 26.3 us
    ppermute x10, waiting for transfers between devices: 8.74 us -> 3.98 us  [swapped(): lax.ppermute(array, axis, [(i, i ^ bit) for i in range(lax.axis_size(axis...]
    ppermute x10, starting transfers between devices: 17 us -> 18 us  [swapped(): lax.ppermute(array, axis, [(i, i ^ bit) for i in range(lax.axis_size(axis...]
    pallas_call x1, Pallas kernels: 19.4 us -> 20.1 us  [local(): pl.pallas_call(functools.partial(band_kernel, half, (chan0, chan1, chan2)...]
where the time goes in v16:
time: 54.6 us; the launch traced here: 54.5 us
  Pallas kernels  26.3 us (48%)
  starting transfers between devices  21.6 us (40%)
  waiting for transfers between devices  5.57 us (10%)
  between operations  0.84 us (2%)
    pallas_call x1, Pallas kernels, local(): pl.pallas_call(functools.partial(band_kernel, half, (chan0, chan1, chan2)...  20.1 us
    ppermute x10, starting transfers between devices, swapped(): lax.ppermute(array, axis, [(i, i ^ bit) for i in range(lax.axis_size(axis...  18 us
    ppermute x10, waiting for transfers between devices, swapped(): lax.ppermute(array, axis, [(i, i ^ bit) for i in range(lax.axis_size(axis...  3.98 us
    ppermute x2, starting transfers between devices, shifted(): return lax.ppermute(array, axis, pairs)  3.65 us
    pallas_call x1, Pallas kernels, local(): pl.pallas_call(functools.partial(prepare_kernel, half, chan0, chan2), in_...  2.13 us
    pallas_call x1, Pallas kernels, local(): pl.pallas_call(functools.partial(edge_kernel, half, chan2), in_specs=[hbm...  2.13 us
    ppermute x2, waiting for transfers between devices, shifted(): return lax.ppermute(array, axis, pairs)  1.58 us
  transfers between devices with their start and end apart: 12, of which 6 were waited for; matrix products, arithmetic and copies ran while one was open for 0% of the time, Pallas kernels for 6%

profile of v16, /device:TPU:0, one launch (start us, length us, event | category | flops | bytes accessed | tf_op | source)
XLA Modules:
  0.0 54.5 jit_solution(10121565705993466308)
XLA Ops:
  0.7 2.1 %edges.1 = (bf16[50,8,128]{2,1,0:T(8,128)(2,1)}, bf16[1,6400]{1,0:T(2,128)(2,1)}) custom-call(bf16[1,8,23040]{2,1,0:T(8,128)(2,1)} %latent_hbm.1, bf16[1,32,23040]{2,1,0:T(8,128)(2,1)} %targets_hbm.1, s32[32,48]{1,0:T(8,128)} %land_hbm.1), custom_call_target="tpu_custom_call" | custom-call | tf_op jit(solution)/shard_map/edges/pallas_call | solution.py:563
  2.9 2.4 %collective-permute-start = (bf16[50,8,128]{2,1,0:T(8,128)(2,1)}, bf16[50,8,128]{2,1,0:T(8,128)(2,1)S(1)}, u32[]{:S(2)}, u32[]{:S(2)}) collective-permute-start(bf16[50,8,128]{2,1,0:T(8,128)(2,1)} %get-tuple-element.29), channel_id=1, source_target_pairs={{0,4},{4,8},{8,12},{12,16},{16,20},{20,24},{24,28},{1,5},{5,9},{9,... | collective-permute-start | bytes 307208 | tf_op jit(solution)/shard_map/ppermute | solution.py:24
  5.2 1.3 %collective-permute-start.1 = (bf16[1,6400]{1,0:T(2,128)(2,1)}, bf16[1,6400]{1,0:T(2,128)(2,1)S(1)}, u32[]{:S(2)}, u32[]{:S(2)}) collective-permute-start(bf16[1,6400]{1,0:T(2,128)(2,1)} %get-tuple-element.30), channel_id=1, source_target_pairs={{4,0},{8,4},{12,8},{16,12},{20,16},{24,20},{28,24},{5,1},{9,5},{13... | collective-permute-start | bytes 38408 | tf_op jit(solution)/shard_map/ppermute | solution.py:24
  6.6 2.1 %prepare.1 = (bf16[8,25,16,128]{3,2,1,0:T(8,128)(2,1)S(1)}, f32[48,32,128]{2,1,0:T(8,128)S(1)}, f32[48,32,128]{2,1,0:T(8,128)S(1)}) custom-call(s32[8]{0:T(128)S(1)} %copy-done.3, f32[64]{0:T(128)S(1)} %copy-done.4, f32[16]{0:T(128)S(1)} %copy-done.5, bf16[1,8,23040]{2,1,0:T(8,128)(2,1)S(1)} %copy-done.1, bf16[1,32,23040]{2,1,0:T(8,128)(2,1)S(1)} %copy-done, ...), custom_call_target="tpu_custom_call" | custom-call | flops 100000000 | bytes 10000000 | tf_op jit(solution)/shard_map/prepare/pallas_call | solution.py:583
  8.7 0.3 bands.1
  9.0 1.6 %collective-permute-done.1.below = bf16[1,6400]{1,0:T(2,128)(2,1)S(1)} collective-permute-done((bf16[1,6400]{1,0:T(2,128)(2,1)}, bf16[1,6400]{1,0:T(2,128)(2,1)S(1)}, u32[]{:S(2)}, u32[]{:S(2)}) %collective-permute-start.1) | collective-permute-done | bytes 12832 | tf_op jit(solution)/shard_map/ppermute | solution.py:24
  10.6 20.1 %band.1 = (bf16[8,5760]{1,0:T(8,128)(2,1)S(1)}, f32[104,128]{1,0:T(8,128)S(1)}, f32[104,128]{1,0:T(8,128)S(1)}) custom-call(s32[8]{0:T(128)S(1)} %copy-done.3, f32[64]{0:T(128)S(1)} %copy-done.4, f32[16]{0:T(128)S(1)} %copy-done.5, bf16[8,25,16,128]{3,2,1,0:T(8,128)(2,1)S(1)} %get-tuple-element.26.own_source, f32[48,32,128]{2,1,0:T(8,128)S(1)} %get-tuple-element.27.aims, ...), custom_call_target="tpu_custom_call" | custom-call | tf_op jit(solution)/shard_map/band/pallas_call | solution.py:606
  30.7 2.6 %collective-permute-start.2 = (f32[104,128]{1,0:T(8,128)S(1)}, f32[104,128]{1,0:T(8,128)S(1)}, u32[]{:S(2)}, u32[]{:S(2)}) collective-permute-start(f32[104,128]{1,0:T(8,128)S(1)} %get-tuple-element.39), channel_id=1, source_target_pairs={{0,4},{4,0},{8,12},{12,8},{16,20},{20,16},{24,28},{28,24},{1,5},{5... | collective-permute-start | bytes 159752 | tf_op jit(solution)/shard_map/ppermute | solution.py:536
  33.3 0.9 %collective-permute-done.2 = f32[104,128]{1,0:T(8,128)S(1)} collective-permute-done((f32[104,128]{1,0:T(8,128)S(1)}, f32[104,128]{1,0:T(8,128)S(1)}, u32[]{:S(2)}, u32[]{:S(2)}) %collective-permute-start.2) | collective-permute-done | bytes 53280 | tf_op jit(solution)/shard_map/ppermute | solution.py:536
  34.2 3.7 %collective-permute-start.5 = (bf16[104,128]{1,0:T(8,128)(2,1)S(1)}, bf16[104,128]{1,0:T(8,128)(2,1)S(1)}, u32[]{:S(2)}, u32[]{:S(2)}) collective-permute-start(bf16[104,128]{1,0:T(8,128)(2,1)S(1)} %add_convert_fusion), channel_id=1, source_target_pairs={{0,3},{1,2},{2,1},{3,0},{4,7},{5,6},{6,5},{7,4},{8,11},{9,10},{10,... | collective-permute-start | bytes 79880 | tf_op jit(solution)/shard_map/ppermute | solution.py:536
  37.9 0.8 %collective-permute-start.3 = (bf16[104,128]{1,0:T(8,128)(2,1)S(1)}, bf16[104,128]{1,0:T(8,128)(2,1)S(1)}, u32[]{:S(2)}, u32[]{:S(2)}) collective-permute-start(bf16[104,128]{1,0:T(8,128)(2,1)S(1)} %add_convert_fusion), channel_id=1, source_target_pairs={{0,1},{1,0},{2,3},{3,2},{4,5},{5,4},{6,7},{7,6},{8,9},{9,8},{10,11... | collective-permute-start | bytes 79880 | tf_op jit(solution)/shard_map/ppermute | solution.py:536
  38.7 3.6 %collective-permute-start.8 = (bf16[8,5760]{1,0:T(8,128)(2,1)S(1)}, bf16[8,5760]{1,0:T(8,128)(2,1)S(1)}, u32[]{:S(2)}, u32[]{:S(2)}) collective-permute-start(bf16[8,5760]{1,0:T(8,128)(2,1)S(1)} %get-tuple-element.37.part0), channel_id=1, source_target_pairs={{0,3},{1,2},{2,1},{3,0},{4,7},{5,6},{6,5},{7,4},{8,11},{9,10},{10,... | collective-permute-start | bytes 276488 | tf_op jit(solution)/shard_map/ppermute | solution.py:536
  42.3 0.0 collective-permute-done.5
  42.3 0.6 %collective-permute-done.4 = bf16[104,128]{1,0:T(8,128)(2,1)S(1)} collective-permute-done((bf16[104,128]{1,0:T(8,128)(2,1)S(1)}, bf16[104,128]{1,0:T(8,128)(2,1)S(1)}, u32[]{:S(2)}, u32[]{:S(2)}) %collective-permute-start.4) | collective-permute-done | bytes 26656 | tf_op jit(solution)/shard_map/ppermute | solution.py:536
  42.9 0.0 collective-permute-done.3
  42.9 2.5 %collective-permute-start.6 = (f32[104,128]{1,0:T(8,128)S(1)}, f32[104,128]{1,0:T(8,128)S(1)}, u32[]{:S(2)}, u32[]{:S(2)}) collective-permute-start(f32[104,128]{1,0:T(8,128)S(1)} %add_add_fusion), channel_id=1, source_target_pairs={{0,8},{4,12},{8,0},{12,4},{16,24},{20,28},{24,16},{28,20},{1,9},{5... | collective-permute-start | bytes 159752 | tf_op jit(solution)/shard_map/ppermute | solution.py:536
  45.4 2.1 %collective-permute-start.10 = (bf16[8,5760]{1,0:T(8,128)(2,1)S(1)}, bf16[8,5760]{1,0:T(8,128)(2,1)S(1)}, u32[]{:S(2)}, u32[]{:S(2)}) collective-permute-start(bf16[8,5760]{1,0:T(8,128)(2,1)S(1)} %get-tuple-element.37.part0), channel_id=1, source_target_pairs={{0,2},{1,3},{2,0},{3,1},{4,6},{5,7},{6,4},{7,5},{8,10},{9,11},{10,... | collective-permute-start | bytes 276488 | tf_op jit(solution)/shard_map/ppermute | solution.py:536
  47.4 0.1 collective-permute-done.6
  47.5 2.7 %collective-permute-start.9 = (f32[104,128]{1,0:T(8,128)S(1)}, f32[104,128]{1,0:T(8,128)S(1)}, u32[]{:S(2)}, u32[]{:S(2)}) collective-permute-start(f32[104,128]{1,0:T(8,128)S(1)} %add.22), channel_id=1, source_target_pairs={{0,16},{4,20},{8,24},{12,28},{16,0},{20,4},{24,8},{28,12},{1,17},{... | collective-permute-start | bytes 159752 | tf_op jit(solution)/shard_map/ppermute | solution.py:536
  50.2 2.1 %collective-permute-done.9 = f32[104,128]{1,0:T(8,128)S(1)} collective-permute-done((f32[104,128]{1,0:T(8,128)S(1)}, f32[104,128]{1,0:T(8,128)S(1)}, u32[]{:S(2)}, u32[]{:S(2)}) %collective-permute-start.9) | collective-permute-done | bytes 53280 | tf_op jit(solution)/shard_map/ppermute | solution.py:536
  52.4 0.1 collective-permute-start.11
  52.5 0.9 %place.1 = f32[1,8,23040]{2,1,0:T(8,128)} custom-call(bf16[8,5760]{1,0:T(8,128)(2,1)S(1)} %get-tuple-element.37.part0, bf16[8,5760]{1,0:T(8,128)(2,1)S(1)} %collective-permute-done.7.part1, bf16[8,5760]{1,0:T(8,128)(2,1)S(1)} %collective-permute-done.10.part2, bf16[8,5760]{1,0:T(8,128)(2,1)S(1)} %collective-permute-done.8.part3), custom_call_target="tpu_custom_call" | custom-call | tf_op jit(solution)/shard_map/place/pallas_call | solution.py:658
  53.4 0.3 collective-permute-done.11.other
  53.7 0.8 %taps.1 = (f32[3,3,32,64]{3,2,1,0:T(8,128)}, f32[3,3,16,32]{3,2,1,0:T(8,128)}) custom-call(f32[104,128]{1,0:T(8,128)S(1)} %add.23.mine, f32[104,128]{1,0:T(8,128)S(1)} %collective-permute-done.11.other), custom_call_target="tpu_custom_call" | custom-call | tf_op jit(solution)/shard_map/taps/pallas_call | solution.py:666
  (26 shorter events, 0.1 us)
Async XLA Ops:
  0.6 5.9 %copy-start.2 = (s32[32,48]{1,0:T(8,128)S(1)}, s32[32,48]{1,0:T(8,128)}, u32[]{:S(2)}) copy-start(s32[32,48]{1,0:T(8,128)} %land_hbm.1) | copy-start | bytes 18436
  0.6 5.9 %copy-start = (bf16[1,32,23040]{2,1,0:T(8,128)(2,1)S(1)}, bf16[1,32,23040]{2,1,0:T(8,128)(2,1)}, u32[]{:S(2)}) copy-start(bf16[1,32,23040]{2,1,0:T(8,128)(2,1)} %targets_hbm.1) | copy-start | bytes 4423684
  0.7 5.9 %copy-start.1 = (bf16[1,8,23040]{2,1,0:T(8,128)(2,1)S(1)}, bf16[1,8,23040]{2,1,0:T(8,128)(2,1)}, u32[]{:S(2)}) copy-start(bf16[1,8,23040]{2,1,0:T(8,128)(2,1)} %latent_hbm.1) | copy-start | bytes 1105924
  0.7 5.9 %copy-start.5 = (f32[16]{0:T(128)S(1)}, f32[16]{0:T(128)}, u32[]{:S(2)}) copy-start(f32[16]{0:T(128)} %channel_weight.3) | copy-start | bytes 196
  0.7 5.9 %copy-start.4 = (f32[64]{0:T(128)S(1)}, f32[64]{0:T(128)}, u32[]{:S(2)}) copy-start(f32[64]{0:T(128)} %scale.3) | copy-start | bytes 772
  0.7 5.9 %copy-start.3 = (s32[8]{0:T(128)S(1)}, s32[8]{0:T(128)}, u32[]{:S(2)}) copy-start(s32[8]{0:T(128)} %seeds.3) | copy-start | bytes 100
  0.7 8.0 %copy-start.7 = (bf16[3,3,32,16]{2,3,1,0:T(8,128)(2,1)S(1)}, bf16[3,3,32,16]{2,3,1,0:T(8,128)(2,1)}, u32[]{:S(2)}) copy-start(bf16[3,3,32,16]{2,3,1,0:T(8,128)(2,1)} %param.12) | copy-start | bytes 27652
  0.7 8.0 %copy-start.6 = (bf16[3,3,64,32]{2,3,1,0:T(8,128)(2,1)S(1)}, bf16[3,3,64,32]{2,3,1,0:T(8,128)(2,1)}, u32[]{:S(2)}) copy-start(bf16[3,3,64,32]{2,3,1,0:T(8,128)(2,1)} %param.11) | copy-start | bytes 110596
  2.9 7.8 %collective-permute-start = (bf16[50,8,128]{2,1,0:T(8,128)(2,1)}, bf16[50,8,128]{2,1,0:T(8,128)(2,1)S(1)}, u32[]{:S(2)}, u32[]{:S(2)}) collective-permute-start(bf16[50,8,128]{2,1,0:T(8,128)(2,1)} %get-tuple-element.29), channel_id=1, source_target_pairs={{0,4},{4,8},{8,12},{12,16},{16,20},{20,24},{24,28},{1,5},{5,9},{9,... | collective-permute-start | bytes 307208 | tf_op jit(solution)/shard_map/ppermute | solution.py:24
  5.2 5.4 %collective-permute-start.1 = (bf16[1,6400]{1,0:T(2,128)(2,1)}, bf16[1,6400]{1,0:T(2,128)(2,1)S(1)}, u32[]{:S(2)}, u32[]{:S(2)}) collective-permute-start(bf16[1,6400]{1,0:T(2,128)(2,1)} %get-tuple-element.30), channel_id=1, source_target_pairs={{4,0},{8,4},{12,8},{16,12},{20,16},{24,20},{28,24},{5,1},{9,5},{13... | collective-permute-start | bytes 38408 | tf_op jit(solution)/shard_map/ppermute | solution.py:24
  30.7 3.5 %collective-permute-start.2 = (f32[104,128]{1,0:T(8,128)S(1)}, f32[104,128]{1,0:T(8,128)S(1)}, u32[]{:S(2)}, u32[]{:S(2)}) collective-permute-start(f32[104,128]{1,0:T(8,128)S(1)} %get-tuple-element.39), channel_id=1, source_target_pairs={{0,4},{4,0},{8,12},{12,8},{16,20},{20,16},{24,28},{28,24},{1,5},{5... | collective-permute-start | bytes 159752 | tf_op jit(solution)/shard_map/ppermute | solution.py:536
  34.2 8.0 %collective-permute-start.5 = (bf16[104,128]{1,0:T(8,128)(2,1)S(1)}, bf16[104,128]{1,0:T(8,128)(2,1)S(1)}, u32[]{:S(2)}, u32[]{:S(2)}) collective-permute-start(bf16[104,128]{1,0:T(8,128)(2,1)S(1)} %add_convert_fusion), channel_id=1, source_target_pairs={{0,3},{1,2},{2,1},{3,0},{4,7},{5,6},{6,5},{7,4},{8,11},{9,10},{10,... | collective-permute-start | bytes 79880 | tf_op jit(solution)/shard_map/ppermute | solution.py:536
  37.9 5.0 %collective-permute-start.4 = (bf16[104,128]{1,0:T(8,128)(2,1)S(1)}, bf16[104,128]{1,0:T(8,128)(2,1)S(1)}, u32[]{:S(2)}, u32[]{:S(2)}) collective-permute-start(bf16[104,128]{1,0:T(8,128)(2,1)S(1)} %add_convert_fusion), channel_id=1, source_target_pairs={{0,2},{1,3},{2,0},{3,1},{4,6},{5,7},{6,4},{7,5},{8,10},{9,11},{10,... | collective-permute-start | bytes 79880 | tf_op jit(solution)/shard_map/ppermute | solution.py:536
  37.9 5.0 %collective-permute-start.3 = (bf16[104,128]{1,0:T(8,128)(2,1)S(1)}, bf16[104,128]{1,0:T(8,128)(2,1)S(1)}, u32[]{:S(2)}, u32[]{:S(2)}) collective-permute-start(bf16[104,128]{1,0:T(8,128)(2,1)S(1)} %add_convert_fusion), channel_id=1, source_target_pairs={{0,1},{1,0},{2,3},{3,2},{4,5},{5,4},{6,7},{7,6},{8,9},{9,8},{10,11... | collective-permute-start | bytes 79880 | tf_op jit(solution)/shard_map/ppermute | solution.py:536
  38.7 8.8 %collective-permute-start.8 = (bf16[8,5760]{1,0:T(8,128)(2,1)S(1)}, bf16[8,5760]{1,0:T(8,128)(2,1)S(1)}, u32[]{:S(2)}, u32[]{:S(2)}) collective-permute-start(bf16[8,5760]{1,0:T(8,128)(2,1)S(1)} %get-tuple-element.37.part0), channel_id=1, source_target_pairs={{0,3},{1,2},{2,1},{3,0},{4,7},{5,6},{6,5},{7,4},{8,11},{9,10},{10,... | collective-permute-start | bytes 276488 | tf_op jit(solution)/shard_map/ppermute | solution.py:536
  42.3 5.2 %collective-permute-start.7 = (bf16[8,5760]{1,0:T(8,128)(2,1)S(1)}, bf16[8,5760]{1,0:T(8,128)(2,1)S(1)}, u32[]{:S(2)}, u32[]{:S(2)}) collective-permute-start(bf16[8,5760]{1,0:T(8,128)(2,1)S(1)} %get-tuple-element.37.part0), channel_id=1, source_target_pairs={{0,1},{1,0},{2,3},{3,2},{4,5},{5,4},{6,7},{7,6},{8,9},{9,8},{10,11... | collective-permute-start | bytes 276488 | tf_op jit(solution)/shard_map/ppermute | solution.py:536
  42.9 4.6 %collective-permute-start.6 = (f32[104,128]{1,0:T(8,128)S(1)}, f32[104,128]{1,0:T(8,128)S(1)}, u32[]{:S(2)}, u32[]{:S(2)}) collective-permute-start(f32[104,128]{1,0:T(8,128)S(1)} %add_add_fusion), channel_id=1, source_target_pairs={{0,8},{4,12},{8,0},{12,4},{16,24},{20,28},{24,16},{28,20},{1,9},{5... | collective-permute-start | bytes 159752 | tf_op jit(solution)/shard_map/ppermute | solution.py:536
  45.4 7.0 %collective-permute-start.10 = (bf16[8,5760]{1,0:T(8,128)(2,1)S(1)}, bf16[8,5760]{1,0:T(8,128)(2,1)S(1)}, u32[]{:S(2)}, u32[]{:S(2)}) collective-permute-start(bf16[8,5760]{1,0:T(8,128)(2,1)S(1)} %get-tuple-element.37.part0), channel_id=1, source_target_pairs={{0,2},{1,3},{2,0},{3,1},{4,6},{5,7},{6,4},{7,5},{8,10},{9,11},{10,... | collective-permute-start | bytes 276488 | tf_op jit(solution)/shard_map/ppermute | solution.py:536
  47.5 4.8 %collective-permute-start.9 = (f32[104,128]{1,0:T(8,128)S(1)}, f32[104,128]{1,0:T(8,128)S(1)}, u32[]{:S(2)}, u32[]{:S(2)}) collective-permute-start(f32[104,128]{1,0:T(8,128)S(1)} %add.22), channel_id=1, source_target_pairs={{0,16},{4,20},{8,24},{12,28},{16,0},{20,4},{24,8},{28,12},{1,17},{... | collective-permute-start | bytes 159752 | tf_op jit(solution)/shard_map/ppermute | solution.py:536
  52.4 1.3 %collective-permute-start.11 = (f32[104,128]{1,0:T(8,128)S(1)}, f32[104,128]{1,0:T(8,128)S(1)}, u32[]{:S(2)}, u32[]{:S(2)}) collective-permute-start(f32[104,128]{1,0:T(8,128)S(1)} %add.23.mine), channel_id=1, source_target_pairs={{0,4},{4,0},{8,12},{12,8},{16,20},{20,16},{24,28},{28,24},{1,5},{5... | collective-permute-start | bytes 159752 | tf_op jit(solution)/shard_map/ppermute | solution.py:536

commit v17 on v15

--- a/solution.py
+++ b/solution.py
@@ -313,6 +313,8 @@
     cast_odd,
     fgrad_even,
     fgrad_odd,
+    grads_even,
+    grads_odd,
     carry,
     sums,
     lat_lines,
@@ -448,16 +450,16 @@
                 fgrad[line, t + 1] = jnp.concatenate(parts, axis=0).astype(bf16)
             yield
 
-    def pull_back(n, fgrad, with_taps=True):
+    def add_taps(g, x, acc, acc_next, chan_out):
+        turned = g.T
+        acc[...] += jnp.dot(turned, x[:, :256], preferred_element_type=f32)
+        last = [turned[k * LANES - chan_out : k * LANES] for k in (1, 2)]
+        last = jnp.concatenate(last, axis=0)
+        acc_next[...] += jnp.dot(last, x[:, 256:], preferred_element_type=f32)
+
+    def pull_back(n, fgrad, grads_ref, with_taps=True):
         def flat(line, start, count):
             return fgrad[line, start : start + count].reshape(count * 16, LANES)
-
-        def add_taps(g, x, acc, acc_next, chan_out):
-            turned = g.T
-            acc[...] += jnp.dot(turned, x[:, :256], preferred_element_type=f32)
-            last = [turned[k * LANES - chan_out : k * LANES] for k in (1, 2)]
-            last = jnp.concatenate(last, axis=0)
-            acc_next[...] += jnp.dot(last, x[:, 256:], preferred_element_type=f32)
 
         g = [
             jnp.concatenate(
@@ -474,15 +476,19 @@
         carry[...] = pulled[members:, LANES:]
         grads = [(grads[k] * slope[2 * n + k].reshape(members, LANES)).astype(bf16) for k in range(2)]
         yield
-        grads = jnp.concatenate(grads, axis=1)
-        g = [jnp.concatenate([flat(2 * k, 2, half), flat(2 * k + 1, 2, half)], axis=1) for k in range(2)]
-        x = [operand(act, 2 * n + k, 1, half) for k in range(2)]
+        grads_ref[...] = jnp.concatenate(grads, axis=1)
         if with_taps:
+            g = [jnp.concatenate([flat(2 * k, 2, half), flat(2 * k + 1, 2, half)], axis=1) for k in range(2)]
+            x = [operand(act, 2 * n + k, 1, half) for k in range(2)]
             add_taps(jnp.concatenate(g, axis=0), jnp.concatenate(x, axis=0), acc_two, acc_two_next, chan2)
             yield
-            add_taps(grads[16:], operand(source, n, 1, half), acc_one, acc_one_next, chan1)
-            yield
-        z = jnp.dot(pick, grads, preferred_element_type=f32)
+
+    def first_taps(n, grads_ref, keep=None):
+        g = grads_ref[16:]
+        g = g if keep is None else g * keep
+        add_taps(g, operand(source, n, 1, half), acc_one, acc_one_next, chan1)
+        yield
+        z = jnp.dot(pick, grads_ref[...], preferred_element_type=f32)
         z = jnp.concatenate([z[:48], z[48:]], axis=1)
         high = z.astype(bf16)
         sums[0, n] = high
@@ -496,12 +502,14 @@
         take_turns(
             second_product(2 * m + 3, cast_odd),
             own_gradient(2 * m + 2, cast_even, fgrad_even),
-            pull_back(2 * m + 1, fgrad_odd),
+            pull_back(2 * m + 1, fgrad_odd, grads_odd),
+            first_taps(2 * m, grads_even, jnp.where(m >= 1, 1.0, 0.0).astype(bf16)),
         )
         take_turns(
             second_product(2 * m + 4, cast_even),
             own_gradient(2 * m + 3, cast_odd, fgrad_odd),
-            pull_back(2 * m + 2, fgrad_even),
+            pull_back(2 * m + 2, fgrad_even, grads_even),
+            first_taps(2 * m + 1, grads_odd),
         )
         return 0
 
@@ -513,11 +521,16 @@
     take_turns(
         second_product(2, cast_even),
         own_gradient(1, cast_odd, fgrad_odd),
-        pull_back(0, fgrad_even, with_taps=False),
+        pull_back(0, fgrad_even, grads_even, with_taps=False),
     )
     lax.fori_loop(0, rows // 2 - 1, second_segment, 0)
-    take_turns(own_gradient(rows, cast_even, fgrad_even), pull_back(rows - 1, fgrad_odd))
-    take_turns(pull_back(rows, fgrad_even))
+    take_turns(
+        own_gradient(rows, cast_even, fgrad_even),
+        pull_back(rows - 1, fgrad_odd, grads_odd),
+        first_taps(rows - 2, grads_even),
+    )
+    take_turns(pull_back(rows, fgrad_even, grads_even), first_taps(rows - 1, grads_odd))
+    take_turns(first_taps(rows, grads_even))
 
     z = jnp.dot(sums[...].reshape(2 * (rows + 1) * 48, 512), back_one[...], preferred_element_type=f32)
     z = z.reshape(2, rows + 1, 48, 2 * LANES)
@@ -627,6 +640,8 @@
             pltpu.VMEM((4, front, 16, LANES), bf16),
             pltpu.VMEM((4, front + 1, 16, LANES), bf16),
             pltpu.VMEM((4, front + 1, 16, LANES), bf16),
+            pltpu.VMEM((front * 16, 2 * LANES), bf16),
+            pltpu.VMEM((front * 16, 2 * LANES), bf16),
             pltpu.VMEM((front * 16, LANES), f32),
             pltpu.VMEM((2, rows + 1, 48, 512), bf16),
             pltpu.VMEM((48 * rows, LANES), f32),
@@ -651,13 +666,13 @@
     )
     taps = (taps + swapped(taps_send, "lat", 1)).astype(bf16)
     taps = total(taps, "mem", 1, 2)
-    one, three = (swapped(lat_grad, "mem", k) for k in (1, 3))
+    one, two, three = (swapped(lat_grad, "mem", k) for k in range(1, 4))
     bits = [1 << k for k in range(1, lat_count.bit_length() - 1)]
     for bit in bits:
         if bit == bits[-1]:
-            taps, one, three, late = lax.optimization_barrier((taps, one, three, lat_grad))
-            two = swapped(late, "mem", 2)
+            taps, one, three = lax.optimization_barrier((taps, one, three))
         taps = taps + swapped(taps, "lat", bit)
+    taps, two = lax.optimization_barrier((taps, two))
     other = swapped(taps, "lat", 1)
     latent_grad = pl.pallas_call(
         functools.partial(place_kernel, own),
@@ -667,7 +682,6 @@
         compiler_params=small,
         name="place",
     )(lat_grad, one, two, three)
-    other, latent_grad = lax.optimization_barrier((other, latent_grad))
     one, two = pl.pallas_call(
         taps_kernel,
         in_specs=[vmem] * 2,

time: 57.7 us -> 53.9 us (0.934)
  waiting for transfers between devices: 10.3 us -> 5.57 us
  starting transfers between devices: 20.7 us -> 21.7 us
    ppermute x10, waiting for transfers between devices: 8.74 us -> 3.98 us  [swapped(): lax.ppermute(array, axis, [(i, i ^ bit) for i in range(lax.axis_size(axis...]
    ppermute x10, starting transfers between devices: 17 us -> 18 us  [swapped(): lax.ppermute(array, axis, [(i, i ^ bit) for i in range(lax.axis_size(axis...]
where the time goes in v17:
time: 53.9 us; the launch traced here: 53.8 us
  Pallas kernels  25.6 us (47%)
  starting transfers between devices  21.7 us (40%)
  waiting for transfers between devices  5.57 us (10%)
  between operations  0.85 us (2%)
    pallas_call x1, Pallas kernels, local(): pl.pallas_call(functools.partial(band_kernel, half, (chan0, chan1, chan2)...  19.3 us
    ppermute x10, starting transfers between devices, swapped(): lax.ppermute(array, axis, [(i, i ^ bit) for i in range(lax.axis_size(axis...  18 us
    ppermute x10, waiting for transfers between devices, swapped(): lax.ppermute(array, axis, [(i, i ^ bit) for i in range(lax.axis_size(axis...  3.98 us
    ppermute x2, starting transfers between devices, shifted(): return lax.ppermute(array, axis, pairs)  3.65 us
    pallas_call x1, Pallas kernels, local(): pl.pallas_call(functools.partial(prepare_kernel, half, chan0, chan2), in_...  2.13 us
    pallas_call x1, Pallas kernels, local(): pl.pallas_call(functools.partial(edge_kernel, half, chan2), in_specs=[hbm...  2.13 us
    ppermute x2, waiting for transfers between devices, shifted(): return lax.ppermute(array, axis, pairs)  1.58 us
  transfers between devices with their start and end apart: 12, of which 6 were waited for; matrix products, arithmetic and copies ran while one was open for 0% of the time, Pallas kernels for 6%

profile of v17, /device:TPU:0, one launch (start us, length us, event | category | flops | bytes accessed | tf_op | source)
XLA Modules:
  0.0 53.8 jit_solution(2912543381854231625)
XLA Ops:
  0.7 2.1 %edges.1 = (bf16[50,8,128]{2,1,0:T(8,128)(2,1)}, bf16[1,6400]{1,0:T(2,128)(2,1)}) custom-call(bf16[1,8,23040]{2,1,0:T(8,128)(2,1)} %latent_hbm.1, bf16[1,32,23040]{2,1,0:T(8,128)(2,1)} %targets_hbm.1, s32[32,48]{1,0:T(8,128)} %land_hbm.1), custom_call_target="tpu_custom_call" | custom-call | tf_op jit(solution)/shard_map/edges/pallas_call | solution.py:578
  2.9 2.4 %collective-permute-start = (bf16[50,8,128]{2,1,0:T(8,128)(2,1)}, bf16[50,8,128]{2,1,0:T(8,128)(2,1)S(1)}, u32[]{:S(2)}, u32[]{:S(2)}) collective-permute-start(bf16[50,8,128]{2,1,0:T(8,128)(2,1)} %get-tuple-element.29), channel_id=1, source_target_pairs={{0,4},{4,8},{8,12},{12,16},{16,20},{20,24},{24,28},{1,5},{5,9},{9,... | collective-permute-start | bytes 307208 | tf_op jit(solution)/shard_map/ppermute | solution.py:24
  5.2 1.3 %collective-permute-start.1 = (bf16[1,6400]{1,0:T(2,128)(2,1)}, bf16[1,6400]{1,0:T(2,128)(2,1)S(1)}, u32[]{:S(2)}, u32[]{:S(2)}) collective-permute-start(bf16[1,6400]{1,0:T(2,128)(2,1)} %get-tuple-element.30), channel_id=1, source_target_pairs={{4,0},{8,4},{12,8},{16,12},{20,16},{24,20},{28,24},{5,1},{9,5},{13... | collective-permute-start | bytes 38408 | tf_op jit(solution)/shard_map/ppermute | solution.py:24
  6.6 2.1 %prepare.1 = (bf16[8,25,16,128]{3,2,1,0:T(8,128)(2,1)S(1)}, f32[48,32,128]{2,1,0:T(8,128)S(1)}, f32[48,32,128]{2,1,0:T(8,128)S(1)}) custom-call(s32[8]{0:T(128)S(1)} %copy-done.3, f32[64]{0:T(128)S(1)} %copy-done.4, f32[16]{0:T(128)S(1)} %copy-done.5, bf16[1,8,23040]{2,1,0:T(8,128)(2,1)S(1)} %copy-done.1, bf16[1,32,23040]{2,1,0:T(8,128)(2,1)S(1)} %copy-done, ...), custom_call_target="tpu_custom_call" | custom-call | flops 100000000 | bytes 10000000 | tf_op jit(solution)/shard_map/prepare/pallas_call | solution.py:598
  8.7 0.3 bands.1
  9.0 1.6 %collective-permute-done.1.below = bf16[1,6400]{1,0:T(2,128)(2,1)S(1)} collective-permute-done((bf16[1,6400]{1,0:T(2,128)(2,1)}, bf16[1,6400]{1,0:T(2,128)(2,1)S(1)}, u32[]{:S(2)}, u32[]{:S(2)}) %collective-permute-start.1) | collective-permute-done | bytes 12832 | tf_op jit(solution)/shard_map/ppermute | solution.py:24
  10.6 19.3 %band.1 = (bf16[8,5760]{1,0:T(8,128)(2,1)S(1)}, f32[104,128]{1,0:T(8,128)S(1)}, f32[104,128]{1,0:T(8,128)S(1)}) custom-call(s32[8]{0:T(128)S(1)} %copy-done.3, f32[64]{0:T(128)S(1)} %copy-done.4, f32[16]{0:T(128)S(1)} %copy-done.5, bf16[8,25,16,128]{3,2,1,0:T(8,128)(2,1)S(1)} %get-tuple-element.26.own_source, f32[48,32,128]{2,1,0:T(8,128)S(1)} %get-tuple-element.27.aims, ...), custom_call_target="tpu_custom_call" | custom-call | tf_op jit(solution)/shard_map/band/pallas_call | solution.py:621
  30.0 2.6 %collective-permute-start.2 = (f32[104,128]{1,0:T(8,128)S(1)}, f32[104,128]{1,0:T(8,128)S(1)}, u32[]{:S(2)}, u32[]{:S(2)}) collective-permute-start(f32[104,128]{1,0:T(8,128)S(1)} %get-tuple-element.39), channel_id=1, source_target_pairs={{0,4},{4,0},{8,12},{12,8},{16,20},{20,16},{24,28},{28,24},{1,5},{5... | collective-permute-start | bytes 159752 | tf_op jit(solution)/shard_map/ppermute | solution.py:551
  32.6 0.9 %collective-permute-done.2 = f32[104,128]{1,0:T(8,128)S(1)} collective-permute-done((f32[104,128]{1,0:T(8,128)S(1)}, f32[104,128]{1,0:T(8,128)S(1)}, u32[]{:S(2)}, u32[]{:S(2)}) %collective-permute-start.2) | collective-permute-done | bytes 53280 | tf_op jit(solution)/shard_map/ppermute | solution.py:551
  33.5 3.7 %collective-permute-start.5 = (bf16[104,128]{1,0:T(8,128)(2,1)S(1)}, bf16[104,128]{1,0:T(8,128)(2,1)S(1)}, u32[]{:S(2)}, u32[]{:S(2)}) collective-permute-start(bf16[104,128]{1,0:T(8,128)(2,1)S(1)} %add_convert_fusion), channel_id=1, source_target_pairs={{0,3},{1,2},{2,1},{3,0},{4,7},{5,6},{6,5},{7,4},{8,11},{9,10},{10,... | collective-permute-start | bytes 79880 | tf_op jit(solution)/shard_map/ppermute | solution.py:551
  37.2 0.8 %collective-permute-start.3 = (bf16[104,128]{1,0:T(8,128)(2,1)S(1)}, bf16[104,128]{1,0:T(8,128)(2,1)S(1)}, u32[]{:S(2)}, u32[]{:S(2)}) collective-permute-start(bf16[104,128]{1,0:T(8,128)(2,1)S(1)} %add_convert_fusion), channel_id=1, source_target_pairs={{0,1},{1,0},{2,3},{3,2},{4,5},{5,4},{6,7},{7,6},{8,9},{9,8},{10,11... | collective-permute-start | bytes 79880 | tf_op jit(solution)/shard_map/ppermute | solution.py:551
  38.0 3.6 %collective-permute-start.8 = (bf16[8,5760]{1,0:T(8,128)(2,1)S(1)}, bf16[8,5760]{1,0:T(8,128)(2,1)S(1)}, u32[]{:S(2)}, u32[]{:S(2)}) collective-permute-start(bf16[8,5760]{1,0:T(8,128)(2,1)S(1)} %get-tuple-element.37.part0), channel_id=1, source_target_pairs={{0,3},{1,2},{2,1},{3,0},{4,7},{5,6},{6,5},{7,4},{8,11},{9,10},{10,... | collective-permute-start | bytes 276488 | tf_op jit(solution)/shard_map/ppermute | solution.py:551
  41.6 0.0 collective-permute-start.7
  41.6 0.6 %collective-permute-done.4 = bf16[104,128]{1,0:T(8,128)(2,1)S(1)} collective-permute-done((bf16[104,128]{1,0:T(8,128)(2,1)S(1)}, bf16[104,128]{1,0:T(8,128)(2,1)S(1)}, u32[]{:S(2)}, u32[]{:S(2)}) %collective-permute-start.4) | collective-permute-done | bytes 26656 | tf_op jit(solution)/shard_map/ppermute | solution.py:551
  42.2 0.0 collective-permute-done.3
  42.2 2.5 %collective-permute-start.6 = (f32[104,128]{1,0:T(8,128)S(1)}, f32[104,128]{1,0:T(8,128)S(1)}, u32[]{:S(2)}, u32[]{:S(2)}) collective-permute-start(f32[104,128]{1,0:T(8,128)S(1)} %add_add_fusion), channel_id=1, source_target_pairs={{0,8},{4,12},{8,0},{12,4},{16,24},{20,28},{24,16},{28,20},{1,9},{5... | collective-permute-start | bytes 159752 | tf_op jit(solution)/shard_map/ppermute | solution.py:551
  44.7 2.1 %collective-permute-start.10 = (bf16[8,5760]{1,0:T(8,128)(2,1)S(1)}, bf16[8,5760]{1,0:T(8,128)(2,1)S(1)}, u32[]{:S(2)}, u32[]{:S(2)}) collective-permute-start(bf16[8,5760]{1,0:T(8,128)(2,1)S(1)} %get-tuple-element.37.part0), channel_id=1, source_target_pairs={{0,2},{1,3},{2,0},{3,1},{4,6},{5,7},{6,4},{7,5},{8,10},{9,11},{10,... | collective-permute-start | bytes 276488 | tf_op jit(solution)/shard_map/ppermute | solution.py:551
  46.7 0.1 collective-permute-done.6
  46.8 2.7 %collective-permute-start.9 = (f32[104,128]{1,0:T(8,128)S(1)}, f32[104,128]{1,0:T(8,128)S(1)}, u32[]{:S(2)}, u32[]{:S(2)}) collective-permute-start(f32[104,128]{1,0:T(8,128)S(1)} %add.22), channel_id=1, source_target_pairs={{0,16},{4,20},{8,24},{12,28},{16,0},{20,4},{24,8},{28,12},{1,17},{... | collective-permute-start | bytes 159752 | tf_op jit(solution)/shard_map/ppermute | solution.py:551
  49.5 2.1 %collective-permute-done.9 = f32[104,128]{1,0:T(8,128)S(1)} collective-permute-done((f32[104,128]{1,0:T(8,128)S(1)}, f32[104,128]{1,0:T(8,128)S(1)}, u32[]{:S(2)}, u32[]{:S(2)}) %collective-permute-start.9) | collective-permute-done | bytes 53280 | tf_op jit(solution)/shard_map/ppermute | solution.py:551
  51.7 0.1 collective-permute-start.11
  51.7 0.9 %place.1 = f32[1,8,23040]{2,1,0:T(8,128)} custom-call(bf16[8,5760]{1,0:T(8,128)(2,1)S(1)} %get-tuple-element.37.part0, bf16[8,5760]{1,0:T(8,128)(2,1)S(1)} %collective-permute-done.7.part1, bf16[8,5760]{1,0:T(8,128)(2,1)S(1)} %collective-permute-done.10.part2, bf16[8,5760]{1,0:T(8,128)(2,1)S(1)} %collective-permute-done.8.part3), custom_call_target="tpu_custom_call" | custom-call | tf_op jit(solution)/shard_map/place/pallas_call | solution.py:677
  52.7 0.3 collective-permute-done.11.other
  53.0 0.8 %taps.1 = (f32[3,3,32,64]{3,2,1,0:T(8,128)}, f32[3,3,16,32]{3,2,1,0:T(8,128)}) custom-call(f32[104,128]{1,0:T(8,128)S(1)} %add.23.mine, f32[104,128]{1,0:T(8,128)S(1)} %collective-permute-done.11.other), custom_call_target="tpu_custom_call" | custom-call | tf_op jit(solution)/shard_map/taps/pallas_call | solution.py:685
  (26 shorter events, 0.1 us)
Async XLA Ops:
  0.6 5.9 %copy-start.2 = (s32[32,48]{1,0:T(8,128)S(1)}, s32[32,48]{1,0:T(8,128)}, u32[]{:S(2)}) copy-start(s32[32,48]{1,0:T(8,128)} %land_hbm.1) | copy-start | bytes 18436
  0.6 5.9 %copy-start = (bf16[1,32,23040]{2,1,0:T(8,128)(2,1)S(1)}, bf16[1,32,23040]{2,1,0:T(8,128)(2,1)}, u32[]{:S(2)}) copy-start(bf16[1,32,23040]{2,1,0:T(8,128)(2,1)} %targets_hbm.1) | copy-start | bytes 4423684
  0.7 5.9 %copy-start.1 = (bf16[1,8,23040]{2,1,0:T(8,128)(2,1)S(1)}, bf16[1,8,23040]{2,1,0:T(8,128)(2,1)}, u32[]{:S(2)}) copy-start(bf16[1,8,23040]{2,1,0:T(8,128)(2,1)} %latent_hbm.1) | copy-start | bytes 1105924
  0.7 5.9 %copy-start.5 = (f32[16]{0:T(128)S(1)}, f32[16]{0:T(128)}, u32[]{:S(2)}) copy-start(f32[16]{0:T(128)} %channel_weight.3) | copy-start | bytes 196
  0.7 5.9 %copy-start.4 = (f32[64]{0:T(128)S(1)}, f32[64]{0:T(128)}, u32[]{:S(2)}) copy-start(f32[64]{0:T(128)} %scale.3) | copy-start | bytes 772
  0.7 5.9 %copy-start.3 = (s32[8]{0:T(128)S(1)}, s32[8]{0:T(128)}, u32[]{:S(2)}) copy-start(s32[8]{0:T(128)} %seeds.3) | copy-start | bytes 100
  0.7 8.0 %copy-start.7 = (bf16[3,3,32,16]{2,3,1,0:T(8,128)(2,1)S(1)}, bf16[3,3,32,16]{2,3,1,0:T(8,128)(2,1)}, u32[]{:S(2)}) copy-start(bf16[3,3,32,16]{2,3,1,0:T(8,128)(2,1)} %param.12) | copy-start | bytes 27652
  0.7 8.0 %copy-start.6 = (bf16[3,3,64,32]{2,3,1,0:T(8,128)(2,1)S(1)}, bf16[3,3,64,32]{2,3,1,0:T(8,128)(2,1)}, u32[]{:S(2)}) copy-start(bf16[3,3,64,32]{2,3,1,0:T(8,128)(2,1)} %param.11) | copy-start | bytes 110596
  2.9 7.8 %collective-permute-start = (bf16[50,8,128]{2,1,0:T(8,128)(2,1)}, bf16[50,8,128]{2,1,0:T(8,128)(2,1)S(1)}, u32[]{:S(2)}, u32[]{:S(2)}) collective-permute-start(bf16[50,8,128]{2,1,0:T(8,128)(2,1)} %get-tuple-element.29), channel_id=1, source_target_pairs={{0,4},{4,8},{8,12},{12,16},{16,20},{20,24},{24,28},{1,5},{5,9},{9,... | collective-permute-start | bytes 307208 | tf_op jit(solution)/shard_map/ppermute | solution.py:24
  5.2 5.4 %collective-permute-start.1 = (bf16[1,6400]{1,0:T(2,128)(2,1)}, bf16[1,6400]{1,0:T(2,128)(2,1)S(1)}, u32[]{:S(2)}, u32[]{:S(2)}) collective-permute-start(bf16[1,6400]{1,0:T(2,128)(2,1)} %get-tuple-element.30), channel_id=1, source_target_pairs={{4,0},{8,4},{12,8},{16,12},{20,16},{24,20},{28,24},{5,1},{9,5},{13... | collective-permute-start | bytes 38408 | tf_op jit(solution)/shard_map/ppermute | solution.py:24
  30.0 3.5 %collective-permute-start.2 = (f32[104,128]{1,0:T(8,128)S(1)}, f32[104,128]{1,0:T(8,128)S(1)}, u32[]{:S(2)}, u32[]{:S(2)}) collective-permute-start(f32[104,128]{1,0:T(8,128)S(1)} %get-tuple-element.39), channel_id=1, source_target_pairs={{0,4},{4,0},{8,12},{12,8},{16,20},{20,16},{24,28},{28,24},{1,5},{5... | collective-permute-start | bytes 159752 | tf_op jit(solution)/shard_map/ppermute | solution.py:551
  33.5 8.1 %collective-permute-start.5 = (bf16[104,128]{1,0:T(8,128)(2,1)S(1)}, bf16[104,128]{1,0:T(8,128)(2,1)S(1)}, u32[]{:S(2)}, u32[]{:S(2)}) collective-permute-start(bf16[104,128]{1,0:T(8,128)(2,1)S(1)} %add_convert_fusion), channel_id=1, source_target_pairs={{0,3},{1,2},{2,1},{3,0},{4,7},{5,6},{6,5},{7,4},{8,11},{9,10},{10,... | collective-permute-start | bytes 79880 | tf_op jit(solution)/shard_map/ppermute | solution.py:551
  37.2 5.0 %collective-permute-start.4 = (bf16[104,128]{1,0:T(8,128)(2,1)S(1)}, bf16[104,128]{1,0:T(8,128)(2,1)S(1)}, u32[]{:S(2)}, u32[]{:S(2)}) collective-permute-start(bf16[104,128]{1,0:T(8,128)(2,1)S(1)} %add_convert_fusion), channel_id=1, source_target_pairs={{0,2},{1,3},{2,0},{3,1},{4,6},{5,7},{6,4},{7,5},{8,10},{9,11},{10,... | collective-permute-start | bytes 79880 | tf_op jit(solution)/shard_map/ppermute | solution.py:551
  37.2 5.0 %collective-permute-start.3 = (bf16[104,128]{1,0:T(8,128)(2,1)S(1)}, bf16[104,128]{1,0:T(8,128)(2,1)S(1)}, u32[]{:S(2)}, u32[]{:S(2)}) collective-permute-start(bf16[104,128]{1,0:T(8,128)(2,1)S(1)} %add_convert_fusion), channel_id=1, source_target_pairs={{0,1},{1,0},{2,3},{3,2},{4,5},{5,4},{6,7},{7,6},{8,9},{9,8},{10,11... | collective-permute-start | bytes 79880 | tf_op jit(solution)/shard_map/ppermute | solution.py:551
  38.0 8.8 %collective-permute-start.8 = (bf16[8,5760]{1,0:T(8,128)(2,1)S(1)}, bf16[8,5760]{1,0:T(8,128)(2,1)S(1)}, u32[]{:S(2)}, u32[]{:S(2)}) collective-permute-start(bf16[8,5760]{1,0:T(8,128)(2,1)S(1)} %get-tuple-element.37.part0), channel_id=1, source_target_pairs={{0,3},{1,2},{2,1},{3,0},{4,7},{5,6},{6,5},{7,4},{8,11},{9,10},{10,... | collective-permute-start | bytes 276488 | tf_op jit(solution)/shard_map/ppermute | solution.py:551
  41.6 5.2 %collective-permute-start.7 = (bf16[8,5760]{1,0:T(8,128)(2,1)S(1)}, bf16[8,5760]{1,0:T(8,128)(2,1)S(1)}, u32[]{:S(2)}, u32[]{:S(2)}) collective-permute-start(bf16[8,5760]{1,0:T(8,128)(2,1)S(1)} %get-tuple-element.37.part0), channel_id=1, source_target_pairs={{0,1},{1,0},{2,3},{3,2},{4,5},{5,4},{6,7},{7,6},{8,9},{9,8},{10,11... | collective-permute-start | bytes 276488 | tf_op jit(solution)/shard_map/ppermute | solution.py:551
  42.2 4.6 %collective-permute-start.6 = (f32[104,128]{1,0:T(8,128)S(1)}, f32[104,128]{1,0:T(8,128)S(1)}, u32[]{:S(2)}, u32[]{:S(2)}) collective-permute-start(f32[104,128]{1,0:T(8,128)S(1)} %add_add_fusion), channel_id=1, source_target_pairs={{0,8},{4,12},{8,0},{12,4},{16,24},{20,28},{24,16},{28,20},{1,9},{5... | collective-permute-start | bytes 159752 | tf_op jit(solution)/shard_map/ppermute | solution.py:551
  44.7 7.0 %collective-permute-start.10 = (bf16[8,5760]{1,0:T(8,128)(2,1)S(1)}, bf16[8,5760]{1,0:T(8,128)(2,1)S(1)}, u32[]{:S(2)}, u32[]{:S(2)}) collective-permute-start(bf16[8,5760]{1,0:T(8,128)(2,1)S(1)} %get-tuple-element.37.part0), channel_id=1, source_target_pairs={{0,2},{1,3},{2,0},{3,1},{4,6},{5,7},{6,4},{7,5},{8,10},{9,11},{10,... | collective-permute-start | bytes 276488 | tf_op jit(solution)/shard_map/ppermute | solution.py:551
  46.8 4.8 %collective-permute-start.9 = (f32[104,128]{1,0:T(8,128)S(1)}, f32[104,128]{1,0:T(8,128)S(1)}, u32[]{:S(2)}, u32[]{:S(2)}) collective-permute-start(f32[104,128]{1,0:T(8,128)S(1)} %add.22), channel_id=1, source_target_pairs={{0,16},{4,20},{8,24},{12,28},{16,0},{20,4},{24,8},{28,12},{1,17},{... | collective-permute-start | bytes 159752 | tf_op jit(solution)/shard_map/ppermute | solution.py:551
  51.7 1.3 %collective-permute-start.11 = (f32[104,128]{1,0:T(8,128)S(1)}, f32[104,128]{1,0:T(8,128)S(1)}, u32[]{:S(2)}, u32[]{:S(2)}) collective-permute-start(f32[104,128]{1,0:T(8,128)S(1)} %add.23.mine), channel_id=1, source_target_pairs={{0,4},{4,0},{8,12},{12,8},{16,20},{20,16},{24,28},{28,24},{1,5},{5... | collective-permute-start | bytes 159752 | tf_op jit(solution)/shard_map/ppermute | solution.py:551

commit v18 on v17

--- a/solution.py
+++ b/solution.py
@@ -313,6 +313,7 @@
     cast_odd,
     fgrad_even,
     fgrad_odd,
+    twice,
     grads_even,
     grads_odd,
     carry,
@@ -436,9 +437,11 @@
                     f = both[part * 8 : part * 8 + 8]
                     d = f - spread_line(aim_ref, t * 2 + part, first + line)
                     goal = d * lax.rsqrt(d * d + SMOOTH)
+                    for start in (0, 2 * MEM):
+                        twice[line, t * 2 + part, pl.ds(start, MEM, stride=2), :] = f
                     gs = []
                     for k in range(1, 5):
-                        d = f - pltpu.roll(f, k, 0)
+                        d = f - twice[line, t * 2 + part, pl.ds(2 * (MEM - k), MEM, stride=2), :]
                         gs.append(d * lax.rsqrt(d * d + SMOOTH))
                     back = gs[2]
                     for k in (1, 0):
@@ -640,6 +643,7 @@
             pltpu.VMEM((4, front, 16, LANES), bf16),
             pltpu.VMEM((4, front + 1, 16, LANES), bf16),
             pltpu.VMEM((4, front + 1, 16, LANES), bf16),
+            pltpu.VMEM((4, 2 * front, 4 * MEM, LANES), f32),
             pltpu.VMEM((front * 16, 2 * LANES), bf16),
             pltpu.VMEM((front * 16, 2 * LANES), bf16),
             pltpu.VMEM((front * 16, LANES), f32),

time: 53.9 us -> 54.4 us (level)
  no operation moved by 1% of the time
where the time goes in v18:
time: 54.4 us; the launch traced here: 54.2 us
  Pallas kernels  26 us (48%)
  starting transfers between devices  21.7 us (40%)
  waiting for transfers between devices  5.57 us (10%)
  between operations  0.85 us (2%)
    pallas_call x1, Pallas kernels, local(): pl.pallas_call(functools.partial(band_kernel, half, (chan0, chan1, chan2)...  19.8 us
    ppermute x10, starting transfers between devices, swapped(): lax.ppermute(array, axis, [(i, i ^ bit) for i in range(lax.axis_size(axis...  18 us
    ppermute x10, waiting for transfers between devices, swapped(): lax.ppermute(array, axis, [(i, i ^ bit) for i in range(lax.axis_size(axis...  3.98 us
    ppermute x2, starting transfers between devices, shifted(): return lax.ppermute(array, axis, pairs)  3.65 us
    pallas_call x1, Pallas kernels, local(): pl.pallas_call(functools.partial(prepare_kernel, half, chan0, chan2), in_...  2.13 us
    pallas_call x1, Pallas kernels, local(): pl.pallas_call(functools.partial(edge_kernel, half, chan2), in_specs=[hbm...  2.13 us
    ppermute x2, waiting for transfers between devices, shifted(): return lax.ppermute(array, axis, pairs)  1.58 us
  transfers between devices with their start and end apart: 12, of which 6 were waited for; matrix products, arithmetic and copies ran while one was open for 0% of the time, Pallas kernels for 6%

profile of v18, /device:TPU:0, one launch (start us, length us, event | category | flops | bytes accessed | tf_op | source)
XLA Modules:
  0.0 54.2 jit_solution(522426509678659886)
XLA Ops:
  0.7 2.1 %edges.1 = (bf16[50,8,128]{2,1,0:T(8,128)(2,1)}, bf16[1,6400]{1,0:T(2,128)(2,1)}) custom-call(bf16[1,8,23040]{2,1,0:T(8,128)(2,1)} %latent_hbm.1, bf16[1,32,23040]{2,1,0:T(8,128)(2,1)} %targets_hbm.1, s32[32,48]{1,0:T(8,128)} %land_hbm.1), custom_call_target="tpu_custom_call" | custom-call | tf_op jit(solution)/shard_map/edges/pallas_call | solution.py:581
  2.9 2.4 %collective-permute-start = (bf16[50,8,128]{2,1,0:T(8,128)(2,1)}, bf16[50,8,128]{2,1,0:T(8,128)(2,1)S(1)}, u32[]{:S(2)}, u32[]{:S(2)}) collective-permute-start(bf16[50,8,128]{2,1,0:T(8,128)(2,1)} %get-tuple-element.29), channel_id=1, source_target_pairs={{0,4},{4,8},{8,12},{12,16},{16,20},{20,24},{24,28},{1,5},{5,9},{9,... | collective-permute-start | bytes 307208 | tf_op jit(solution)/shard_map/ppermute | solution.py:24
  5.2 1.3 %collective-permute-start.1 = (bf16[1,6400]{1,0:T(2,128)(2,1)}, bf16[1,6400]{1,0:T(2,128)(2,1)S(1)}, u32[]{:S(2)}, u32[]{:S(2)}) collective-permute-start(bf16[1,6400]{1,0:T(2,128)(2,1)} %get-tuple-element.30), channel_id=1, source_target_pairs={{4,0},{8,4},{12,8},{16,12},{20,16},{24,20},{28,24},{5,1},{9,5},{13... | collective-permute-start | bytes 38408 | tf_op jit(solution)/shard_map/ppermute | solution.py:24
  6.6 2.1 %prepare.1 = (bf16[8,25,16,128]{3,2,1,0:T(8,128)(2,1)S(1)}, f32[48,32,128]{2,1,0:T(8,128)S(1)}, f32[48,32,128]{2,1,0:T(8,128)S(1)}) custom-call(s32[8]{0:T(128)S(1)} %copy-done.3, f32[64]{0:T(128)S(1)} %copy-done.4, f32[16]{0:T(128)S(1)} %copy-done.5, bf16[1,8,23040]{2,1,0:T(8,128)(2,1)S(1)} %copy-done.1, bf16[1,32,23040]{2,1,0:T(8,128)(2,1)S(1)} %copy-done, ...), custom_call_target="tpu_custom_call" | custom-call | flops 100000000 | bytes 10000000 | tf_op jit(solution)/shard_map/prepare/pallas_call | solution.py:601
  8.7 0.3 bands.1
  9.0 1.6 %collective-permute-done.1.below = bf16[1,6400]{1,0:T(2,128)(2,1)S(1)} collective-permute-done((bf16[1,6400]{1,0:T(2,128)(2,1)}, bf16[1,6400]{1,0:T(2,128)(2,1)S(1)}, u32[]{:S(2)}, u32[]{:S(2)}) %collective-permute-start.1) | collective-permute-done | bytes 12832 | tf_op jit(solution)/shard_map/ppermute | solution.py:24
  10.6 19.8 %band.1 = (bf16[8,5760]{1,0:T(8,128)(2,1)S(1)}, f32[104,128]{1,0:T(8,128)S(1)}, f32[104,128]{1,0:T(8,128)S(1)}) custom-call(s32[8]{0:T(128)S(1)} %copy-done.3, f32[64]{0:T(128)S(1)} %copy-done.4, f32[16]{0:T(128)S(1)} %copy-done.5, bf16[8,25,16,128]{3,2,1,0:T(8,128)(2,1)S(1)} %get-tuple-element.26.own_source, f32[48,32,128]{2,1,0:T(8,128)S(1)} %get-tuple-element.27.aims, ...), custom_call_target="tpu_custom_call" | custom-call | tf_op jit(solution)/shard_map/band/pallas_call | solution.py:624
  30.4 2.6 %collective-permute-start.2 = (f32[104,128]{1,0:T(8,128)S(1)}, f32[104,128]{1,0:T(8,128)S(1)}, u32[]{:S(2)}, u32[]{:S(2)}) collective-permute-start(f32[104,128]{1,0:T(8,128)S(1)} %get-tuple-element.39), channel_id=1, source_target_pairs={{0,4},{4,0},{8,12},{12,8},{16,20},{20,16},{24,28},{28,24},{1,5},{5... | collective-permute-start | bytes 159752 | tf_op jit(solution)/shard_map/ppermute | solution.py:554
  33.0 0.9 %collective-permute-done.2 = f32[104,128]{1,0:T(8,128)S(1)} collective-permute-done((f32[104,128]{1,0:T(8,128)S(1)}, f32[104,128]{1,0:T(8,128)S(1)}, u32[]{:S(2)}, u32[]{:S(2)}) %collective-permute-start.2) | collective-permute-done | bytes 53280 | tf_op jit(solution)/shard_map/ppermute | solution.py:554
  33.9 3.7 %collective-permute-start.5 = (bf16[104,128]{1,0:T(8,128)(2,1)S(1)}, bf16[104,128]{1,0:T(8,128)(2,1)S(1)}, u32[]{:S(2)}, u32[]{:S(2)}) collective-permute-start(bf16[104,128]{1,0:T(8,128)(2,1)S(1)} %add_convert_fusion), channel_id=1, source_target_pairs={{0,3},{1,2},{2,1},{3,0},{4,7},{5,6},{6,5},{7,4},{8,11},{9,10},{10,... | collective-permute-start | bytes 79880 | tf_op jit(solution)/shard_map/ppermute | solution.py:554
  37.6 0.0 collective-permute-start.4
  37.6 0.8 %collective-permute-start.3 = (bf16[104,128]{1,0:T(8,128)(2,1)S(1)}, bf16[104,128]{1,0:T(8,128)(2,1)S(1)}, u32[]{:S(2)}, u32[]{:S(2)}) collective-permute-start(bf16[104,128]{1,0:T(8,128)(2,1)S(1)} %add_convert_fusion), channel_id=1, source_target_pairs={{0,1},{1,0},{2,3},{3,2},{4,5},{5,4},{6,7},{7,6},{8,9},{9,8},{10,11... | collective-permute-start | bytes 79880 | tf_op jit(solution)/shard_map/ppermute | solution.py:554
  38.4 3.6 %collective-permute-start.8 = (bf16[8,5760]{1,0:T(8,128)(2,1)S(1)}, bf16[8,5760]{1,0:T(8,128)(2,1)S(1)}, u32[]{:S(2)}, u32[]{:S(2)}) collective-permute-start(bf16[8,5760]{1,0:T(8,128)(2,1)S(1)} %get-tuple-element.37.part0), channel_id=1, source_target_pairs={{0,3},{1,2},{2,1},{3,0},{4,7},{5,6},{6,5},{7,4},{8,11},{9,10},{10,... | collective-permute-start | bytes 276488 | tf_op jit(solution)/shard_map/ppermute | solution.py:554
  42.0 0.0 collective-permute-start.7
  42.0 0.6 %collective-permute-done.4 = bf16[104,128]{1,0:T(8,128)(2,1)S(1)} collective-permute-done((bf16[104,128]{1,0:T(8,128)(2,1)S(1)}, bf16[104,128]{1,0:T(8,128)(2,1)S(1)}, u32[]{:S(2)}, u32[]{:S(2)}) %collective-permute-start.4) | collective-permute-done | bytes 26656 | tf_op jit(solution)/shard_map/ppermute | solution.py:554
  42.6 2.5 %collective-permute-start.6 = (f32[104,128]{1,0:T(8,128)S(1)}, f32[104,128]{1,0:T(8,128)S(1)}, u32[]{:S(2)}, u32[]{:S(2)}) collective-permute-start(f32[104,128]{1,0:T(8,128)S(1)} %add_add_fusion), channel_id=1, source_target_pairs={{0,8},{4,12},{8,0},{12,4},{16,24},{20,28},{24,16},{28,20},{1,9},{5... | collective-permute-start | bytes 159752 | tf_op jit(solution)/shard_map/ppermute | solution.py:554
  45.1 2.1 %collective-permute-start.10 = (bf16[8,5760]{1,0:T(8,128)(2,1)S(1)}, bf16[8,5760]{1,0:T(8,128)(2,1)S(1)}, u32[]{:S(2)}, u32[]{:S(2)}) collective-permute-start(bf16[8,5760]{1,0:T(8,128)(2,1)S(1)} %get-tuple-element.37.part0), channel_id=1, source_target_pairs={{0,2},{1,3},{2,0},{3,1},{4,6},{5,7},{6,4},{7,5},{8,10},{9,11},{10,... | collective-permute-start | bytes 276488 | tf_op jit(solution)/shard_map/ppermute | solution.py:554
  47.2 0.1 collective-permute-done.6
  47.2 2.7 %collective-permute-start.9 = (f32[104,128]{1,0:T(8,128)S(1)}, f32[104,128]{1,0:T(8,128)S(1)}, u32[]{:S(2)}, u32[]{:S(2)}) collective-permute-start(f32[104,128]{1,0:T(8,128)S(1)} %add.22), channel_id=1, source_target_pairs={{0,16},{4,20},{8,24},{12,28},{16,0},{20,4},{24,8},{28,12},{1,17},{... | collective-permute-start | bytes 159752 | tf_op jit(solution)/shard_map/ppermute | solution.py:554
  50.0 2.1 %collective-permute-done.9 = f32[104,128]{1,0:T(8,128)S(1)} collective-permute-done((f32[104,128]{1,0:T(8,128)S(1)}, f32[104,128]{1,0:T(8,128)S(1)}, u32[]{:S(2)}, u32[]{:S(2)}) %collective-permute-start.9) | collective-permute-done | bytes 53280 | tf_op jit(solution)/shard_map/ppermute | solution.py:554
  52.1 0.1 collective-permute-start.11
  52.2 0.9 %place.1 = f32[1,8,23040]{2,1,0:T(8,128)} custom-call(bf16[8,5760]{1,0:T(8,128)(2,1)S(1)} %get-tuple-element.37.part0, bf16[8,5760]{1,0:T(8,128)(2,1)S(1)} %collective-permute-done.7.part1, bf16[8,5760]{1,0:T(8,128)(2,1)S(1)} %collective-permute-done.10.part2, bf16[8,5760]{1,0:T(8,128)(2,1)S(1)} %collective-permute-done.8.part3), custom_call_target="tpu_custom_call" | custom-call | tf_op jit(solution)/shard_map/place/pallas_call | solution.py:681
  53.1 0.3 collective-permute-done.11.other
  53.4 0.8 %taps.1 = (f32[3,3,32,64]{3,2,1,0:T(8,128)}, f32[3,3,16,32]{3,2,1,0:T(8,128)}) custom-call(f32[104,128]{1,0:T(8,128)S(1)} %add.23.mine, f32[104,128]{1,0:T(8,128)S(1)} %collective-permute-done.11.other), custom_call_target="tpu_custom_call" | custom-call | tf_op jit(solution)/shard_map/taps/pallas_call | solution.py:689
  (26 shorter events, 0.1 us)
Async XLA Ops:
  0.6 5.9 %copy-start.2 = (s32[32,48]{1,0:T(8,128)S(1)}, s32[32,48]{1,0:T(8,128)}, u32[]{:S(2)}) copy-start(s32[32,48]{1,0:T(8,128)} %land_hbm.1) | copy-start | bytes 18436
  0.6 5.9 %copy-start = (bf16[1,32,23040]{2,1,0:T(8,128)(2,1)S(1)}, bf16[1,32,23040]{2,1,0:T(8,128)(2,1)}, u32[]{:S(2)}) copy-start(bf16[1,32,23040]{2,1,0:T(8,128)(2,1)} %targets_hbm.1) | copy-start | bytes 4423684
  0.7 5.9 %copy-start.1 = (bf16[1,8,23040]{2,1,0:T(8,128)(2,1)S(1)}, bf16[1,8,23040]{2,1,0:T(8,128)(2,1)}, u32[]{:S(2)}) copy-start(bf16[1,8,23040]{2,1,0:T(8,128)(2,1)} %latent_hbm.1) | copy-start | bytes 1105924
  0.7 5.9 %copy-start.5 = (f32[16]{0:T(128)S(1)}, f32[16]{0:T(128)}, u32[]{:S(2)}) copy-start(f32[16]{0:T(128)} %channel_weight.3) | copy-start | bytes 196
  0.7 5.9 %copy-start.4 = (f32[64]{0:T(128)S(1)}, f32[64]{0:T(128)}, u32[]{:S(2)}) copy-start(f32[64]{0:T(128)} %scale.3) | copy-start | bytes 772
  0.7 5.9 %copy-start.3 = (s32[8]{0:T(128)S(1)}, s32[8]{0:T(128)}, u32[]{:S(2)}) copy-start(s32[8]{0:T(128)} %seeds.3) | copy-start | bytes 100
  0.7 8.0 %copy-start.7 = (bf16[3,3,32,16]{2,3,1,0:T(8,128)(2,1)S(1)}, bf16[3,3,32,16]{2,3,1,0:T(8,128)(2,1)}, u32[]{:S(2)}) copy-start(bf16[3,3,32,16]{2,3,1,0:T(8,128)(2,1)} %param.12) | copy-start | bytes 27652
  0.7 8.0 %copy-start.6 = (bf16[3,3,64,32]{2,3,1,0:T(8,128)(2,1)S(1)}, bf16[3,3,64,32]{2,3,1,0:T(8,128)(2,1)}, u32[]{:S(2)}) copy-start(bf16[3,3,64,32]{2,3,1,0:T(8,128)(2,1)} %param.11) | copy-start | bytes 110596
  2.9 7.8 %collective-permute-start = (bf16[50,8,128]{2,1,0:T(8,128)(2,1)}, bf16[50,8,128]{2,1,0:T(8,128)(2,1)S(1)}, u32[]{:S(2)}, u32[]{:S(2)}) collective-permute-start(bf16[50,8,128]{2,1,0:T(8,128)(2,1)} %get-tuple-element.29), channel_id=1, source_target_pairs={{0,4},{4,8},{8,12},{12,16},{16,20},{20,24},{24,28},{1,5},{5,9},{9,... | collective-permute-start | bytes 307208 | tf_op jit(solution)/shard_map/ppermute | solution.py:24
  5.2 5.4 %collective-permute-start.1 = (bf16[1,6400]{1,0:T(2,128)(2,1)}, bf16[1,6400]{1,0:T(2,128)(2,1)S(1)}, u32[]{:S(2)}, u32[]{:S(2)}) collective-permute-start(bf16[1,6400]{1,0:T(2,128)(2,1)} %get-tuple-element.30), channel_id=1, source_target_pairs={{4,0},{8,4},{12,8},{16,12},{20,16},{24,20},{28,24},{5,1},{9,5},{13... | collective-permute-start | bytes 38408 | tf_op jit(solution)/shard_map/ppermute | solution.py:24
  30.4 3.5 %collective-permute-start.2 = (f32[104,128]{1,0:T(8,128)S(1)}, f32[104,128]{1,0:T(8,128)S(1)}, u32[]{:S(2)}, u32[]{:S(2)}) collective-permute-start(f32[104,128]{1,0:T(8,128)S(1)} %get-tuple-element.39), channel_id=1, source_target_pairs={{0,4},{4,0},{8,12},{12,8},{16,20},{20,16},{24,28},{28,24},{1,5},{5... | collective-permute-start | bytes 159752 | tf_op jit(solution)/shard_map/ppermute | solution.py:554
  33.9 8.1 %collective-permute-start.5 = (bf16[104,128]{1,0:T(8,128)(2,1)S(1)}, bf16[104,128]{1,0:T(8,128)(2,1)S(1)}, u32[]{:S(2)}, u32[]{:S(2)}) collective-permute-start(bf16[104,128]{1,0:T(8,128)(2,1)S(1)} %add_convert_fusion), channel_id=1, source_target_pairs={{0,3},{1,2},{2,1},{3,0},{4,7},{5,6},{6,5},{7,4},{8,11},{9,10},{10,... | collective-permute-start | bytes 79880 | tf_op jit(solution)/shard_map/ppermute | solution.py:554
  37.6 5.0 %collective-permute-start.4 = (bf16[104,128]{1,0:T(8,128)(2,1)S(1)}, bf16[104,128]{1,0:T(8,128)(2,1)S(1)}, u32[]{:S(2)}, u32[]{:S(2)}) collective-permute-start(bf16[104,128]{1,0:T(8,128)(2,1)S(1)} %add_convert_fusion), channel_id=1, source_target_pairs={{0,2},{1,3},{2,0},{3,1},{4,6},{5,7},{6,4},{7,5},{8,10},{9,11},{10,... | collective-permute-start | bytes 79880 | tf_op jit(solution)/shard_map/ppermute | solution.py:554
  37.6 5.0 %collective-permute-start.3 = (bf16[104,128]{1,0:T(8,128)(2,1)S(1)}, bf16[104,128]{1,0:T(8,128)(2,1)S(1)}, u32[]{:S(2)}, u32[]{:S(2)}) collective-permute-start(bf16[104,128]{1,0:T(8,128)(2,1)S(1)} %add_convert_fusion), channel_id=1, source_target_pairs={{0,1},{1,0},{2,3},{3,2},{4,5},{5,4},{6,7},{7,6},{8,9},{9,8},{10,11... | collective-permute-start | bytes 79880 | tf_op jit(solution)/shard_map/ppermute | solution.py:554
  38.4 8.8 %collective-permute-start.8 = (bf16[8,5760]{1,0:T(8,128)(2,1)S(1)}, bf16[8,5760]{1,0:T(8,128)(2,1)S(1)}, u32[]{:S(2)}, u32[]{:S(2)}) collective-permute-start(bf16[8,5760]{1,0:T(8,128)(2,1)S(1)} %get-tuple-element.37.part0), channel_id=1, source_target_pairs={{0,3},{1,2},{2,1},{3,0},{4,7},{5,6},{6,5},{7,4},{8,11},{9,10},{10,... | collective-permute-start | bytes 276488 | tf_op jit(solution)/shard_map/ppermute | solution.py:554
  42.0 5.2 %collective-permute-start.7 = (bf16[8,5760]{1,0:T(8,128)(2,1)S(1)}, bf16[8,5760]{1,0:T(8,128)(2,1)S(1)}, u32[]{:S(2)}, u32[]{:S(2)}) collective-permute-start(bf16[8,5760]{1,0:T(8,128)(2,1)S(1)} %get-tuple-element.37.part0), channel_id=1, source_target_pairs={{0,1},{1,0},{2,3},{3,2},{4,5},{5,4},{6,7},{7,6},{8,9},{9,8},{10,11... | collective-permute-start | bytes 276488 | tf_op jit(solution)/shard_map/ppermute | solution.py:554
  42.6 4.6 %collective-permute-start.6 = (f32[104,128]{1,0:T(8,128)S(1)}, f32[104,128]{1,0:T(8,128)S(1)}, u32[]{:S(2)}, u32[]{:S(2)}) collective-permute-start(f32[104,128]{1,0:T(8,128)S(1)} %add_add_fusion), channel_id=1, source_target_pairs={{0,8},{4,12},{8,0},{12,4},{16,24},{20,28},{24,16},{28,20},{1,9},{5... | collective-permute-start | bytes 159752 | tf_op jit(solution)/shard_map/ppermute | solution.py:554
  45.1 7.0 %collective-permute-start.10 = (bf16[8,5760]{1,0:T(8,128)(2,1)S(1)}, bf16[8,5760]{1,0:T(8,128)(2,1)S(1)}, u32[]{:S(2)}, u32[]{:S(2)}) collective-permute-start(bf16[8,5760]{1,0:T(8,128)(2,1)S(1)} %get-tuple-element.37.part0), channel_id=1, source_target_pairs={{0,2},{1,3},{2,0},{3,1},{4,6},{5,7},{6,4},{7,5},{8,10},{9,11},{10,... | collective-permute-start | bytes 276488 | tf_op jit(solution)/shard_map/ppermute | solution.py:554
  47.2 4.8 %collective-permute-start.9 = (f32[104,128]{1,0:T(8,128)S(1)}, f32[104,128]{1,0:T(8,128)S(1)}, u32[]{:S(2)}, u32[]{:S(2)}) collective-permute-start(f32[104,128]{1,0:T(8,128)S(1)} %add.22), channel_id=1, source_target_pairs={{0,16},{4,20},{8,24},{12,28},{16,0},{20,4},{24,8},{28,12},{1,17},{... | collective-permute-start | bytes 159752 | tf_op jit(solution)/shard_map/ppermute | solution.py:554
  52.1 1.3 %collective-permute-start.11 = (f32[104,128]{1,0:T(8,128)S(1)}, f32[104,128]{1,0:T(8,128)S(1)}, u32[]{:S(2)}, u32[]{:S(2)}) collective-permute-start(f32[104,128]{1,0:T(8,128)S(1)} %add.23.mine), channel_id=1, source_target_pairs={{0,4},{4,0},{8,12},{12,8},{16,20},{20,16},{24,28},{28,24},{1,5},{5... | collective-permute-start | bytes 159752 | tf_op jit(solution)/shard_map/ppermute | solution.py:554

commit v19 on v17

--- a/solution.py
+++ b/solution.py
@@ -273,12 +273,10 @@
     build_back(kernel_two, back_two)
 
 
-def take_turns(*parts):
-    parts = list(parts)
-    while parts:
-        for part in tuple(parts):
-            if next(part, part) is part:
-                parts.remove(part)
+def in_order(*parts):
+    for part in parts:
+        for _ in part:
+            pass
 
 
 def band_kernel(
@@ -379,17 +377,17 @@
         taken = jnp.concatenate([operand(source, 2 * pair + k, 0, wide) for k in range(2)], axis=0)
         pre[...] = jnp.dot(taken, band_one[...], preferred_element_type=f32)
 
-    def first_gelu(pair, pre):
+    def first_gelu(pair, pre, last=False):
         for k in range(2):
             for t in range(wide):
-                for sub in range(2):
+                for sub in range(1 if last and k == 1 else 2):
                     at = (k * wide + t) * 16
                     x = pre[at : at + 16, sub * LANES : (sub + 1) * LANES]
                     square = x * x
                     th = jnp.tanh(x * (GELU_A + (GELU_A * GELU_B) * square))
                     plus = 0.5 + 0.5 * th
                     act[4 * pair + 2 * k + sub, t] = (x * plus).astype(bf16)
-                    if t < front:
+                    if t < front and not (last and k == 1):
                         d = plus + (x * plus) * (1.0 - th) * (GELU_A + (3.0 * GELU_A * GELU_B) * square)
                         if t == half:
                             d = jnp.where(iota((16, LANES), 0) < 8, d, 0.0)
@@ -404,7 +402,7 @@
 
     first_product(0, pre_even)
     lax.fori_loop(0, rows // 4, first_segment, 0)
-    first_gelu(rows // 2, pre_even)
+    first_gelu(rows // 2, pre_even, last=True)
 
     members = front * 16
     owner = iota((48, members), 0)
@@ -499,13 +497,13 @@
         return loss_gradient(cast, fgrad, aims, weights, 4 * (n - 1), range(4))
 
     def second_segment(m, _):
-        take_turns(
+        in_order(
             second_product(2 * m + 3, cast_odd),
             own_gradient(2 * m + 2, cast_even, fgrad_even),
             pull_back(2 * m + 1, fgrad_odd, grads_odd),
             first_taps(2 * m, grads_even, jnp.where(m >= 1, 1.0, 0.0).astype(bf16)),
         )
-        take_turns(
+        in_order(
             second_product(2 * m + 4, cast_even),
             own_gradient(2 * m + 3, cast_odd, fgrad_odd),
             pull_back(2 * m + 2, fgrad_even, grads_even),
@@ -513,24 +511,24 @@
         )
         return 0
 
-    take_turns(second_product(0, cast_even))
-    take_turns(
+    in_order(second_product(0, cast_even))
+    in_order(
         second_product(1, cast_odd),
         loss_gradient(cast_even, fgrad_even, edge_aims, edge_weights, 0, range(1, 4)),
     )
-    take_turns(
+    in_order(
         second_product(2, cast_even),
         own_gradient(1, cast_odd, fgrad_odd),
         pull_back(0, fgrad_even, grads_even, with_taps=False),
     )
     lax.fori_loop(0, rows // 2 - 1, second_segment, 0)
-    take_turns(
+    in_order(
         own_gradient(rows, cast_even, fgrad_even),
         pull_back(rows - 1, fgrad_odd, grads_odd),
         first_taps(rows - 2, grads_even),
     )
-    take_turns(pull_back(rows, fgrad_even, grads_even), first_taps(rows - 1, grads_odd))
-    take_turns(first_taps(rows, grads_even))
+    in_order(pull_back(rows, fgrad_even, grads_even), first_taps(rows - 1, grads_odd))
+    in_order(first_taps(rows, grads_even))
 
     z = jnp.dot(sums[...].reshape(2 * (rows + 1) * 48, 512), back_one[...], preferred_element_type=f32)
     z = z.reshape(2, rows + 1, 48, 2 * LANES)

time: 53.9 us -> 54.5 us (1.011)
  Pallas kernels: 25.6 us -> 26.2 us
    pallas_call x1, Pallas kernels: 19.3 us -> 19.9 us  [local(): pl.pallas_call(functools.partial(band_kernel, half, (chan0, chan1, chan2)...]
where the time goes in v19:
time: 54.5 us; the launch traced here: 54.3 us
  Pallas kernels  26.2 us (48%)
  starting transfers between devices  21.7 us (40%)
  waiting for transfers between devices  5.57 us (10%)
  between operations  0.85 us (2%)
    pallas_call x1, Pallas kernels, local(): pl.pallas_call(functools.partial(band_kernel, half, (chan0, chan1, chan2)...  19.9 us
    ppermute x10, starting transfers between devices, swapped(): lax.ppermute(array, axis, [(i, i ^ bit) for i in range(lax.axis_size(axis...  18 us
    ppermute x10, waiting for transfers between devices, swapped(): lax.ppermute(array, axis, [(i, i ^ bit) for i in range(lax.axis_size(axis...  3.98 us
    ppermute x2, starting transfers between devices, shifted(): return lax.ppermute(array, axis, pairs)  3.65 us
    pallas_call x1, Pallas kernels, local(): pl.pallas_call(functools.partial(prepare_kernel, half, chan0, chan2), in_...  2.13 us
    pallas_call x1, Pallas kernels, local(): pl.pallas_call(functools.partial(edge_kernel, half, chan2), in_specs=[hbm...  2.13 us
    ppermute x2, waiting for transfers between devices, shifted(): return lax.ppermute(array, axis, pairs)  1.58 us
  transfers between devices with their start and end apart: 12, of which 6 were waited for; matrix products, arithmetic and copies ran while one was open for 0% of the time, Pallas kernels for 6%

profile of v19, /device:TPU:0, one launch (start us, length us, event | category | flops | bytes accessed | tf_op | source)
XLA Modules:
  0.0 54.3 jit_solution(14652693229928517732)
XLA Ops:
  0.7 2.1 %edges.1 = (bf16[50,8,128]{2,1,0:T(8,128)(2,1)}, bf16[1,6400]{1,0:T(2,128)(2,1)}) custom-call(bf16[1,8,23040]{2,1,0:T(8,128)(2,1)} %latent_hbm.1, bf16[1,32,23040]{2,1,0:T(8,128)(2,1)} %targets_hbm.1, s32[32,48]{1,0:T(8,128)} %land_hbm.1), custom_call_target="tpu_custom_call" | custom-call | tf_op jit(solution)/shard_map/edges/pallas_call | solution.py:576
  2.9 2.4 %collective-permute-start = (bf16[50,8,128]{2,1,0:T(8,128)(2,1)}, bf16[50,8,128]{2,1,0:T(8,128)(2,1)S(1)}, u32[]{:S(2)}, u32[]{:S(2)}) collective-permute-start(bf16[50,8,128]{2,1,0:T(8,128)(2,1)} %get-tuple-element.29), channel_id=1, source_target_pairs={{0,4},{4,8},{8,12},{12,16},{16,20},{20,24},{24,28},{1,5},{5,9},{9,... | collective-permute-start | bytes 307208 | tf_op jit(solution)/shard_map/ppermute | solution.py:24
  5.2 1.3 %collective-permute-start.1 = (bf16[1,6400]{1,0:T(2,128)(2,1)}, bf16[1,6400]{1,0:T(2,128)(2,1)S(1)}, u32[]{:S(2)}, u32[]{:S(2)}) collective-permute-start(bf16[1,6400]{1,0:T(2,128)(2,1)} %get-tuple-element.30), channel_id=1, source_target_pairs={{4,0},{8,4},{12,8},{16,12},{20,16},{24,20},{28,24},{5,1},{9,5},{13... | collective-permute-start | bytes 38408 | tf_op jit(solution)/shard_map/ppermute | solution.py:24
  6.6 2.1 %prepare.1 = (bf16[8,25,16,128]{3,2,1,0:T(8,128)(2,1)S(1)}, f32[48,32,128]{2,1,0:T(8,128)S(1)}, f32[48,32,128]{2,1,0:T(8,128)S(1)}) custom-call(s32[8]{0:T(128)S(1)} %copy-done.3, f32[64]{0:T(128)S(1)} %copy-done.4, f32[16]{0:T(128)S(1)} %copy-done.5, bf16[1,8,23040]{2,1,0:T(8,128)(2,1)S(1)} %copy-done.1, bf16[1,32,23040]{2,1,0:T(8,128)(2,1)S(1)} %copy-done, ...), custom_call_target="tpu_custom_call" | custom-call | flops 100000000 | bytes 10000000 | tf_op jit(solution)/shard_map/prepare/pallas_call | solution.py:596
  8.7 0.3 bands.1
  9.0 1.6 %collective-permute-done.1.below = bf16[1,6400]{1,0:T(2,128)(2,1)S(1)} collective-permute-done((bf16[1,6400]{1,0:T(2,128)(2,1)}, bf16[1,6400]{1,0:T(2,128)(2,1)S(1)}, u32[]{:S(2)}, u32[]{:S(2)}) %collective-permute-start.1) | collective-permute-done | bytes 12832 | tf_op jit(solution)/shard_map/ppermute | solution.py:24
  10.6 0.0 collective-permute-done.above
  10.6 19.9 %band.1 = (bf16[8,5760]{1,0:T(8,128)(2,1)S(1)}, f32[104,128]{1,0:T(8,128)S(1)}, f32[104,128]{1,0:T(8,128)S(1)}) custom-call(s32[8]{0:T(128)S(1)} %copy-done.3, f32[64]{0:T(128)S(1)} %copy-done.4, f32[16]{0:T(128)S(1)} %copy-done.5, bf16[8,25,16,128]{3,2,1,0:T(8,128)(2,1)S(1)} %get-tuple-element.26.own_source, f32[48,32,128]{2,1,0:T(8,128)S(1)} %get-tuple-element.27.aims, ...), custom_call_target="tpu_custom_call" | custom-call | tf_op jit(solution)/shard_map/band/pallas_call | solution.py:619
  30.5 2.6 %collective-permute-start.2 = (f32[104,128]{1,0:T(8,128)S(1)}, f32[104,128]{1,0:T(8,128)S(1)}, u32[]{:S(2)}, u32[]{:S(2)}) collective-permute-start(f32[104,128]{1,0:T(8,128)S(1)} %get-tuple-element.39), channel_id=1, source_target_pairs={{0,4},{4,0},{8,12},{12,8},{16,20},{20,16},{24,28},{28,24},{1,5},{5... | collective-permute-start | bytes 159752 | tf_op jit(solution)/shard_map/ppermute | solution.py:549
  33.2 0.9 %collective-permute-done.2 = f32[104,128]{1,0:T(8,128)S(1)} collective-permute-done((f32[104,128]{1,0:T(8,128)S(1)}, f32[104,128]{1,0:T(8,128)S(1)}, u32[]{:S(2)}, u32[]{:S(2)}) %collective-permute-start.2) | collective-permute-done | bytes 53280 | tf_op jit(solution)/shard_map/ppermute | solution.py:549
  34.1 3.7 %collective-permute-start.5 = (bf16[104,128]{1,0:T(8,128)(2,1)S(1)}, bf16[104,128]{1,0:T(8,128)(2,1)S(1)}, u32[]{:S(2)}, u32[]{:S(2)}) collective-permute-start(bf16[104,128]{1,0:T(8,128)(2,1)S(1)} %add_convert_fusion), channel_id=1, source_target_pairs={{0,3},{1,2},{2,1},{3,0},{4,7},{5,6},{6,5},{7,4},{8,11},{9,10},{10,... | collective-permute-start | bytes 79880 | tf_op jit(solution)/shard_map/ppermute | solution.py:549
  37.8 0.8 %collective-permute-start.3 = (bf16[104,128]{1,0:T(8,128)(2,1)S(1)}, bf16[104,128]{1,0:T(8,128)(2,1)S(1)}, u32[]{:S(2)}, u32[]{:S(2)}) collective-permute-start(bf16[104,128]{1,0:T(8,128)(2,1)S(1)} %add_convert_fusion), channel_id=1, source_target_pairs={{0,1},{1,0},{2,3},{3,2},{4,5},{5,4},{6,7},{7,6},{8,9},{9,8},{10,11... | collective-permute-start | bytes 79880 | tf_op jit(solution)/shard_map/ppermute | solution.py:549
  38.5 3.6 %collective-permute-start.8 = (bf16[8,5760]{1,0:T(8,128)(2,1)S(1)}, bf16[8,5760]{1,0:T(8,128)(2,1)S(1)}, u32[]{:S(2)}, u32[]{:S(2)}) collective-permute-start(bf16[8,5760]{1,0:T(8,128)(2,1)S(1)} %get-tuple-element.37.part0), channel_id=1, source_target_pairs={{0,3},{1,2},{2,1},{3,0},{4,7},{5,6},{6,5},{7,4},{8,11},{9,10},{10,... | collective-permute-start | bytes 276488 | tf_op jit(solution)/shard_map/ppermute | solution.py:549
  42.1 0.6 %collective-permute-done.4 = bf16[104,128]{1,0:T(8,128)(2,1)S(1)} collective-permute-done((bf16[104,128]{1,0:T(8,128)(2,1)S(1)}, bf16[104,128]{1,0:T(8,128)(2,1)S(1)}, u32[]{:S(2)}, u32[]{:S(2)}) %collective-permute-start.4) | collective-permute-done | bytes 26656 | tf_op jit(solution)/shard_map/ppermute | solution.py:549
  42.8 0.0 collective-permute-done.3
  42.8 2.5 %collective-permute-start.6 = (f32[104,128]{1,0:T(8,128)S(1)}, f32[104,128]{1,0:T(8,128)S(1)}, u32[]{:S(2)}, u32[]{:S(2)}) collective-permute-start(f32[104,128]{1,0:T(8,128)S(1)} %add_add_fusion), channel_id=1, source_target_pairs={{0,8},{4,12},{8,0},{12,4},{16,24},{20,28},{24,16},{28,20},{1,9},{5... | collective-permute-start | bytes 159752 | tf_op jit(solution)/shard_map/ppermute | solution.py:549
  45.2 2.1 %collective-permute-start.10 = (bf16[8,5760]{1,0:T(8,128)(2,1)S(1)}, bf16[8,5760]{1,0:T(8,128)(2,1)S(1)}, u32[]{:S(2)}, u32[]{:S(2)}) collective-permute-start(bf16[8,5760]{1,0:T(8,128)(2,1)S(1)} %get-tuple-element.37.part0), channel_id=1, source_target_pairs={{0,2},{1,3},{2,0},{3,1},{4,6},{5,7},{6,4},{7,5},{8,10},{9,11},{10,... | collective-permute-start | bytes 276488 | tf_op jit(solution)/shard_map/ppermute | solution.py:549
  47.3 0.1 collective-permute-done.6
  47.4 2.7 %collective-permute-start.9 = (f32[104,128]{1,0:T(8,128)S(1)}, f32[104,128]{1,0:T(8,128)S(1)}, u32[]{:S(2)}, u32[]{:S(2)}) collective-permute-start(f32[104,128]{1,0:T(8,128)S(1)} %add.22), channel_id=1, source_target_pairs={{0,16},{4,20},{8,24},{12,28},{16,0},{20,4},{24,8},{28,12},{1,17},{... | collective-permute-start | bytes 159752 | tf_op jit(solution)/shard_map/ppermute | solution.py:549
  50.1 2.1 %collective-permute-done.9 = f32[104,128]{1,0:T(8,128)S(1)} collective-permute-done((f32[104,128]{1,0:T(8,128)S(1)}, f32[104,128]{1,0:T(8,128)S(1)}, u32[]{:S(2)}, u32[]{:S(2)}) %collective-permute-start.9) | collective-permute-done | bytes 53280 | tf_op jit(solution)/shard_map/ppermute | solution.py:549
  52.2 0.1 collective-permute-start.11
  52.3 0.9 %place.1 = f32[1,8,23040]{2,1,0:T(8,128)} custom-call(bf16[8,5760]{1,0:T(8,128)(2,1)S(1)} %get-tuple-element.37.part0, bf16[8,5760]{1,0:T(8,128)(2,1)S(1)} %collective-permute-done.7.part1, bf16[8,5760]{1,0:T(8,128)(2,1)S(1)} %collective-permute-done.10.part2, bf16[8,5760]{1,0:T(8,128)(2,1)S(1)} %collective-permute-done.8.part3), custom_call_target="tpu_custom_call" | custom-call | tf_op jit(solution)/shard_map/place/pallas_call | solution.py:675
  53.2 0.3 collective-permute-done.11.other
  53.5 0.8 %taps.1 = (f32[3,3,32,64]{3,2,1,0:T(8,128)}, f32[3,3,16,32]{3,2,1,0:T(8,128)}) custom-call(f32[104,128]{1,0:T(8,128)S(1)} %add.23.mine, f32[104,128]{1,0:T(8,128)S(1)} %collective-permute-done.11.other), custom_call_target="tpu_custom_call" | custom-call | tf_op jit(solution)/shard_map/taps/pallas_call | solution.py:683
  (26 shorter events, 0.1 us)
Async XLA Ops:
  0.6 5.9 %copy-start.2 = (s32[32,48]{1,0:T(8,128)S(1)}, s32[32,48]{1,0:T(8,128)}, u32[]{:S(2)}) copy-start(s32[32,48]{1,0:T(8,128)} %land_hbm.1) | copy-start | bytes 18436
  0.6 5.9 %copy-start = (bf16[1,32,23040]{2,1,0:T(8,128)(2,1)S(1)}, bf16[1,32,23040]{2,1,0:T(8,128)(2,1)}, u32[]{:S(2)}) copy-start(bf16[1,32,23040]{2,1,0:T(8,128)(2,1)} %targets_hbm.1) | copy-start | bytes 4423684
  0.7 5.9 %copy-start.1 = (bf16[1,8,23040]{2,1,0:T(8,128)(2,1)S(1)}, bf16[1,8,23040]{2,1,0:T(8,128)(2,1)}, u32[]{:S(2)}) copy-start(bf16[1,8,23040]{2,1,0:T(8,128)(2,1)} %latent_hbm.1) | copy-start | bytes 1105924
  0.7 5.9 %copy-start.5 = (f32[16]{0:T(128)S(1)}, f32[16]{0:T(128)}, u32[]{:S(2)}) copy-start(f32[16]{0:T(128)} %channel_weight.3) | copy-start | bytes 196
  0.7 5.9 %copy-start.4 = (f32[64]{0:T(128)S(1)}, f32[64]{0:T(128)}, u32[]{:S(2)}) copy-start(f32[64]{0:T(128)} %scale.3) | copy-start | bytes 772
  0.7 5.9 %copy-start.3 = (s32[8]{0:T(128)S(1)}, s32[8]{0:T(128)}, u32[]{:S(2)}) copy-start(s32[8]{0:T(128)} %seeds.3) | copy-start | bytes 100
  0.7 8.0 %copy-start.7 = (bf16[3,3,32,16]{2,3,1,0:T(8,128)(2,1)S(1)}, bf16[3,3,32,16]{2,3,1,0:T(8,128)(2,1)}, u32[]{:S(2)}) copy-start(bf16[3,3,32,16]{2,3,1,0:T(8,128)(2,1)} %param.12) | copy-start | bytes 27652
  0.7 8.0 %copy-start.6 = (bf16[3,3,64,32]{2,3,1,0:T(8,128)(2,1)S(1)}, bf16[3,3,64,32]{2,3,1,0:T(8,128)(2,1)}, u32[]{:S(2)}) copy-start(bf16[3,3,64,32]{2,3,1,0:T(8,128)(2,1)} %param.11) | copy-start | bytes 110596
  2.9 7.8 %collective-permute-start = (bf16[50,8,128]{2,1,0:T(8,128)(2,1)}, bf16[50,8,128]{2,1,0:T(8,128)(2,1)S(1)}, u32[]{:S(2)}, u32[]{:S(2)}) collective-permute-start(bf16[50,8,128]{2,1,0:T(8,128)(2,1)} %get-tuple-element.29), channel_id=1, source_target_pairs={{0,4},{4,8},{8,12},{12,16},{16,20},{20,24},{24,28},{1,5},{5,9},{9,... | collective-permute-start | bytes 307208 | tf_op jit(solution)/shard_map/ppermute | solution.py:24
  5.2 5.4 %collective-permute-start.1 = (bf16[1,6400]{1,0:T(2,128)(2,1)}, bf16[1,6400]{1,0:T(2,128)(2,1)S(1)}, u32[]{:S(2)}, u32[]{:S(2)}) collective-permute-start(bf16[1,6400]{1,0:T(2,128)(2,1)} %get-tuple-element.30), channel_id=1, source_target_pairs={{4,0},{8,4},{12,8},{16,12},{20,16},{24,20},{28,24},{5,1},{9,5},{13... | collective-permute-start | bytes 38408 | tf_op jit(solution)/shard_map/ppermute | solution.py:24
  30.5 3.5 %collective-permute-start.2 = (f32[104,128]{1,0:T(8,128)S(1)}, f32[104,128]{1,0:T(8,128)S(1)}, u32[]{:S(2)}, u32[]{:S(2)}) collective-permute-start(f32[104,128]{1,0:T(8,128)S(1)} %get-tuple-element.39), channel_id=1, source_target_pairs={{0,4},{4,0},{8,12},{12,8},{16,20},{20,16},{24,28},{28,24},{1,5},{5... | collective-permute-start | bytes 159752 | tf_op jit(solution)/shard_map/ppermute | solution.py:549
  34.1 8.1 %collective-permute-start.5 = (bf16[104,128]{1,0:T(8,128)(2,1)S(1)}, bf16[104,128]{1,0:T(8,128)(2,1)S(1)}, u32[]{:S(2)}, u32[]{:S(2)}) collective-permute-start(bf16[104,128]{1,0:T(8,128)(2,1)S(1)} %add_convert_fusion), channel_id=1, source_target_pairs={{0,3},{1,2},{2,1},{3,0},{4,7},{5,6},{6,5},{7,4},{8,11},{9,10},{10,... | collective-permute-start | bytes 79880 | tf_op jit(solution)/shard_map/ppermute | solution.py:549
  37.8 5.0 %collective-permute-start.4 = (bf16[104,128]{1,0:T(8,128)(2,1)S(1)}, bf16[104,128]{1,0:T(8,128)(2,1)S(1)}, u32[]{:S(2)}, u32[]{:S(2)}) collective-permute-start(bf16[104,128]{1,0:T(8,128)(2,1)S(1)} %add_convert_fusion), channel_id=1, source_target_pairs={{0,2},{1,3},{2,0},{3,1},{4,6},{5,7},{6,4},{7,5},{8,10},{9,11},{10,... | collective-permute-start | bytes 79880 | tf_op jit(solution)/shard_map/ppermute | solution.py:549
  37.8 5.0 %collective-permute-start.3 = (bf16[104,128]{1,0:T(8,128)(2,1)S(1)}, bf16[104,128]{1,0:T(8,128)(2,1)S(1)}, u32[]{:S(2)}, u32[]{:S(2)}) collective-permute-start(bf16[104,128]{1,0:T(8,128)(2,1)S(1)} %add_convert_fusion), channel_id=1, source_target_pairs={{0,1},{1,0},{2,3},{3,2},{4,5},{5,4},{6,7},{7,6},{8,9},{9,8},{10,11... | collective-permute-start | bytes 79880 | tf_op jit(solution)/shard_map/ppermute | solution.py:549
  38.5 8.8 %collective-permute-start.8 = (bf16[8,5760]{1,0:T(8,128)(2,1)S(1)}, bf16[8,5760]{1,0:T(8,128)(2,1)S(1)}, u32[]{:S(2)}, u32[]{:S(2)}) collective-permute-start(bf16[8,5760]{1,0:T(8,128)(2,1)S(1)} %get-tuple-element.37.part0), channel_id=1, source_target_pairs={{0,3},{1,2},{2,1},{3,0},{4,7},{5,6},{6,5},{7,4},{8,11},{9,10},{10,... | collective-permute-start | bytes 276488 | tf_op jit(solution)/shard_map/ppermute | solution.py:549
  42.1 5.2 %collective-permute-start.7 = (bf16[8,5760]{1,0:T(8,128)(2,1)S(1)}, bf16[8,5760]{1,0:T(8,128)(2,1)S(1)}, u32[]{:S(2)}, u32[]{:S(2)}) collective-permute-start(bf16[8,5760]{1,0:T(8,128)(2,1)S(1)} %get-tuple-element.37.part0), channel_id=1, source_target_pairs={{0,1},{1,0},{2,3},{3,2},{4,5},{5,4},{6,7},{7,6},{8,9},{9,8},{10,11... | collective-permute-start | bytes 276488 | tf_op jit(solution)/shard_map/ppermute | solution.py:549
  42.8 4.6 %collective-permute-start.6 = (f32[104,128]{1,0:T(8,128)S(1)}, f32[104,128]{1,0:T(8,128)S(1)}, u32[]{:S(2)}, u32[]{:S(2)}) collective-permute-start(f32[104,128]{1,0:T(8,128)S(1)} %add_add_fusion), channel_id=1, source_target_pairs={{0,8},{4,12},{8,0},{12,4},{16,24},{20,28},{24,16},{28,20},{1,9},{5... | collective-permute-start | bytes 159752 | tf_op jit(solution)/shard_map/ppermute | solution.py:549
  45.2 7.0 %collective-permute-start.10 = (bf16[8,5760]{1,0:T(8,128)(2,1)S(1)}, bf16[8,5760]{1,0:T(8,128)(2,1)S(1)}, u32[]{:S(2)}, u32[]{:S(2)}) collective-permute-start(bf16[8,5760]{1,0:T(8,128)(2,1)S(1)} %get-tuple-element.37.part0), channel_id=1, source_target_pairs={{0,2},{1,3},{2,0},{3,1},{4,6},{5,7},{6,4},{7,5},{8,10},{9,11},{10,... | collective-permute-start | bytes 276488 | tf_op jit(solution)/shard_map/ppermute | solution.py:549
  47.4 4.8 %collective-permute-start.9 = (f32[104,128]{1,0:T(8,128)S(1)}, f32[104,128]{1,0:T(8,128)S(1)}, u32[]{:S(2)}, u32[]{:S(2)}) collective-permute-start(f32[104,128]{1,0:T(8,128)S(1)} %add.22), channel_id=1, source_target_pairs={{0,16},{4,20},{8,24},{12,28},{16,0},{20,4},{24,8},{28,12},{1,17},{... | collective-permute-start | bytes 159752 | tf_op jit(solution)/shard_map/ppermute | solution.py:549
  52.2 1.3 %collective-permute-start.11 = (f32[104,128]{1,0:T(8,128)S(1)}, f32[104,128]{1,0:T(8,128)S(1)}, u32[]{:S(2)}, u32[]{:S(2)}) collective-permute-start(f32[104,128]{1,0:T(8,128)S(1)} %add.23.mine), channel_id=1, source_target_pairs={{0,4},{4,0},{8,12},{12,8},{16,20},{20,16},{24,28},{28,24},{1,5},{5... | collective-permute-start | bytes 159752 | tf_op jit(solution)/shard_map/ppermute | solution.py:549

commit v20 on v17

--- a/solution.py
+++ b/solution.py
@@ -379,17 +379,17 @@
         taken = jnp.concatenate([operand(source, 2 * pair + k, 0, wide) for k in range(2)], axis=0)
         pre[...] = jnp.dot(taken, band_one[...], preferred_element_type=f32)
 
-    def first_gelu(pair, pre):
+    def first_gelu(pair, pre, last=False):
         for k in range(2):
             for t in range(wide):
-                for sub in range(2):
+                for sub in range(1 if last and k == 1 else 2):
                     at = (k * wide + t) * 16
                     x = pre[at : at + 16, sub * LANES : (sub + 1) * LANES]
                     square = x * x
                     th = jnp.tanh(x * (GELU_A + (GELU_A * GELU_B) * square))
                     plus = 0.5 + 0.5 * th
                     act[4 * pair + 2 * k + sub, t] = (x * plus).astype(bf16)
-                    if t < front:
+                    if t < front and not (last and k == 1):
                         d = plus + (x * plus) * (1.0 - th) * (GELU_A + (3.0 * GELU_A * GELU_B) * square)
                         if t == half:
                             d = jnp.where(iota((16, LANES), 0) < 8, d, 0.0)
@@ -404,7 +404,7 @@
 
     first_product(0, pre_even)
     lax.fori_loop(0, rows // 4, first_segment, 0)
-    first_gelu(rows // 2, pre_even)
+    first_gelu(rows // 2, pre_even, last=True)
 
     members = front * 16
     owner = iota((48, members), 0)

time: 53.9 us -> 53.9 us (level)
  no operation moved by 1% of the time
where the time goes in v20:
time: 53.9 us; the launch traced here: 53.7 us
  Pallas kernels  25.6 us (47%)
  starting transfers between devices  21.6 us (40%)
  waiting for transfers between devices  5.57 us (10%)
  between operations  0.85 us (2%)
    pallas_call x1, Pallas kernels, local(): pl.pallas_call(functools.partial(band_kernel, half, (chan0, chan1, chan2)...  19.3 us
    ppermute x10, starting transfers between devices, swapped(): lax.ppermute(array, axis, [(i, i ^ bit) for i in range(lax.axis_size(axis...  18 us
    ppermute x10, waiting for transfers between devices, swapped(): lax.ppermute(array, axis, [(i, i ^ bit) for i in range(lax.axis_size(axis...  3.98 us
    ppermute x2, starting transfers between devices, shifted(): return lax.ppermute(array, axis, pairs)  3.65 us
    pallas_call x1, Pallas kernels, local(): pl.pallas_call(functools.partial(prepare_kernel, half, chan0, chan2), in_...  2.13 us
    pallas_call x1, Pallas kernels, local(): pl.pallas_call(functools.partial(edge_kernel, half, chan2), in_specs=[hbm...  2.13 us
    ppermute x2, waiting for transfers between devices, shifted(): return lax.ppermute(array, axis, pairs)  1.58 us
  transfers between devices with their start and end apart: 12, of which 6 were waited for; matrix products, arithmetic and copies ran while one was open for 0% of the time, Pallas kernels for 6%

profile of v20, /device:TPU:0, one launch (start us, length us, event | category | flops | bytes accessed | tf_op | source)
XLA Modules:
  0.0 53.7 jit_solution(10354053433284165844)
XLA Ops:
  0.7 2.1 %edges.1 = (bf16[50,8,128]{2,1,0:T(8,128)(2,1)}, bf16[1,6400]{1,0:T(2,128)(2,1)}) custom-call(bf16[1,8,23040]{2,1,0:T(8,128)(2,1)} %latent_hbm.1, bf16[1,32,23040]{2,1,0:T(8,128)(2,1)} %targets_hbm.1, s32[32,48]{1,0:T(8,128)} %land_hbm.1), custom_call_target="tpu_custom_call" | custom-call | tf_op jit(solution)/shard_map/edges/pallas_call | solution.py:578
  2.9 2.4 %collective-permute-start = (bf16[50,8,128]{2,1,0:T(8,128)(2,1)}, bf16[50,8,128]{2,1,0:T(8,128)(2,1)S(1)}, u32[]{:S(2)}, u32[]{:S(2)}) collective-permute-start(bf16[50,8,128]{2,1,0:T(8,128)(2,1)} %get-tuple-element.29), channel_id=1, source_target_pairs={{0,4},{4,8},{8,12},{12,16},{16,20},{20,24},{24,28},{1,5},{5,9},{9,... | collective-permute-start | bytes 307208 | tf_op jit(solution)/shard_map/ppermute | solution.py:24
  5.2 1.3 %collective-permute-start.1 = (bf16[1,6400]{1,0:T(2,128)(2,1)}, bf16[1,6400]{1,0:T(2,128)(2,1)S(1)}, u32[]{:S(2)}, u32[]{:S(2)}) collective-permute-start(bf16[1,6400]{1,0:T(2,128)(2,1)} %get-tuple-element.30), channel_id=1, source_target_pairs={{4,0},{8,4},{12,8},{16,12},{20,16},{24,20},{28,24},{5,1},{9,5},{13... | collective-permute-start | bytes 38408 | tf_op jit(solution)/shard_map/ppermute | solution.py:24
  6.6 2.1 %prepare.1 = (bf16[8,25,16,128]{3,2,1,0:T(8,128)(2,1)S(1)}, f32[48,32,128]{2,1,0:T(8,128)S(1)}, f32[48,32,128]{2,1,0:T(8,128)S(1)}) custom-call(s32[8]{0:T(128)S(1)} %copy-done.3, f32[64]{0:T(128)S(1)} %copy-done.4, f32[16]{0:T(128)S(1)} %copy-done.5, bf16[1,8,23040]{2,1,0:T(8,128)(2,1)S(1)} %copy-done.1, bf16[1,32,23040]{2,1,0:T(8,128)(2,1)S(1)} %copy-done, ...), custom_call_target="tpu_custom_call" | custom-call | flops 100000000 | bytes 10000000 | tf_op jit(solution)/shard_map/prepare/pallas_call | solution.py:598
  8.7 0.3 bands.1
  9.0 1.6 %collective-permute-done.1.below = bf16[1,6400]{1,0:T(2,128)(2,1)S(1)} collective-permute-done((bf16[1,6400]{1,0:T(2,128)(2,1)}, bf16[1,6400]{1,0:T(2,128)(2,1)S(1)}, u32[]{:S(2)}, u32[]{:S(2)}) %collective-permute-start.1) | collective-permute-done | bytes 12832 | tf_op jit(solution)/shard_map/ppermute | solution.py:24
  10.6 19.3 %band.1 = (bf16[8,5760]{1,0:T(8,128)(2,1)S(1)}, f32[104,128]{1,0:T(8,128)S(1)}, f32[104,128]{1,0:T(8,128)S(1)}) custom-call(s32[8]{0:T(128)S(1)} %copy-done.3, f32[64]{0:T(128)S(1)} %copy-done.4, f32[16]{0:T(128)S(1)} %copy-done.5, bf16[8,25,16,128]{3,2,1,0:T(8,128)(2,1)S(1)} %get-tuple-element.26.own_source, f32[48,32,128]{2,1,0:T(8,128)S(1)} %get-tuple-element.27.aims, ...), custom_call_target="tpu_custom_call" | custom-call | tf_op jit(solution)/shard_map/band/pallas_call | solution.py:621
  29.9 2.6 %collective-permute-start.2 = (f32[104,128]{1,0:T(8,128)S(1)}, f32[104,128]{1,0:T(8,128)S(1)}, u32[]{:S(2)}, u32[]{:S(2)}) collective-permute-start(f32[104,128]{1,0:T(8,128)S(1)} %get-tuple-element.39), channel_id=1, source_target_pairs={{0,4},{4,0},{8,12},{12,8},{16,20},{20,16},{24,28},{28,24},{1,5},{5... | collective-permute-start | bytes 159752 | tf_op jit(solution)/shard_map/ppermute | solution.py:551
  32.6 0.9 %collective-permute-done.2 = f32[104,128]{1,0:T(8,128)S(1)} collective-permute-done((f32[104,128]{1,0:T(8,128)S(1)}, f32[104,128]{1,0:T(8,128)S(1)}, u32[]{:S(2)}, u32[]{:S(2)}) %collective-permute-start.2) | collective-permute-done | bytes 53280 | tf_op jit(solution)/shard_map/ppermute | solution.py:551
  33.5 3.7 %collective-permute-start.5 = (bf16[104,128]{1,0:T(8,128)(2,1)S(1)}, bf16[104,128]{1,0:T(8,128)(2,1)S(1)}, u32[]{:S(2)}, u32[]{:S(2)}) collective-permute-start(bf16[104,128]{1,0:T(8,128)(2,1)S(1)} %add_convert_fusion), channel_id=1, source_target_pairs={{0,3},{1,2},{2,1},{3,0},{4,7},{5,6},{6,5},{7,4},{8,11},{9,10},{10,... | collective-permute-start | bytes 79880 | tf_op jit(solution)/shard_map/ppermute | solution.py:551
  37.1 0.8 %collective-permute-start.3 = (bf16[104,128]{1,0:T(8,128)(2,1)S(1)}, bf16[104,128]{1,0:T(8,128)(2,1)S(1)}, u32[]{:S(2)}, u32[]{:S(2)}) collective-permute-start(bf16[104,128]{1,0:T(8,128)(2,1)S(1)} %add_convert_fusion), channel_id=1, source_target_pairs={{0,1},{1,0},{2,3},{3,2},{4,5},{5,4},{6,7},{7,6},{8,9},{9,8},{10,11... | collective-permute-start | bytes 79880 | tf_op jit(solution)/shard_map/ppermute | solution.py:551
  37.9 3.6 %collective-permute-start.8 = (bf16[8,5760]{1,0:T(8,128)(2,1)S(1)}, bf16[8,5760]{1,0:T(8,128)(2,1)S(1)}, u32[]{:S(2)}, u32[]{:S(2)}) collective-permute-start(bf16[8,5760]{1,0:T(8,128)(2,1)S(1)} %get-tuple-element.37.part0), channel_id=1, source_target_pairs={{0,3},{1,2},{2,1},{3,0},{4,7},{5,6},{6,5},{7,4},{8,11},{9,10},{10,... | collective-permute-start | bytes 276488 | tf_op jit(solution)/shard_map/ppermute | solution.py:551
  41.5 0.6 %collective-permute-done.4 = bf16[104,128]{1,0:T(8,128)(2,1)S(1)} collective-permute-done((bf16[104,128]{1,0:T(8,128)(2,1)S(1)}, bf16[104,128]{1,0:T(8,128)(2,1)S(1)}, u32[]{:S(2)}, u32[]{:S(2)}) %collective-permute-start.4) | collective-permute-done | bytes 26656 | tf_op jit(solution)/shard_map/ppermute | solution.py:551
  42.2 0.0 collective-permute-done.3
  42.2 2.5 %collective-permute-start.6 = (f32[104,128]{1,0:T(8,128)S(1)}, f32[104,128]{1,0:T(8,128)S(1)}, u32[]{:S(2)}, u32[]{:S(2)}) collective-permute-start(f32[104,128]{1,0:T(8,128)S(1)} %add_add_fusion), channel_id=1, source_target_pairs={{0,8},{4,12},{8,0},{12,4},{16,24},{20,28},{24,16},{28,20},{1,9},{5... | collective-permute-start | bytes 159752 | tf_op jit(solution)/shard_map/ppermute | solution.py:551
  44.6 2.1 %collective-permute-start.10 = (bf16[8,5760]{1,0:T(8,128)(2,1)S(1)}, bf16[8,5760]{1,0:T(8,128)(2,1)S(1)}, u32[]{:S(2)}, u32[]{:S(2)}) collective-permute-start(bf16[8,5760]{1,0:T(8,128)(2,1)S(1)} %get-tuple-element.37.part0), channel_id=1, source_target_pairs={{0,2},{1,3},{2,0},{3,1},{4,6},{5,7},{6,4},{7,5},{8,10},{9,11},{10,... | collective-permute-start | bytes 276488 | tf_op jit(solution)/shard_map/ppermute | solution.py:551
  46.7 0.1 collective-permute-done.6
  46.8 0.0 collective-permute-done.7.part1
  46.8 2.7 %collective-permute-start.9 = (f32[104,128]{1,0:T(8,128)S(1)}, f32[104,128]{1,0:T(8,128)S(1)}, u32[]{:S(2)}, u32[]{:S(2)}) collective-permute-start(f32[104,128]{1,0:T(8,128)S(1)} %add.22), channel_id=1, source_target_pairs={{0,16},{4,20},{8,24},{12,28},{16,0},{20,4},{24,8},{28,12},{1,17},{... | collective-permute-start | bytes 159752 | tf_op jit(solution)/shard_map/ppermute | solution.py:551
  49.5 2.1 %collective-permute-done.9 = f32[104,128]{1,0:T(8,128)S(1)} collective-permute-done((f32[104,128]{1,0:T(8,128)S(1)}, f32[104,128]{1,0:T(8,128)S(1)}, u32[]{:S(2)}, u32[]{:S(2)}) %collective-permute-start.9) | collective-permute-done | bytes 53280 | tf_op jit(solution)/shard_map/ppermute | solution.py:551
  51.6 0.1 collective-permute-start.11
  51.7 0.9 %place.1 = f32[1,8,23040]{2,1,0:T(8,128)} custom-call(bf16[8,5760]{1,0:T(8,128)(2,1)S(1)} %get-tuple-element.37.part0, bf16[8,5760]{1,0:T(8,128)(2,1)S(1)} %collective-permute-done.7.part1, bf16[8,5760]{1,0:T(8,128)(2,1)S(1)} %collective-permute-done.10.part2, bf16[8,5760]{1,0:T(8,128)(2,1)S(1)} %collective-permute-done.8.part3), custom_call_target="tpu_custom_call" | custom-call | tf_op jit(solution)/shard_map/place/pallas_call | solution.py:677
  52.6 0.3 collective-permute-done.11.other
  52.9 0.8 %taps.1 = (f32[3,3,32,64]{3,2,1,0:T(8,128)}, f32[3,3,16,32]{3,2,1,0:T(8,128)}) custom-call(f32[104,128]{1,0:T(8,128)S(1)} %add.23.mine, f32[104,128]{1,0:T(8,128)S(1)} %collective-permute-done.11.other), custom_call_target="tpu_custom_call" | custom-call | tf_op jit(solution)/shard_map/taps/pallas_call | solution.py:685
  (26 shorter events, 0.1 us)
Async XLA Ops:
  0.6 5.9 %copy-start.2 = (s32[32,48]{1,0:T(8,128)S(1)}, s32[32,48]{1,0:T(8,128)}, u32[]{:S(2)}) copy-start(s32[32,48]{1,0:T(8,128)} %land_hbm.1) | copy-start | bytes 18436
  0.6 5.9 %copy-start = (bf16[1,32,23040]{2,1,0:T(8,128)(2,1)S(1)}, bf16[1,32,23040]{2,1,0:T(8,128)(2,1)}, u32[]{:S(2)}) copy-start(bf16[1,32,23040]{2,1,0:T(8,128)(2,1)} %targets_hbm.1) | copy-start | bytes 4423684
  0.7 5.9 %copy-start.1 = (bf16[1,8,23040]{2,1,0:T(8,128)(2,1)S(1)}, bf16[1,8,23040]{2,1,0:T(8,128)(2,1)}, u32[]{:S(2)}) copy-start(bf16[1,8,23040]{2,1,0:T(8,128)(2,1)} %latent_hbm.1) | copy-start | bytes 1105924
  0.7 5.9 %copy-start.5 = (f32[16]{0:T(128)S(1)}, f32[16]{0:T(128)}, u32[]{:S(2)}) copy-start(f32[16]{0:T(128)} %channel_weight.3) | copy-start | bytes 196
  0.7 5.9 %copy-start.4 = (f32[64]{0:T(128)S(1)}, f32[64]{0:T(128)}, u32[]{:S(2)}) copy-start(f32[64]{0:T(128)} %scale.3) | copy-start | bytes 772
  0.7 5.9 %copy-start.3 = (s32[8]{0:T(128)S(1)}, s32[8]{0:T(128)}, u32[]{:S(2)}) copy-start(s32[8]{0:T(128)} %seeds.3) | copy-start | bytes 100
  0.7 8.0 %copy-start.7 = (bf16[3,3,32,16]{2,3,1,0:T(8,128)(2,1)S(1)}, bf16[3,3,32,16]{2,3,1,0:T(8,128)(2,1)}, u32[]{:S(2)}) copy-start(bf16[3,3,32,16]{2,3,1,0:T(8,128)(2,1)} %param.12) | copy-start | bytes 27652
  0.7 8.0 %copy-start.6 = (bf16[3,3,64,32]{2,3,1,0:T(8,128)(2,1)S(1)}, bf16[3,3,64,32]{2,3,1,0:T(8,128)(2,1)}, u32[]{:S(2)}) copy-start(bf16[3,3,64,32]{2,3,1,0:T(8,128)(2,1)} %param.11) | copy-start | bytes 110596
  2.9 7.8 %collective-permute-start = (bf16[50,8,128]{2,1,0:T(8,128)(2,1)}, bf16[50,8,128]{2,1,0:T(8,128)(2,1)S(1)}, u32[]{:S(2)}, u32[]{:S(2)}) collective-permute-start(bf16[50,8,128]{2,1,0:T(8,128)(2,1)} %get-tuple-element.29), channel_id=1, source_target_pairs={{0,4},{4,8},{8,12},{12,16},{16,20},{20,24},{24,28},{1,5},{5,9},{9,... | collective-permute-start | bytes 307208 | tf_op jit(solution)/shard_map/ppermute | solution.py:24
  5.2 5.4 %collective-permute-start.1 = (bf16[1,6400]{1,0:T(2,128)(2,1)}, bf16[1,6400]{1,0:T(2,128)(2,1)S(1)}, u32[]{:S(2)}, u32[]{:S(2)}) collective-permute-start(bf16[1,6400]{1,0:T(2,128)(2,1)} %get-tuple-element.30), channel_id=1, source_target_pairs={{4,0},{8,4},{12,8},{16,12},{20,16},{24,20},{28,24},{5,1},{9,5},{13... | collective-permute-start | bytes 38408 | tf_op jit(solution)/shard_map/ppermute | solution.py:24
  29.9 3.5 %collective-permute-start.2 = (f32[104,128]{1,0:T(8,128)S(1)}, f32[104,128]{1,0:T(8,128)S(1)}, u32[]{:S(2)}, u32[]{:S(2)}) collective-permute-start(f32[104,128]{1,0:T(8,128)S(1)} %get-tuple-element.39), channel_id=1, source_target_pairs={{0,4},{4,0},{8,12},{12,8},{16,20},{20,16},{24,28},{28,24},{1,5},{5... | collective-permute-start | bytes 159752 | tf_op jit(solution)/shard_map/ppermute | solution.py:551
  33.5 8.1 %collective-permute-start.5 = (bf16[104,128]{1,0:T(8,128)(2,1)S(1)}, bf16[104,128]{1,0:T(8,128)(2,1)S(1)}, u32[]{:S(2)}, u32[]{:S(2)}) collective-permute-start(bf16[104,128]{1,0:T(8,128)(2,1)S(1)} %add_convert_fusion), channel_id=1, source_target_pairs={{0,3},{1,2},{2,1},{3,0},{4,7},{5,6},{6,5},{7,4},{8,11},{9,10},{10,... | collective-permute-start | bytes 79880 | tf_op jit(solution)/shard_map/ppermute | solution.py:551
  37.1 5.0 %collective-permute-start.4 = (bf16[104,128]{1,0:T(8,128)(2,1)S(1)}, bf16[104,128]{1,0:T(8,128)(2,1)S(1)}, u32[]{:S(2)}, u32[]{:S(2)}) collective-permute-start(bf16[104,128]{1,0:T(8,128)(2,1)S(1)} %add_convert_fusion), channel_id=1, source_target_pairs={{0,2},{1,3},{2,0},{3,1},{4,6},{5,7},{6,4},{7,5},{8,10},{9,11},{10,... | collective-permute-start | bytes 79880 | tf_op jit(solution)/shard_map/ppermute | solution.py:551
  37.1 5.0 %collective-permute-start.3 = (bf16[104,128]{1,0:T(8,128)(2,1)S(1)}, bf16[104,128]{1,0:T(8,128)(2,1)S(1)}, u32[]{:S(2)}, u32[]{:S(2)}) collective-permute-start(bf16[104,128]{1,0:T(8,128)(2,1)S(1)} %add_convert_fusion), channel_id=1, source_target_pairs={{0,1},{1,0},{2,3},{3,2},{4,5},{5,4},{6,7},{7,6},{8,9},{9,8},{10,11... | collective-permute-start | bytes 79880 | tf_op jit(solution)/shard_map/ppermute | solution.py:551
  37.9 8.8 %collective-permute-start.8 = (bf16[8,5760]{1,0:T(8,128)(2,1)S(1)}, bf16[8,5760]{1,0:T(8,128)(2,1)S(1)}, u32[]{:S(2)}, u32[]{:S(2)}) collective-permute-start(bf16[8,5760]{1,0:T(8,128)(2,1)S(1)} %get-tuple-element.37.part0), channel_id=1, source_target_pairs={{0,3},{1,2},{2,1},{3,0},{4,7},{5,6},{6,5},{7,4},{8,11},{9,10},{10,... | collective-permute-start | bytes 276488 | tf_op jit(solution)/shard_map/ppermute | solution.py:551
  41.5 5.2 %collective-permute-start.7 = (bf16[8,5760]{1,0:T(8,128)(2,1)S(1)}, bf16[8,5760]{1,0:T(8,128)(2,1)S(1)}, u32[]{:S(2)}, u32[]{:S(2)}) collective-permute-start(bf16[8,5760]{1,0:T(8,128)(2,1)S(1)} %get-tuple-element.37.part0), channel_id=1, source_target_pairs={{0,1},{1,0},{2,3},{3,2},{4,5},{5,4},{6,7},{7,6},{8,9},{9,8},{10,11... | collective-permute-start | bytes 276488 | tf_op jit(solution)/shard_map/ppermute | solution.py:551
  42.2 4.6 %collective-permute-start.6 = (f32[104,128]{1,0:T(8,128)S(1)}, f32[104,128]{1,0:T(8,128)S(1)}, u32[]{:S(2)}, u32[]{:S(2)}) collective-permute-start(f32[104,128]{1,0:T(8,128)S(1)} %add_add_fusion), channel_id=1, source_target_pairs={{0,8},{4,12},{8,0},{12,4},{16,24},{20,28},{24,16},{28,20},{1,9},{5... | collective-permute-start | bytes 159752 | tf_op jit(solution)/shard_map/ppermute | solution.py:551
  44.6 7.0 %collective-permute-start.10 = (bf16[8,5760]{1,0:T(8,128)(2,1)S(1)}, bf16[8,5760]{1,0:T(8,128)(2,1)S(1)}, u32[]{:S(2)}, u32[]{:S(2)}) collective-permute-start(bf16[8,5760]{1,0:T(8,128)(2,1)S(1)} %get-tuple-element.37.part0), channel_id=1, source_target_pairs={{0,2},{1,3},{2,0},{3,1},{4,6},{5,7},{6,4},{7,5},{8,10},{9,11},{10,... | collective-permute-start | bytes 276488 | tf_op jit(solution)/shard_map/ppermute | solution.py:551
  46.8 4.8 %collective-permute-start.9 = (f32[104,128]{1,0:T(8,128)S(1)}, f32[104,128]{1,0:T(8,128)S(1)}, u32[]{:S(2)}, u32[]{:S(2)}) collective-permute-start(f32[104,128]{1,0:T(8,128)S(1)} %add.22), channel_id=1, source_target_pairs={{0,16},{4,20},{8,24},{12,28},{16,0},{20,4},{24,8},{28,12},{1,17},{... | collective-permute-start | bytes 159752 | tf_op jit(solution)/shard_map/ppermute | solution.py:551
  51.6 1.3 %collective-permute-start.11 = (f32[104,128]{1,0:T(8,128)S(1)}, f32[104,128]{1,0:T(8,128)S(1)}, u32[]{:S(2)}, u32[]{:S(2)}) collective-permute-start(f32[104,128]{1,0:T(8,128)S(1)} %add.23.mine), channel_id=1, source_target_pairs={{0,4},{4,0},{8,12},{12,8},{16,20},{20,16},{24,28},{28,24},{1,5},{5... | collective-permute-start | bytes 159752 | tf_op jit(solution)/shard_map/ppermute | solution.py:551
